TPU v7x, 32 devices: a whole 2x2x4 slice. The times are simulated.
32 devices in a mesh: seq: 8 (over z, y), head: 4 (over x, core).
Axes of the slice: x: 2, y: 2, z: 4, core: 2. Of those that a mesh axis runs over, the one named last changes fastest.
Arguments:
- queries: bfloat16 [1024, 8192], P('seq', 'head'), may hold values from -6 to 6
- key_vectors: bfloat16 [1024, 8192], P('seq', 'head'), may hold values from -6 to 6
- value_vectors: bfloat16 [1024, 8192], P('seq', 'head'), may hold values from -6 to 6
- log_decay: float32 [1024, 64], P('seq', 'head'), may hold values from -2 to 0
- doc_ids: int32 [1024], P('seq'), may hold values from 0 to 3, as said below
- head_gain: float32 [8192], P('head'), may hold values from 0.4 to 1.6
- output_weight: bfloat16 [8192, 3072], P('head', 'seq'), may hold values from -0.0625 to 0.0625
- residual: bfloat16 [1024, 3072], P('seq', 'head'), may hold values from -8 to 8
- norm_gain: float32 [3072], replicated, may hold values from 0.4 to 1.6
- routing: int32 [1024, 2], P('seq'), may hold values from 0 to 7, all different within a row; in each aligned block of 128 rows (0 to 127, 128 to 255, ...) at most 64 rows name the same one
- route_weights: float32 [1024, 2], P('seq'), may hold values from 0.1 to 1
- gate_weight: bfloat16 [8, 3072, 4608], P('seq', None, 'head'), may hold values from -0.109375 to 0.109375
- up_weight: bfloat16 [8, 3072, 4608], P('seq', None, 'head'), may hold values from -0.109375 to 0.109375
- down_weight: bfloat16 [8, 4608, 3072], P('seq', 'head'), may hold values from -0.09375 to 0.09375
Outputs:
- mixed: bfloat16 [1024, 3072], P('seq', 'head')
Inputs may be any that keep to these rules, and one draw needn't show every extreme that they name: `doc_ids`: ids never fall along the sequence and rise by one where a document starts; every id occurs. `routing`: the two experts of a position differ; among the rows of one index of seq no expert is named more than 64 times.
All inputs are finite; a program needn't handle non-finite values.
Results may differ from a plain program's by a relative error of at most 0.014.
Values may be sent and summed in bfloat16 or wider, within the bound.
No kernel may reach another device: no remote copies, remote signals or barrier semaphores. Data moves between devices by JAX's collectives and lax.ppermute only.
A program may use at most 128 MiB of HBM per device.

v0:
```python
import jax
import jax.numpy as jnp
from jax import lax
from jax.sharding import PartitionSpec as P

EPSILON = 1e-06
FULL_PRECISION = lax.Precision.HIGHEST


def carried_in(value, axis, join, neutral):
    count, mine = (lax.axis_size(axis), lax.axis_index(axis))
    pieces = jax.tree.map(lambda part: lax.all_gather(part, axis), value)
    running = jax.tree.map(
        lambda part, zero: jnp.full_like(part, 0) + jnp.asarray(zero, part.dtype), value, neutral
    )

    def lap(position, running):
        longer = join(running, jax.tree.map(lambda part: part[position], pieces))
        return jax.tree.map(lambda new, old: jnp.where(position < mine, new, old), longer, running)

    return lax.fori_loop(0, count - 1, lap, running)


def link_summaries(earlier, later):
    gain_early, state_early, first_early, last_early = earlier
    gain_late, state_late, first_late, last_late = later
    joined = (first_late == last_early) | (last_early < 0.0) | (first_late < 0.0)
    through = gain_late * joined.astype(jnp.float32)
    return (
        gain_early * through,
        through[:, None, None] * state_early + state_late,
        jnp.where(first_early < 0.0, first_late, first_early),
        jnp.where(last_late < 0.0, last_early, last_late),
    )


def shards(
    queries,
    key_vectors,
    value_vectors,
    log_decay,
    doc_ids,
    head_gain,
    output_weight,
    residual,
    norm_gain,
    routing,
    route_weights,
    gate_weight,
    up_weight,
    down_weight,
):
    tokens, heads = log_decay.shape
    head_width = queries.shape[1] // heads
    query_heads = queries.reshape(tokens, heads, head_width)
    key_heads = key_vectors.reshape(tokens, heads, head_width)
    value_heads = value_vectors.reshape(tokens, heads, head_width)
    decay_sum = jnp.cumsum(log_decay, axis=0)
    decay_rows = decay_sum.T
    gap_matrix = decay_rows[:, :, None] - decay_rows[:, None, :]
    row_index = lax.broadcasted_iota(jnp.int32, (tokens, tokens), 0)
    col_index = lax.broadcasted_iota(jnp.int32, (tokens, tokens), 1)
    kept_mask = (col_index <= row_index) & (doc_ids[:, None] == doc_ids[None, :])
    decay_matrix = jnp.where(kept_mask[None], jnp.exp(jnp.minimum(gap_matrix, 0.0)), 0.0)
    scores = jnp.einsum("thd,shd->hts", query_heads, key_heads, preferred_element_type=jnp.float32)
    weighted = (scores * decay_matrix).astype(jnp.bfloat16)
    inside = jnp.einsum("hts,shd->thd", weighted, value_heads, preferred_element_type=jnp.float32)
    doc_float = doc_ids.astype(jnp.float32)
    tail_gain = (
        jnp.exp(decay_sum[-1][None, :] - decay_sum)
        * (doc_ids == doc_ids[-1]).astype(jnp.float32)[:, None]
    )
    own_state = jnp.einsum(
        "thd,the->hde",
        key_heads.astype(jnp.float32) * tail_gain[:, :, None],
        value_heads.astype(jnp.float32),
        precision=FULL_PRECISION,
    )
    own_gain = jnp.exp(decay_sum[-1]) * (doc_ids[0] == doc_ids[-1]).astype(jnp.float32)
    summary = (own_gain, own_state, doc_float[:1], doc_float[-1:])
    identity = (
        jnp.ones((heads,), jnp.float32),
        jnp.zeros_like(own_state),
        jnp.full((1,), -1.0, jnp.float32),
        jnp.full((1,), -1.0, jnp.float32),
    )
    _, entered, _, before = carried_in(summary, "seq", link_summaries, identity)
    reach_gain = jnp.exp(decay_sum) * (doc_float == before[0]).astype(jnp.float32)[:, None]
    outside = (
        jnp.einsum(
            "thd,hde->the", query_heads.astype(jnp.float32), entered, precision=FULL_PRECISION
        )
        * reach_gain[:, :, None]
    )
    heads_raw = inside + outside
    inv_norm = lax.rsqrt(jnp.mean(heads_raw * heads_raw, axis=2, keepdims=True) + EPSILON)
    attended = ((heads_raw * inv_norm).reshape(tokens, heads * head_width) * head_gain).astype(
        jnp.bfloat16
    )
    partial_value = jnp.dot(
        attended,
        lax.all_gather(output_weight, "seq", axis=1, tiled=True),
        preferred_element_type=jnp.float32,
    )
    model_width = partial_value.shape[1]
    head_count = lax.axis_size("head")
    part_width = model_width // head_count
    offset = lax.axis_index("head") * part_width
    summed = lax.psum_scatter(
        partial_value.astype(jnp.bfloat16), "head", scatter_dimension=1, tiled=True
    ).astype(jnp.float32)
    middle = lax.optimization_barrier((summed + residual.astype(jnp.float32)).astype(jnp.bfloat16))
    middle_float = middle.astype(jnp.float32)
    squares = lax.psum(jnp.sum(middle_float * middle_float, axis=1), "head")
    row_norm = lax.rsqrt(squares / model_width + EPSILON)[:, None]
    gain_part = lax.dynamic_slice_in_dim(norm_gain, offset, part_width, 0)
    normed_part = (middle_float * row_norm * gain_part).astype(jnp.bfloat16)
    experts = lax.axis_size("seq")
    capacity = 4 * tokens // experts
    flat_ids = routing.reshape(-1)
    hit_table = (flat_ids[:, None] == jnp.arange(experts, dtype=jnp.int32)[None, :]).astype(
        jnp.int32
    )
    slot_rank = jnp.sum((jnp.cumsum(hit_table, axis=0) - 1) * hit_table, axis=1)
    slot_place = flat_ids * capacity + slot_rank
    owner_row = jnp.arange(2 * tokens, dtype=jnp.int32) // 2
    slot_table = jnp.full((experts * capacity,), tokens, jnp.int32).at[slot_place].set(owner_row)
    mix_weights = route_weights.reshape(-1)[:, None]
    gate_local = gate_weight[0]
    up_local = up_weight[0]
    down_local = down_weight[0]
    padded = jnp.concatenate([normed_part, jnp.zeros((1, part_width), jnp.bfloat16)], axis=0)
    outgoing = padded[slot_table].reshape(experts, capacity, part_width)
    gathered = lax.all_gather(
        lax.all_to_all(outgoing, "seq", split_axis=0, concat_axis=0, tiled=True),
        "head",
        axis=2,
        tiled=True,
    )
    sources = gathered.shape[0]
    slot_count = gathered.shape[1]
    row_block = gathered.reshape(sources * slot_count, model_width)
    gate_proj = jnp.dot(row_block, gate_local, preferred_element_type=jnp.float32)
    up_proj = jnp.dot(row_block, up_local, preferred_element_type=jnp.float32)
    hidden = (jax.nn.silu(gate_proj) * up_proj).astype(jnp.bfloat16)
    result = (
        jnp.dot(hidden, down_local, preferred_element_type=jnp.float32)
        .astype(jnp.bfloat16)
        .astype(jnp.float32)
    )
    summed_out = lax.psum_scatter(
        result.reshape(sources, slot_count, model_width).astype(jnp.bfloat16),
        "head",
        scatter_dimension=2,
        tiled=True,
    ).astype(jnp.float32)
    returned = lax.all_to_all(
        summed_out.astype(jnp.bfloat16), "seq", split_axis=0, concat_axis=0, tiled=True
    ).astype(summed_out.dtype)
    picked = returned.reshape(-1, part_width)[slot_place] * mix_weights
    expert_sum = jnp.sum(picked.reshape(tokens, 2, part_width), axis=1)
    return (middle_float + expert_sum).astype(jnp.bfloat16)


def solution(mesh):
    placed = (
        P("seq", "head"),
        P("seq", "head"),
        P("seq", "head"),
        P("seq", "head"),
        P("seq"),
        P("head"),
        P("head", "seq"),
        P("seq", "head"),
        P(),
        P("seq", None),
        P("seq", None),
        P("seq", None, "head"),
        P("seq", None, "head"),
        P("seq", "head", None),
    )
    return jax.shard_map(
        shards, mesh=mesh, in_specs=placed, out_specs=P("seq", "head"), check_vma=False
    )
```

profile of v0, /device:TPU:0, one launch (start us, length us, event | category | flops | bytes accessed | tf_op | source)
XLA Modules:
  0.0 507.5 jit_solution(2142257175020821645)
XLA Ops:
  7.4 1.3 fusion.57
  8.7 1.3 compare_convert_fusion.1
  11.7 1.3 copy.57
  13.1 1.6 fusion.22
  17.7 23.6 %all-reduce.3 = (f32[8]{0:T(128)S(1)}, f32[8]{0:T(128)S(1)}) all-reduce(f32[8]{0:T(128)S(1)} %slice_dynamic-update-slice_fusion.1, f32[8]{0:T(128)S(1)} %slice_dynamic-update-slice_fusion), channel_id=2, replica_groups=mesh['seq'=8,'head'=4] {'seq'}, use_global_device_ids=true, to_apply=%add.1 | all-reduce | flops 16 | bytes 128
  41.4 16.4 %all-gather.3 = f32[8,1,16]{2,1,0:T(1,128)S(1)} all-gather(f32[1,1,16]{2,1,0:T(1,128)S(1)} %get-tuple-element.195), channel_id=1, replica_groups=mesh['seq'=8,'head'=4] {'seq'}, dimensions={0}, use_global_device_ids=true | all-gather | bytes 576 | tf_op jit(solution)/shard_map/all_gather | solution.py:12
  57.9 85.1 %all-gather.12.cloned.1.call-done = f32[128,128,128]{2,1,0:T(8,128)} async-done(((f32[16,128,128]{2,1,0:T(8,128)}), f32[128,128,128]{2,1,0:T(8,128)}) %all-gather.12.cloned.1.call-update) | async-done | bytes 8388624 | tf_op jit(solution)/shard_map/all_gather | solution.py:12
  143.0 32.3 %while.16 = (s32[]{:T(128)}, f32[16,128,128]{2,1,0:T(8,128)S(1)}, f32[1]{0:T(128)}, s32[]{:T(128)}, f32[8,16]{1,0:T(8,128)S(1)}, /*index=5*/f32[8,1]{0,1:T(1,128...) while((s32[]{:T(128)}, f32[16,128,128]{2,1,0:T(8,128)S(1)}, ...), condition=%wide.region_2.3_spmd.clone, body=%wide.region_1.2_spmd.clone.sunk | while | flops 1048605 | bytes 3146154 | solution.py:21
  144.9 1.5 fusion.73
  149.5 1.6 fusion.73
  154.2 1.5 fusion.73
  158.9 1.5 fusion.73
  163.5 1.5 fusion.73
  168.0 1.5 fusion.73
  172.6 1.5 fusion.73
  175.5 2.1 fusion.19
  177.6 1.8 multiply_reduce_fusion
  179.9 140.0 %all-gather.8.cloned.1.call-done = bf16[2048,3072]{1,0:T(8,128)(2,1)} async-done(((bf16[2048,384]{1,0:T(8,128)(2,1)}), bf16[2048,3072]{1,0:T(8,128)(2,1)}) %all-gather.8.cloned.1.call-update) | async-done | bytes 12582928 | tf_op jit(solution)/shard_map/all_gather | solution.py:102
  319.9 7.3 %convolution_convert_fusion = bf16[128,3072]{1,0:T(8,128)(2,1)} fusion(bf16[128,2048]{0,1:T(8,128)(2,1)S(1)} %fusion.21, bf16[2048,3072]{1,0:T(8,128)(2,1)} %all-gather.8.cloned.1.call-done), kind=kOutput, calls=%fused_computation.17 | convolution fusion | flops 1611005952 | bytes 13893632 | tf_op jit(solution)/shard_map/dot_general | solution.py:100
  329.7 1.4 scatter_custom_fusion
  331.1 17.7 %reduce-scatter.3.cloned.1.call-done = bf16[128,768]{1,0:T(8,128)(2,1)} async-done(((bf16[128,3072]{1,0:T(8,128)(2,1)}), bf16[128,768]{1,0:T(8,128)(2,1)}) %reduce-scatter.3.cloned.1.call-update) | async-done | bytes 196624 | tf_op jit(solution)/shard_map/reduce_scatter | solution.py:109
  349.9 5.8 %psum.7 = f32[128]{0:T(128)S(1)} all-reduce(f32[128]{0:T(128)S(1)} %fusion.46), channel_id=1, replica_groups=mesh['seq'=8,'head'=4] {'head'}, use_global_device_ids=true, to_apply=%region_6.7 | all-reduce | flops 128 | bytes 1024 | tf_op jit(solution)/shard_map/psum | solution.py:114
  355.9 2.0 gather_fusion
  357.9 25.5 %all_to_all.10 = bf16[8,64,768]{2,1,0:T(8,128)(2,1)} all-to-all(bf16[8,64,768]{2,1,0:T(8,128)(2,1)S(1)} %bitcast.117), channel_id=1, replica_groups=mesh['seq'=8,'head'=4] {'seq'}, dimensions={0} | all-to-all | bytes 1572864 | tf_op jit(solution)/shard_map/all_to_all | solution.py:135
  383.6 26.6 %all-gather.10.cloned.1.call-done = bf16[8,64,3072]{2,1,0:T(8,128)(2,1)} async-done(((bf16[8,64,768]{2,1,0:T(8,128)(2,1)}), bf16[8,64,3072]{2,1,0:T(8,128)(2,1)}) %all-gather.10.cloned.1.call-update) | async-done | bytes 3145744 | tf_op jit(solution)/shard_map/all_gather | solution.py:134
  410.2 8.2 %fusion.7 = f32[512,1152]{1,0:T(8,128)S(1)} fusion(bf16[512,3072]{1,0:T(8,128)(2,1)} %bitcast.127, bf16[1,3072,1152]{2,1,0:T(8,128)(2,1)} %param.27), kind=kOutput, calls=%fused_computation.14 | convolution fusion | flops 3623878656 | bytes 12582912 | tf_op jit(solution)/shard_map/dot_general | solution.py:143
  418.4 15.2 %fusion.9 = bf16[512,3072]{1,0:T(8,128)(2,1)} fusion(bf16[1,1152,3072]{2,1,0:T(8,128)(2,1)} %param.29, bf16[512,3072]{1,0:T(8,128)(2,1)} %bitcast.128, bf16[1,3072,1152]{2,1,0:T(8,128)(2,1)} %param.28, f32[512,1152]{1,0:T(8,128)S(1)} %fusion.7), kind=kOutput, calls=%fused_computation.16 | convolution fusion | flops 7252869120 | bytes 22806528 | tf_op jit(solution)/shard_map/dot_general | solution.py:147
  433.7 38.1 %reduce-scatter.5.cloned.1.call-done = bf16[8,64,768]{2,1,0:T(8,128)(2,1)} async-done(((bf16[8,64,3072]{2,1,0:T(8,128)(2,1)}), bf16[8,64,768]{2,1,0:T(8,128)(2,1)}) %reduce-scatter.5.cloned.1.call-update) | async-done | bytes 786448 | tf_op jit(solution)/shard_map/reduce_scatter | solution.py:151
  471.8 5.5 %all-to-all-start.1 = ((bf16[8,64,768]{2,1,0:T(8,128)(2,1)}), bf16[8,64,768]{2,1,0:T(8,128)(2,1)S(1)}, u32[]{:S(2)}, u32[]{:S(2)}) async-start(bf16[8,64,768]{2,1,0:T(8,128)(2,1)} %reduce-scatter.5.cloned.1.call-done), calls=%async_computation.3 | async-start | bytes 1572864 | tf_op jit(solution)/shard_map/all_to_all | solution.py:157
  477.4 20.1 %all-to-all-done.1 = bf16[8,64,768]{2,1,0:T(8,128)(2,1)S(1)} async-done(((bf16[8,64,768]{2,1,0:T(8,128)(2,1)}), bf16[8,64,768]{2,1,0:T(8,128)(2,1)S(1)}, u32[]{:S(2)}, u32[]{:S(2)}) %all-to-all-start.1) | async-done | bytes 786464 | tf_op jit(solution)/shard_map/all_to_all | solution.py:157
  497.6 1.1 gather_fusion.1
  499.2 1.0 multiply_reduce_fusion.1
  (87 shorter events, 14.7 us)
Async XLA Ops:
  6.5 6.5 %copy-start = (bf16[128,2048]{1,0:T(8,128)(2,1)S(1)}, bf16[128,2048]{1,0:T(8,128)(2,1)}, u32[]{:S(2)}) copy-start(bf16[128,2048]{1,0:T(8,128)(2,1)} %param.18) | copy-start | bytes 1572868
  6.5 9.0 %copy-start.7 = (u32[32]{0:T(128)S(1)}, u32[32]{0:T(128)}, u32[]{:S(2)}) copy-start(u32[32]{0:T(128)} %constant.103) | copy-start | bytes 388
  6.5 9.0 %copy-start.4 = (s32[128]{0:T(128)S(1)}, s32[128]{0:T(128)}, u32[]{:S(2)}) copy-start(s32[128]{0:T(128)} %param.20) | copy-start | bytes 1540
  6.5 136.5 %all-gather.12.cloned.1.call-start = ((), (), s32[]{:S(2)}) async-start(), calls=%async_computation.8 | async-start | bytes 9437184 | tf_op jit(solution)/shard_map/all_gather | solution.py:12
  14.7 305.2 %all-gather.8.cloned.1.call-start = ((), (), s32[]{:S(2)}) async-start(), calls=%async_computation.4 | async-start | bytes 14155776 | tf_op jit(solution)/shard_map/all_gather | solution.py:102
  15.5 333.4 %reduce-scatter.3.cloned.1.call-start = ((), (), s32[]{:S(2)}) async-start(), calls=%async_computation.5 | async-start | bytes 983040 | tf_op jit(solution)/shard_map/reduce_scatter | solution.py:109
  177.6 1.9 copy-start.3
  179.9 147.4 %copy-start.5 = (s32[128,2]{0,1:T(2,128)S(1)}, s32[128,2]{0,1:T(2,128)}, u32[]{:S(2)}) copy-start(s32[128,2]{0,1:T(2,128)} %param.25) | copy-start | bytes 3076
  179.9 169.0 %copy-start.2 = (bf16[128,768]{1,0:T(8,128)(2,1)S(1)}, bf16[128,768]{1,0:T(8,128)(2,1)}, u32[]{:S(2)}) copy-start(bf16[128,768]{1,0:T(8,128)(2,1)} %param.23) | copy-start | bytes 589828
  327.2 83.0 %all-gather.10.cloned.1.call-start = ((), (), s32[]{:S(2)}) async-start(), calls=%async_computation.6 | async-start | bytes 3932160 | tf_op jit(solution)/shard_map/all_gather | solution.py:134
  383.4 88.4 %reduce-scatter.5.cloned.1.call-start = ((), (), s32[]{:S(2)}) async-start(), calls=%async_computation.7 | async-start | bytes 3932160 | tf_op jit(solution)/shard_map/reduce_scatter | solution.py:151
  433.6 43.6 %copy-start.6 = (f32[128,2]{0,1:T(2,128)S(1)}, f32[128,2]{0,1:T(2,128)}, u32[]{:S(2)}) copy-start(f32[128,2]{0,1:T(2,128)} %param.26) | copy-start | bytes 3076
  471.8 25.7 %all-to-all-start.1 = ((bf16[8,64,768]{2,1,0:T(8,128)(2,1)}), bf16[8,64,768]{2,1,0:T(8,128)(2,1)S(1)}, u32[]{:S(2)}, u32[]{:S(2)}) async-start(bf16[8,64,768]{2,1,0:T(8,128)(2,1)} %reduce-scatter.5.cloned.1.call-done), calls=%async_computation.3 | async-start | bytes 1572864 | tf_op jit(solution)/shard_map/all_to_all | solution.py:157
  497.6 3.3 copy-start.1
Sparse Core Ops, SparseCore 0:
  14.8 128.1 all-gather.11
  145.1 174.7 all-gather.7
  327.3 21.4 reduce-scatter.2
  383.5 26.6 all-gather.9
  433.8 37.9 reduce-scatter.4
where the time goes:
time: 509 us; the launch traced here: 507 us
  waiting for transfers between devices  328 us (64%)
  blocking collectives  71.3 us (14%)
  matrix products  36.3 us (7%)
  loops' own time  17.5 us (3%)
  local copies, waits for them, and re-layouts  16.9 us (3%)
  other arithmetic  16.5 us (3%)
  between operations  14.8 us (3%)
  starting transfers between devices  5.86 us (1%)
    all_gather x1, waiting for transfers between devices, shards(): lax.all_gather(output_weight, 'seq', axis=1, tiled=True)  140 us
    all_gather x1, waiting for transfers between devices, carried_in(): pieces = jax.tree.map(lambda part: lax.all_gather(part, axis), value)  85.1 us
    reduce_scatter x1, waiting for transfers between devices, shards(): lax.psum_scatter(result.reshape(sources, slot_count, model_width).astype(...  38.1 us
    all_gather x1, waiting for transfers between devices, shards(): lax.all_gather(lax.all_to_all(outgoing, 'seq', split_axis=0, concat_axis=...  26.6 us
    all_to_all x1, blocking collectives, shards(): lax.all_to_all(outgoing, 'seq', split_axis=0, concat_axis=0, tiled=True)  25.5 us
    unnamed x1, blocking collectives  23.6 us
    all_to_all x1, waiting for transfers between devices, shards(): lax.all_to_all(summed_out.astype(jnp.bfloat16), 'seq', split_axis=0, conc...  20.1 us
    reduce_scatter x1, waiting for transfers between devices, shards(): lax.psum_scatter(partial_value.astype(jnp.bfloat16), 'head', scatter_dime...  17.7 us
  transfers between devices with their start and end apart: 6, of which 6 were waited for; matrix products, arithmetic and copies ran while one was open for 5% of the time, Pallas kernels for 0%

commit v1 on v0

v1 whole, which is shorter than its diff:
```python
import jax
import jax.numpy as jnp
from jax import lax
from jax.sharding import PartitionSpec as P

EPSILON = 1e-06
CORES = 2
F32 = jnp.float32
BF16 = jnp.bfloat16


def permute_seq(value, move):
    count = lax.axis_size("seq")
    return lax.ppermute(value, "seq", [(source, move(source)) for source in range(count)])


def permute_head(value, move):
    count = lax.axis_size("head")
    return lax.ppermute(value, "head", [(source, move(source)) for source in range(count)])


def pick(stack, index, axis=0):
    return lax.dynamic_index_in_dim(stack, index, axis, keepdims=False)


def shards(
    queries,
    key_vectors,
    value_vectors,
    log_decay,
    doc_ids,
    head_gain,
    output_weight,
    residual,
    norm_gain,
    routing,
    route_weights,
    gate_weight,
    up_weight,
    down_weight,
):
    tokens, heads = log_decay.shape
    hw = queries.shape[1] // heads
    n_seq, n_head = lax.axis_size("seq"), lax.axis_size("head")
    ny, nz, nx = n_seq // n_head, n_head, n_head // CORES
    s, h = lax.axis_index("seq"), lax.axis_index("head")
    z, y = s // ny, s % ny
    x, c = h // CORES, h % CORES
    part = residual.shape[1]
    model_width = part * n_head

    cols = output_weight.shape[1]
    w_z = jnp.zeros((output_weight.shape[0], ny * cols), BF16)
    w_z = lax.dynamic_update_slice(w_z, output_weight, (0, y * cols))
    for k in range(1, ny):
        got = permute_seq(output_weight, lambda q, k=k: q // ny * ny + (q % ny - k) % ny)
        w_z = lax.dynamic_update_slice(w_z, got, (0, (y + k) % ny * cols))

    qh = queries.reshape(tokens, heads, hw)
    kh = key_vectors.reshape(tokens, heads, hw)
    vh = value_vectors.reshape(tokens, heads, hw)
    row = lax.broadcasted_iota(jnp.int32, (tokens, tokens), 0)
    col = lax.broadcasted_iota(jnp.int32, (tokens, tokens), 1)
    decay_sum = jnp.dot(
        (col <= row).astype(F32), log_decay, precision=lax.Precision.HIGHEST
    )
    tail = jnp.exp(decay_sum[-1][None, :] - decay_sum) * (
        doc_ids == doc_ids[-1]
    ).astype(F32)[:, None]
    own_state = jnp.einsum(
        "thd,the->hde",
        (kh.astype(F32) * tail[:, :, None]).astype(BF16),
        vh,
        preferred_element_type=F32,
    )
    own_gain = jnp.exp(decay_sum[-1]) * (doc_ids[0] == doc_ids[-1]).astype(F32)

    rows = heads * hw // n_seq
    hc = max(1, rows // hw)
    extra = -(-(2 * hc + 2) // 16) * 16
    chunk_gain = jnp.repeat(own_gain, hw).reshape(n_seq, hc, rows // hc)[:, :, 0]
    gain_hi = chunk_gain.astype(BF16)
    gain_lo = (chunk_gain - gain_hi.astype(F32)).astype(BF16)
    first = jnp.full((n_seq, 1), doc_ids[0].astype(BF16))
    last = jnp.full((n_seq, 1), doc_ids[-1].astype(BF16))
    notes = jnp.concatenate([gain_hi, gain_lo, first, last], axis=1)
    notes = jnp.pad(notes, ((0, 0), (0, extra - notes.shape[1])))
    notes = jnp.broadcast_to(notes[:, :, None], (n_seq, extra, hw))
    payload = jnp.concatenate(
        [own_state.astype(BF16).reshape(n_seq, rows, hw), notes], axis=1
    )
    blocks = lax.all_to_all(payload, "seq", split_axis=0, concat_axis=0, tiled=True)
    states = blocks[:, :rows].astype(F32).reshape(n_seq, hc, rows // hc, hw)
    info = blocks[:, rows:, 0].astype(F32)
    gains = info[:, :hc] + info[:, hc : 2 * hc]
    firsts, lasts = info[:, 2 * hc], info[:, 2 * hc + 1]
    entered = [jnp.zeros_like(states[0])]
    for b in range(1, n_seq):
        before = states[b - 1] + gains[b - 1][:, None, None] * entered[-1]
        entered.append(before * (firsts[b] == lasts[b - 1]).astype(F32))
    back = jnp.stack(entered).astype(BF16).reshape(n_seq, rows, hw)
    carried = lax.all_to_all(back, "seq", split_axis=0, concat_axis=0, tiled=True)
    carried = carried.reshape(heads, hw, hw)

    decay_rows = decay_sum.T
    gap = decay_rows[:, :, None] - decay_rows[:, None, :]
    kept = (col <= row) & (doc_ids[:, None] == doc_ids[None, :])
    decay_matrix = jnp.where(kept[None], jnp.exp(jnp.minimum(gap, 0.0)), 0.0)
    scores = jnp.einsum("thd,shd->hts", qh, kh, preferred_element_type=F32)
    weighted = (scores * decay_matrix).astype(BF16)
    inside = jnp.einsum("hts,shd->thd", weighted, vh, preferred_element_type=F32)
    reach = jnp.exp(decay_sum) * (doc_ids == doc_ids[0]).astype(F32)[:, None]
    outside = jnp.einsum("thd,hde->the", qh, carried, preferred_element_type=F32)
    heads_raw = inside + outside * reach[:, :, None]
    inv_norm = lax.rsqrt(jnp.mean(heads_raw * heads_raw, axis=2, keepdims=True) + EPSILON)
    attended = ((heads_raw * inv_norm).reshape(tokens, heads * hw) * head_gain).astype(BF16)

    products = []
    for k in range(nz):
        rows_k = attended
        if k:
            rows_k = permute_seq(
                attended, lambda q, k=k: (q // ny - k) % nz * ny + q % ny
            )
        products.append(jnp.dot(rows_k, w_z, preferred_element_type=F32).astype(BF16))
    products = jnp.stack(products)
    total = pick(products, (h - z) % nz).astype(F32)
    for m in range(1, n_head):
        sent = pick(products, (h + m - z) % nz)
        total = total + permute_head(sent, lambda q, m=m: (q + m) % n_head).astype(F32)
    spots = [
        ((zz * ny + yy) * n_head + hh, (hh * ny + yy) * n_head + zz)
        for zz in range(nz)
        for yy in range(ny)
        for hh in range(n_head)
    ]
    summed = lax.ppermute(total.astype(BF16), ("seq", "head"), spots).astype(F32)
    middle = lax.optimization_barrier((summed + residual.astype(F32)).astype(BF16))

    experts = n_seq
    capacity = 4 * tokens // experts
    flat_ids = routing.reshape(-1)
    hits = (flat_ids[:, None] == jnp.arange(experts, dtype=jnp.int32)[None, :]).astype(F32)
    pair_row = lax.broadcasted_iota(jnp.int32, (2 * tokens, 2 * tokens), 0)
    pair_col = lax.broadcasted_iota(jnp.int32, (2 * tokens, 2 * tokens), 1)
    earlier = jnp.dot((pair_col < pair_row).astype(F32), hits)
    rank = jnp.sum(earlier * hits, axis=1).astype(jnp.int32)
    place = (flat_ids * capacity + rank).reshape(tokens, 2)
    slots = jnp.arange(experts * capacity, dtype=jnp.int32)
    here = place[:, :, None] == slots[None, None, :]
    take = jnp.any(here, axis=1).astype(BF16)
    mix = jnp.sum(jnp.where(here, route_weights[:, :, None], 0.0), axis=1)

    outgoing = lax.dot_general(
        take, middle, (((0,), (0,)), ((), ())), preferred_element_type=F32
    ).astype(BF16)
    got = lax.all_to_all(
        outgoing.reshape(experts, capacity, part), "seq", split_axis=0, concat_axis=0, tiled=True
    ).reshape(experts * capacity, part)
    x_all = jnp.zeros((experts * capacity, model_width), BF16)
    pieces = [(h, got)]
    for m in range(1, nx):
        far = permute_head(got, lambda q, m=m: (q - m * CORES) % n_head)
        pieces.append(((h + m * CORES) % n_head, far))
    for owner, piece in list(pieces):
        for m in range(1, CORES):
            near = permute_head(piece, lambda q, m=m: q // CORES * CORES + (q % CORES - m) % CORES)
            pieces.append((owner // CORES * CORES + (owner % CORES + m) % CORES, near))
    for owner, piece in pieces:
        x_all = lax.dynamic_update_slice(x_all, piece, (0, owner * part))
    x_float = x_all.astype(F32)
    row_norm = lax.rsqrt(jnp.mean(x_float * x_float, axis=1, keepdims=True) + EPSILON)
    normed = (x_float * row_norm * norm_gain).astype(BF16)
    gate_proj = jnp.dot(normed, gate_weight[0], preferred_element_type=F32)
    up_proj = jnp.dot(normed, up_weight[0], preferred_element_type=F32)
    hidden = (jax.nn.silu(gate_proj) * up_proj).astype(BF16)
    result = jnp.dot(hidden, down_weight[0], preferred_element_type=F32).astype(BF16)

    result = result.reshape(experts * capacity, nx, CORES, part)
    near_sum = pick(result, c, 2).astype(F32)
    for m in range(1, CORES):
        sent = pick(result, (c + m) % CORES, 2)
        near_sum = near_sum + permute_head(
            sent, lambda q, m=m: q // CORES * CORES + (q % CORES + m) % CORES
        ).astype(F32)
    near_half = near_sum.astype(BF16)
    far_sum = pick(near_sum, x, 1)
    for m in range(1, nx):
        sent = pick(near_half, (x + m) % nx, 1)
        far_sum = far_sum + permute_head(sent, lambda q, m=m: (q + m * CORES) % n_head).astype(F32)
    returned = lax.all_to_all(
        far_sum.astype(BF16).reshape(experts, capacity, part),
        "seq",
        split_axis=0,
        concat_axis=0,
        tiled=True,
    ).reshape(experts * capacity, part)
    expert_sum = jnp.dot(
        mix, returned.astype(F32), precision=lax.Precision.HIGHEST, preferred_element_type=F32
    )
    return (middle.astype(F32) + expert_sum).astype(BF16)


def solution(mesh):
    placed = (
        P("seq", "head"),
        P("seq", "head"),
        P("seq", "head"),
        P("seq", "head"),
        P("seq"),
        P("head"),
        P("head", "seq"),
        P("seq", "head"),
        P(),
        P("seq", None),
        P("seq", None),
        P("seq", None, "head"),
        P("seq", None, "head"),
        P("seq", "head", None),
    )
    return jax.shard_map(
        shards, mesh=mesh, in_specs=placed, out_specs=P("seq", "head"), check_vma=False
    )
```

time: 509 us -> 312 us (0.61)
  waiting for transfers between devices: 328 us -> 141 us
  blocking collectives: 71.3 us -> 34.1 us
  starting transfers between devices: 5.86 us -> 27.4 us
  local copies, waits for them, and re-layouts: 16.9 us -> 37.4 us
  loops' own time: 17.5 us -> 0 us
  matrix products: 36.3 us -> 43.1 us
    all_gather x3 -> x0, waiting for transfers between devices: 252 us -> none  [the longest x1 140 us: shards(): lax.all_gather(output_weight, 'seq', axis=1, tiled=True)]
    ppermute x0 -> x13, waiting for transfers between devices: none -> 99.8 us  [the longest x4 51.1 us: permute_seq(): lax.ppermute(value, 'seq', [(source, move(source)) for source in range(co...]
    reduce_scatter x2 -> x0, waiting for transfers between devices: 55.8 us -> none  [the longest x1 38.1 us: shards(): lax.psum_scatter(result.reshape(sources, slot_count, model_width).astype(...]
    unnamed x1 -> x0, blocking collectives: 23.6 us -> none
    all_to_all x1 -> x3, waiting for transfers between devices: 20.1 us -> 40.9 us  [the longest x1 19.8 us: shards(): lax.all_to_all(far_sum.astype(BF16).reshape(experts, capacity, part), 'se...]
    another operation x1 -> x0, loops' own time: 17.5 us -> none  [carried_in(): return lax.fori_loop(0, count - 1, lap, running)]
    all_gather x1 -> x0, blocking collectives: 16.4 us -> none  [carried_in(): pieces = jax.tree.map(lambda part: lax.all_gather(part, axis), value)]
    ppermute x0 -> x13, starting transfers between devices: none -> 12.6 us  [the longest x4 7.08 us: permute_seq(): lax.ppermute(value, 'seq', [(source, move(source)) for source in range(co...]
  transfers between devices with their start and end apart: 6 -> 16, of which waited for: 6 -> 11; matrix products, arithmetic and copies ran while one was open for 5% -> 8% of each run, Pallas kernels for 0% -> 0%
where the time goes in v1:
time: 312 us; the launch traced here: 311 us
  waiting for transfers between devices  141 us (45%)
  matrix products  43.1 us (14%)
  local copies, waits for them, and re-layouts  37.4 us (12%)
  blocking collectives  34.1 us (11%)
  starting transfers between devices  27.4 us (9%)
  other arithmetic  16.1 us (5%)
  between operations  12 us (4%)
    ppermute x4, waiting for transfers between devices, permute_seq(): lax.ppermute(value, 'seq', [(source, move(source)) for source in range(co...  51.1 us
    ppermute x8, waiting for transfers between devices, permute_head(): lax.ppermute(value, 'head', [(source, move(source)) for source in range(c...  48.6 us
    all_to_all x1, blocking collectives, shards(): lax.all_to_all(outgoing.reshape(experts, capacity, part), 'seq', split_ax...  34.1 us
    all_to_all x1, waiting for transfers between devices, shards(): lax.all_to_all(far_sum.astype(BF16).reshape(experts, capacity, part), 'se...  19.8 us
    dot_general x1, matrix products, shards(): jnp.dot(hidden, down_weight[0], preferred_element_type=F32).astype(BF16)  16.5 us
    all_to_all x1, waiting for transfers between devices, shards(): lax.all_to_all(payload, 'seq', split_axis=0, concat_axis=0, tiled=True)  14.6 us
    dot_general x4, matrix products, shards(): jnp.dot(rows_k, w_z, preferred_element_type=F32).astype(BF16)  10.1 us
    dynamic_slice x1, local copies, waits for them, and re-layouts, pick(): return lax.dynamic_index_in_dim(stack, index, axis, keepdims=False)  8.11 us
  transfers between devices with their start and end apart: 16, of which 11 were waited for; matrix products, arithmetic and copies ran while one was open for 8% of the time, Pallas kernels for 0%

profile of v1, /device:TPU:0, one launch (start us, length us, event | category | flops | bytes accessed | tf_op | source)
XLA Modules:
  0.0 310.7 jit_solution(2331808501598499259)
XLA Ops:
  2.7 2.0 compare_convert_fusion
  11.1 7.3 %all-to-all-start = ((bf16[8,272,128]{2,1,0:T(8,128)(2,1)}), bf16[8,272,128]{2,1,0:T(8,128)(2,1)S(1)}, u32[]{:S(2)}, u32[]{:S(2)}) async-start(bf16[8,272,128]{2,1,0:T(8,128)(2,1)} %pad_maximum_fusion.1), calls=%async_computation | async-start | bytes 1114112 | tf_op jit(solution)/shard_map/all_to_all | solution.py:92
  19.0 14.6 %all-to-all-done = bf16[8,272,128]{2,1,0:T(8,128)(2,1)S(1)} async-done(((bf16[8,272,128]{2,1,0:T(8,128)(2,1)}), bf16[8,272,128]{2,1,0:T(8,128)(2,1)S(1)}, u32[]{:S(2)}, u32[]{:S(2)}) %all-to-all-start) | async-done | bytes 557088 | tf_op jit(solution)/shard_map/all_to_all | solution.py:92
  49.0 2.1 copy.73
  51.1 3.6 %all-to-all-start.1 = ((bf16[8,256,128]{1,2,0:T(8,128)(2,1)}), bf16[8,256,128]{1,2,0:T(8,128)(2,1)S(1)}, u32[]{:S(2)}, u32[]{:S(2)}) async-start(bf16[8,256,128]{1,2,0:T(8,128)(2,1)} %copy.73), calls=%async_computation.1 | async-start | bytes 1048576 | tf_op jit(solution)/shard_map/all_to_all | solution.py:102
  54.7 2.0 collective-permute-start
  56.8 1.8 broadcast_in_dim.35
  60.1 2.8 convolution_bitcast_fusion.1
  62.9 6.5 %all-to-all-done.1 = bf16[8,256,128]{1,2,0:T(8,128)(2,1)S(1)} async-done(((bf16[8,256,128]{1,2,0:T(8,128)(2,1)}), bf16[8,256,128]{1,2,0:T(8,128)(2,1)S(1)}, u32[]{:S(2)}, u32[]{:S(2)}) %all-to-all-start.1) | async-done | bytes 524320 | tf_op jit(solution)/shard_map/all_to_all | solution.py:102
  69.7 1.8 multiply_reduce_fusion
  73.1 23.6 %collective-permute-done = bf16[2048,384]{1,0:T(8,128)(2,1)} collective-permute-done((bf16[2048,384]{1,0:T(8,128)(2,1)S(1)}, bf16[2048,384]{1,0:T(8,128)(2,1)}, u32[]{:S(2)}, u32[]{:S(2)}) %collective-permute-start) | collective-permute-done | bytes 1572896 | tf_op jit(solution)/shard_map/ppermute | solution.py:14
  96.7 2.8 constant_dynamic-update-slice_fusion.4
  99.5 2.4 collective-permute-start.2
  103.3 2.5 fusion.17
  105.8 2.5 fusion.18
  108.4 27.6 %collective-permute-done.2 = bf16[128,2048]{0,1:T(8,128)(2,1)S(1)} collective-permute-done((bf16[128,2048]{0,1:T(8,128)(2,1)S(1)}, bf16[128,2048]{0,1:T(8,128)(2,1)S(1)}, u32[]{:S(2)}, u32[]{:S(2)}) %collective-permute-start.2) | collective-permute-done | bytes 524320 | tf_op jit(solution)/shard_map/ppermute | solution.py:14
  136.0 2.5 fusion.19
  138.5 2.5 fusion.20
  144.9 3.0 collective-permute-done.4
  149.1 2.6 collective-permute-done.6
  153.1 34.1 %all_to_all.20 = bf16[8,64,768]{2,1,0:T(8,128)(2,1)} all-to-all(bf16[8,64,768]{2,1,0:T(8,128)(2,1)S(1)} %bitcast.151), channel_id=1, replica_groups=mesh['seq'=8,'head'=4] {'seq'}, dimensions={0} | all-to-all | bytes 1572864 | tf_op jit(solution)/shard_map/all_to_all | solution.py:157
  188.2 18.9 %collective-permute-done.8 = bf16[512,768]{1,0:T(8,128)(2,1)} collective-permute-done((bf16[512,768]{1,0:T(8,128)(2,1)}, bf16[512,768]{1,0:T(8,128)(2,1)}, u32[]{:S(2)}, u32[]{:S(2)}) %collective-permute-start.8) | collective-permute-done | bytes 786464 | tf_op jit(solution)/shard_map/ppermute | solution.py:19
  213.2 8.0 %fusion.2 = f32[512,1152]{1,0:T(8,128)} fusion(bf16[1,3072,1152]{2,1,0:T(8,128)(2,1)} %param.26, bf16[512,3072]{1,0:T(8,128)(2,1)S(1)} %constant_dynamic-update-slice_fusion, f32[3072]{0:T(1024)S(1)} %copy-done.9, f32[512]{0:T(512)S(1)} %add_rsqrt_fusion.1), kind=kOutput, calls=%fused_computation.4 | convolution fusion | flops 3630170112 | bytes 12597248 | tf_op jit(solution)/shard_map/dot_general | solution.py:175
  221.2 16.5 %fusion.9 = bf16[512,3072]{1,0:T(8,128)(2,1)} fusion(bf16[1,1152,3072]{2,1,0:T(8,128)(2,1)} %param.27, f32[512,1152]{1,0:T(8,128)} %fusion.2, bf16[1,3072,1152]{2,1,0:T(8,128)(2,1)} %param.25, bf16[512,3072]{1,0:T(8,128)(2,1)S(1)} %constant_dynamic-update-slice_fusion, f32[3072]{0:T(1024)S(1)} %copy-done.9, f32[512]{0:T(512)S(1)} %add_rsqrt_fusion.1), kind=kOutput, calls=%fused_computation.11 | convolution fusion | flops 7259160576 | bytes 22820864 | tf_op jit(solution)/shard_map/dot_general | solution.py:177
  237.7 7.3 %reshape.319 = bf16[512,2,2,768]{3,2,1,0:T(2,128)(2,1)S(1)} reshape(bf16[512,3072]{1,0:T(8,128)(2,1)} %fusion.9) | data formatting | bytes 6291456 | tf_op jit(solution)/shard_map/reshape | solution.py:179
  245.0 8.1 %constant_dynamic-slice_fusion.1 = (bf16[512,2,1,768]{3,2,1,0:T(2,128)(2,1)}, bf16[512,2,1,768]{3,2,1,0:T(2,128)(2,1)S(1)}) fusion(bf16[512,2,2,768]{3,2,1,0:T(2,128)(2,1)S(1)} %reshape.319, s32[]{:T(128)S(6)} %select_n.146, s32[]{:T(128)S(6)} %select_n.147), kind=kLoop, calls=%fused_computation.114 | loop fusion | bytes 6291464 | tf_op jit(solution)/shard_map/jit(dynamic_index_in_dim)/dynamic_slice | solution.py:23
  255.1 3.4 %collective-permute-done.11 = bf16[512,2,768]{2,0,1:T(8,128)(2,1)} collective-permute-done((bf16[512,2,768]{2,0,1:T(8,128)(2,1)}, bf16[512,2,768]{2,0,1:T(8,128)(2,1)}, u32[]{:S(2)}, u32[]{:S(2)}) %collective-permute-start.11) | collective-permute-done | bytes 1572896 | tf_op jit(solution)/shard_map/ppermute | solution.py:19
  258.4 3.4 %convert_add_fusion = f32[512,2,768]{2,0,1:T(8,128)} fusion(bf16[512,2,768]{2,0,1:T(8,128)(2,1)} %collective-permute-done.11, bf16[512,2,1,768]{3,2,1,0:T(2,128)(2,1)S(1)} %copy-done.2), kind=kLoop, calls=%fused_computation.12 | loop fusion | flops 2359296 | bytes 6291456 | tf_op jit(solution)/shard_map/add | solution.py:183
  263.7 19.5 %collective-permute-done.12 = bf16[512,768]{1,0:T(8,128)(2,1)S(1)} collective-permute-done((bf16[512,768]{1,0:T(8,128)(2,1)S(1)}, bf16[512,768]{1,0:T(8,128)(2,1)S(1)}, u32[]{:S(2)}, u32[]{:S(2)}) %collective-permute-start.12) | collective-permute-done | bytes 786464 | tf_op jit(solution)/shard_map/ppermute | solution.py:19
  283.2 2.4 fusion.12
  285.6 3.9 %all-to-all-start.3 = ((bf16[8,64,768]{2,1,0:T(8,128)(2,1)}), bf16[8,64,768]{2,1,0:T(8,128)(2,1)S(1)}, u32[]{:S(2)}, u32[]{:S(2)}) async-start(bf16[8,64,768]{2,1,0:T(8,128)(2,1)} %bitcast.48), calls=%async_computation.3 | async-start | bytes 1572864 | tf_op jit(solution)/shard_map/all_to_all | solution.py:191
  289.7 19.8 %all-to-all-done.3 = bf16[8,64,768]{2,1,0:T(8,128)(2,1)S(1)} async-done(((bf16[8,64,768]{2,1,0:T(8,128)(2,1)}), bf16[8,64,768]{2,1,0:T(8,128)(2,1)S(1)}, u32[]{:S(2)}, u32[]{:S(2)}) %all-to-all-start.3) | async-done | bytes 786464 | tf_op jit(solution)/shard_map/all_to_all | solution.py:191
  (100 shorter events, 37.0 us)
Async XLA Ops:
  0.0 60.1 %copy-start = (bf16[128,2048]{1,0:T(8,128)(2,1)S(1)}, bf16[128,2048]{1,0:T(8,128)(2,1)}, u32[]{:S(2)}) copy-start(bf16[128,2048]{1,0:T(8,128)(2,1)} %param.14) | copy-start | bytes 1572868
  11.1 22.5 %all-to-all-start = ((bf16[8,272,128]{2,1,0:T(8,128)(2,1)}), bf16[8,272,128]{2,1,0:T(8,128)(2,1)S(1)}, u32[]{:S(2)}, u32[]{:S(2)}) async-start(bf16[8,272,128]{2,1,0:T(8,128)(2,1)} %pad_maximum_fusion.1), calls=%async_computation | async-start | bytes 1114112 | tf_op jit(solution)/shard_map/all_to_all | solution.py:92
  43.7 11.0 %copy-start.3 = (bf16[2048,384]{1,0:T(8,128)(2,1)S(1)}, bf16[2048,384]{1,0:T(8,128)(2,1)}, u32[]{:S(2)}) copy-start(bf16[2048,384]{1,0:T(8,128)(2,1)} %param.20) | copy-start | bytes 4718596
  43.7 13.0 %copy-start.5 = (s32[128]{0:T(128)S(1)}, s32[128]{0:T(128)}, u32[]{:S(2)}) copy-start(s32[128]{0:T(128)} %param.18) | copy-start | bytes 1540
  51.1 18.3 %all-to-all-start.1 = ((bf16[8,256,128]{1,2,0:T(8,128)(2,1)}), bf16[8,256,128]{1,2,0:T(8,128)(2,1)S(1)}, u32[]{:S(2)}, u32[]{:S(2)}) async-start(bf16[8,256,128]{1,2,0:T(8,128)(2,1)} %copy.73), calls=%async_computation.1 | async-start | bytes 1048576 | tf_op jit(solution)/shard_map/all_to_all | solution.py:102
  54.7 42.0 %collective-permute-start = (bf16[2048,384]{1,0:T(8,128)(2,1)S(1)}, bf16[2048,384]{1,0:T(8,128)(2,1)}, u32[]{:S(2)}, u32[]{:S(2)}) collective-permute-start(bf16[2048,384]{1,0:T(8,128)(2,1)S(1)} %copy-done.3), channel_id=1, source_target_pairs={{0,4},{4,0},{8,12},{12,8},{16,20},{20,16},{24,28},{28,24},{1,5},{5... | collective-permute-start | bytes 4718600 | tf_op jit(solution)/shard_map/ppermute | solution.py:14
  62.9 8.6 %copy-start.6 = (f32[2048]{0:T(1024)S(1)}, f32[2048]{0:T(1024)}, u32[]{:S(2)}) copy-start(f32[2048]{0:T(1024)} %param.19) | copy-start | bytes 24580
  71.9 34.0 %collective-permute-start.1 = (bf16[128,2048]{0,1:T(8,128)(2,1)S(1)}, bf16[128,2048]{0,1:T(8,128)(2,1)S(1)}, u32[]{:S(2)}, u32[]{:S(2)}) collective-permute-start(bf16[128,2048]{0,1:T(8,128)(2,1)S(1)} %fusion.22), channel_id=1, source_target_pairs={{0,24},{4,28},{8,0},{12,4},{16,8},{20,12},{24,16},{28,20},{1,25},{... | collective-permute-start | bytes 1572872 | tf_op jit(solution)/shard_map/ppermute | solution.py:14
  99.5 36.5 %collective-permute-start.2 = (bf16[128,2048]{0,1:T(8,128)(2,1)S(1)}, bf16[128,2048]{0,1:T(8,128)(2,1)S(1)}, u32[]{:S(2)}, u32[]{:S(2)}) collective-permute-start(bf16[128,2048]{0,1:T(8,128)(2,1)S(1)} %fusion.22), channel_id=1, source_target_pairs={{0,16},{4,20},{8,24},{12,28},{16,0},{20,4},{24,8},{28,12},{1,17},{... | collective-permute-start | bytes 1572872 | tf_op jit(solution)/shard_map/ppermute | solution.py:14
  101.9 36.6 %collective-permute-start.3 = (bf16[128,2048]{0,1:T(8,128)(2,1)S(1)}, bf16[128,2048]{0,1:T(8,128)(2,1)S(1)}, u32[]{:S(2)}, u32[]{:S(2)}) collective-permute-start(bf16[128,2048]{0,1:T(8,128)(2,1)S(1)} %fusion.22), channel_id=1, source_target_pairs={{0,8},{4,12},{8,16},{12,20},{16,24},{20,28},{24,0},{28,4},{1,9},{5... | collective-permute-start | bytes 1572872 | tf_op jit(solution)/shard_map/ppermute | solution.py:14
  138.5 5.8 %copy-start.7 = (s32[128,2]{0,1:T(2,128)S(1)}, s32[128,2]{0,1:T(2,128)}, u32[]{:S(2)}) copy-start(s32[128,2]{0,1:T(2,128)} %param.23) | copy-start | bytes 3076
  138.5 14.2 %copy-start.4 = (bf16[128,768]{1,0:T(8,128)(2,1)S(1)}, bf16[128,768]{1,0:T(8,128)(2,1)}, u32[]{:S(2)}) copy-start(bf16[128,768]{1,0:T(8,128)(2,1)} %param.21) | copy-start | bytes 589828
  141.2 6.6 %collective-permute-start.4 = (bf16[128,768]{1,0:T(8,128)(2,1)S(1)}, bf16[128,768]{1,0:T(8,128)(2,1)S(1)}, u32[]{:S(2)}, u32[]{:S(2)}) collective-permute-start(bf16[128,768]{1,0:T(8,128)(2,1)S(1)} %get-tuple-element.17), channel_id=1, source_target_pairs={{0,1},{1,2},{2,3},{3,0},{4,5},{5,6},{6,7},{7,4},{8,9},{9,10},{10,1... | collective-permute-start | bytes 589832 | tf_op jit(solution)/shard_map/ppermute | solution.py:19
  141.3 7.8 %collective-permute-start.5 = (bf16[128,768]{1,0:T(8,128)(2,1)S(1)}, bf16[128,768]{1,0:T(8,128)(2,1)S(1)}, u32[]{:S(2)}, u32[]{:S(2)}) collective-permute-start(bf16[128,768]{1,0:T(8,128)(2,1)S(1)} %get-tuple-element.19), channel_id=1, source_target_pairs={{0,2},{1,3},{2,0},{3,1},{4,6},{5,7},{6,4},{7,5},{8,10},{9,11},{10,... | collective-permute-start | bytes 589832 | tf_op jit(solution)/shard_map/ppermute | solution.py:19
  142.8 8.9 %collective-permute-start.6 = (bf16[128,768]{1,0:T(8,128)(2,1)S(1)}, bf16[128,768]{1,0:T(8,128)(2,1)S(1)}, u32[]{:S(2)}, u32[]{:S(2)}) collective-permute-start(bf16[128,768]{1,0:T(8,128)(2,1)S(1)} %get-tuple-element.18), channel_id=1, source_target_pairs={{0,3},{1,0},{2,1},{3,2},{4,7},{5,4},{6,5},{7,6},{8,11},{9,8},{10,9... | collective-permute-start | bytes 589832 | tf_op jit(solution)/shard_map/ppermute | solution.py:19
  151.8 0.8 collective-permute-start.7
  187.2 19.9 %collective-permute-start.8 = (bf16[512,768]{1,0:T(8,128)(2,1)}, bf16[512,768]{1,0:T(8,128)(2,1)}, u32[]{:S(2)}, u32[]{:S(2)}) collective-permute-start(bf16[512,768]{1,0:T(8,128)(2,1)} %bitcast.40), channel_id=1, source_target_pairs={{0,2},{1,3},{2,0},{3,1},{4,6},{5,7},{6,4},{7,5},{8,10},{9,11},{10,... | collective-permute-start | bytes 2359304 | tf_op jit(solution)/shard_map/ppermute | solution.py:19
  188.2 21.8 %collective-permute-start.9 = (bf16[512,768]{1,0:T(8,128)(2,1)}, bf16[512,768]{1,0:T(8,128)(2,1)}, u32[]{:S(2)}, u32[]{:S(2)}) collective-permute-start(bf16[512,768]{1,0:T(8,128)(2,1)} %bitcast.40), channel_id=1, source_target_pairs={{0,1},{1,0},{2,3},{3,2},{4,5},{5,4},{6,7},{7,6},{8,9},{9,8},{10,11... | collective-permute-start | bytes 2359304 | tf_op jit(solution)/shard_map/ppermute | solution.py:19
  207.1 4.1 %collective-permute-start.10 = (bf16[512,768]{1,0:T(8,128)(2,1)}, bf16[512,768]{1,0:T(8,128)(2,1)}, u32[]{:S(2)}, u32[]{:S(2)}) collective-permute-start(bf16[512,768]{1,0:T(8,128)(2,1)} %collective-permute-done.8), channel_id=1, source_target_pairs={{0,1},{1,0},{2,3},{3,2},{4,5},{5,4},{6,7},{7,6},{8,9},{9,8},{10,11... | collective-permute-start | bytes 2359304 | tf_op jit(solution)/shard_map/ppermute | solution.py:19
  210.0 3.2 %copy-start.9 = (f32[3072]{0:T(1024)S(1)}, f32[3072]{0:T(1024)}, u32[]{:S(2)}) copy-start(f32[3072]{0:T(1024)} %param.22) | copy-start | bytes 36868
  253.1 5.3 %copy-start.2 = (bf16[512,2,1,768]{3,2,1,0:T(2,128)(2,1)S(1)}, bf16[512,2,1,768]{3,2,1,0:T(2,128)(2,1)}, u32[]{:S(2)}) copy-start(bf16[512,2,1,768]{3,2,1,0:T(2,128)(2,1)} %get-tuple-element.15) | copy-start | bytes 4718596
  254.5 3.9 %collective-permute-start.11 = (bf16[512,2,768]{2,0,1:T(8,128)(2,1)}, bf16[512,2,768]{2,0,1:T(8,128)(2,1)}, u32[]{:S(2)}, u32[]{:S(2)}) collective-permute-start(bf16[512,2,768]{2,0,1:T(8,128)(2,1)} %bitcast.150), channel_id=1, source_target_pairs={{0,1},{1,0},{2,3},{3,2},{4,5},{5,4},{6,7},{7,6},{8,9},{9,8},{10,11... | collective-permute-start | bytes 4718600 | tf_op jit(solution)/shard_map/ppermute | solution.py:19
  261.8 27.7 %copy-start.8 = (f32[128,2]{0,1:T(2,128)S(1)}, f32[128,2]{0,1:T(2,128)}, u32[]{:S(2)}) copy-start(f32[128,2]{0,1:T(2,128)} %param.24) | copy-start | bytes 3076
  263.3 19.9 %collective-permute-start.12 = (bf16[512,768]{1,0:T(8,128)(2,1)S(1)}, bf16[512,768]{1,0:T(8,128)(2,1)S(1)}, u32[]{:S(2)}, u32[]{:S(2)}) collective-permute-start(bf16[512,768]{1,0:T(8,128)(2,1)S(1)} %fusion.37), channel_id=1, source_target_pairs={{0,2},{1,3},{2,0},{3,1},{4,6},{5,7},{6,4},{7,5},{8,10},{9,11},{10,... | collective-permute-start | bytes 2359304 | tf_op jit(solution)/shard_map/ppermute | solution.py:19
  263.7 47.0 %copy-start.1 = (bf16[128,2048]{1,0:T(8,128)(2,1)S(1)}, bf16[128,2048]{1,0:T(8,128)(2,1)}, u32[]{:S(2)}) copy-start(bf16[128,2048]{1,0:T(8,128)(2,1)} %param.14) | copy-start | bytes 1572868
  285.6 23.9 %all-to-all-start.3 = ((bf16[8,64,768]{2,1,0:T(8,128)(2,1)}), bf16[8,64,768]{2,1,0:T(8,128)(2,1)S(1)}, u32[]{:S(2)}, u32[]{:S(2)}) async-start(bf16[8,64,768]{2,1,0:T(8,128)(2,1)} %bitcast.48), calls=%async_computation.3 | async-start | bytes 1572864 | tf_op jit(solution)/shard_map/all_to_all | solution.py:191

commit v2 on v1

v2 whole, which is shorter than its diff:
```python
import functools
import math

import jax
import jax.numpy as jnp
from jax import lax
from jax.experimental import pallas as pl
from jax.experimental.pallas import tpu as pltpu
from jax.sharding import PartitionSpec as P

EPSILON = 1e-06
CORES = 2
HALVES = 2
F32 = jnp.float32
BF16 = jnp.bfloat16
HIGHEST = lax.Precision.HIGHEST
VMEM_BYTES = 48 * 1024 * 1024


def permute_seq(value, move):
    count = lax.axis_size("seq")
    return lax.ppermute(value, "seq", [(source, move(source)) for source in range(count)])


def permute_head(value, move):
    count = lax.axis_size("head")
    return lax.ppermute(value, "head", [(source, move(source)) for source in range(count)])


def pick(stack, index, axis=0):
    return lax.dynamic_index_in_dim(stack, index, axis, keepdims=False)


def doc_column(doc):
    count = doc.shape[1]
    return jnp.broadcast_to(doc, (count, count)).T


def chunk_plan(heads, hw, n_seq):
    rows = heads * hw // n_seq
    held = max(1, rows // hw)
    extra = -(-(2 * held + 2) // 16) * 16
    return rows, held, extra


def state_kernel(doc_ref, decay_ref, k_ref, v_ref, out_ref, sum_ref):
    tokens, heads = decay_ref.shape
    n_seq, _, hw = out_ref.shape
    rows, held, extra = chunk_plan(heads, hw, n_seq)
    doc = doc_ref[...].astype(F32)
    row = lax.broadcasted_iota(jnp.int32, (tokens, tokens), 0)
    col = lax.broadcasted_iota(jnp.int32, (tokens, tokens), 1)
    sums = jnp.dot(
        (col <= row).astype(F32), decay_ref[...], precision=HIGHEST, preferred_element_type=F32
    )
    sum_ref[...] = sums
    final = sums[tokens - 1 :, :]
    last = doc[:, tokens - 1 :]
    tail = jnp.exp(final - sums) * (doc_column(doc)[:, :1] == last).astype(F32)
    gain = jnp.exp(final) * (doc[:, :1] == last).astype(F32)
    for i in range(heads):
        lanes = slice(i * hw, (i + 1) * hw)
        faded = (k_ref[:, lanes].astype(F32) * tail[:, i : i + 1]).astype(BF16)
        state = lax.dot_general(
            faded, v_ref[:, lanes], (((0,), (0,)), ((), ())), preferred_element_type=F32
        ).astype(BF16)
        if rows >= hw:
            out_ref[i // held, i % held * hw : (i % held + 1) * hw, :] = state
        else:
            for j in range(hw // rows):
                out_ref[i * (hw // rows) + j, :rows, :] = state[j * rows : (j + 1) * rows]
    line = lax.broadcasted_iota(jnp.int32, (extra, hw), 0)
    for q in range(n_seq):
        note = jnp.where(line == 2 * held, doc[:, :1], 0.0)
        note = jnp.where(line == 2 * held + 1, last, note)
        for j in range(held):
            i = q * rows // hw + j
            whole = gain[:, i : i + 1]
            high = whole.astype(BF16).astype(F32)
            note = jnp.where(line == j, high, note)
            note = jnp.where(line == held + j, whole - high, note)
        out_ref[q, rows:, :] = note.astype(BF16)


def scan_kernel(blocks_ref, out_ref):
    n_seq, rows, hw = out_ref.shape
    held = max(1, rows // hw)
    part = rows // held
    for j in range(held):
        running = jnp.zeros((part, hw), F32)
        out_ref[0, j * part : (j + 1) * part, :] = running.astype(BF16)
        for b in range(1, n_seq):
            notes = blocks_ref[b - 1, rows:, :].astype(F32)
            gain = notes[j : j + 1] + notes[held + j : held + j + 1]
            first = blocks_ref[b, rows:, :].astype(F32)[2 * held : 2 * held + 1]
            joined = (first == notes[2 * held + 1 : 2 * held + 2]).astype(F32)
            state = blocks_ref[b - 1, j * part : (j + 1) * part, :].astype(F32)
            running = (state + gain * running) * joined
            out_ref[b, j * part : (j + 1) * part, :] = running.astype(BF16)


def inside_kernel(doc_ref, sum_ref, sum_rows_ref, q_ref, k_ref, v_ref, out_ref):
    tokens, heads = sum_ref.shape
    hw = q_ref.shape[1] // heads
    doc = doc_ref[...].astype(F32)
    row = lax.broadcasted_iota(jnp.int32, (tokens, tokens), 0)
    col = lax.broadcasted_iota(jnp.int32, (tokens, tokens), 1)
    kept = (col <= row) & (doc_column(doc) == doc)
    for i in range(heads):
        lanes = slice(i * hw, (i + 1) * hw)
        gap = sum_ref[:, i : i + 1] - sum_rows_ref[i : i + 1, :]
        fade = jnp.where(kept, jnp.exp(jnp.minimum(gap, 0.0)), 0.0)
        scores = lax.dot_general(
            q_ref[:, lanes], k_ref[:, lanes], (((1,), (1,)), ((), ())), preferred_element_type=F32
        )
        out_ref[:, lanes] = jnp.dot(
            (scores * fade).astype(BF16), v_ref[:, lanes], preferred_element_type=F32
        )


def outside_kernel(doc_ref, sum_ref, q_ref, carried_ref, inside_ref, gain_ref, out_ref):
    tokens, heads = sum_ref.shape
    hw = q_ref.shape[1] // heads
    doc = doc_ref[...].astype(F32)
    reach = jnp.exp(sum_ref[...]) * (doc_column(doc)[:, :1] == doc[:, :1]).astype(F32)
    for i in range(heads):
        lanes = slice(i * hw, (i + 1) * hw)
        outside = jnp.dot(q_ref[:, lanes], carried_ref[i], preferred_element_type=F32)
        raw = inside_ref[:, lanes] + outside * reach[:, i : i + 1]
        scale = lax.rsqrt(jnp.mean(raw * raw, axis=1, keepdims=True) + EPSILON)
        out_ref[:, lanes] = (raw * scale * gain_ref[:, lanes]).astype(BF16)


def expert_kernel(n_head, steps, owner_ref, *refs):
    pieces = refs[:n_head]
    gain_ref, gate_ref, up_ref, down_ref, sent_ref, kept_ref, rows_ref, hidden_ref = refs[n_head:]
    part = pieces[0].shape[1]
    width = gate_ref.shape[2]
    step = pl.program_id(0)

    @pl.when(step == 0)
    def _():
        squares = 0.0
        for piece in pieces:
            value = piece[...].astype(F32)
            squares = squares + jnp.sum(value * value, axis=1, keepdims=True)
        scale = lax.rsqrt(squares / (part * n_head) + EPSILON)
        for i, piece in enumerate(pieces):
            lanes = pl.ds(pl.multiple_of(owner_ref[i] * part, 128), part)
            value = piece[...].astype(F32) * scale * gain_ref[:, lanes]
            rows_ref[:, lanes] = value.astype(BF16)

    @pl.when(step < steps)
    def _():
        gate = jnp.dot(rows_ref[...], gate_ref[0], preferred_element_type=F32)
        up = jnp.dot(rows_ref[...], up_ref[0], preferred_element_type=F32)
        hidden = (gate / (1.0 + jnp.exp(-gate)) * up).astype(BF16)
        if steps == 1:
            hidden_ref[...] = hidden
        else:
            hidden_ref[:, pl.ds(pl.multiple_of(step * width, 128), width)] = hidden

    @pl.when((step >= steps) & (step < steps + n_head // CORES))
    def _():
        sent_ref[0] = jnp.dot(
            hidden_ref[...], down_ref[0], preferred_element_type=F32
        ).astype(BF16)

    @pl.when(step >= steps + n_head // CORES)
    def _():
        kept_ref[0] = jnp.dot(
            hidden_ref[...], down_ref[0], preferred_element_type=F32
        ).astype(BF16)


def expert_call(owners, pieces, norm_gain, gate_weight, up_weight, down_weight):
    n_head = len(pieces)
    count, part = pieces[0].shape
    _, depth, units = gate_weight.shape
    width = units
    for tried in (384, 256, 128):
        if units % tried == 0:
            width = tried
            break
    steps, nx = units // width, n_head // CORES
    whole = lambda shape: pl.BlockSpec(shape, lambda i, o: (0,) * len(shape))
    grid_spec = pltpu.PrefetchScalarGridSpec(
        num_scalar_prefetch=1,
        grid=(steps + n_head,),
        in_specs=[whole((count, part))] * n_head
        + [
            whole((1, depth)),
            pl.BlockSpec((1, depth, width), lambda i, o: (0, 0, jnp.minimum(i, steps - 1))),
            pl.BlockSpec((1, depth, width), lambda i, o: (0, 0, jnp.minimum(i, steps - 1))),
            pl.BlockSpec(
                (1, units, part), lambda i, o: (0, 0, o[n_head + jnp.maximum(i - steps, 0)])
            ),
        ],
        out_specs=[
            pl.BlockSpec((1, count, part), lambda i, o: (jnp.clip(i - steps, 0, nx - 1), 0, 0)),
            pl.BlockSpec(
                (1, count, part), lambda i, o: (jnp.clip(i - steps - nx, 0, n_head - nx - 1), 0, 0)
            ),
        ],
        scratch_shapes=[pltpu.VMEM((count, depth), BF16), pltpu.VMEM((count, units), BF16)],
    )
    return pl.pallas_call(
        functools.partial(expert_kernel, n_head, steps),
        grid_spec=grid_spec,
        out_shape=[
            jax.ShapeDtypeStruct((nx, count, part), BF16),
            jax.ShapeDtypeStruct((n_head - nx, count, part), BF16),
        ],
        compiler_params=pltpu.CompilerParams(vmem_limit_bytes=VMEM_BYTES),
        cost_estimate=pl.CostEstimate(
            flops=6 * count * depth * units,
            bytes_accessed=6 * depth * units + 4 * count * depth,
            transcendentals=count * units,
        ),
        name="expert",
    )(owners, *pieces, norm_gain.reshape(1, depth), gate_weight, up_weight, down_weight)


def local_call(kernel, name, out_shape, flops, *operands):
    many = isinstance(out_shape, list)
    shapes = out_shape if many else [out_shape]
    sizes = [a.size * a.dtype.itemsize for a in operands]
    sizes += [math.prod(o.shape) * o.dtype.itemsize for o in shapes]
    return pl.pallas_call(
        kernel,
        out_shape=out_shape,
        compiler_params=pltpu.CompilerParams(vmem_limit_bytes=VMEM_BYTES),
        cost_estimate=pl.CostEstimate(flops=flops, bytes_accessed=sum(sizes), transcendentals=0),
        name=name,
    )(*operands)


def shards(
    queries,
    key_vectors,
    value_vectors,
    log_decay,
    doc_ids,
    head_gain,
    output_weight,
    residual,
    norm_gain,
    routing,
    route_weights,
    gate_weight,
    up_weight,
    down_weight,
):
    tokens, heads = log_decay.shape
    hw = queries.shape[1] // heads
    n_seq, n_head = lax.axis_size("seq"), lax.axis_size("head")
    ny, nz, nx = n_seq // n_head, n_head, n_head // CORES
    s, h = lax.axis_index("seq"), lax.axis_index("head")
    z, y = s // ny, s % ny
    x, c = h // CORES, h % CORES
    part = residual.shape[1]
    model_width = part * n_head

    cols = output_weight.shape[1]
    w_z = jnp.zeros((output_weight.shape[0], ny * cols), BF16)
    w_z = lax.dynamic_update_slice(w_z, output_weight, (0, y * cols))
    for k in range(1, ny):
        got = permute_seq(output_weight, lambda q, k=k: q // ny * ny + (q % ny - k) % ny)
        w_z = lax.dynamic_update_slice(w_z, got, (0, (y + k) % ny * cols))

    struct = jax.ShapeDtypeStruct
    doc_row = doc_ids.reshape(1, tokens)
    rows, held, extra = chunk_plan(heads, hw, n_seq)
    work = 2 * tokens * hw * hw * heads
    payload, decay_sum = local_call(
        state_kernel,
        "block_state",
        [struct((n_seq, rows + extra, hw), BF16), struct((tokens, heads), F32)],
        work,
        doc_row,
        log_decay,
        key_vectors,
        value_vectors,
    )
    blocks = lax.all_to_all(payload, "seq", split_axis=0, concat_axis=0, tiled=True)
    back = local_call(scan_kernel, "carry", struct((n_seq, rows, hw), BF16), work, blocks)
    back, w_z = lax.optimization_barrier((back, w_z))
    carried = lax.all_to_all(back, "seq", split_axis=0, concat_axis=0, tiled=True)
    carried = carried.reshape(heads, hw, hw)
    inside = local_call(
        inside_kernel,
        "inside",
        struct((tokens, heads * hw), F32),
        2 * work,
        doc_row,
        decay_sum,
        decay_sum.T,
        queries,
        key_vectors,
        value_vectors,
    )
    attended = local_call(
        outside_kernel,
        "outside",
        struct((tokens, heads * hw), BF16),
        work,
        doc_row,
        decay_sum,
        queries,
        carried,
        inside,
        head_gain.reshape(1, heads * hw),
    )

    products = []
    for k in range(nz):
        rows_k = attended
        if k:
            rows_k = permute_seq(
                attended, lambda q, k=k: (q // ny - k) % nz * ny + q % ny
            )
        products.append(jnp.dot(rows_k, w_z, preferred_element_type=F32).astype(BF16))
    products = jnp.stack(products)
    total = pick(products, (h - z) % nz).astype(F32)
    for m in range(1, n_head):
        sent = pick(products, (h + m - z) % nz)
        total = total + permute_head(sent, lambda q, m=m: (q + m) % n_head).astype(F32)
    spots = [
        ((zz * ny + yy) * n_head + hh, (hh * ny + yy) * n_head + zz)
        for zz in range(nz)
        for yy in range(ny)
        for hh in range(n_head)
    ]
    summed = lax.ppermute(total.astype(BF16), ("seq", "head"), spots).astype(F32)
    middle = lax.optimization_barrier((summed + residual.astype(F32)).astype(BF16))

    experts = n_seq
    capacity = 4 * tokens // experts
    flat_ids = routing.reshape(-1)
    hits = (flat_ids[:, None] == jnp.arange(experts, dtype=jnp.int32)[None, :]).astype(F32)
    pair_row = lax.broadcasted_iota(jnp.int32, (2 * tokens, 2 * tokens), 0)
    pair_col = lax.broadcasted_iota(jnp.int32, (2 * tokens, 2 * tokens), 1)
    earlier = jnp.dot((pair_col < pair_row).astype(F32), hits)
    rank = jnp.sum(earlier * hits, axis=1).astype(jnp.int32)
    place = (flat_ids * capacity + rank).reshape(tokens, 2)
    half = capacity // HALVES
    slot = jnp.arange(experts * half, dtype=jnp.int32)
    slot = slot // half * capacity + slot % half
    in_owner = [h] + [(h + m * CORES) % n_head for m in range(1, nx)]
    in_owner += [
        o // CORES * CORES + (o % CORES + m) % CORES for o in in_owner for m in range(1, CORES)
    ]
    out_owner = [
        (x + m) % nx * CORES + (c + k) % CORES for k in [*range(1, CORES), 0] for m in range(nx)
    ]
    owners = jnp.stack(in_owner + out_owner).astype(jnp.int32)

    mixed = middle.astype(F32)
    for q in range(HALVES):
        here = place[:, :, None] == (slot + q * half)[None, None, :]
        take = jnp.any(here, axis=1).astype(BF16)
        mix = jnp.sum(jnp.where(here, route_weights[:, :, None], 0.0), axis=1)

        outgoing = lax.dot_general(
            take, middle, (((0,), (0,)), ((), ())), preferred_element_type=F32
        ).astype(BF16)
        got = lax.all_to_all(
            outgoing.reshape(experts, half, part), "seq", split_axis=0, concat_axis=0, tiled=True
        ).reshape(experts * half, part)
        pieces = [got]
        for m in range(1, nx):
            pieces.append(permute_head(got, lambda q, m=m: (q - m * CORES) % n_head))
        for piece in list(pieces):
            for m in range(1, CORES):
                pieces.append(
                    permute_head(
                        piece, lambda q, m=m: q // CORES * CORES + (q % CORES - m) % CORES
                    )
                )
        sent, kept = expert_call(owners, pieces, norm_gain, gate_weight, up_weight, down_weight)

        near = permute_head(sent, lambda q: q // CORES * CORES + (q % CORES + 1) % CORES)
        near_sum = kept.astype(F32) + near.astype(F32)
        total = near_sum[0]
        for m in range(1, nx):
            total = total + permute_head(
                near_sum[m].astype(BF16), lambda q, m=m: (q + m * CORES) % n_head
            ).astype(F32)
        returned = lax.all_to_all(
            total.astype(BF16).reshape(experts, half, part),
            "seq",
            split_axis=0,
            concat_axis=0,
            tiled=True,
        ).reshape(experts * half, part)
        mixed = mixed + jnp.dot(
            mix, returned.astype(F32), precision=HIGHEST, preferred_element_type=F32
        )
    return mixed.astype(BF16)


def solution(mesh):
    placed = (
        P("seq", "head"),
        P("seq", "head"),
        P("seq", "head"),
        P("seq", "head"),
        P("seq"),
        P("head"),
        P("head", "seq"),
        P("seq", "head"),
        P(),
        P("seq", None),
        P("seq", None),
        P("seq", None, "head"),
        P("seq", None, "head"),
        P("seq", "head", None),
    )
    return jax.shard_map(
        shards, mesh=mesh, in_specs=placed, out_specs=P("seq", "head"), check_vma=False
    )
```

time: 312 us -> 261 us (0.84)
  Pallas kernels: 0 us -> 36.7 us
  blocking collectives: 34.1 us -> 0 us
  matrix products: 43.1 us -> 13.6 us
  local copies, waits for them, and re-layouts: 37.4 us -> 10.3 us
  starting transfers between devices: 27.4 us -> 52.4 us
  other arithmetic: 16.1 us -> 2.48 us
  between operations: 12 us -> 0.32 us
    pallas_call x0 -> x6, Pallas kernels: none -> 36.7 us  [the longest x2 29.5 us: expert_call(): pl.pallas_call(functools.partial(expert_kernel, n_head, steps), grid_spec...]
    all_to_all x1 -> x0, blocking collectives: 34.1 us -> none  [shards(): lax.all_to_all(outgoing.reshape(experts, capacity, part), 'seq', split_ax...]
    dot_general x7 -> x2, matrix products: 32.4 us -> 1.35 us  [shards(): jnp.dot(mix, returned.astype(F32), precision=HIGHEST, preferred_element_t...]
    all_to_all x1 -> x4, starting transfers between devices: 3.9 us -> 29.8 us  [the longest x2 18.1 us: shards(): lax.all_to_all(outgoing.reshape(experts, half, part), 'seq', split_axis=0...]
    ppermute x4, waiting for transfers between devices: 51.1 us -> 36.4 us  [permute_seq(): lax.ppermute(value, 'seq', [(source, move(source)) for source in range(co...]
    all_to_all x1 -> x4, waiting for transfers between devices: 19.8 us -> 33.2 us  [the longest x2 23.4 us: shards(): lax.all_to_all(outgoing.reshape(experts, half, part), 'seq', split_axis=0...]
    all_to_all x1, waiting for transfers between devices: 14.6 us -> 27 us  [shards(): lax.all_to_all(payload, 'seq', split_axis=0, concat_axis=0, tiled=True)]
    ppermute x8 -> x13, waiting for transfers between devices: 48.6 us -> 36.4 us  [permute_head(): lax.ppermute(value, 'head', [(source, move(source)) for source in range(c...]
  transfers between devices with their start and end apart: 16 -> 24, of which waited for: 11 -> 15; matrix products, arithmetic and copies ran while one was open for 8% -> 6% of each run, Pallas kernels for 0% -> 13%
where the time goes in v2:
time: 261 us; the launch traced here: 260 us
  waiting for transfers between devices  144 us (55%)
  starting transfers between devices  52.4 us (20%)
  Pallas kernels  36.7 us (14%)
  matrix products  13.6 us (5%)
  local copies, waits for them, and re-layouts  10.3 us (4%)
    ppermute x4, waiting for transfers between devices, permute_seq(): lax.ppermute(value, 'seq', [(source, move(source)) for source in range(co...  36.4 us
    ppermute x13, waiting for transfers between devices, permute_head(): lax.ppermute(value, 'head', [(source, move(source)) for source in range(c...  36.4 us
    pallas_call x2, Pallas kernels, expert_call(): pl.pallas_call(functools.partial(expert_kernel, n_head, steps), grid_spec...  29.5 us
    all_to_all x1, waiting for transfers between devices, shards(): lax.all_to_all(payload, 'seq', split_axis=0, concat_axis=0, tiled=True)  27 us
    all_to_all x2, waiting for transfers between devices, shards(): lax.all_to_all(outgoing.reshape(experts, half, part), 'seq', split_axis=0...  23.4 us
    all_to_all x2, starting transfers between devices, shards(): lax.all_to_all(outgoing.reshape(experts, half, part), 'seq', split_axis=0...  18.1 us
    all_to_all x2, starting transfers between devices, shards(): lax.all_to_all(total.astype(BF16).reshape(experts, half, part), 'seq', sp...  11.8 us
    all_to_all x1, waiting for transfers between devices, shards(): lax.all_to_all(back, 'seq', split_axis=0, concat_axis=0, tiled=True)  11.1 us
  transfers between devices with their start and end apart: 24, of which 15 were waited for; matrix products, arithmetic and copies ran while one was open for 6% of the time, Pallas kernels for 13%

profile of v2, /device:TPU:0, one launch (start us, length us, event | category | flops | bytes accessed | tf_op | source)
XLA Modules:
  0.0 259.9 jit_solution(17031563529372344742)
XLA Ops:
  0.0 3.0 %collective-permute-start = (bf16[2048,384]{1,0:T(8,128)(2,1)}, bf16[2048,384]{1,0:T(8,128)(2,1)}, u32[]{:S(2)}, u32[]{:S(2)}) collective-permute-start(bf16[2048,384]{1,0:T(8,128)(2,1)} %param.20), channel_id=1, source_target_pairs={{0,4},{4,0},{8,12},{12,8},{16,20},{20,16},{24,28},{28,24},{1,5},{5... | collective-permute-start | bytes 4718600 | tf_op jit(solution)/shard_map/ppermute | solution.py:22
  6.5 1.9 block_state.1
  8.4 4.9 %all-to-all-start = ((bf16[8,272,128]{2,1,0:T(8,128)(2,1)}), bf16[8,272,128]{2,1,0:T(8,128)(2,1)S(1)}, u32[]{:S(2)}, u32[]{:S(2)}) async-start(bf16[8,272,128]{2,1,0:T(8,128)(2,1)} %get-tuple-element.14), calls=%async_computation | async-start | bytes 1114112 | tf_op jit(solution)/shard_map/all_to_all | solution.py:285
  13.3 1.8 broadcast_in_dim.24
  16.5 27.0 %all-to-all-done.blocks_ref = bf16[8,272,128]{2,1,0:T(8,128)(2,1)S(1)} async-done(((bf16[8,272,128]{2,1,0:T(8,128)(2,1)}), bf16[8,272,128]{2,1,0:T(8,128)(2,1)S(1)}, u32[]{:S(2)}, u32[]{:S(2)}) %all-to-all-start) | async-done | bytes 557088 | tf_op jit(solution)/shard_map/all_to_all | solution.py:285
  44.5 2.8 %constant_dynamic-update-slice_fusion = bf16[2048,768]{1,0:T(8,128)(2,1)} fusion(bf16[2048,768]{1,0:T(8,128)(2,1)} %constant_dynamic-update-slice_fusion.1, bf16[2048,384]{1,0:T(8,128)(2,1)} %collective-permute-done, s32[]{:T(128)S(6)} %select_n.140), kind=kLoop, calls=%fused_computation.51 | loop fusion | bytes 3145732 | tf_op jit(solution)/shard_map/dynamic_update_slice | solution.py:269
  47.3 6.2 %all-to-all-start.1 = ((bf16[8,256,128]{2,1,0:T(8,128)(2,1)}), bf16[8,256,128]{2,1,0:T(8,128)(2,1)S(1)}, u32[]{:S(2)}, u32[]{:S(2)}) async-start(bf16[8,256,128]{2,1,0:T(8,128)(2,1)} %carry.1), calls=%async_computation.1 | async-start | bytes 1048576 | tf_op jit(solution)/shard_map/all_to_all | solution.py:288
  53.6 2.6 %inside.1.inside_ref = f32[128,2048]{1,0:T(8,128)S(1)} custom-call(s32[1,128]{1,0:T(1,128)S(1)} %bitcast.82, f32[128,16]{1,0:T(8,128)S(1)} %get-tuple-element.13.sum_ref, f32[16,128]{1,0:T(8,128)S(1)} %bitcast.79, bf16[128,2048]{1,0:T(8,128)(2,1)S(1)} %copy-done.4, bf16[128,2048]{1,0:T(8,128)(2,1)S(1)} %copy-done.1, bf16[128,2048]{1,0:T(8,128)(2,1)S(1)} %copy-done.3), custom_call_target="tpu_custom_call" | custom-call | flops 134217728 | bytes 2638336 | tf_op jit(solution)/shard_map/inside/pallas_call | solution.py:229
  56.2 11.1 %all-to-all-done.1 = bf16[8,256,128]{2,1,0:T(8,128)(2,1)S(1)} async-done(((bf16[8,256,128]{2,1,0:T(8,128)(2,1)}), bf16[8,256,128]{2,1,0:T(8,128)(2,1)S(1)}, u32[]{:S(2)}, u32[]{:S(2)}) %all-to-all-start.1) | async-done | bytes 524320 | tf_op jit(solution)/shard_map/all_to_all | solution.py:288
  67.3 1.7 outside.1
  72.5 2.5 fusion.1
  75.0 8.6 %collective-permute-done.1 = bf16[128,2048]{1,0:T(8,128)(2,1)S(1)} collective-permute-done((bf16[128,2048]{1,0:T(8,128)(2,1)S(1)}, bf16[128,2048]{1,0:T(8,128)(2,1)S(1)}, u32[]{:S(2)}, u32[]{:S(2)}) %collective-permute-start.1) | collective-permute-done | bytes 524320 | tf_op jit(solution)/shard_map/ppermute | solution.py:22
  83.6 2.5 fusion.2
  86.0 27.9 %collective-permute-done.2 = bf16[128,2048]{1,0:T(8,128)(2,1)S(1)} collective-permute-done((bf16[128,2048]{1,0:T(8,128)(2,1)S(1)}, bf16[128,2048]{1,0:T(8,128)(2,1)S(1)}, u32[]{:S(2)}, u32[]{:S(2)}) %collective-permute-start.2) | collective-permute-done | bytes 524320 | tf_op jit(solution)/shard_map/ppermute | solution.py:22
  113.9 2.5 fusion.3
  116.4 2.5 fusion.4
  119.2 1.6 collective-permute-start.5
  122.1 3.6 %collective-permute-done.4 = bf16[128,768]{1,0:T(8,128)(2,1)S(1)} collective-permute-done((bf16[128,768]{1,0:T(8,128)(2,1)S(1)}, bf16[128,768]{1,0:T(8,128)(2,1)S(1)}, u32[]{:S(2)}, u32[]{:S(2)}) %collective-permute-start.4) | collective-permute-done | bytes 196640 | tf_op jit(solution)/shard_map/ppermute | solution.py:27
  127.0 2.6 %collective-permute-done.6 = bf16[128,768]{1,0:T(8,128)(2,1)S(1)} collective-permute-done((bf16[128,768]{1,0:T(8,128)(2,1)S(1)}, bf16[128,768]{1,0:T(8,128)(2,1)S(1)}, u32[]{:S(2)}, u32[]{:S(2)}) %collective-permute-start.6) | collective-permute-done | bytes 196640 | tf_op jit(solution)/shard_map/ppermute | solution.py:27
  131.6 14.4 %all-to-all-start.2 = ((bf16[8,32,768]{2,1,0:T(8,128)(2,1)}), bf16[8,32,768]{2,1,0:T(8,128)(2,1)S(1)}, u32[]{:S(2)}, u32[]{:S(2)}) async-start(bf16[8,32,768]{2,1,0:T(8,128)(2,1)} %bitcast.20), calls=%async_computation.2 | async-start | bytes 786432 | tf_op jit(solution)/shard_map/all_to_all | solution.py:367
  147.1 11.6 %all-to-all-done.2 = bf16[8,32,768]{2,1,0:T(8,128)(2,1)S(1)} async-done(((bf16[8,32,768]{2,1,0:T(8,128)(2,1)}), bf16[8,32,768]{2,1,0:T(8,128)(2,1)S(1)}, u32[]{:S(2)}, u32[]{:S(2)}) %all-to-all-start.2) | async-done | bytes 393248 | tf_op jit(solution)/shard_map/all_to_all | solution.py:367
  158.7 3.6 %all-to-all-start.4 = ((bf16[8,32,768]{2,1,0:T(8,128)(2,1)}), bf16[8,32,768]{2,1,0:T(8,128)(2,1)S(1)}, u32[]{:S(2)}, u32[]{:S(2)}) async-start(bf16[8,32,768]{2,1,0:T(8,128)(2,1)} %bitcast.27), calls=%async_computation.4 | async-start | bytes 786432 | tf_op jit(solution)/shard_map/all_to_all | solution.py:367
  162.4 11.8 %all-to-all-done.4 = bf16[8,32,768]{2,1,0:T(8,128)(2,1)S(1)} async-done(((bf16[8,32,768]{2,1,0:T(8,128)(2,1)}), bf16[8,32,768]{2,1,0:T(8,128)(2,1)S(1)}, u32[]{:S(2)}, u32[]{:S(2)}) %all-to-all-start.4) | async-done | bytes 393248 | tf_op jit(solution)/shard_map/all_to_all | solution.py:367
  174.9 7.7 %collective-permute-done.13.refs_1_ = bf16[256,768]{1,0:T(8,128)(2,1)S(1)} collective-permute-done((bf16[256,768]{1,0:T(8,128)(2,1)S(1)}, bf16[256,768]{1,0:T(8,128)(2,1)S(1)}, u32[]{:S(2)}, u32[]{:S(2)}) %collective-permute-start.13) | collective-permute-done | bytes 393248 | tf_op jit(solution)/shard_map/ppermute | solution.py:27
  182.7 14.8 %expert.2 = (bf16[2,256,768]{2,1,0:T(8,128)(2,1)S(1)}, bf16[2,256,768]{2,1,0:T(8,128)(2,1)S(1)}) custom-call(s32[8]{0:T(128)S(1)} %stack.55.owner_ref, bf16[256,768]{1,0:T(8,128)(2,1)S(1)} %bitcast.76, bf16[256,768]{1,0:T(8,128)(2,1)S(1)} %collective-permute-done.8.refs_1_, bf16[256,768]{1,0:T(8,128)(2,1)S(1)} %collective-permute-done.9.refs_2_, ...), custom_call_target="tpu_custom_call" | custom-call | flops 5435817984 | bytes 24379392 | tf_op jit(solution)/shard_map/expert/pallas_call | solution.py:207
  198.0 14.8 %expert.3 = (bf16[2,256,768]{2,1,0:T(8,128)(2,1)S(1)}, bf16[2,256,768]{2,1,0:T(8,128)(2,1)S(1)}) custom-call(s32[8]{0:T(128)S(1)} %stack.55.owner_ref, bf16[256,768]{1,0:T(8,128)(2,1)S(1)} %bitcast.73, bf16[256,768]{1,0:T(8,128)(2,1)S(1)} %collective-permute-done.13.refs_1_, bf16[256,768]{1,0:T(8,128)(2,1)S(1)} %collective-permute-done.14.refs_2_, ...), custom_call_target="tpu_custom_call" | custom-call | flops 5435817984 | bytes 24379392 | tf_op jit(solution)/shard_map/expert/pallas_call | solution.py:207
  213.4 1.7 collective-permute-done.16
  215.3 9.4 %collective-permute-done.12 = bf16[256,768]{1,0:T(8,128)(2,1)S(1)} collective-permute-done((bf16[256,768]{1,0:T(8,128)(2,1)S(1)}, bf16[256,768]{1,0:T(8,128)(2,1)S(1)}, u32[]{:S(2)}, u32[]{:S(2)}) %collective-permute-start.12) | collective-permute-done | bytes 393248 | tf_op jit(solution)/shard_map/ppermute | solution.py:27
  225.5 6.3 %all-to-all-start.3 = ((bf16[8,32,768]{2,1,0:T(8,128)(2,1)}), bf16[8,32,768]{2,1,0:T(8,128)(2,1)S(1)}, u32[]{:S(2)}, u32[]{:S(2)}) async-start(bf16[8,32,768]{2,1,0:T(8,128)(2,1)} %bitcast.25), calls=%async_computation.3 | async-start | bytes 786432 | tf_op jit(solution)/shard_map/all_to_all | solution.py:389
  232.1 10.1 %collective-permute-done.17 = bf16[256,768]{1,0:T(8,128)(2,1)S(1)} collective-permute-done((bf16[256,768]{1,0:T(8,128)(2,1)S(1)}, bf16[256,768]{1,0:T(8,128)(2,1)S(1)}, u32[]{:S(2)}, u32[]{:S(2)}) %collective-permute-start.17) | collective-permute-done | bytes 393248 | tf_op jit(solution)/shard_map/ppermute | solution.py:27
  243.3 5.5 %all-to-all-start.5 = ((bf16[8,32,768]{2,1,0:T(8,128)(2,1)}), bf16[8,32,768]{2,1,0:T(8,128)(2,1)S(1)}, u32[]{:S(2)}, u32[]{:S(2)}) async-start(bf16[8,32,768]{2,1,0:T(8,128)(2,1)} %bitcast.31), calls=%async_computation.5 | async-start | bytes 786432 | tf_op jit(solution)/shard_map/all_to_all | solution.py:389
  249.3 9.6 %all-to-all-done.5 = bf16[8,32,768]{2,1,0:T(8,128)(2,1)S(1)} async-done(((bf16[8,32,768]{2,1,0:T(8,128)(2,1)}), bf16[8,32,768]{2,1,0:T(8,128)(2,1)S(1)}, u32[]{:S(2)}, u32[]{:S(2)}) %all-to-all-start.5) | async-done | bytes 393248 | tf_op jit(solution)/shard_map/all_to_all | solution.py:389
  (82 shorter events, 21.3 us)
Async XLA Ops:
  0.0 44.5 %collective-permute-start = (bf16[2048,384]{1,0:T(8,128)(2,1)}, bf16[2048,384]{1,0:T(8,128)(2,1)}, u32[]{:S(2)}, u32[]{:S(2)}) collective-permute-start(bf16[2048,384]{1,0:T(8,128)(2,1)} %param.20), channel_id=1, source_target_pairs={{0,4},{4,0},{8,12},{12,8},{16,20},{20,16},{24,28},{28,24},{1,5},{5... | collective-permute-start | bytes 4718600 | tf_op jit(solution)/shard_map/ppermute | solution.py:22
  8.4 35.1 %all-to-all-start = ((bf16[8,272,128]{2,1,0:T(8,128)(2,1)}), bf16[8,272,128]{2,1,0:T(8,128)(2,1)S(1)}, u32[]{:S(2)}, u32[]{:S(2)}) async-start(bf16[8,272,128]{2,1,0:T(8,128)(2,1)} %get-tuple-element.14), calls=%async_computation | async-start | bytes 1114112 | tf_op jit(solution)/shard_map/all_to_all | solution.py:285
  16.5 37.0 %copy-start.1 = (bf16[128,2048]{1,0:T(8,128)(2,1)S(1)}, bf16[128,2048]{1,0:T(8,128)(2,1)}, u32[]{:S(2)}) copy-start(bf16[128,2048]{1,0:T(8,128)(2,1)} %k_ref.3) | copy-start | bytes 1572868
  16.5 37.0 %copy-start.3 = (bf16[128,2048]{1,0:T(8,128)(2,1)S(1)}, bf16[128,2048]{1,0:T(8,128)(2,1)}, u32[]{:S(2)}) copy-start(bf16[128,2048]{1,0:T(8,128)(2,1)} %v_ref.3) | copy-start | bytes 1572868
  16.5 37.1 %copy-start.4 = (bf16[128,2048]{1,0:T(8,128)(2,1)S(1)}, bf16[128,2048]{1,0:T(8,128)(2,1)}, u32[]{:S(2)}) copy-start(bf16[128,2048]{1,0:T(8,128)(2,1)} %q_ref.3) | copy-start | bytes 1572868
  16.5 37.1 %copy-start.8 = (s32[128]{0:T(128)S(1)}, s32[128]{0:T(128)}, u32[]{:S(2)}) copy-start(s32[128]{0:T(128)} %param.18) | copy-start | bytes 1540
  44.5 22.8 %copy-start.6 = (f32[2048]{0:T(1024)S(1)}, f32[2048]{0:T(1024)}, u32[]{:S(2)}) copy-start(f32[2048]{0:T(1024)} %param.19) | copy-start | bytes 24580
  47.3 22.8 %copy-start.11 = (s32[128,2]{0,1:T(2,128)S(1)}, s32[128,2]{0,1:T(2,128)}, u32[]{:S(2)}) copy-start(s32[128,2]{0,1:T(2,128)} %param.23) | copy-start | bytes 3076
  47.3 19.9 %all-to-all-start.1 = ((bf16[8,256,128]{2,1,0:T(8,128)(2,1)}), bf16[8,256,128]{2,1,0:T(8,128)(2,1)S(1)}, u32[]{:S(2)}, u32[]{:S(2)}) async-start(bf16[8,256,128]{2,1,0:T(8,128)(2,1)} %carry.1), calls=%async_computation.1 | async-start | bytes 1048576 | tf_op jit(solution)/shard_map/all_to_all | solution.py:288
  69.0 14.6 %collective-permute-start.1 = (bf16[128,2048]{1,0:T(8,128)(2,1)S(1)}, bf16[128,2048]{1,0:T(8,128)(2,1)S(1)}, u32[]{:S(2)}, u32[]{:S(2)}) collective-permute-start(bf16[128,2048]{1,0:T(8,128)(2,1)S(1)} %outside.1), channel_id=1, source_target_pairs={{0,24},{4,28},{8,0},{12,4},{16,8},{20,12},{24,16},{28,20},{1,25},{... | collective-permute-start | bytes 1572872 | tf_op jit(solution)/shard_map/ppermute | solution.py:22
  70.8 43.1 %collective-permute-start.2 = (bf16[128,2048]{1,0:T(8,128)(2,1)S(1)}, bf16[128,2048]{1,0:T(8,128)(2,1)S(1)}, u32[]{:S(2)}, u32[]{:S(2)}) collective-permute-start(bf16[128,2048]{1,0:T(8,128)(2,1)S(1)} %outside.1), channel_id=1, source_target_pairs={{0,16},{4,20},{8,24},{12,28},{16,0},{20,4},{24,8},{28,12},{1,17},{... | collective-permute-start | bytes 1572872 | tf_op jit(solution)/shard_map/ppermute | solution.py:22
  71.9 44.5 %collective-permute-start.3 = (bf16[128,2048]{1,0:T(8,128)(2,1)S(1)}, bf16[128,2048]{1,0:T(8,128)(2,1)S(1)}, u32[]{:S(2)}, u32[]{:S(2)}) collective-permute-start(bf16[128,2048]{1,0:T(8,128)(2,1)S(1)} %outside.1), channel_id=1, source_target_pairs={{0,8},{4,12},{8,16},{12,20},{16,24},{20,28},{24,0},{28,4},{1,9},{5... | collective-permute-start | bytes 1572872 | tf_op jit(solution)/shard_map/ppermute | solution.py:22
  119.0 63.6 %copy-start.5 = (f32[3072]{0:T(1024)S(1)}, f32[3072]{0:T(1024)}, u32[]{:S(2)}) copy-start(f32[3072]{0:T(1024)} %param.22) | copy-start | bytes 36868
  119.1 6.6 %collective-permute-start.4 = (bf16[128,768]{1,0:T(8,128)(2,1)S(1)}, bf16[128,768]{1,0:T(8,128)(2,1)S(1)}, u32[]{:S(2)}, u32[]{:S(2)}) collective-permute-start(bf16[128,768]{1,0:T(8,128)(2,1)S(1)} %get-tuple-element.25), channel_id=1, source_target_pairs={{0,1},{1,2},{2,3},{3,0},{4,5},{5,6},{6,7},{7,4},{8,9},{9,10},{10,1... | collective-permute-start | bytes 589832 | tf_op jit(solution)/shard_map/ppermute | solution.py:27
  119.2 7.8 %collective-permute-start.5 = (bf16[128,768]{1,0:T(8,128)(2,1)S(1)}, bf16[128,768]{1,0:T(8,128)(2,1)S(1)}, u32[]{:S(2)}, u32[]{:S(2)}) collective-permute-start(bf16[128,768]{1,0:T(8,128)(2,1)S(1)} %get-tuple-element.27), channel_id=1, source_target_pairs={{0,2},{1,3},{2,0},{3,1},{4,6},{5,7},{6,4},{7,5},{8,10},{9,11},{10,... | collective-permute-start | bytes 589832 | tf_op jit(solution)/shard_map/ppermute | solution.py:27
  120.7 8.9 %collective-permute-start.6 = (bf16[128,768]{1,0:T(8,128)(2,1)S(1)}, bf16[128,768]{1,0:T(8,128)(2,1)S(1)}, u32[]{:S(2)}, u32[]{:S(2)}) collective-permute-start(bf16[128,768]{1,0:T(8,128)(2,1)S(1)} %get-tuple-element.26), channel_id=1, source_target_pairs={{0,3},{1,0},{2,1},{3,2},{4,7},{5,4},{6,5},{7,6},{8,11},{9,8},{10,9... | collective-permute-start | bytes 589832 | tf_op jit(solution)/shard_map/ppermute | solution.py:27
  129.7 0.8 collective-permute-start.7
  131.6 27.1 %all-to-all-start.2 = ((bf16[8,32,768]{2,1,0:T(8,128)(2,1)}), bf16[8,32,768]{2,1,0:T(8,128)(2,1)S(1)}, u32[]{:S(2)}, u32[]{:S(2)}) async-start(bf16[8,32,768]{2,1,0:T(8,128)(2,1)} %bitcast.20), calls=%async_computation.2 | async-start | bytes 786432 | tf_op jit(solution)/shard_map/all_to_all | solution.py:367
  158.7 15.6 %all-to-all-start.4 = ((bf16[8,32,768]{2,1,0:T(8,128)(2,1)}), bf16[8,32,768]{2,1,0:T(8,128)(2,1)S(1)}, u32[]{:S(2)}, u32[]{:S(2)}) async-start(bf16[8,32,768]{2,1,0:T(8,128)(2,1)} %bitcast.27), calls=%async_computation.4 | async-start | bytes 786432 | tf_op jit(solution)/shard_map/all_to_all | solution.py:367
  162.3 11.9 %collective-permute-start.8 = (bf16[256,768]{1,0:T(8,128)(2,1)S(1)}, bf16[256,768]{1,0:T(8,128)(2,1)S(1)}, u32[]{:S(2)}, u32[]{:S(2)}) collective-permute-start(bf16[256,768]{1,0:T(8,128)(2,1)S(1)} %bitcast.74), channel_id=1, source_target_pairs={{0,2},{1,3},{2,0},{3,1},{4,6},{5,7},{6,4},{7,5},{8,10},{9,11},{10,... | collective-permute-start | bytes 1179656 | tf_op jit(solution)/shard_map/ppermute | solution.py:27
  174.2 8.4 %collective-permute-start.13 = (bf16[256,768]{1,0:T(8,128)(2,1)S(1)}, bf16[256,768]{1,0:T(8,128)(2,1)S(1)}, u32[]{:S(2)}, u32[]{:S(2)}) collective-permute-start(bf16[256,768]{1,0:T(8,128)(2,1)S(1)} %bitcast.71), channel_id=1, source_target_pairs={{0,2},{1,3},{2,0},{3,1},{4,6},{5,7},{6,4},{7,5},{8,10},{9,11},{10,... | collective-permute-start | bytes 1179656 | tf_op jit(solution)/shard_map/ppermute | solution.py:27
  174.2 8.4 %collective-permute-start.9 = (bf16[256,768]{1,0:T(8,128)(2,1)S(1)}, bf16[256,768]{1,0:T(8,128)(2,1)S(1)}, u32[]{:S(2)}, u32[]{:S(2)}) collective-permute-start(bf16[256,768]{1,0:T(8,128)(2,1)S(1)} %bitcast.75), channel_id=1, source_target_pairs={{0,1},{1,0},{2,3},{3,2},{4,5},{5,4},{6,7},{7,6},{8,9},{9,8},{10,11... | collective-permute-start | bytes 1179656 | tf_op jit(solution)/shard_map/ppermute | solution.py:27
  174.3 8.4 %collective-permute-start.10 = (bf16[256,768]{1,0:T(8,128)(2,1)S(1)}, bf16[256,768]{1,0:T(8,128)(2,1)S(1)}, u32[]{:S(2)}, u32[]{:S(2)}) collective-permute-start(bf16[256,768]{1,0:T(8,128)(2,1)S(1)} %collective-permute-done.8.refs_1_), channel_id=1, source_target_pairs={{0,1},{1,0},{2,3},{3,2},{4,5},{5,4},{6,7},{7,6},{8,9},{9,8},{10,11... | collective-permute-start | bytes 1179656 | tf_op jit(solution)/shard_map/ppermute | solution.py:27
  174.8 23.1 %collective-permute-start.14 = (bf16[256,768]{1,0:T(8,128)(2,1)S(1)}, bf16[256,768]{1,0:T(8,128)(2,1)S(1)}, u32[]{:S(2)}, u32[]{:S(2)}) collective-permute-start(bf16[256,768]{1,0:T(8,128)(2,1)S(1)} %bitcast.72), channel_id=1, source_target_pairs={{0,1},{1,0},{2,3},{3,2},{4,5},{5,4},{6,7},{7,6},{8,9},{9,8},{10,11... | collective-permute-start | bytes 1179656 | tf_op jit(solution)/shard_map/ppermute | solution.py:27
  182.6 15.4 %collective-permute-start.15 = (bf16[256,768]{1,0:T(8,128)(2,1)S(1)}, bf16[256,768]{1,0:T(8,128)(2,1)S(1)}, u32[]{:S(2)}, u32[]{:S(2)}) collective-permute-start(bf16[256,768]{1,0:T(8,128)(2,1)S(1)} %collective-permute-done.13.refs_1_), channel_id=1, source_target_pairs={{0,1},{1,0},{2,3},{3,2},{4,5},{5,4},{6,7},{7,6},{8,9},{9,8},{10,11... | collective-permute-start | bytes 1179656 | tf_op jit(solution)/shard_map/ppermute | solution.py:27
  197.4 15.4 %collective-permute-start.11 = (bf16[2,256,768]{2,1,0:T(8,128)(2,1)S(1)}, bf16[2,256,768]{2,1,0:T(8,128)(2,1)S(1)}, u32[]{:S(2)}, u32[]{:S(2)}) collective-permute-start(bf16[2,256,768]{2,1,0:T(8,128)(2,1)S(1)} %get-tuple-element.18), channel_id=1, source_target_pairs={{0,1},{1,0},{2,3},{3,2},{4,5},{5,4},{6,7},{7,6},{8,9},{9,8},{10,11... | collective-permute-start | bytes 2359304 | tf_op jit(solution)/shard_map/ppermute | solution.py:27
  212.8 2.4 collective-permute-start.16
  213.1 11.6 %collective-permute-start.12 = (bf16[256,768]{1,0:T(8,128)(2,1)S(1)}, bf16[256,768]{1,0:T(8,128)(2,1)S(1)}, u32[]{:S(2)}, u32[]{:S(2)}) collective-permute-start(bf16[256,768]{1,0:T(8,128)(2,1)S(1)} %fusion.10), channel_id=1, source_target_pairs={{0,2},{1,3},{2,0},{3,1},{4,6},{5,7},{6,4},{7,5},{8,10},{9,11},{10,... | collective-permute-start | bytes 1179656 | tf_op jit(solution)/shard_map/ppermute | solution.py:27
  215.3 33.5 %copy-start.12 = (f32[128,2]{0,1:T(2,128)S(1)}, f32[128,2]{0,1:T(2,128)}, u32[]{:S(2)}) copy-start(f32[128,2]{0,1:T(2,128)} %param.24) | copy-start | bytes 3076
  225.5 17.8 %all-to-all-start.3 = ((bf16[8,32,768]{2,1,0:T(8,128)(2,1)}), bf16[8,32,768]{2,1,0:T(8,128)(2,1)S(1)}, u32[]{:S(2)}, u32[]{:S(2)}) async-start(bf16[8,32,768]{2,1,0:T(8,128)(2,1)} %bitcast.25), calls=%async_computation.3 | async-start | bytes 786432 | tf_op jit(solution)/shard_map/all_to_all | solution.py:389
  231.8 10.5 %collective-permute-start.17 = (bf16[256,768]{1,0:T(8,128)(2,1)S(1)}, bf16[256,768]{1,0:T(8,128)(2,1)S(1)}, u32[]{:S(2)}, u32[]{:S(2)}) collective-permute-start(bf16[256,768]{1,0:T(8,128)(2,1)S(1)} %fusion.11), channel_id=1, source_target_pairs={{0,2},{1,3},{2,0},{3,1},{4,6},{5,7},{6,4},{7,5},{8,10},{9,11},{10,... | collective-permute-start | bytes 1179656 | tf_op jit(solution)/shard_map/ppermute | solution.py:27
  243.3 15.5 %all-to-all-start.5 = ((bf16[8,32,768]{2,1,0:T(8,128)(2,1)}), bf16[8,32,768]{2,1,0:T(8,128)(2,1)S(1)}, u32[]{:S(2)}, u32[]{:S(2)}) async-start(bf16[8,32,768]{2,1,0:T(8,128)(2,1)} %bitcast.31), calls=%async_computation.5 | async-start | bytes 786432 | tf_op jit(solution)/shard_map/all_to_all | solution.py:389
  (5 other events, 25.5 us)

commit v3 on v2

v3 whole, which is shorter than its diff:
```python
import functools
import math

import jax
import jax.numpy as jnp
from jax import lax
from jax.experimental import pallas as pl
from jax.experimental.pallas import tpu as pltpu
from jax.sharding import PartitionSpec as P

EPSILON = 1e-06
CORES = 2
F32 = jnp.float32
BF16 = jnp.bfloat16
HIGHEST = lax.Precision.HIGHEST
SMALL_VMEM = 12 * 1024 * 1024
EXPERT_VMEM = 40 * 1024 * 1024


def permute_seq(value, move):
    count = lax.axis_size("seq")
    return lax.ppermute(value, "seq", [(source, move(source)) for source in range(count)])


def permute_head(value, move):
    count = lax.axis_size("head")
    return lax.ppermute(value, "head", [(source, move(source)) for source in range(count)])


def swap_seq(blocks):
    swapped = [blocks[0]]
    for d in range(1, len(blocks)):
        swapped.append(permute_seq(blocks[d], lambda q, d=d: q ^ d))
    return swapped


def pick(stack, index, axis=0):
    return lax.dynamic_index_in_dim(stack, index, axis, keepdims=False)


def doc_column(doc):
    count = doc.shape[1]
    return jnp.broadcast_to(doc, (count, count)).T


def chunk_plan(heads, hw, n_seq):
    rows = heads * hw // n_seq
    held = max(1, rows // hw)
    extra = -(-(2 * held + 2) // 16) * 16
    return rows, held, extra


def state_kernel(me_ref, doc_ref, decay_ref, k_ref, v_ref, *refs):
    outs, sum_ref, state_ref = refs[:-2], refs[-2], refs[-1]
    tokens, heads = decay_ref.shape
    n_seq, hw = len(outs), outs[0].shape[1]
    rows, held, extra = chunk_plan(heads, hw, n_seq)
    doc = doc_ref[...].astype(F32)
    row = lax.broadcasted_iota(jnp.int32, (tokens, tokens), 0)
    col = lax.broadcasted_iota(jnp.int32, (tokens, tokens), 1)
    sums = jnp.dot(
        (col <= row).astype(F32), decay_ref[...], precision=HIGHEST, preferred_element_type=F32
    )
    sum_ref[...] = sums
    final = sums[tokens - 1 :, :]
    last = doc[:, tokens - 1 :]
    tail = jnp.exp(final - sums) * (doc_column(doc)[:, :1] == last).astype(F32)
    gain = jnp.exp(final) * (doc[:, :1] == last).astype(F32)
    lane = lax.broadcasted_iota(jnp.int32, (1, heads), 1)
    line = lax.broadcasted_iota(jnp.int32, (extra, hw), 0)
    for d in reversed(range(n_seq)):
        chunk = me_ref[0] ^ d
        note = jnp.where(line == 2 * held, doc[:, :1], 0.0)
        note = jnp.where(line == 2 * held + 1, last, note)
        for j in range(held):
            i = chunk * rows // hw + j
            mine = (lane == i).astype(F32)
            lanes = pl.ds(pl.multiple_of(i * hw, 128), hw)
            fade = jnp.sum(tail * mine, axis=1, keepdims=True)
            faded = (k_ref[:, lanes].astype(F32) * fade).astype(BF16)
            state = lax.dot_general(
                faded, v_ref[:, lanes], (((0,), (0,)), ((), ())), preferred_element_type=F32
            )
            if rows >= hw:
                outs[d][j * hw : (j + 1) * hw, :] = state.astype(BF16)
            else:
                state_ref[...] = state
                start = pl.multiple_of(chunk % (hw // rows) * rows, rows)
                outs[d][:rows, :] = state_ref[pl.ds(start, rows), :].astype(BF16)
            whole = jnp.sum(gain * mine, axis=1, keepdims=True)
            high = whole.astype(BF16).astype(F32)
            note = jnp.where(line == j, high, note)
            note = jnp.where(line == held + j, whole - high, note)
        outs[d][rows:, :] = note.astype(BF16)


def scan_kernel(me_ref, *refs):
    n_seq = (len(refs) - 2) // 2
    ins, outs, blocks_ref, entered_ref = refs[:n_seq], refs[n_seq:-2], refs[-2], refs[-1]
    _, rows, hw = entered_ref.shape
    held = max(1, rows // hw)
    part = rows // held
    for d in range(n_seq):
        blocks_ref[me_ref[0] ^ d] = ins[d][...]
    for j in range(held):
        running = jnp.zeros((part, hw), F32)
        entered_ref[0, j * part : (j + 1) * part, :] = running.astype(BF16)
        for b in range(1, n_seq):
            notes = blocks_ref[b - 1, rows:, :].astype(F32)
            gain = notes[j : j + 1] + notes[held + j : held + j + 1]
            first = blocks_ref[b, rows:, :].astype(F32)[2 * held : 2 * held + 1]
            joined = (first == notes[2 * held + 1 : 2 * held + 2]).astype(F32)
            state = blocks_ref[b - 1, j * part : (j + 1) * part, :].astype(F32)
            running = (state + gain * running) * joined
            entered_ref[b, j * part : (j + 1) * part, :] = running.astype(BF16)
    for d in range(n_seq):
        outs[d][...] = entered_ref[me_ref[0] ^ d]


def inside_kernel(doc_ref, sum_ref, sum_rows_ref, q_ref, k_ref, v_ref, out_ref):
    tokens, heads = sum_ref.shape
    hw = q_ref.shape[1] // heads
    doc = doc_ref[...].astype(F32)
    row = lax.broadcasted_iota(jnp.int32, (tokens, tokens), 0)
    col = lax.broadcasted_iota(jnp.int32, (tokens, tokens), 1)
    kept = (col <= row) & (doc_column(doc) == doc)
    for i in range(heads):
        lanes = slice(i * hw, (i + 1) * hw)
        gap = sum_ref[:, i : i + 1] - sum_rows_ref[i : i + 1, :]
        fade = jnp.where(kept, jnp.exp(jnp.minimum(gap, 0.0)), 0.0)
        scores = lax.dot_general(
            q_ref[:, lanes], k_ref[:, lanes], (((1,), (1,)), ((), ())), preferred_element_type=F32
        )
        out_ref[:, lanes] = jnp.dot(
            (scores * fade).astype(BF16), v_ref[:, lanes], preferred_element_type=F32
        )


def outside_kernel(me_ref, doc_ref, sum_ref, q_ref, inside_ref, gain_ref, *refs):
    ins, out_ref, carried_ref = refs[:-2], refs[-2], refs[-1]
    tokens, heads = sum_ref.shape
    hw = q_ref.shape[1] // heads
    rows = ins[0].shape[0]
    for d in range(len(ins)):
        start = pl.multiple_of((me_ref[0] ^ d) * rows, rows)
        carried_ref[pl.ds(start, rows), :] = ins[d][...]
    doc = doc_ref[...].astype(F32)
    reach = jnp.exp(sum_ref[...]) * (doc_column(doc)[:, :1] == doc[:, :1]).astype(F32)
    for i in range(heads):
        lanes = slice(i * hw, (i + 1) * hw)
        outside = jnp.dot(q_ref[:, lanes], carried_ref[lanes, :], preferred_element_type=F32)
        raw = inside_ref[:, lanes] + outside * reach[:, i : i + 1]
        scale = lax.rsqrt(jnp.mean(raw * raw, axis=1, keepdims=True) + EPSILON)
        out_ref[:, lanes] = (raw * scale * gain_ref[:, lanes]).astype(BF16)


def dispatch_kernel(summed_ref, residual_ref, take_ref, middle_ref, *outs):
    middle = (summed_ref[...].astype(F32) + residual_ref[...].astype(F32)).astype(BF16)
    middle_ref[...] = middle
    count = outs[0].shape[0]
    rows = jnp.dot(take_ref[...], middle, preferred_element_type=F32).astype(BF16)
    for d in range(len(outs)):
        outs[d][...] = rows[d * count : (d + 1) * count]


def mix_kernel(middle_ref, mix_ref, *refs):
    ins, out_ref, rows_ref = refs[:-2], refs[-2], refs[-1]
    count = ins[0].shape[0]
    for d in range(len(ins)):
        rows_ref[d * count : (d + 1) * count, :] = ins[d][...]
    mix = mix_ref[...]
    high = mix.astype(BF16)
    low = (mix - high.astype(F32)).astype(BF16)
    rows = rows_ref[...]
    total = jnp.dot(high, rows, preferred_element_type=F32)
    total = total + jnp.dot(low, rows, preferred_element_type=F32)
    out_ref[...] = (middle_ref[...].astype(F32) + total).astype(BF16)


def expert_kernel(n_head, owner_ref, *refs):
    pieces = refs[:n_head]
    gain_ref, gate_ref, up_ref, down_ref, sent_ref, kept_ref, rows_ref, hidden_ref = refs[n_head:]
    part = pieces[0].shape[1]
    units, nx = hidden_ref.shape[1], sent_ref.shape[0]
    squares = 0.0
    for piece in pieces:
        value = piece[...].astype(F32)
        squares = squares + jnp.sum(value * value, axis=1, keepdims=True)
    scale = lax.rsqrt(squares / (part * n_head) + EPSILON)
    for i, piece in enumerate(pieces):
        lanes = pl.ds(pl.multiple_of(owner_ref[i] * part, 128), part)
        value = piece[...].astype(F32) * scale * gain_ref[:, lanes]
        rows_ref[:, lanes] = value.astype(BF16)

    def fill(lanes):
        gate = jnp.dot(rows_ref[...], gate_ref[0, :, lanes], preferred_element_type=F32)
        up = jnp.dot(rows_ref[...], up_ref[0, :, lanes], preferred_element_type=F32)
        hidden_ref[:, lanes] = (gate / (1.0 + jnp.exp(-gate)) * up).astype(BF16)

    width = 256
    steps = units // width

    @pl.loop(0, steps)
    def _(i):
        fill(pl.ds(pl.multiple_of(i * width, 128), width))

    if units % width:
        fill(slice(steps * width, units))

    for j, out_ref in enumerate((sent_ref, kept_ref)):

        @pl.loop(0, out_ref.shape[0])
        def _(i, j=j, out_ref=out_ref):
            start = owner_ref[n_head + j * nx + i] * part
            lanes = pl.ds(pl.multiple_of(start, 128), part)
            out_ref[i] = jnp.dot(
                hidden_ref[...], down_ref[0, :, lanes], preferred_element_type=F32
            ).astype(BF16)


def local_call(kernel, name, out_shape, flops, *operands, scratch=(), scalars=0, vmem=SMALL_VMEM):
    shapes = out_shape if isinstance(out_shape, list) else [out_shape]
    sizes = [math.prod(o.shape) * o.dtype.itemsize for o in [*operands, *shapes]]
    return pl.pallas_call(
        kernel,
        out_shape=out_shape,
        in_specs=[pl.BlockSpec(memory_space=pltpu.SMEM)] * scalars
        + [pl.BlockSpec(memory_space=pltpu.VMEM)] * (len(operands) - scalars),
        scratch_shapes=list(scratch),
        compiler_params=pltpu.CompilerParams(vmem_limit_bytes=vmem),
        cost_estimate=pl.CostEstimate(flops=flops, bytes_accessed=sum(sizes), transcendentals=0),
        name=name,
    )(*operands)


def shards(
    queries,
    key_vectors,
    value_vectors,
    log_decay,
    doc_ids,
    head_gain,
    output_weight,
    residual,
    norm_gain,
    routing,
    route_weights,
    gate_weight,
    up_weight,
    down_weight,
):
    tokens, heads = log_decay.shape
    hw = queries.shape[1] // heads
    n_seq, n_head = lax.axis_size("seq"), lax.axis_size("head")
    ny, nz, nx = n_seq // n_head, n_head, n_head // CORES
    s, h = lax.axis_index("seq"), lax.axis_index("head")
    z, y = s // ny, s % ny
    x, c = h // CORES, h % CORES
    part = residual.shape[1]
    model_width = part * n_head

    struct = jax.ShapeDtypeStruct
    me = s.astype(jnp.int32).reshape(1)
    doc_row = doc_ids.reshape(1, tokens)
    rows, held, extra = chunk_plan(heads, hw, n_seq)
    work = 2 * tokens * hw * hw * heads
    *payload, decay_sum = local_call(
        state_kernel,
        "block_state",
        [struct((rows + extra, hw), BF16)] * n_seq + [struct((tokens, heads), F32)],
        work,
        me,
        doc_row,
        log_decay,
        key_vectors,
        value_vectors,
        scratch=[pltpu.VMEM((hw, hw), F32)],
        scalars=1,
    )
    entered = local_call(
        scan_kernel,
        "carry",
        [struct((rows, hw), BF16)] * n_seq,
        work,
        me,
        *swap_seq(payload),
        scratch=[
            pltpu.VMEM((n_seq, rows + extra, hw), BF16),
            pltpu.VMEM((n_seq, rows, hw), BF16),
        ],
        scalars=1,
    )
    carried = swap_seq(entered)
    inside = local_call(
        inside_kernel,
        "inside",
        struct((tokens, heads * hw), F32),
        2 * work,
        doc_row,
        decay_sum,
        decay_sum.T,
        queries,
        key_vectors,
        value_vectors,
    )
    attended = local_call(
        outside_kernel,
        "outside",
        struct((tokens, heads * hw), BF16),
        work,
        me,
        doc_row,
        decay_sum,
        queries,
        inside,
        head_gain.reshape(1, heads * hw),
        *carried,
        scratch=[pltpu.VMEM((heads * hw, hw), BF16)],
        scalars=1,
    )
    attended, output_weight = lax.optimization_barrier((attended, output_weight))

    cols = output_weight.shape[1]
    w_z = jnp.zeros((output_weight.shape[0], ny * cols), BF16)
    w_z = lax.dynamic_update_slice(w_z, output_weight, (0, y * cols))
    for k in range(1, ny):
        got = permute_seq(output_weight, lambda q, k=k: q // ny * ny + (q % ny - k) % ny)
        w_z = lax.dynamic_update_slice(w_z, got, (0, (y + k) % ny * cols))

    products = []
    for k in range(nz):
        rows_k = attended
        if k:
            rows_k = permute_seq(
                attended, lambda q, k=k: (q // ny - k) % nz * ny + q % ny
            )
        products.append(jnp.dot(rows_k, w_z, preferred_element_type=F32).astype(BF16))
    products = jnp.stack(products)
    total = pick(products, (h - z) % nz).astype(F32)
    for m in range(1, n_head):
        sent = pick(products, (h + m - z) % nz)
        total = total + permute_head(sent, lambda q, m=m: (q + m) % n_head).astype(F32)
    spots = [
        ((zz * ny + yy) * n_head + hh, (hh * ny + yy) * n_head + zz)
        for zz in range(nz)
        for yy in range(ny)
        for hh in range(n_head)
    ]
    summed = lax.ppermute(total.astype(BF16), ("seq", "head"), spots)

    experts = n_seq
    capacity = 4 * tokens // experts
    flat_ids = routing.reshape(-1)
    hits = (flat_ids[:, None] == jnp.arange(experts, dtype=jnp.int32)[None, :]).astype(F32)
    pair_row = lax.broadcasted_iota(jnp.int32, (2 * tokens, 2 * tokens), 0)
    pair_col = lax.broadcasted_iota(jnp.int32, (2 * tokens, 2 * tokens), 1)
    earlier = jnp.dot((pair_col < pair_row).astype(F32), hits)
    rank = jnp.sum(earlier * hits, axis=1).astype(jnp.int32)
    place = (flat_ids * capacity + rank).reshape(tokens, 2)
    slot = jnp.arange(experts * capacity, dtype=jnp.int32)
    slot = (slot // capacity ^ s) * capacity + slot % capacity
    here = place[:, None, :] == slot[None, :, None]
    mix = jnp.sum(jnp.where(here, route_weights[:, None, :], 0.0), axis=2)
    take = jnp.any(here, axis=2).astype(BF16).T
    in_owner = [h] + [(h + m * CORES) % n_head for m in range(1, nx)]
    in_owner += [
        o // CORES * CORES + (o % CORES + m) % CORES for o in in_owner for m in range(1, CORES)
    ]
    out_owner = [
        (x + m) % nx * CORES + (c + k) % CORES for k in [*range(1, CORES), 0] for m in range(nx)
    ]
    owners = jnp.stack(in_owner + out_owner).astype(jnp.int32)

    middle, *outgoing = local_call(
        dispatch_kernel,
        "dispatch",
        [struct((tokens, part), BF16)] + [struct((capacity, part), BF16)] * experts,
        2 * tokens * tokens * 4 * part,
        summed,
        residual,
        take,
    )
    arrived = swap_seq(outgoing)
    depth, units = gate_weight.shape[1:]
    half = experts // 2
    count = half * capacity
    results = {}
    for group in (0, 1):
        got = jnp.concatenate(arrived[group * half : (group + 1) * half])
        pieces = [got]
        for m in range(1, nx):
            pieces.append(permute_head(got, lambda q, m=m: (q - m * CORES) % n_head))
        for piece in list(pieces):
            for m in range(1, CORES):
                pieces.append(
                    permute_head(
                        piece, lambda q, m=m: q // CORES * CORES + (q % CORES - m) % CORES
                    )
                )
        results[group] = local_call(
            functools.partial(expert_kernel, n_head),
            "expert",
            [struct((nx, count, part), BF16), struct((n_head - nx, count, part), BF16)],
            6 * count * depth * units,
            owners,
            *pieces,
            norm_gain.reshape(1, depth),
            gate_weight,
            up_weight,
            down_weight,
            scratch=[pltpu.VMEM((count, depth), BF16), pltpu.VMEM((count, units), BF16)],
            scalars=1,
            vmem=EXPERT_VMEM,
        )

    returning = [None] * experts
    for group in (1, 0):
        sent, kept = results[group]
        near = permute_head(sent, lambda q: q // CORES * CORES + (q % CORES + 1) % CORES)
        near_sum = kept.astype(F32) + near.astype(F32)
        total = near_sum[0]
        for m in range(1, nx):
            total = total + permute_head(
                near_sum[m].astype(BF16), lambda q, m=m: (q + m * CORES) % n_head
            ).astype(F32)
        total = total.astype(BF16)
        for k in range(half):
            returning[group * half + k] = total[k * capacity : (k + 1) * capacity]
    return local_call(
        mix_kernel,
        "mix",
        struct((tokens, part), BF16),
        4 * tokens * experts * capacity * part,
        middle,
        mix,
        *swap_seq(returning),
        scratch=[pltpu.VMEM((experts * capacity, part), BF16)],
    )


def solution(mesh):
    placed = (
        P("seq", "head"),
        P("seq", "head"),
        P("seq", "head"),
        P("seq", "head"),
        P("seq"),
        P("head"),
        P("head", "seq"),
        P("seq", "head"),
        P(),
        P("seq", None),
        P("seq", None),
        P("seq", None, "head"),
        P("seq", None, "head"),
        P("seq", "head", None),
    )
    return jax.shard_map(
        shards, mesh=mesh, in_specs=placed, out_specs=P("seq", "head"), check_vma=False
    )
```

time: 261 us -> 229 us (0.88)
  waiting for transfers between devices: 144 us -> 95.3 us
  starting transfers between devices: 52.4 us -> 73.7 us
  matrix products: 13.6 us -> 2.62 us
  local copies, waits for them, and re-layouts: 10.3 us -> 18.2 us
    all_to_all x6 -> x0, waiting for transfers between devices: 71.3 us -> none  [the longest x1 27 us: shards(): lax.all_to_all(payload, 'seq', split_axis=0, concat_axis=0, tiled=True)]
    ppermute x4 -> x32, starting transfers between devices: 5.86 us -> 61.9 us  [permute_seq(): lax.ppermute(value, 'seq', [(source, move(source)) for source in range(co...]
    all_to_all x6 -> x0, starting transfers between devices: 40.9 us -> none  [the longest x2 18.1 us: shards(): lax.all_to_all(outgoing.reshape(experts, half, part), 'seq', split_axis=0...]
    ppermute x4 -> x32, waiting for transfers between devices: 36.4 us -> 72.4 us  [permute_seq(): lax.ppermute(value, 'seq', [(source, move(source)) for source in range(co...]
    ppermute x13, waiting for transfers between devices: 36.4 us -> 22.8 us  [permute_head(): lax.ppermute(value, 'head', [(source, move(source)) for source in range(c...]
    unnamed x28 -> x44, local copies, waits for them, and re-layouts: 3.7 us -> 12.5 us
    dot_general x4, matrix products: 9.92 us -> 2.42 us  [shards(): jnp.dot(rows_k, w_z, preferred_element_type=F32).astype(BF16)]
    ppermute x13, starting transfers between devices: 5.02 us -> 11 us  [permute_head(): lax.ppermute(value, 'head', [(source, move(source)) for source in range(c...]
  transfers between devices with their start and end apart: 24 -> 46, of which waited for: 15 -> 20; matrix products, arithmetic and copies ran while one was open for 6% -> 4% of each run, Pallas kernels for 13% -> 13%
where the time goes in v3:
time: 229 us; the launch traced here: 228 us
  waiting for transfers between devices  95.3 us (42%)
  starting transfers between devices  73.7 us (32%)
  Pallas kernels  34.9 us (15%)
  local copies, waits for them, and re-layouts  18.2 us (8%)
  other arithmetic  3.09 us (1%)
  matrix products  2.62 us (1%)
    ppermute x32, waiting for transfers between devices, permute_seq(): lax.ppermute(value, 'seq', [(source, move(source)) for source in range(co...  72.4 us
    ppermute x32, starting transfers between devices, permute_seq(): lax.ppermute(value, 'seq', [(source, move(source)) for source in range(co...  61.9 us
    pallas_call x8, Pallas kernels, local_call(): pl.pallas_call(kernel, out_shape=out_shape, in_specs=[pl.BlockSpec(memory...  34.9 us
    ppermute x13, waiting for transfers between devices, permute_head(): lax.ppermute(value, 'head', [(source, move(source)) for source in range(c...  22.8 us
    unnamed x44, local copies, waits for them, and re-layouts  12.5 us
    ppermute x13, starting transfers between devices, permute_head(): lax.ppermute(value, 'head', [(source, move(source)) for source in range(c...  11 us
  transfers between devices with their start and end apart: 46, of which 20 were waited for; matrix products, arithmetic and copies ran while one was open for 4% of the time, Pallas kernels for 13%

profile of v3, /device:TPU:0, one launch (start us, length us, event | category | flops | bytes accessed | tf_op | source)
XLA Modules:
  0.0 228.2 jit_solution(16605645729449336854)
XLA Ops:
  4.5 3.0 %collective-permute-start = (bf16[272,128]{1,0:T(8,128)(2,1)S(1)}, bf16[272,128]{1,0:T(8,128)(2,1)S(1)}, u32[]{:S(2)}, u32[]{:S(2)}) collective-permute-start(bf16[272,128]{1,0:T(8,128)(2,1)S(1)} %get-tuple-element.39), channel_id=1, source_target_pairs={{0,4},{4,0},{8,12},{12,8},{16,20},{20,16},{24,28},{28,24},{1,5},{5... | collective-permute-start | bytes 208904 | tf_op jit(solution)/shard_map/ppermute | solution.py:22
  9.1 3.0 %collective-permute-start.3 = (bf16[272,128]{1,0:T(8,128)(2,1)S(1)}, bf16[272,128]{1,0:T(8,128)(2,1)S(1)}, u32[]{:S(2)}, u32[]{:S(2)}) collective-permute-start(bf16[272,128]{1,0:T(8,128)(2,1)S(1)} %get-tuple-element.42), channel_id=1, source_target_pairs={{0,16},{4,20},{8,24},{12,28},{16,0},{20,4},{24,8},{28,12},{1,17},{... | collective-permute-start | bytes 208904 | tf_op jit(solution)/shard_map/ppermute | solution.py:22
  13.4 3.6 %collective-permute-start.5 = (bf16[272,128]{1,0:T(8,128)(2,1)S(1)}, bf16[272,128]{1,0:T(8,128)(2,1)S(1)}, u32[]{:S(2)}, u32[]{:S(2)}) collective-permute-start(bf16[272,128]{1,0:T(8,128)(2,1)S(1)} %get-tuple-element.44), channel_id=1, source_target_pairs={{0,24},{4,28},{8,16},{12,20},{16,8},{20,12},{24,0},{28,4},{1,25},{... | collective-permute-start | bytes 208904 | tf_op jit(solution)/shard_map/ppermute | solution.py:22
  17.0 5.8 %collective-permute-done.4.refs_5_ = bf16[272,128]{1,0:T(8,128)(2,1)S(1)} collective-permute-done((bf16[272,128]{1,0:T(8,128)(2,1)S(1)}, bf16[272,128]{1,0:T(8,128)(2,1)S(1)}, u32[]{:S(2)}, u32[]{:S(2)}) %collective-permute-start.4) | collective-permute-done | bytes 69664 | tf_op jit(solution)/shard_map/ppermute | solution.py:22
  24.4 3.5 %collective-permute-start.10 = (bf16[256,128]{1,0:T(8,128)(2,1)S(1)}, bf16[256,128]{1,0:T(8,128)(2,1)S(1)}, u32[]{:S(2)}, u32[]{:S(2)}) collective-permute-start(bf16[256,128]{1,0:T(8,128)(2,1)S(1)} %get-tuple-element.50), channel_id=1, source_target_pairs={{0,16},{4,20},{8,24},{12,28},{16,0},{20,4},{24,8},{28,12},{1,17},{... | collective-permute-start | bytes 196616 | tf_op jit(solution)/shard_map/ppermute | solution.py:22
  29.4 3.2 %collective-permute-start.13 = (bf16[256,128]{1,0:T(8,128)(2,1)S(1)}, bf16[256,128]{1,0:T(8,128)(2,1)S(1)}, u32[]{:S(2)}, u32[]{:S(2)}) collective-permute-start(bf16[256,128]{1,0:T(8,128)(2,1)S(1)} %get-tuple-element.53), channel_id=1, source_target_pairs={{0,28},{4,24},{8,20},{12,16},{16,12},{20,8},{24,4},{28,0},{1,29},{... | collective-permute-start | bytes 196616 | tf_op jit(solution)/shard_map/ppermute | solution.py:22
  33.2 2.2 collective-permute-done.10.refs_4_
  35.4 2.3 %collective-permute-done.11.refs_5_ = bf16[256,128]{1,0:T(8,128)(2,1)S(1)} collective-permute-done((bf16[256,128]{1,0:T(8,128)(2,1)S(1)}, bf16[256,128]{1,0:T(8,128)(2,1)S(1)}, u32[]{:S(2)}, u32[]{:S(2)}) %collective-permute-start.11) | collective-permute-done | bytes 65568 | tf_op jit(solution)/shard_map/ppermute | solution.py:22
  41.5 2.6 %inside.1.inside_ref = f32[128,2048]{1,0:T(8,128)S(1)} custom-call(s32[1,128]{1,0:T(1,128)S(1)} %bitcast.63, f32[128,16]{1,0:T(8,128)S(1)} %get-tuple-element.37.sum_ref, f32[16,128]{1,0:T(8,128)S(1)} %bitcast.60, bf16[128,2048]{1,0:T(8,128)(2,1)S(1)} %copy-done.5, bf16[128,2048]{1,0:T(8,128)(2,1)S(1)} %copy-done.2, bf16[128,2048]{1,0:T(8,128)(2,1)S(1)} %copy-done.4), custom_call_target="tpu_custom_call" | custom-call | flops 134217728 | bytes 2638336 | tf_op jit(solution)/shard_map/inside/pallas_call | solution.py:224
  49.6 2.1 collective-permute-start.16
  52.9 27.8 %collective-permute-done.14 = bf16[2048,384]{1,0:T(8,128)(2,1)} collective-permute-done((bf16[2048,384]{1,0:T(8,128)(2,1)S(1)}, bf16[2048,384]{1,0:T(8,128)(2,1)}, u32[]{:S(2)}, u32[]{:S(2)}) %collective-permute-start.14) | collective-permute-done | bytes 1572896 | tf_op jit(solution)/shard_map/ppermute | solution.py:22
  83.7 11.3 %collective-permute-done.16 = bf16[128,2048]{1,0:T(8,128)(2,1)S(1)} collective-permute-done((bf16[128,2048]{1,0:T(8,128)(2,1)S(1)}, bf16[128,2048]{1,0:T(8,128)(2,1)S(1)}, u32[]{:S(2)}, u32[]{:S(2)}) %collective-permute-start.16) | collective-permute-done | bytes 524320 | tf_op jit(solution)/shard_map/ppermute | solution.py:22
  97.3 2.0 dynamic-slice_bitcast_fusion.2
  102.8 3.5 %collective-permute-done.18 = bf16[128,768]{1,0:T(8,128)(2,1)} collective-permute-done((bf16[128,768]{1,0:T(8,128)(2,1)}, bf16[128,768]{1,0:T(8,128)(2,1)}, u32[]{:S(2)}, u32[]{:S(2)}) %collective-permute-start.18) | collective-permute-done | bytes 196640 | tf_op jit(solution)/shard_map/ppermute | solution.py:27
  107.4 2.8 %collective-permute-done.20 = bf16[128,768]{1,0:T(8,128)(2,1)} collective-permute-done((bf16[128,768]{1,0:T(8,128)(2,1)S(1)}, bf16[128,768]{1,0:T(8,128)(2,1)}, u32[]{:S(2)}, u32[]{:S(2)}) %collective-permute-start.20) | collective-permute-done | bytes 196640 | tf_op jit(solution)/shard_map/ppermute | solution.py:27
  112.7 15.1 %collective-permute-start.33 = (bf16[64,768]{1,0:T(8,128)(2,1)S(1)}, bf16[64,768]{1,0:T(8,128)(2,1)S(1)}, u32[]{:S(2)}, u32[]{:S(2)}) collective-permute-start(bf16[64,768]{1,0:T(8,128)(2,1)S(1)} %get-tuple-element.63), channel_id=1, source_target_pairs={{0,16},{4,20},{8,24},{12,28},{16,0},{20,4},{24,8},{28,12},{1,17},{... | collective-permute-start | bytes 294920 | tf_op jit(solution)/shard_map/ppermute | solution.py:22
  127.8 4.8 %collective-permute-start.36 = (bf16[64,768]{1,0:T(8,128)(2,1)S(1)}, bf16[64,768]{1,0:T(8,128)(2,1)S(1)}, u32[]{:S(2)}, u32[]{:S(2)}) collective-permute-start(bf16[64,768]{1,0:T(8,128)(2,1)S(1)} %get-tuple-element.66), channel_id=1, source_target_pairs={{0,28},{4,24},{8,20},{12,16},{16,12},{20,8},{24,4},{28,0},{1,29},{... | collective-permute-start | bytes 294920 | tf_op jit(solution)/shard_map/ppermute | solution.py:22
  133.1 3.2 %collective-permute-done.33 = bf16[64,768]{1,0:T(8,128)(2,1)S(1)} collective-permute-done((bf16[64,768]{1,0:T(8,128)(2,1)S(1)}, bf16[64,768]{1,0:T(8,128)(2,1)S(1)}, u32[]{:S(2)}, u32[]{:S(2)}) %collective-permute-start.33) | collective-permute-done | bytes 98336 | tf_op jit(solution)/shard_map/ppermute | solution.py:22
  136.9 1.7 collective-permute-done.34
  140.6 3.0 %collective-permute-start.37 = (bf16[256,768]{1,0:T(8,128)(2,1)}, bf16[256,768]{1,0:T(8,128)(2,1)}, u32[]{:S(2)}, u32[]{:S(2)}) collective-permute-start(bf16[256,768]{1,0:T(8,128)(2,1)} %constant_dynamic-update-slice_fusion.4.refs_0_), channel_id=1, source_target_pairs={{0,2},{1,3},{2,0},{3,1},{4,6},{5,7},{6,4},{7,5},{8,10},{9,11},{10,... | collective-permute-start | bytes 1179656 | tf_op jit(solution)/shard_map/ppermute | solution.py:27
  146.4 1.8 collective-permute-done.23
  148.2 2.2 collective-permute-done.24
  151.3 7.1 %collective-permute-done.25.refs_1_ = bf16[256,768]{1,0:T(8,128)(2,1)} collective-permute-done((bf16[256,768]{1,0:T(8,128)(2,1)S(1)}, bf16[256,768]{1,0:T(8,128)(2,1)}, u32[]{:S(2)}, u32[]{:S(2)}) %collective-permute-start.25) | collective-permute-done | bytes 393248 | tf_op jit(solution)/shard_map/ppermute | solution.py:27
  158.4 3.0 %copy-done = bf16[1,3072,1152]{2,1,0:T(8,128)(2,1)S(1)} copy-done((bf16[1,3072,1152]{2,1,0:T(8,128)(2,1)S(1)}, bf16[1,3072,1152]{2,1,0:T(8,128)(2,1)}, u32[]{:S(2)}) %copy-start) | copy-done | bytes 7077912
  161.4 14.3 %expert.3 = (bf16[2,256,768]{2,1,0:T(8,128)(2,1)S(1)}, bf16[2,256,768]{2,1,0:T(8,128)(2,1)S(1)}) custom-call(s32[8]{0:T(128)S(1)} %stack.55.owner_ref, bf16[256,768]{1,0:T(8,128)(2,1)} %constant_dynamic-update-slice_fusion.4.refs_0_, bf16[256,768]{1,0:T(8,128)(2,1)} %collective-permute-done.37.refs_1_, bf16[256,768]{1,0:T(8,128)(2,1)} %collective-permute-done.38.refs_2_, ...), custom_call_target="tpu_custom_call" | custom-call | flops 5435817984 | bytes 24391712 | tf_op jit(solution)/shard_map/expert/pallas_call | solution.py:224
  176.3 13.8 %expert.2 = (bf16[2,256,768]{2,1,0:T(8,128)(2,1)S(1)}, bf16[2,256,768]{2,1,0:T(8,128)(2,1)S(1)}) custom-call(s32[8]{0:T(128)S(1)} %stack.55.owner_ref, bf16[256,768]{1,0:T(8,128)(2,1)S(1)} %constant_dynamic-update-slice_fusion.refs_0_, bf16[256,768]{1,0:T(8,128)(2,1)} %collective-permute-done.25.refs_1_, ...), custom_call_target="tpu_custom_call" | custom-call | flops 5435817984 | bytes 24391712 | tf_op jit(solution)/shard_map/expert/pallas_call | solution.py:224
  194.4 8.0 %collective-permute-done.41 = bf16[256,768]{1,0:T(8,128)(2,1)S(1)} collective-permute-done((bf16[256,768]{1,0:T(8,128)(2,1)S(1)}, bf16[256,768]{1,0:T(8,128)(2,1)S(1)}, u32[]{:S(2)}, u32[]{:S(2)}) %collective-permute-start.41) | collective-permute-done | bytes 393248 | tf_op jit(solution)/shard_map/ppermute | solution.py:27
  202.5 5.2 %collective-permute-start.42 = (bf16[64,768]{1,0:T(8,128)(2,1)S(1)}, bf16[64,768]{1,0:T(8,128)(2,1)S(1)}, u32[]{:S(2)}, u32[]{:S(2)}) collective-permute-start(bf16[64,768]{1,0:T(8,128)(2,1)S(1)} %get-tuple-element.75), channel_id=1, source_target_pairs={{0,16},{4,20},{8,24},{12,28},{16,0},{20,4},{24,8},{28,12},{1,17},{... | collective-permute-start | bytes 294920 | tf_op jit(solution)/shard_map/ppermute | solution.py:22
  209.4 3.1 %collective-permute-start.45 = (bf16[64,768]{1,0:T(8,128)(2,1)S(1)}, bf16[64,768]{1,0:T(8,128)(2,1)S(1)}, u32[]{:S(2)}, u32[]{:S(2)}) collective-permute-start(bf16[64,768]{1,0:T(8,128)(2,1)S(1)} %get-tuple-element.72), channel_id=1, source_target_pairs={{0,28},{4,24},{8,20},{12,16},{16,12},{20,8},{24,4},{28,0},{1,29},{... | collective-permute-start | bytes 294920 | tf_op jit(solution)/shard_map/ppermute | solution.py:22
  214.2 4.4 %collective-permute-done.42.refs_4_ = bf16[64,768]{1,0:T(8,128)(2,1)S(1)} collective-permute-done((bf16[64,768]{1,0:T(8,128)(2,1)S(1)}, bf16[64,768]{1,0:T(8,128)(2,1)S(1)}, u32[]{:S(2)}, u32[]{:S(2)}) %collective-permute-start.42) | collective-permute-done | bytes 98336 | tf_op jit(solution)/shard_map/ppermute | solution.py:22
  218.7 3.0 %collective-permute-done.43.refs_5_ = bf16[64,768]{1,0:T(8,128)(2,1)S(1)} collective-permute-done((bf16[64,768]{1,0:T(8,128)(2,1)S(1)}, bf16[64,768]{1,0:T(8,128)(2,1)S(1)}, u32[]{:S(2)}, u32[]{:S(2)}) %collective-permute-start.43) | collective-permute-done | bytes 98336 | tf_op jit(solution)/shard_map/ppermute | solution.py:22
  223.3 3.9 %collective-permute-done.32.refs_3_ = bf16[64,768]{1,0:T(8,128)(2,1)S(1)} collective-permute-done((bf16[64,768]{1,0:T(8,128)(2,1)S(1)}, bf16[64,768]{1,0:T(8,128)(2,1)S(1)}, u32[]{:S(2)}, u32[]{:S(2)}) %collective-permute-start.32) | collective-permute-done | bytes 98336 | tf_op jit(solution)/shard_map/ppermute | solution.py:22
  (146 shorter events, 51.4 us)
Async XLA Ops:
  4.5 8.9 %collective-permute-start = (bf16[272,128]{1,0:T(8,128)(2,1)S(1)}, bf16[272,128]{1,0:T(8,128)(2,1)S(1)}, u32[]{:S(2)}, u32[]{:S(2)}) collective-permute-start(bf16[272,128]{1,0:T(8,128)(2,1)S(1)} %get-tuple-element.39), channel_id=1, source_target_pairs={{0,4},{4,0},{8,12},{12,8},{16,20},{20,16},{24,28},{28,24},{1,5},{5... | collective-permute-start | bytes 208904 | tf_op jit(solution)/shard_map/ppermute | solution.py:22
  7.6 9.5 %collective-permute-start.1 = (bf16[272,128]{1,0:T(8,128)(2,1)S(1)}, bf16[272,128]{1,0:T(8,128)(2,1)S(1)}, u32[]{:S(2)}, u32[]{:S(2)}) collective-permute-start(bf16[272,128]{1,0:T(8,128)(2,1)S(1)} %get-tuple-element.40), channel_id=1, source_target_pairs={{0,8},{4,12},{8,0},{12,4},{16,24},{20,28},{24,16},{28,20},{1,9},{5... | collective-permute-start | bytes 208904 | tf_op jit(solution)/shard_map/ppermute | solution.py:22
  12.1 10.7 %collective-permute-start.4 = (bf16[272,128]{1,0:T(8,128)(2,1)S(1)}, bf16[272,128]{1,0:T(8,128)(2,1)S(1)}, u32[]{:S(2)}, u32[]{:S(2)}) collective-permute-start(bf16[272,128]{1,0:T(8,128)(2,1)S(1)} %get-tuple-element.43), channel_id=1, source_target_pairs={{0,20},{4,16},{8,28},{12,24},{16,4},{20,0},{24,12},{28,8},{1,21},{... | collective-permute-start | bytes 208904 | tf_op jit(solution)/shard_map/ppermute | solution.py:22
  13.4 9.4 %collective-permute-start.5 = (bf16[272,128]{1,0:T(8,128)(2,1)S(1)}, bf16[272,128]{1,0:T(8,128)(2,1)S(1)}, u32[]{:S(2)}, u32[]{:S(2)}) collective-permute-start(bf16[272,128]{1,0:T(8,128)(2,1)S(1)} %get-tuple-element.44), channel_id=1, source_target_pairs={{0,24},{4,28},{8,16},{12,20},{16,8},{20,12},{24,0},{28,4},{1,25},{... | collective-permute-start | bytes 208904 | tf_op jit(solution)/shard_map/ppermute | solution.py:22
  24.4 11.0 %collective-permute-start.10 = (bf16[256,128]{1,0:T(8,128)(2,1)S(1)}, bf16[256,128]{1,0:T(8,128)(2,1)S(1)}, u32[]{:S(2)}, u32[]{:S(2)}) collective-permute-start(bf16[256,128]{1,0:T(8,128)(2,1)S(1)} %get-tuple-element.50), channel_id=1, source_target_pairs={{0,16},{4,20},{8,24},{12,28},{16,0},{20,4},{24,8},{28,12},{1,17},{... | collective-permute-start | bytes 196616 | tf_op jit(solution)/shard_map/ppermute | solution.py:22
  27.8 9.8 %collective-permute-start.11 = (bf16[256,128]{1,0:T(8,128)(2,1)S(1)}, bf16[256,128]{1,0:T(8,128)(2,1)S(1)}, u32[]{:S(2)}, u32[]{:S(2)}) collective-permute-start(bf16[256,128]{1,0:T(8,128)(2,1)S(1)} %get-tuple-element.51), channel_id=1, source_target_pairs={{0,20},{4,16},{8,28},{12,24},{16,4},{20,0},{24,12},{28,8},{1,21},{... | collective-permute-start | bytes 196616 | tf_op jit(solution)/shard_map/ppermute | solution.py:22
  27.9 16.3 %collective-permute-start.12 = (bf16[256,128]{1,0:T(8,128)(2,1)S(1)}, bf16[256,128]{1,0:T(8,128)(2,1)S(1)}, u32[]{:S(2)}, u32[]{:S(2)}) collective-permute-start(bf16[256,128]{1,0:T(8,128)(2,1)S(1)} %get-tuple-element.52), channel_id=1, source_target_pairs={{0,24},{4,28},{8,16},{12,20},{16,8},{20,12},{24,0},{28,4},{1,25},{... | collective-permute-start | bytes 196616 | tf_op jit(solution)/shard_map/ppermute | solution.py:22
  29.4 14.8 %collective-permute-start.13 = (bf16[256,128]{1,0:T(8,128)(2,1)S(1)}, bf16[256,128]{1,0:T(8,128)(2,1)S(1)}, u32[]{:S(2)}, u32[]{:S(2)}) collective-permute-start(bf16[256,128]{1,0:T(8,128)(2,1)S(1)} %get-tuple-element.53), channel_id=1, source_target_pairs={{0,28},{4,24},{8,20},{12,16},{16,12},{20,8},{24,4},{28,0},{1,29},{... | collective-permute-start | bytes 196616 | tf_op jit(solution)/shard_map/ppermute | solution.py:22
  32.6 11.5 %collective-permute-start.7 = (bf16[256,128]{1,0:T(8,128)(2,1)S(1)}, bf16[256,128]{1,0:T(8,128)(2,1)S(1)}, u32[]{:S(2)}, u32[]{:S(2)}) collective-permute-start(bf16[256,128]{1,0:T(8,128)(2,1)S(1)} %get-tuple-element.47), channel_id=1, source_target_pairs={{0,4},{4,0},{8,12},{12,8},{16,20},{20,16},{24,28},{28,24},{1,5},{5... | collective-permute-start | bytes 196616 | tf_op jit(solution)/shard_map/ppermute | solution.py:22
  35.4 8.8 %collective-permute-start.8 = (bf16[256,128]{1,0:T(8,128)(2,1)S(1)}, bf16[256,128]{1,0:T(8,128)(2,1)S(1)}, u32[]{:S(2)}, u32[]{:S(2)}) collective-permute-start(bf16[256,128]{1,0:T(8,128)(2,1)S(1)} %get-tuple-element.48), channel_id=1, source_target_pairs={{0,8},{4,12},{8,0},{12,4},{16,24},{20,28},{24,16},{28,20},{1,9},{5... | collective-permute-start | bytes 196616 | tf_op jit(solution)/shard_map/ppermute | solution.py:22
  46.0 34.8 %collective-permute-start.14 = (bf16[2048,384]{1,0:T(8,128)(2,1)S(1)}, bf16[2048,384]{1,0:T(8,128)(2,1)}, u32[]{:S(2)}, u32[]{:S(2)}) collective-permute-start(bf16[2048,384]{1,0:T(8,128)(2,1)S(1)} %copy-done.13), channel_id=1, source_target_pairs={{0,4},{4,0},{8,12},{12,8},{16,20},{20,16},{24,28},{28,24},{1,5},{5... | collective-permute-start | bytes 4718600 | tf_op jit(solution)/shard_map/ppermute | solution.py:22
  47.9 35.2 %collective-permute-start.15 = (bf16[128,2048]{1,0:T(8,128)(2,1)S(1)}, bf16[128,2048]{1,0:T(8,128)(2,1)S(1)}, u32[]{:S(2)}, u32[]{:S(2)}) collective-permute-start(bf16[128,2048]{1,0:T(8,128)(2,1)S(1)} %outside.1), channel_id=1, source_target_pairs={{0,24},{4,28},{8,0},{12,4},{16,8},{20,12},{24,16},{28,20},{1,25},{... | collective-permute-start | bytes 1572872 | tf_op jit(solution)/shard_map/ppermute | solution.py:22
  49.6 45.4 %collective-permute-start.16 = (bf16[128,2048]{1,0:T(8,128)(2,1)S(1)}, bf16[128,2048]{1,0:T(8,128)(2,1)S(1)}, u32[]{:S(2)}, u32[]{:S(2)}) collective-permute-start(bf16[128,2048]{1,0:T(8,128)(2,1)S(1)} %outside.1), channel_id=1, source_target_pairs={{0,16},{4,20},{8,24},{12,28},{16,0},{20,4},{24,8},{28,12},{1,17},{... | collective-permute-start | bytes 1572872 | tf_op jit(solution)/shard_map/ppermute | solution.py:22
  51.7 43.9 %collective-permute-start.17 = (bf16[128,2048]{1,0:T(8,128)(2,1)S(1)}, bf16[128,2048]{1,0:T(8,128)(2,1)S(1)}, u32[]{:S(2)}, u32[]{:S(2)}) collective-permute-start(bf16[128,2048]{1,0:T(8,128)(2,1)S(1)} %outside.1), channel_id=1, source_target_pairs={{0,8},{4,12},{8,16},{12,20},{16,24},{20,28},{24,0},{28,4},{1,9},{5... | collective-permute-start | bytes 1572872 | tf_op jit(solution)/shard_map/ppermute | solution.py:22
  99.3 8.1 %collective-permute-start.19 = (bf16[128,768]{1,0:T(8,128)(2,1)}, bf16[128,768]{1,0:T(8,128)(2,1)}, u32[]{:S(2)}, u32[]{:S(2)}) collective-permute-start(bf16[128,768]{1,0:T(8,128)(2,1)} %get-tuple-element.71), channel_id=1, source_target_pairs={{0,2},{1,3},{2,0},{3,1},{4,6},{5,7},{6,4},{7,5},{8,10},{9,11},{10,... | collective-permute-start | bytes 589832 | tf_op jit(solution)/shard_map/ppermute | solution.py:27
  101.0 9.1 %collective-permute-start.20 = (bf16[128,768]{1,0:T(8,128)(2,1)S(1)}, bf16[128,768]{1,0:T(8,128)(2,1)}, u32[]{:S(2)}, u32[]{:S(2)}) collective-permute-start(bf16[128,768]{1,0:T(8,128)(2,1)S(1)} %get-tuple-element.70), channel_id=1, source_target_pairs={{0,3},{1,0},{2,1},{3,2},{4,7},{5,4},{6,5},{7,6},{8,11},{9,8},{10,9... | collective-permute-start | bytes 589832 | tf_op jit(solution)/shard_map/ppermute | solution.py:27
  112.7 23.5 %collective-permute-start.33 = (bf16[64,768]{1,0:T(8,128)(2,1)S(1)}, bf16[64,768]{1,0:T(8,128)(2,1)S(1)}, u32[]{:S(2)}, u32[]{:S(2)}) collective-permute-start(bf16[64,768]{1,0:T(8,128)(2,1)S(1)} %get-tuple-element.63), channel_id=1, source_target_pairs={{0,16},{4,20},{8,24},{12,28},{16,0},{20,4},{24,8},{28,12},{1,17},{... | collective-permute-start | bytes 294920 | tf_op jit(solution)/shard_map/ppermute | solution.py:22
  127.8 10.8 %collective-permute-start.34 = (bf16[64,768]{1,0:T(8,128)(2,1)S(1)}, bf16[64,768]{1,0:T(8,128)(2,1)S(1)}, u32[]{:S(2)}, u32[]{:S(2)}) collective-permute-start(bf16[64,768]{1,0:T(8,128)(2,1)S(1)} %get-tuple-element.64), channel_id=1, source_target_pairs={{0,20},{4,16},{8,28},{12,24},{16,4},{20,0},{24,12},{28,8},{1,21},{... | collective-permute-start | bytes 294920 | tf_op jit(solution)/shard_map/ppermute | solution.py:22
  127.8 11.5 %collective-permute-start.35 = (bf16[64,768]{1,0:T(8,128)(2,1)S(1)}, bf16[64,768]{1,0:T(8,128)(2,1)S(1)}, u32[]{:S(2)}, u32[]{:S(2)}) collective-permute-start(bf16[64,768]{1,0:T(8,128)(2,1)S(1)} %get-tuple-element.65), channel_id=1, source_target_pairs={{0,24},{4,28},{8,16},{12,20},{16,8},{20,12},{24,0},{28,4},{1,25},{... | collective-permute-start | bytes 294920 | tf_op jit(solution)/shard_map/ppermute | solution.py:22
  127.8 12.1 %collective-permute-start.36 = (bf16[64,768]{1,0:T(8,128)(2,1)S(1)}, bf16[64,768]{1,0:T(8,128)(2,1)S(1)}, u32[]{:S(2)}, u32[]{:S(2)}) collective-permute-start(bf16[64,768]{1,0:T(8,128)(2,1)S(1)} %get-tuple-element.66), channel_id=1, source_target_pairs={{0,28},{4,24},{8,20},{12,16},{16,12},{20,8},{24,4},{28,0},{1,29},{... | collective-permute-start | bytes 294920 | tf_op jit(solution)/shard_map/ppermute | solution.py:22
  132.6 13.7 %collective-permute-start.22 = (bf16[64,768]{1,0:T(8,128)(2,1)S(1)}, bf16[64,768]{1,0:T(8,128)(2,1)S(1)}, u32[]{:S(2)}, u32[]{:S(2)}) collective-permute-start(bf16[64,768]{1,0:T(8,128)(2,1)S(1)} %get-tuple-element.58), channel_id=1, source_target_pairs={{0,4},{4,0},{8,12},{12,8},{16,20},{20,16},{24,28},{28,24},{1,5},{5... | collective-permute-start | bytes 294920 | tf_op jit(solution)/shard_map/ppermute | solution.py:22
  140.6 10.1 %collective-permute-start.37 = (bf16[256,768]{1,0:T(8,128)(2,1)}, bf16[256,768]{1,0:T(8,128)(2,1)}, u32[]{:S(2)}, u32[]{:S(2)}) collective-permute-start(bf16[256,768]{1,0:T(8,128)(2,1)} %constant_dynamic-update-slice_fusion.4.refs_0_), channel_id=1, source_target_pairs={{0,2},{1,3},{2,0},{3,1},{4,6},{5,7},{6,4},{7,5},{8,10},{9,11},{10,... | collective-permute-start | bytes 1179656 | tf_op jit(solution)/shard_map/ppermute | solution.py:27
  151.2 25.0 %collective-permute-start.26 = (bf16[256,768]{1,0:T(8,128)(2,1)S(1)}, bf16[256,768]{1,0:T(8,128)(2,1)S(1)}, u32[]{:S(2)}, u32[]{:S(2)}) collective-permute-start(bf16[256,768]{1,0:T(8,128)(2,1)S(1)} %constant_dynamic-update-slice_fusion.refs_0_), channel_id=1, source_target_pairs={{0,1},{1,0},{2,3},{3,2},{4,5},{5,4},{6,7},{7,6},{8,9},{9,8},{10,11... | collective-permute-start | bytes 1179656 | tf_op jit(solution)/shard_map/ppermute | solution.py:27
  158.4 17.9 %collective-permute-start.27 = (bf16[256,768]{1,0:T(8,128)(2,1)}, bf16[256,768]{1,0:T(8,128)(2,1)S(1)}, u32[]{:S(2)}, u32[]{:S(2)}) collective-permute-start(bf16[256,768]{1,0:T(8,128)(2,1)} %collective-permute-done.25.refs_1_), channel_id=1, source_target_pairs={{0,1},{1,0},{2,3},{3,2},{4,5},{5,4},{6,7},{7,6},{8,9},{9,8},{10,11... | collective-permute-start | bytes 1179656 | tf_op jit(solution)/shard_map/ppermute | solution.py:27
  175.7 14.5 %collective-permute-start.40 = (bf16[2,256,768]{2,1,0:T(8,128)(2,1)S(1)}, bf16[2,256,768]{2,1,0:T(8,128)(2,1)S(1)}, u32[]{:S(2)}, u32[]{:S(2)}) collective-permute-start(bf16[2,256,768]{2,1,0:T(8,128)(2,1)S(1)} %get-tuple-element.68), channel_id=1, source_target_pairs={{0,1},{1,0},{2,3},{3,2},{4,5},{5,4},{6,7},{7,6},{8,9},{9,8},{10,11... | collective-permute-start | bytes 2359304 | tf_op jit(solution)/shard_map/ppermute | solution.py:27
  190.4 12.0 %collective-permute-start.41 = (bf16[256,768]{1,0:T(8,128)(2,1)S(1)}, bf16[256,768]{1,0:T(8,128)(2,1)S(1)}, u32[]{:S(2)}, u32[]{:S(2)}) collective-permute-start(bf16[256,768]{1,0:T(8,128)(2,1)S(1)} %fusion.11), channel_id=1, source_target_pairs={{0,2},{1,3},{2,0},{3,1},{4,6},{5,7},{6,4},{7,5},{8,10},{9,11},{10,... | collective-permute-start | bytes 1179656 | tf_op jit(solution)/shard_map/ppermute | solution.py:27
  192.7 19.9 %collective-permute-start.29 = (bf16[256,768]{1,0:T(8,128)(2,1)S(1)}, bf16[256,768]{1,0:T(8,128)(2,1)S(1)}, u32[]{:S(2)}, u32[]{:S(2)}) collective-permute-start(bf16[256,768]{1,0:T(8,128)(2,1)S(1)} %fusion.10), channel_id=1, source_target_pairs={{0,2},{1,3},{2,0},{3,1},{4,6},{5,7},{6,4},{7,5},{8,10},{9,11},{10,... | collective-permute-start | bytes 1179656 | tf_op jit(solution)/shard_map/ppermute | solution.py:27
  202.5 16.2 %collective-permute-start.42 = (bf16[64,768]{1,0:T(8,128)(2,1)S(1)}, bf16[64,768]{1,0:T(8,128)(2,1)S(1)}, u32[]{:S(2)}, u32[]{:S(2)}) collective-permute-start(bf16[64,768]{1,0:T(8,128)(2,1)S(1)} %get-tuple-element.75), channel_id=1, source_target_pairs={{0,16},{4,20},{8,24},{12,28},{16,0},{20,4},{24,8},{28,12},{1,17},{... | collective-permute-start | bytes 294920 | tf_op jit(solution)/shard_map/ppermute | solution.py:22
  207.7 14.0 %collective-permute-start.43 = (bf16[64,768]{1,0:T(8,128)(2,1)S(1)}, bf16[64,768]{1,0:T(8,128)(2,1)S(1)}, u32[]{:S(2)}, u32[]{:S(2)}) collective-permute-start(bf16[64,768]{1,0:T(8,128)(2,1)S(1)} %get-tuple-element.74), channel_id=1, source_target_pairs={{0,20},{4,16},{8,28},{12,24},{16,4},{20,0},{24,12},{28,8},{1,21},{... | collective-permute-start | bytes 294920 | tf_op jit(solution)/shard_map/ppermute | solution.py:22
  208.8 13.1 %collective-permute-start.44 = (bf16[64,768]{1,0:T(8,128)(2,1)S(1)}, bf16[64,768]{1,0:T(8,128)(2,1)S(1)}, u32[]{:S(2)}, u32[]{:S(2)}) collective-permute-start(bf16[64,768]{1,0:T(8,128)(2,1)S(1)} %get-tuple-element.73), channel_id=1, source_target_pairs={{0,24},{4,28},{8,16},{12,20},{16,8},{20,12},{24,0},{28,4},{1,25},{... | collective-permute-start | bytes 294920 | tf_op jit(solution)/shard_map/ppermute | solution.py:22
  209.4 12.4 %collective-permute-start.45 = (bf16[64,768]{1,0:T(8,128)(2,1)S(1)}, bf16[64,768]{1,0:T(8,128)(2,1)S(1)}, u32[]{:S(2)}, u32[]{:S(2)}) collective-permute-start(bf16[64,768]{1,0:T(8,128)(2,1)S(1)} %get-tuple-element.72), channel_id=1, source_target_pairs={{0,28},{4,24},{8,20},{12,16},{16,12},{20,8},{24,4},{28,0},{1,29},{... | collective-permute-start | bytes 294920 | tf_op jit(solution)/shard_map/ppermute | solution.py:22
  212.6 9.2 %collective-permute-start.30 = (bf16[64,768]{1,0:T(8,128)(2,1)S(1)}, bf16[64,768]{1,0:T(8,128)(2,1)S(1)}, u32[]{:S(2)}, u32[]{:S(2)}) collective-permute-start(bf16[64,768]{1,0:T(8,128)(2,1)S(1)} %get-tuple-element.78), channel_id=1, source_target_pairs={{0,4},{4,0},{8,12},{12,8},{16,20},{20,16},{24,28},{28,24},{1,5},{5... | collective-permute-start | bytes 294920 | tf_op jit(solution)/shard_map/ppermute | solution.py:22
  (32 other events, 472.2 us)

commit v4 on v3

--- a/solution.py
+++ b/solution.py
@@ -154,13 +154,39 @@
         out_ref[:, lanes] = (raw * scale * gain_ref[:, lanes]).astype(BF16)
 
 
-def dispatch_kernel(summed_ref, residual_ref, take_ref, middle_ref, *outs):
-    middle = (summed_ref[...].astype(F32) + residual_ref[...].astype(F32)).astype(BF16)
+def route_kernel(me_ref, *refs):
+    ins, outs, stage_ref = refs[: (len(refs) - 1) // 2], refs[(len(refs) - 1) // 2 : -1], refs[-1]
+    count = len(ins)
+    for k in range(count):
+        stage_ref[(me_ref[0] + k) % count] = ins[k][...]
+    for m in range(count):
+        outs[m][...] = stage_ref[(me_ref[1] + m) % count]
+
+
+def dispatch_kernel(n_head, residual_ref, take_ref, *refs):
+    total = residual_ref[...].astype(F32)
+    sums = refs[0][...].astype(F32)
+    for ref in refs[1:n_head]:
+        sums = sums + ref[...].astype(F32)
+    middle_ref, outs = refs[n_head], refs[n_head + 1 :]
+    middle = (total + sums).astype(BF16)
     middle_ref[...] = middle
     count = outs[0].shape[0]
     rows = jnp.dot(take_ref[...], middle, preferred_element_type=F32).astype(BF16)
     for d in range(len(outs)):
         outs[d][...] = rows[d * count : (d + 1) * count]
+
+
+def sum_kernel(nz, me_ref, *refs):
+    ins, outs, stage_ref = refs[: len(refs) - 1 - nz], refs[len(refs) - 1 - nz : -1], refs[-1]
+    total = ins[0][...].astype(F32)
+    for ref in ins[1:]:
+        total = total + ref[...].astype(F32)
+    stage_ref[...] = total.astype(BF16)
+    count = outs[0].shape[0]
+    for k in range(nz):
+        start = pl.multiple_of((me_ref[0] ^ k) * count, count)
+        outs[k][...] = stage_ref[pl.ds(start, count), :]
 
 
 def mix_kernel(middle_ref, mix_ref, *refs):
@@ -177,45 +203,103 @@
     out_ref[...] = (middle_ref[...].astype(F32) + total).astype(BF16)
 
 
-def expert_kernel(n_head, owner_ref, *refs):
+def expert_kernel(n_head, aligned, owner_ref, *refs):
     pieces = refs[:n_head]
-    gain_ref, gate_ref, up_ref, down_ref, sent_ref, kept_ref, rows_ref, hidden_ref = refs[n_head:]
-    part = pieces[0].shape[1]
-    units, nx = hidden_ref.shape[1], sent_ref.shape[0]
-    squares = 0.0
-    for piece in pieces:
-        value = piece[...].astype(F32)
-        squares = squares + jnp.sum(value * value, axis=1, keepdims=True)
-    scale = lax.rsqrt(squares / (part * n_head) + EPSILON)
+    gain_ref, gate_ref, up_ref, down_ref, sent_ref, kept_ref = refs[n_head : n_head + 6]
+    rows_ref, hidden_ref, wide_ref, low_ref, wide_sem, low_sem = refs[n_head + 6 :]
+    _, depth, units = gate_ref.shape
+    part = kept_ref.shape[2]
+    nz, nx = depth // part, sent_ref.shape[0]
+    count = pieces[0].shape[0] // nz
+    steps = wide_ref.shape[0] // (1 if aligned else 2)
+    width = units // steps
+
+    def wide_copy(j, k):
+        weight = (gate_ref, up_ref)[k]
+        if aligned:
+            source = weight.at[0, :, pl.ds(j * width, width)]
+            target = wide_ref.at[j, :, pl.ds(k * width, width)]
+        else:
+            source, target = weight.at[0], wide_ref.at[k]
+        return pltpu.make_async_copy(source, target, wide_sem.at[j, k])
+
+    def low_copy(j):
+        start = pl.multiple_of(owner_ref[n_head + j] * part, 128)
+        return pltpu.make_async_copy(
+            down_ref.at[0, :, pl.ds(start, part)], low_ref.at[j], low_sem.at[j]
+        )
+
+    for j in range(steps):
+        for k in range(2):
+            wide_copy(j, k).start()
+    for j in range(n_head):
+        low_copy(j).start()
+
     for i, piece in enumerate(pieces):
-        lanes = pl.ds(pl.multiple_of(owner_ref[i] * part, 128), part)
-        value = piece[...].astype(F32) * scale * gain_ref[:, lanes]
-        rows_ref[:, lanes] = value.astype(BF16)
-
-    def fill(lanes):
-        gate = jnp.dot(rows_ref[...], gate_ref[0, :, lanes], preferred_element_type=F32)
-        up = jnp.dot(rows_ref[...], up_ref[0, :, lanes], preferred_element_type=F32)
-        hidden_ref[:, lanes] = (gate / (1.0 + jnp.exp(-gate)) * up).astype(BF16)
-
-    width = 256
-    steps = units // width
-
-    @pl.loop(0, steps)
-    def _(i):
-        fill(pl.ds(pl.multiple_of(i * width, 128), width))
-
-    if units % width:
-        fill(slice(steps * width, units))
-
-    for j, out_ref in enumerate((sent_ref, kept_ref)):
-
-        @pl.loop(0, out_ref.shape[0])
-        def _(i, j=j, out_ref=out_ref):
-            start = owner_ref[n_head + j * nx + i] * part
-            lanes = pl.ds(pl.multiple_of(start, 128), part)
-            out_ref[i] = jnp.dot(
-                hidden_ref[...], down_ref[0, :, lanes], preferred_element_type=F32
-            ).astype(BF16)
+        squares = 0.0
+        for k in range(nz):
+            value = piece[k * count : (k + 1) * count, :].astype(F32)
+            squares = squares + jnp.sum(value * value, axis=1, keepdims=True)
+        scale = lax.rsqrt(squares / depth + EPSILON)
+        lines = pl.ds(pl.multiple_of(owner_ref[i] * count, count), count)
+        for k in range(nz):
+            lanes = pl.ds(pl.multiple_of((owner_ref[2 * n_head] ^ k) * part, 128), part)
+            value = piece[k * count : (k + 1) * count, :].astype(F32) * scale * gain_ref[:, lanes]
+            rows_ref[lines, lanes] = value.astype(BF16)
+
+    for j in range(steps):
+        for k in range(2):
+            wide_copy(j, k).wait()
+        if aligned:
+            both = jnp.dot(rows_ref[...], wide_ref[j], preferred_element_type=F32)
+            gate, up = both[:, :width], both[:, width:]
+        else:
+            gate = jnp.dot(rows_ref[...], wide_ref[0], preferred_element_type=F32)
+            up = jnp.dot(rows_ref[...], wide_ref[1], preferred_element_type=F32)
+        hidden = (gate / (1.0 + jnp.exp(-gate)) * up).astype(BF16)
+        hidden_ref[:, j * width : (j + 1) * width] = hidden
+
+    for j in range(n_head):
+        low_copy(j).wait()
+        out = jnp.dot(hidden_ref[...], low_ref[j], preferred_element_type=F32).astype(BF16)
+        if j < nx:
+            sent_ref[j] = out
+        else:
+            kept_ref[j - nx] = out
+
+
+def expert_call(owners, pieces, norm_gain, gate_weight, up_weight, down_weight):
+    n_head = len(pieces)
+    lines, part = pieces[0].shape
+    _, depth, units = gate_weight.shape
+    count = lines * part * n_head // depth
+    width = next((w for w in (384, 256, 128) if units % w == 0), units)
+    aligned = width % 128 == 0
+    steps, nx = units // width, n_head // CORES
+    wide = (steps, depth, 2 * width) if aligned else (2, depth, width)
+    struct = jax.ShapeDtypeStruct
+    return pl.pallas_call(
+        functools.partial(expert_kernel, n_head, aligned),
+        out_shape=[struct((nx, count, part), BF16), struct((n_head - nx, count, part), BF16)],
+        in_specs=[pl.BlockSpec(memory_space=pltpu.SMEM)]
+        + [pl.BlockSpec(memory_space=pltpu.VMEM)] * (n_head + 1)
+        + [pl.BlockSpec(memory_space=pl.ANY)] * 3,
+        scratch_shapes=[
+            pltpu.VMEM((count, depth), BF16),
+            pltpu.VMEM((count, units), BF16),
+            pltpu.VMEM(wide, BF16),
+            pltpu.VMEM((n_head, units, part), BF16),
+            pltpu.SemaphoreType.DMA((steps, 2)),
+            pltpu.SemaphoreType.DMA((n_head,)),
+        ],
+        compiler_params=pltpu.CompilerParams(vmem_limit_bytes=EXPERT_VMEM),
+        cost_estimate=pl.CostEstimate(
+            flops=6 * count * depth * units,
+            bytes_accessed=6 * depth * units + 4 * count * depth,
+            transcendentals=count * units,
+        ),
+        name="expert",
+    )(owners, *pieces, norm_gain.reshape(1, depth), gate_weight, up_weight, down_weight)
 
 
 def local_call(kernel, name, out_shape, flops, *operands, scratch=(), scalars=0, vmem=SMALL_VMEM):
@@ -231,6 +315,17 @@
         cost_estimate=pl.CostEstimate(flops=flops, bytes_accessed=sum(sizes), transcendentals=0),
         name=name,
     )(*operands)
+
+
+def slot_places(routing, experts, capacity):
+    tokens = routing.shape[0]
+    flat_ids = routing.reshape(-1)
+    hits = (flat_ids[:, None] == jnp.arange(experts, dtype=jnp.int32)[None, :]).astype(F32)
+    pair_row = lax.broadcasted_iota(jnp.int32, (2 * tokens, 2 * tokens), 0)
+    pair_col = lax.broadcasted_iota(jnp.int32, (2 * tokens, 2 * tokens), 1)
+    earlier = jnp.dot((pair_col < pair_row).astype(F32), hits)
+    rank = jnp.sum(earlier * hits, axis=1).astype(jnp.int32)
+    return (flat_ids * capacity + rank).reshape(tokens, 2)
 
 
 def shards(
@@ -260,6 +355,25 @@
     model_width = part * n_head
 
     struct = jax.ShapeDtypeStruct
+    spots = [
+        ((zz * ny + yy) * n_head + hh, (hh * ny + yy) * n_head + zz)
+        for zz in range(nz)
+        for yy in range(ny)
+        for hh in range(n_head)
+    ]
+    crossed = lambda value: lax.ppermute(value, ("seq", "head"), spots)
+
+    experts = n_seq
+    capacity = 4 * tokens // experts
+    residual_there, routing_there = crossed(residual), crossed(routing)
+    slot = jnp.arange(experts * capacity, dtype=jnp.int32)
+    slot = (slot // capacity ^ s) * capacity + slot % capacity
+    place = slot_places(routing_there, experts, capacity)
+    take = jnp.any(place[:, None, :] == slot[None, :, None], axis=2).astype(BF16).T
+    place = slot_places(routing, experts, capacity)
+    here = place[:, None, :] == slot[None, :, None]
+    mix = jnp.sum(jnp.where(here, route_weights[:, None, :], 0.0), axis=2)
+
     me = s.astype(jnp.int32).reshape(1)
     doc_row = doc_ids.reshape(1, tokens)
     rows, held, extra = chunk_plan(heads, hw, n_seq)
@@ -277,20 +391,6 @@
         scratch=[pltpu.VMEM((hw, hw), F32)],
         scalars=1,
     )
-    entered = local_call(
-        scan_kernel,
-        "carry",
-        [struct((rows, hw), BF16)] * n_seq,
-        work,
-        me,
-        *swap_seq(payload),
-        scratch=[
-            pltpu.VMEM((n_seq, rows + extra, hw), BF16),
-            pltpu.VMEM((n_seq, rows, hw), BF16),
-        ],
-        scalars=1,
-    )
-    carried = swap_seq(entered)
     inside = local_call(
         inside_kernel,
         "inside",
@@ -303,6 +403,23 @@
         key_vectors,
         value_vectors,
     )
+    arrived, inside, residual_there, take = lax.optimization_barrier(
+        (swap_seq(payload), inside, residual_there, take)
+    )
+    entered = local_call(
+        scan_kernel,
+        "carry",
+        [struct((rows, hw), BF16)] * n_seq,
+        work,
+        me,
+        *arrived,
+        scratch=[
+            pltpu.VMEM((n_seq, rows + extra, hw), BF16),
+            pltpu.VMEM((n_seq, rows, hw), BF16),
+        ],
+        scalars=1,
+    )
+    carried = swap_seq(entered)
     attended = local_call(
         outside_kernel,
         "outside",
@@ -335,33 +452,33 @@
                 attended, lambda q, k=k: (q // ny - k) % nz * ny + q % ny
             )
         products.append(jnp.dot(rows_k, w_z, preferred_element_type=F32).astype(BF16))
-    products = jnp.stack(products)
-    total = pick(products, (h - z) % nz).astype(F32)
+    block = struct((tokens, part), BF16)
+    place_me = jnp.stack([z, h]).astype(jnp.int32)
+    own, *sent = local_call(
+        route_kernel,
+        "route",
+        [block] * n_head,
+        tokens * part,
+        place_me,
+        *products,
+        scratch=[pltpu.VMEM((nz, tokens, part), BF16)],
+        scalars=1,
+    )
+    sums = [own]
     for m in range(1, n_head):
-        sent = pick(products, (h + m - z) % nz)
-        total = total + permute_head(sent, lambda q, m=m: (q + m) % n_head).astype(F32)
-    spots = [
-        ((zz * ny + yy) * n_head + hh, (hh * ny + yy) * n_head + zz)
-        for zz in range(nz)
-        for yy in range(ny)
-        for hh in range(n_head)
-    ]
-    summed = lax.ppermute(total.astype(BF16), ("seq", "head"), spots)
-
-    experts = n_seq
-    capacity = 4 * tokens // experts
-    flat_ids = routing.reshape(-1)
-    hits = (flat_ids[:, None] == jnp.arange(experts, dtype=jnp.int32)[None, :]).astype(F32)
-    pair_row = lax.broadcasted_iota(jnp.int32, (2 * tokens, 2 * tokens), 0)
-    pair_col = lax.broadcasted_iota(jnp.int32, (2 * tokens, 2 * tokens), 1)
-    earlier = jnp.dot((pair_col < pair_row).astype(F32), hits)
-    rank = jnp.sum(earlier * hits, axis=1).astype(jnp.int32)
-    place = (flat_ids * capacity + rank).reshape(tokens, 2)
-    slot = jnp.arange(experts * capacity, dtype=jnp.int32)
-    slot = (slot // capacity ^ s) * capacity + slot % capacity
-    here = place[:, None, :] == slot[None, :, None]
-    mix = jnp.sum(jnp.where(here, route_weights[:, None, :], 0.0), axis=2)
-    take = jnp.any(here, axis=2).astype(BF16).T
+        sums.append(permute_head(sent[m - 1], lambda q, m=m: (q + m) % n_head))
+    middle_there, *outgoing = local_call(
+        functools.partial(dispatch_kernel, n_head),
+        "dispatch",
+        [block] + [struct((capacity, part), BF16)] * experts,
+        2 * tokens * tokens * 4 * part,
+        residual_there,
+        take,
+        *sums,
+    )
+
+    arrived = swap_seq(outgoing)
+    middle = crossed(middle_there)
     in_owner = [h] + [(h + m * CORES) % n_head for m in range(1, nx)]
     in_owner += [
         o // CORES * CORES + (o % CORES + m) % CORES for o in in_owner for m in range(1, CORES)
@@ -369,24 +486,11 @@
     out_owner = [
         (x + m) % nx * CORES + (c + k) % CORES for k in [*range(1, CORES), 0] for m in range(nx)
     ]
-    owners = jnp.stack(in_owner + out_owner).astype(jnp.int32)
-
-    middle, *outgoing = local_call(
-        dispatch_kernel,
-        "dispatch",
-        [struct((tokens, part), BF16)] + [struct((capacity, part), BF16)] * experts,
-        2 * tokens * tokens * 4 * part,
-        summed,
-        residual,
-        take,
-    )
-    arrived = swap_seq(outgoing)
-    depth, units = gate_weight.shape[1:]
-    half = experts // 2
-    count = half * capacity
-    results = {}
-    for group in (0, 1):
-        got = jnp.concatenate(arrived[group * half : (group + 1) * half])
+    owners = jnp.stack(in_owner + out_owner + [z]).astype(jnp.int32)
+    count = n_head * capacity
+    returning = [None] * experts
+    for group in range(ny):
+        got = jnp.concatenate([arrived[k * ny + group] for k in range(nz)])
         pieces = [got]
         for m in range(1, nx):
             pieces.append(permute_head(got, lambda q, m=m: (q - m * CORES) % n_head))
@@ -397,39 +501,31 @@
                         piece, lambda q, m=m: q // CORES * CORES + (q % CORES - m) % CORES
                     )
                 )
-        results[group] = local_call(
-            functools.partial(expert_kernel, n_head),
-            "expert",
-            [struct((nx, count, part), BF16), struct((n_head - nx, count, part), BF16)],
-            6 * count * depth * units,
-            owners,
-            *pieces,
-            norm_gain.reshape(1, depth),
-            gate_weight,
-            up_weight,
-            down_weight,
-            scratch=[pltpu.VMEM((count, depth), BF16), pltpu.VMEM((count, units), BF16)],
-            scalars=1,
-            vmem=EXPERT_VMEM,
-        )
-
-    returning = [None] * experts
-    for group in (1, 0):
-        sent, kept = results[group]
+        sent, kept = expert_call(owners, pieces, norm_gain, gate_weight, up_weight, down_weight)
+
         near = permute_head(sent, lambda q: q // CORES * CORES + (q % CORES + 1) % CORES)
         near_sum = kept.astype(F32) + near.astype(F32)
-        total = near_sum[0]
+        parts = [near_sum[0]]
         for m in range(1, nx):
-            total = total + permute_head(
-                near_sum[m].astype(BF16), lambda q, m=m: (q + m * CORES) % n_head
-            ).astype(F32)
-        total = total.astype(BF16)
-        for k in range(half):
-            returning[group * half + k] = total[k * capacity : (k + 1) * capacity]
+            parts.append(
+                permute_head(near_sum[m].astype(BF16), lambda q, m=m: (q + m * CORES) % n_head)
+            )
+        blocks = local_call(
+            functools.partial(sum_kernel, nz),
+            "total",
+            [struct((capacity, part), BF16)] * nz,
+            count * part * nx,
+            z.astype(jnp.int32).reshape(1),
+            *parts,
+            scratch=[pltpu.VMEM((count, part), BF16)],
+            scalars=1,
+        )
+        for k in range(nz):
+            returning[k * ny + group] = blocks[k]
     return local_call(
         mix_kernel,
         "mix",
-        struct((tokens, part), BF16),
+        block,
         4 * tokens * experts * capacity * part,
         middle,
         mix,

time: 229 us -> 237 us (1.035)
  starting transfers between devices: 73.7 us -> 86.3 us
    pallas_call x8 -> x9, Pallas kernels: 34.9 us -> 7.95 us  [local_call(): pl.pallas_call(kernel, out_shape=out_shape, in_specs=[pl.BlockSpec(memory...]
    pallas_call x0 -> x2, Pallas kernels: none -> 24.6 us  [expert_call(): pl.pallas_call(functools.partial(expert_kernel, n_head, aligned), out_sha...]
    ppermute x32, waiting for transfers between devices: 72.4 us -> 58.7 us  [permute_seq(): lax.ppermute(value, 'seq', [(source, move(source)) for source in range(co...]
    ppermute x13, waiting for transfers between devices: 22.8 us -> 34.9 us  [permute_head(): lax.ppermute(value, 'head', [(source, move(source)) for source in range(c...]
    ppermute x13, starting transfers between devices: 11 us -> 19.4 us  [permute_head(): lax.ppermute(value, 'head', [(source, move(source)) for source in range(c...]
    unnamed x44 -> x48, local copies, waits for them, and re-layouts: 12.5 us -> 13.4 us
  transfers between devices with their start and end apart: 46 -> 48, of which waited for: 20 -> 11; matrix products, arithmetic and copies ran while one was open for 4% -> 4% of each run, Pallas kernels for 13% -> 12%
where the time goes in v4:
time: 237 us; the launch traced here: 235 us
  waiting for transfers between devices  93.6 us (39%)
  starting transfers between devices  86.3 us (36%)
  Pallas kernels  32.6 us (14%)
  local copies, waits for them, and re-layouts  17.5 us (7%)
  matrix products  2.8 us (1%)
    ppermute x32, starting transfers between devices, permute_seq(): lax.ppermute(value, 'seq', [(source, move(source)) for source in range(co...  64.2 us
    ppermute x32, waiting for transfers between devices, permute_seq(): lax.ppermute(value, 'seq', [(source, move(source)) for source in range(co...  58.7 us
    ppermute x13, waiting for transfers between devices, permute_head(): lax.ppermute(value, 'head', [(source, move(source)) for source in range(c...  34.9 us
    pallas_call x2, Pallas kernels, expert_call(): pl.pallas_call(functools.partial(expert_kernel, n_head, aligned), out_sha...  24.6 us
    ppermute x13, starting transfers between devices, permute_head(): lax.ppermute(value, 'head', [(source, move(source)) for source in range(c...  19.4 us
    unnamed x48, local copies, waits for them, and re-layouts  13.4 us
    pallas_call x9, Pallas kernels, local_call(): pl.pallas_call(kernel, out_shape=out_shape, in_specs=[pl.BlockSpec(memory...  7.95 us
  transfers between devices with their start and end apart: 48, of which 11 were waited for; matrix products, arithmetic and copies ran while one was open for 4% of the time, Pallas kernels for 12%

profile of v4, /device:TPU:0, one launch (start us, length us, event | category | flops | bytes accessed | tf_op | source)
XLA Modules:
  0.0 235.5 jit_solution(2274751257959996349)
XLA Ops:
  4.5 3.0 %collective-permute-start = (bf16[272,128]{1,0:T(8,128)(2,1)S(1)}, bf16[272,128]{1,0:T(8,128)(2,1)S(1)}, u32[]{:S(2)}, u32[]{:S(2)}) collective-permute-start(bf16[272,128]{1,0:T(8,128)(2,1)S(1)} %get-tuple-element.61), channel_id=1, source_target_pairs={{0,4},{4,0},{8,12},{12,8},{16,20},{20,16},{24,28},{28,24},{1,5},{5... | collective-permute-start | bytes 208904 | tf_op jit(solution)/shard_map/ppermute | solution.py:22
  9.1 3.0 %collective-permute-start.3 = (bf16[272,128]{1,0:T(8,128)(2,1)S(1)}, bf16[272,128]{1,0:T(8,128)(2,1)S(1)}, u32[]{:S(2)}, u32[]{:S(2)}) collective-permute-start(bf16[272,128]{1,0:T(8,128)(2,1)S(1)} %get-tuple-element.64), channel_id=1, source_target_pairs={{0,16},{4,20},{8,24},{12,28},{16,0},{20,4},{24,8},{28,12},{1,17},{... | collective-permute-start | bytes 208904 | tf_op jit(solution)/shard_map/ppermute | solution.py:22
  17.3 2.6 %inside.1.inside_ref = f32[128,2048]{1,0:T(8,128)S(1)} custom-call(s32[1,128]{1,0:T(1,128)S(1)} %bitcast.39, f32[128,16]{1,0:T(8,128)S(1)} %get-tuple-element.68.sum_ref, f32[16,128]{1,0:T(8,128)S(1)} %bitcast.36, bf16[128,2048]{1,0:T(8,128)(2,1)S(1)} %copy-done.5, bf16[128,2048]{1,0:T(8,128)(2,1)S(1)} %copy-done.2, bf16[128,2048]{1,0:T(8,128)(2,1)S(1)} %copy-done.4), custom_call_target="tpu_custom_call" | custom-call | flops 134217728 | bytes 2638336 | tf_op jit(solution)/shard_map/inside/pallas_call | solution.py:308
  19.9 5.5 %collective-permute-start.4 = (bf16[272,128]{1,0:T(8,128)(2,1)S(1)}, bf16[272,128]{1,0:T(8,128)(2,1)S(1)}, u32[]{:S(2)}, u32[]{:S(2)}) collective-permute-start(bf16[272,128]{1,0:T(8,128)(2,1)S(1)} %get-tuple-element.65), channel_id=1, source_target_pairs={{0,20},{4,16},{8,28},{12,24},{16,4},{20,0},{24,12},{28,8},{1,21},{... | collective-permute-start | bytes 208904 | tf_op jit(solution)/shard_map/ppermute | solution.py:22
  26.6 3.7 %collective-permute-start.6 = (bf16[272,128]{1,0:T(8,128)(2,1)S(1)}, bf16[272,128]{1,0:T(8,128)(2,1)S(1)}, u32[]{:S(2)}, u32[]{:S(2)}) collective-permute-start(bf16[272,128]{1,0:T(8,128)(2,1)S(1)} %get-tuple-element.67), channel_id=1, source_target_pairs={{0,28},{4,24},{8,20},{12,16},{16,12},{20,8},{24,4},{28,0},{1,29},{... | collective-permute-start | bytes 208904 | tf_op jit(solution)/shard_map/ppermute | solution.py:22
  31.0 2.4 %collective-permute-done.5.refs_6_ = bf16[272,128]{1,0:T(8,128)(2,1)S(1)} collective-permute-done((bf16[272,128]{1,0:T(8,128)(2,1)S(1)}, bf16[272,128]{1,0:T(8,128)(2,1)S(1)}, u32[]{:S(2)}, u32[]{:S(2)}) %collective-permute-start.5) | collective-permute-done | bytes 69664 | tf_op jit(solution)/shard_map/ppermute | solution.py:22
  34.5 2.1 collective-permute-start.9
  36.6 4.9 %collective-permute-start.10 = (bf16[256,128]{1,0:T(8,128)(2,1)S(1)}, bf16[256,128]{1,0:T(8,128)(2,1)S(1)}, u32[]{:S(2)}, u32[]{:S(2)}) collective-permute-start(bf16[256,128]{1,0:T(8,128)(2,1)S(1)} %get-tuple-element.82), channel_id=1, source_target_pairs={{0,8},{4,12},{8,0},{12,4},{16,24},{20,28},{24,16},{28,20},{1,9},{5... | collective-permute-start | bytes 196616 | tf_op jit(solution)/shard_map/ppermute | solution.py:22
  41.6 4.6 %collective-permute-start.12 = (bf16[256,128]{1,0:T(8,128)(2,1)S(1)}, bf16[256,128]{1,0:T(8,128)(2,1)S(1)}, u32[]{:S(2)}, u32[]{:S(2)}) collective-permute-start(bf16[256,128]{1,0:T(8,128)(2,1)S(1)} %get-tuple-element.84), channel_id=1, source_target_pairs={{0,16},{4,20},{8,24},{12,28},{16,0},{20,4},{24,8},{28,12},{1,17},{... | collective-permute-start | bytes 196616 | tf_op jit(solution)/shard_map/ppermute | solution.py:22
  46.6 2.4 %collective-permute-start.14 = (bf16[256,128]{1,0:T(8,128)(2,1)S(1)}, bf16[256,128]{1,0:T(8,128)(2,1)S(1)}, u32[]{:S(2)}, u32[]{:S(2)}) collective-permute-start(bf16[256,128]{1,0:T(8,128)(2,1)S(1)} %get-tuple-element.86), channel_id=1, source_target_pairs={{0,24},{4,28},{8,16},{12,20},{16,8},{20,12},{24,0},{28,4},{1,25},{... | collective-permute-start | bytes 196616 | tf_op jit(solution)/shard_map/ppermute | solution.py:22
  49.0 1.9 collective-permute-start.15
  50.9 6.1 %collective-permute-done.13.refs_5_ = bf16[256,128]{1,0:T(8,128)(2,1)S(1)} collective-permute-done((bf16[256,128]{1,0:T(8,128)(2,1)S(1)}, bf16[256,128]{1,0:T(8,128)(2,1)S(1)}, u32[]{:S(2)}, u32[]{:S(2)}) %collective-permute-start.13) | collective-permute-done | bytes 65568 | tf_op jit(solution)/shard_map/ppermute | solution.py:22
  59.6 1.9 collective-permute-start.17
  61.5 2.6 %collective-permute-start.18 = (bf16[128,2048]{1,0:T(8,128)(2,1)S(1)}, bf16[128,2048]{1,0:T(8,128)(2,1)S(1)}, u32[]{:S(2)}, u32[]{:S(2)}) collective-permute-start(bf16[128,2048]{1,0:T(8,128)(2,1)S(1)} %outside.1), channel_id=1, source_target_pairs={{0,16},{4,20},{8,24},{12,28},{16,0},{20,4},{24,8},{28,12},{1,17},{... | collective-permute-start | bytes 1572872 | tf_op jit(solution)/shard_map/ppermute | solution.py:22
  67.4 28.0 %collective-permute-done.16 = bf16[2048,384]{1,0:T(8,128)(2,1)S(1)} collective-permute-done((bf16[2048,384]{1,0:T(8,128)(2,1)}, bf16[2048,384]{1,0:T(8,128)(2,1)S(1)}, u32[]{:S(2)}, u32[]{:S(2)}) %collective-permute-start.16) | collective-permute-done | bytes 1572896 | tf_op jit(solution)/shard_map/ppermute | solution.py:22
  96.9 12.4 %collective-permute-done.18 = bf16[128,2048]{1,0:T(8,128)(2,1)S(1)} collective-permute-done((bf16[128,2048]{1,0:T(8,128)(2,1)S(1)}, bf16[128,2048]{1,0:T(8,128)(2,1)S(1)}, u32[]{:S(2)}, u32[]{:S(2)}) %collective-permute-start.18) | collective-permute-done | bytes 524320 | tf_op jit(solution)/shard_map/ppermute | solution.py:22
  113.1 4.8 %collective-permute-done.20.refs_1_ = bf16[128,768]{1,0:T(8,128)(2,1)S(1)} collective-permute-done((bf16[128,768]{1,0:T(8,128)(2,1)S(1)}, bf16[128,768]{1,0:T(8,128)(2,1)S(1)}, u32[]{:S(2)}, u32[]{:S(2)}) %collective-permute-start.20) | collective-permute-done | bytes 196640 | tf_op jit(solution)/shard_map/ppermute | solution.py:27
  121.5 2.5 %collective-permute-start.26 = (bf16[64,768]{1,0:T(8,128)(2,1)S(1)}, bf16[64,768]{1,0:T(8,128)(2,1)S(1)}, u32[]{:S(2)}, u32[]{:S(2)}) collective-permute-start(bf16[64,768]{1,0:T(8,128)(2,1)S(1)} %get-tuple-element.98), channel_id=1, source_target_pairs={{0,24},{4,28},{8,16},{12,20},{16,8},{20,12},{24,0},{28,4},{1,25},{... | collective-permute-start | bytes 294920 | tf_op jit(solution)/shard_map/ppermute | solution.py:22
  127.3 3.6 %collective-permute-start.35 = (bf16[64,768]{1,0:T(8,128)(2,1)S(1)}, bf16[64,768]{1,0:T(8,128)(2,1)S(1)}, u32[]{:S(2)}, u32[]{:S(2)}) collective-permute-start(bf16[64,768]{1,0:T(8,128)(2,1)S(1)} %get-tuple-element.105), channel_id=1, source_target_pairs={{0,28},{4,24},{8,20},{12,16},{16,12},{20,8},{24,4},{28,0},{1,29},{... | collective-permute-start | bytes 294920 | tf_op jit(solution)/shard_map/ppermute | solution.py:22
  130.9 5.6 %collective-permute-start.27 = (bf16[256,768]{1,0:T(8,128)(2,1)S(1)}, bf16[256,768]{1,0:T(8,128)(2,1)}, u32[]{:S(2)}, u32[]{:S(2)}) collective-permute-start(bf16[256,768]{1,0:T(8,128)(2,1)S(1)} %constant_dynamic-update-slice_fusion.refs_0_), channel_id=1, source_target_pairs={{0,2},{1,3},{2,0},{3,1},{4,6},{5,7},{6,4},{7,5},{8,10},{9,11},{10,... | collective-permute-start | bytes 1179656 | tf_op jit(solution)/shard_map/ppermute | solution.py:27
  139.1 4.9 %collective-permute-start.36 = (bf16[256,768]{1,0:T(8,128)(2,1)}, bf16[256,768]{1,0:T(8,128)(2,1)}, u32[]{:S(2)}, u32[]{:S(2)}) collective-permute-start(bf16[256,768]{1,0:T(8,128)(2,1)} %constant_dynamic-update-slice_fusion.4.refs_0_), channel_id=1, source_target_pairs={{0,2},{1,3},{2,0},{3,1},{4,6},{5,7},{6,4},{7,5},{8,10},{9,11},{10,... | collective-permute-start | bytes 1179656 | tf_op jit(solution)/shard_map/ppermute | solution.py:27
  144.0 2.5 %collective-permute-done.27.refs_1_ = bf16[256,768]{1,0:T(8,128)(2,1)} collective-permute-done((bf16[256,768]{1,0:T(8,128)(2,1)S(1)}, bf16[256,768]{1,0:T(8,128)(2,1)}, u32[]{:S(2)}, u32[]{:S(2)}) %collective-permute-start.27) | collective-permute-done | bytes 393248 | tf_op jit(solution)/shard_map/ppermute | solution.py:27
  147.1 7.5 %collective-permute-done.36.refs_1_ = bf16[256,768]{1,0:T(8,128)(2,1)} collective-permute-done((bf16[256,768]{1,0:T(8,128)(2,1)}, bf16[256,768]{1,0:T(8,128)(2,1)}, u32[]{:S(2)}, u32[]{:S(2)}) %collective-permute-start.36) | collective-permute-done | bytes 393248 | tf_op jit(solution)/shard_map/ppermute | solution.py:27
  154.6 3.0 %copy-done = bf16[1,3072,1152]{2,1,0:T(8,128)(2,1)S(1)} copy-done((bf16[1,3072,1152]{2,1,0:T(8,128)(2,1)S(1)}, bf16[1,3072,1152]{2,1,0:T(8,128)(2,1)}, u32[]{:S(2)}) %copy-start) | copy-done | bytes 7077912
  157.6 12.5 %expert.2 = (bf16[2,256,768]{2,1,0:T(8,128)(2,1)}, bf16[2,256,768]{2,1,0:T(8,128)(2,1)S(1)}) custom-call(s32[9]{0:T(128)S(1)} %stack.45.owner_ref, bf16[256,768]{1,0:T(8,128)(2,1)S(1)} %constant_dynamic-update-slice_fusion.refs_0_, bf16[256,768]{1,0:T(8,128)(2,1)} %collective-permute-done.27.refs_1_, bf16[256,768]{1,0:T(8,128)(2,1)} %collective-permute-done.28.refs_2_, ...), custom_call_target="tpu_custom_call" | custom-call | flops 5435817984 | bytes 24379392 | tf_op jit(solution)/shard_map/expert/pallas_call | solution.py:281
  170.7 12.2 %expert.3 = (bf16[2,256,768]{2,1,0:T(8,128)(2,1)}, bf16[2,256,768]{2,1,0:T(8,128)(2,1)S(1)}) custom-call(s32[9]{0:T(128)S(1)} %stack.45.owner_ref, bf16[256,768]{1,0:T(8,128)(2,1)} %constant_dynamic-update-slice_fusion.4.refs_0_, bf16[256,768]{1,0:T(8,128)(2,1)} %collective-permute-done.36.refs_1_, bf16[256,768]{1,0:T(8,128)(2,1)S(1)} %collective-permute-done.37.refs_2_, ...), custom_call_target="tpu_custom_call" | custom-call | flops 5435817984 | bytes 24379392 | tf_op jit(solution)/shard_map/expert/pallas_call | solution.py:281
  187.0 5.7 %collective-permute-start.31 = (bf16[256,768]{1,0:T(8,128)(2,1)S(1)}, bf16[256,768]{1,0:T(8,128)(2,1)S(1)}, u32[]{:S(2)}, u32[]{:S(2)}) collective-permute-start(bf16[256,768]{1,0:T(8,128)(2,1)S(1)} %fusion.2), channel_id=1, source_target_pairs={{0,2},{1,3},{2,0},{3,1},{4,6},{5,7},{6,4},{7,5},{8,10},{9,11},{10,... | collective-permute-start | bytes 1179656 | tf_op jit(solution)/shard_map/ppermute | solution.py:27
  193.1 18.9 %collective-permute-done.40.refs_1_ = bf16[256,768]{1,0:T(8,128)(2,1)S(1)} collective-permute-done((bf16[256,768]{1,0:T(8,128)(2,1)S(1)}, bf16[256,768]{1,0:T(8,128)(2,1)S(1)}, u32[]{:S(2)}, u32[]{:S(2)}) %collective-permute-start.40) | collective-permute-done | bytes 393248 | tf_op jit(solution)/shard_map/ppermute | solution.py:27
  213.4 2.9 %collective-permute-start.42 = (bf16[64,768]{1,0:T(8,128)(2,1)S(1)}, bf16[64,768]{1,0:T(8,128)(2,1)S(1)}, u32[]{:S(2)}, u32[]{:S(2)}) collective-permute-start(bf16[64,768]{1,0:T(8,128)(2,1)S(1)} %get-tuple-element.109), channel_id=1, source_target_pairs={{0,8},{4,12},{8,0},{12,4},{16,24},{20,28},{24,16},{28,20},{1,9},{5... | collective-permute-start | bytes 294920 | tf_op jit(solution)/shard_map/ppermute | solution.py:22
  216.3 3.6 %collective-permute-start.44 = (bf16[64,768]{1,0:T(8,128)(2,1)S(1)}, bf16[64,768]{1,0:T(8,128)(2,1)S(1)}, u32[]{:S(2)}, u32[]{:S(2)}) collective-permute-start(bf16[64,768]{1,0:T(8,128)(2,1)S(1)} %get-tuple-element.111), channel_id=1, source_target_pairs={{0,16},{4,20},{8,24},{12,28},{16,0},{20,4},{24,8},{28,12},{1,17},{... | collective-permute-start | bytes 294920 | tf_op jit(solution)/shard_map/ppermute | solution.py:22
  220.6 3.0 %collective-permute-start.46 = (bf16[64,768]{1,0:T(8,128)(2,1)S(1)}, bf16[64,768]{1,0:T(8,128)(2,1)S(1)}, u32[]{:S(2)}, u32[]{:S(2)}) collective-permute-start(bf16[64,768]{1,0:T(8,128)(2,1)S(1)} %get-tuple-element.113), channel_id=1, source_target_pairs={{0,24},{4,28},{8,16},{12,20},{16,8},{20,12},{24,0},{28,4},{1,25},{... | collective-permute-start | bytes 294920 | tf_op jit(solution)/shard_map/ppermute | solution.py:22
  225.6 8.8 %collective-permute-done.45.refs_5_ = bf16[64,768]{1,0:T(8,128)(2,1)S(1)} collective-permute-done((bf16[64,768]{1,0:T(8,128)(2,1)S(1)}, bf16[64,768]{1,0:T(8,128)(2,1)S(1)}, u32[]{:S(2)}, u32[]{:S(2)}) %collective-permute-start.45) | collective-permute-done | bytes 98336 | tf_op jit(solution)/shard_map/ppermute | solution.py:22
  (160 shorter events, 45.9 us)
Async XLA Ops:
  4.5 21.9 %collective-permute-start = (bf16[272,128]{1,0:T(8,128)(2,1)S(1)}, bf16[272,128]{1,0:T(8,128)(2,1)S(1)}, u32[]{:S(2)}, u32[]{:S(2)}) collective-permute-start(bf16[272,128]{1,0:T(8,128)(2,1)S(1)} %get-tuple-element.61), channel_id=1, source_target_pairs={{0,4},{4,0},{8,12},{12,8},{16,20},{20,16},{24,28},{28,24},{1,5},{5... | collective-permute-start | bytes 208904 | tf_op jit(solution)/shard_map/ppermute | solution.py:22
  7.6 19.0 %collective-permute-start.1 = (bf16[272,128]{1,0:T(8,128)(2,1)S(1)}, bf16[272,128]{1,0:T(8,128)(2,1)S(1)}, u32[]{:S(2)}, u32[]{:S(2)}) collective-permute-start(bf16[272,128]{1,0:T(8,128)(2,1)S(1)} %get-tuple-element.62), channel_id=1, source_target_pairs={{0,8},{4,12},{8,0},{12,4},{16,24},{20,28},{24,16},{28,20},{1,9},{5... | collective-permute-start | bytes 208904 | tf_op jit(solution)/shard_map/ppermute | solution.py:22
  9.1 21.1 %collective-permute-start.2 = (bf16[272,128]{1,0:T(8,128)(2,1)S(1)}, bf16[272,128]{1,0:T(8,128)(2,1)S(1)}, u32[]{:S(2)}, u32[]{:S(2)}) collective-permute-start(bf16[272,128]{1,0:T(8,128)(2,1)S(1)} %get-tuple-element.63), channel_id=1, source_target_pairs={{0,12},{4,8},{8,4},{12,0},{16,28},{20,24},{24,20},{28,16},{1,13},{... | collective-permute-start | bytes 208904 | tf_op jit(solution)/shard_map/ppermute | solution.py:22
  9.1 21.8 %collective-permute-start.3 = (bf16[272,128]{1,0:T(8,128)(2,1)S(1)}, bf16[272,128]{1,0:T(8,128)(2,1)S(1)}, u32[]{:S(2)}, u32[]{:S(2)}) collective-permute-start(bf16[272,128]{1,0:T(8,128)(2,1)S(1)} %get-tuple-element.64), channel_id=1, source_target_pairs={{0,16},{4,20},{8,24},{12,28},{16,0},{20,4},{24,8},{28,12},{1,17},{... | collective-permute-start | bytes 208904 | tf_op jit(solution)/shard_map/ppermute | solution.py:22
  19.9 11.0 %collective-permute-start.4 = (bf16[272,128]{1,0:T(8,128)(2,1)S(1)}, bf16[272,128]{1,0:T(8,128)(2,1)S(1)}, u32[]{:S(2)}, u32[]{:S(2)}) collective-permute-start(bf16[272,128]{1,0:T(8,128)(2,1)S(1)} %get-tuple-element.65), channel_id=1, source_target_pairs={{0,20},{4,16},{8,28},{12,24},{16,4},{20,0},{24,12},{28,8},{1,21},{... | collective-permute-start | bytes 208904 | tf_op jit(solution)/shard_map/ppermute | solution.py:22
  34.5 12.2 %collective-permute-start.9 = (bf16[256,128]{1,0:T(8,128)(2,1)S(1)}, bf16[256,128]{1,0:T(8,128)(2,1)S(1)}, u32[]{:S(2)}, u32[]{:S(2)}) collective-permute-start(bf16[256,128]{1,0:T(8,128)(2,1)S(1)} %get-tuple-element.81), channel_id=1, source_target_pairs={{0,4},{4,0},{8,12},{12,8},{16,20},{20,16},{24,28},{28,24},{1,5},{5... | collective-permute-start | bytes 196616 | tf_op jit(solution)/shard_map/ppermute | solution.py:22
  36.6 12.4 %collective-permute-start.10 = (bf16[256,128]{1,0:T(8,128)(2,1)S(1)}, bf16[256,128]{1,0:T(8,128)(2,1)S(1)}, u32[]{:S(2)}, u32[]{:S(2)}) collective-permute-start(bf16[256,128]{1,0:T(8,128)(2,1)S(1)} %get-tuple-element.82), channel_id=1, source_target_pairs={{0,8},{4,12},{8,0},{12,4},{16,24},{20,28},{24,16},{28,20},{1,9},{5... | collective-permute-start | bytes 196616 | tf_op jit(solution)/shard_map/ppermute | solution.py:22
  41.5 9.5 %collective-permute-start.11 = (bf16[256,128]{1,0:T(8,128)(2,1)S(1)}, bf16[256,128]{1,0:T(8,128)(2,1)S(1)}, u32[]{:S(2)}, u32[]{:S(2)}) collective-permute-start(bf16[256,128]{1,0:T(8,128)(2,1)S(1)} %get-tuple-element.83), channel_id=1, source_target_pairs={{0,12},{4,8},{8,4},{12,0},{16,28},{20,24},{24,20},{28,16},{1,13},{... | collective-permute-start | bytes 196616 | tf_op jit(solution)/shard_map/ppermute | solution.py:22
  46.2 10.9 %collective-permute-start.13 = (bf16[256,128]{1,0:T(8,128)(2,1)S(1)}, bf16[256,128]{1,0:T(8,128)(2,1)S(1)}, u32[]{:S(2)}, u32[]{:S(2)}) collective-permute-start(bf16[256,128]{1,0:T(8,128)(2,1)S(1)} %get-tuple-element.85), channel_id=1, source_target_pairs={{0,20},{4,16},{8,28},{12,24},{16,4},{20,0},{24,12},{28,8},{1,21},{... | collective-permute-start | bytes 196616 | tf_op jit(solution)/shard_map/ppermute | solution.py:22
  46.6 10.4 %collective-permute-start.14 = (bf16[256,128]{1,0:T(8,128)(2,1)S(1)}, bf16[256,128]{1,0:T(8,128)(2,1)S(1)}, u32[]{:S(2)}, u32[]{:S(2)}) collective-permute-start(bf16[256,128]{1,0:T(8,128)(2,1)S(1)} %get-tuple-element.86), channel_id=1, source_target_pairs={{0,24},{4,28},{8,16},{12,20},{16,8},{20,12},{24,0},{28,4},{1,25},{... | collective-permute-start | bytes 196616 | tf_op jit(solution)/shard_map/ppermute | solution.py:22
  58.8 36.5 %collective-permute-start.16 = (bf16[2048,384]{1,0:T(8,128)(2,1)}, bf16[2048,384]{1,0:T(8,128)(2,1)S(1)}, u32[]{:S(2)}, u32[]{:S(2)}) collective-permute-start(bf16[2048,384]{1,0:T(8,128)(2,1)} %param.20), channel_id=1, source_target_pairs={{0,4},{4,0},{8,12},{12,8},{16,20},{20,16},{24,28},{28,24},{1,5},{5... | collective-permute-start | bytes 4718600 | tf_op jit(solution)/shard_map/ppermute | solution.py:22
  59.6 36.7 %collective-permute-start.17 = (bf16[128,2048]{1,0:T(8,128)(2,1)S(1)}, bf16[128,2048]{1,0:T(8,128)(2,1)S(1)}, u32[]{:S(2)}, u32[]{:S(2)}) collective-permute-start(bf16[128,2048]{1,0:T(8,128)(2,1)S(1)} %outside.1), channel_id=1, source_target_pairs={{0,24},{4,28},{8,0},{12,4},{16,8},{20,12},{24,16},{28,20},{1,25},{... | collective-permute-start | bytes 1572872 | tf_op jit(solution)/shard_map/ppermute | solution.py:22
  61.5 47.8 %collective-permute-start.18 = (bf16[128,2048]{1,0:T(8,128)(2,1)S(1)}, bf16[128,2048]{1,0:T(8,128)(2,1)S(1)}, u32[]{:S(2)}, u32[]{:S(2)}) collective-permute-start(bf16[128,2048]{1,0:T(8,128)(2,1)S(1)} %outside.1), channel_id=1, source_target_pairs={{0,16},{4,20},{8,24},{12,28},{16,0},{20,4},{24,8},{28,12},{1,17},{... | collective-permute-start | bytes 1572872 | tf_op jit(solution)/shard_map/ppermute | solution.py:22
  64.1 45.9 %collective-permute-start.19 = (bf16[128,2048]{1,0:T(8,128)(2,1)S(1)}, bf16[128,2048]{1,0:T(8,128)(2,1)S(1)}, u32[]{:S(2)}, u32[]{:S(2)}) collective-permute-start(bf16[128,2048]{1,0:T(8,128)(2,1)S(1)} %outside.1), channel_id=1, source_target_pairs={{0,8},{4,12},{8,16},{12,20},{16,24},{20,28},{24,0},{28,4},{1,9},{5... | collective-permute-start | bytes 1572872 | tf_op jit(solution)/shard_map/ppermute | solution.py:22
  121.5 9.4 %collective-permute-start.26 = (bf16[64,768]{1,0:T(8,128)(2,1)S(1)}, bf16[64,768]{1,0:T(8,128)(2,1)S(1)}, u32[]{:S(2)}, u32[]{:S(2)}) collective-permute-start(bf16[64,768]{1,0:T(8,128)(2,1)S(1)} %get-tuple-element.98), channel_id=1, source_target_pairs={{0,24},{4,28},{8,16},{12,20},{16,8},{20,12},{24,0},{28,4},{1,25},{... | collective-permute-start | bytes 294920 | tf_op jit(solution)/shard_map/ppermute | solution.py:22
  124.0 12.5 %collective-permute-start.32 = (bf16[64,768]{1,0:T(8,128)(2,1)S(1)}, bf16[64,768]{1,0:T(8,128)(2,1)S(1)}, u32[]{:S(2)}, u32[]{:S(2)}) collective-permute-start(bf16[64,768]{1,0:T(8,128)(2,1)S(1)} %get-tuple-element.102), channel_id=1, source_target_pairs={{0,4},{4,0},{8,12},{12,8},{16,20},{20,16},{24,28},{28,24},{1,5},{5... | collective-permute-start | bytes 294920 | tf_op jit(solution)/shard_map/ppermute | solution.py:22
  125.7 11.5 %collective-permute-start.33 = (bf16[64,768]{1,0:T(8,128)(2,1)S(1)}, bf16[64,768]{1,0:T(8,128)(2,1)S(1)}, u32[]{:S(2)}, u32[]{:S(2)}) collective-permute-start(bf16[64,768]{1,0:T(8,128)(2,1)S(1)} %get-tuple-element.103), channel_id=1, source_target_pairs={{0,12},{4,8},{8,4},{12,0},{16,28},{20,24},{24,20},{28,16},{1,13},{... | collective-permute-start | bytes 294920 | tf_op jit(solution)/shard_map/ppermute | solution.py:22
  125.7 12.2 %collective-permute-start.34 = (bf16[64,768]{1,0:T(8,128)(2,1)S(1)}, bf16[64,768]{1,0:T(8,128)(2,1)S(1)}, u32[]{:S(2)}, u32[]{:S(2)}) collective-permute-start(bf16[64,768]{1,0:T(8,128)(2,1)S(1)} %get-tuple-element.104), channel_id=1, source_target_pairs={{0,20},{4,16},{8,28},{12,24},{16,4},{20,0},{24,12},{28,8},{1,21},{... | collective-permute-start | bytes 294920 | tf_op jit(solution)/shard_map/ppermute | solution.py:22
  127.3 11.2 %collective-permute-start.35 = (bf16[64,768]{1,0:T(8,128)(2,1)S(1)}, bf16[64,768]{1,0:T(8,128)(2,1)S(1)}, u32[]{:S(2)}, u32[]{:S(2)}) collective-permute-start(bf16[64,768]{1,0:T(8,128)(2,1)S(1)} %get-tuple-element.105), channel_id=1, source_target_pairs={{0,28},{4,24},{8,20},{12,16},{16,12},{20,8},{24,4},{28,0},{1,29},{... | collective-permute-start | bytes 294920 | tf_op jit(solution)/shard_map/ppermute | solution.py:22
  130.9 15.6 %collective-permute-start.27 = (bf16[256,768]{1,0:T(8,128)(2,1)S(1)}, bf16[256,768]{1,0:T(8,128)(2,1)}, u32[]{:S(2)}, u32[]{:S(2)}) collective-permute-start(bf16[256,768]{1,0:T(8,128)(2,1)S(1)} %constant_dynamic-update-slice_fusion.refs_0_), channel_id=1, source_target_pairs={{0,2},{1,3},{2,0},{3,1},{4,6},{5,7},{6,4},{7,5},{8,10},{9,11},{10,... | collective-permute-start | bytes 1179656 | tf_op jit(solution)/shard_map/ppermute | solution.py:27
  139.1 15.5 %collective-permute-start.36 = (bf16[256,768]{1,0:T(8,128)(2,1)}, bf16[256,768]{1,0:T(8,128)(2,1)}, u32[]{:S(2)}, u32[]{:S(2)}) collective-permute-start(bf16[256,768]{1,0:T(8,128)(2,1)} %constant_dynamic-update-slice_fusion.4.refs_0_), channel_id=1, source_target_pairs={{0,2},{1,3},{2,0},{3,1},{4,6},{5,7},{6,4},{7,5},{8,10},{9,11},{10,... | collective-permute-start | bytes 1179656 | tf_op jit(solution)/shard_map/ppermute | solution.py:27
  144.0 10.6 %collective-permute-start.28 = (bf16[256,768]{1,0:T(8,128)(2,1)S(1)}, bf16[256,768]{1,0:T(8,128)(2,1)}, u32[]{:S(2)}, u32[]{:S(2)}) collective-permute-start(bf16[256,768]{1,0:T(8,128)(2,1)S(1)} %constant_dynamic-update-slice_fusion.refs_0_), channel_id=1, source_target_pairs={{0,1},{1,0},{2,3},{3,2},{4,5},{5,4},{6,7},{7,6},{8,9},{9,8},{10,11... | collective-permute-start | bytes 1179656 | tf_op jit(solution)/shard_map/ppermute | solution.py:27
  146.6 24.1 %collective-permute-start.37 = (bf16[256,768]{1,0:T(8,128)(2,1)}, bf16[256,768]{1,0:T(8,128)(2,1)S(1)}, u32[]{:S(2)}, u32[]{:S(2)}) collective-permute-start(bf16[256,768]{1,0:T(8,128)(2,1)} %constant_dynamic-update-slice_fusion.4.refs_0_), channel_id=1, source_target_pairs={{0,1},{1,0},{2,3},{3,2},{4,5},{5,4},{6,7},{7,6},{8,9},{9,8},{10,11... | collective-permute-start | bytes 1179656 | tf_op jit(solution)/shard_map/ppermute | solution.py:27
  154.6 16.1 %collective-permute-start.38 = (bf16[256,768]{1,0:T(8,128)(2,1)}, bf16[256,768]{1,0:T(8,128)(2,1)S(1)}, u32[]{:S(2)}, u32[]{:S(2)}) collective-permute-start(bf16[256,768]{1,0:T(8,128)(2,1)} %collective-permute-done.36.refs_1_), channel_id=1, source_target_pairs={{0,1},{1,0},{2,3},{3,2},{4,5},{5,4},{6,7},{7,6},{8,9},{9,8},{10,11... | collective-permute-start | bytes 1179656 | tf_op jit(solution)/shard_map/ppermute | solution.py:27
  170.1 15.2 %collective-permute-start.30 = (bf16[2,256,768]{2,1,0:T(8,128)(2,1)}, bf16[2,256,768]{2,1,0:T(8,128)(2,1)}, u32[]{:S(2)}, u32[]{:S(2)}) collective-permute-start(bf16[2,256,768]{2,1,0:T(8,128)(2,1)} %get-tuple-element.100), channel_id=1, source_target_pairs={{0,1},{1,0},{2,3},{3,2},{4,5},{5,4},{6,7},{7,6},{8,9},{9,8},{10,11... | collective-permute-start | bytes 2359304 | tf_op jit(solution)/shard_map/ppermute | solution.py:27
  184.7 35.2 %collective-permute-start.23 = (bf16[128,768]{1,0:T(8,128)(2,1)S(1)}, bf16[128,768]{1,0:T(8,128)(2,1)S(1)}, u32[]{:S(2)}, u32[]{:S(2)}) collective-permute-start(bf16[128,768]{1,0:T(8,128)(2,1)S(1)} %get-tuple-element.94), channel_id=1, source_target_pairs={{0,0},{1,8},{2,16},{3,24},{4,4},{5,12},{6,20},{7,28},{8,1},{9,9},{... | collective-permute-start | bytes 589832 | tf_op jit(solution)/shard_map/ppermute | solution.py:364
  187.0 26.3 %collective-permute-start.31 = (bf16[256,768]{1,0:T(8,128)(2,1)S(1)}, bf16[256,768]{1,0:T(8,128)(2,1)S(1)}, u32[]{:S(2)}, u32[]{:S(2)}) collective-permute-start(bf16[256,768]{1,0:T(8,128)(2,1)S(1)} %fusion.2), channel_id=1, source_target_pairs={{0,2},{1,3},{2,0},{3,1},{4,6},{5,7},{6,4},{7,5},{8,10},{9,11},{10,... | collective-permute-start | bytes 1179656 | tf_op jit(solution)/shard_map/ppermute | solution.py:27
  192.9 19.1 %collective-permute-start.40 = (bf16[256,768]{1,0:T(8,128)(2,1)S(1)}, bf16[256,768]{1,0:T(8,128)(2,1)S(1)}, u32[]{:S(2)}, u32[]{:S(2)}) collective-permute-start(bf16[256,768]{1,0:T(8,128)(2,1)S(1)} %fusion.3), channel_id=1, source_target_pairs={{0,2},{1,3},{2,0},{3,1},{4,6},{5,7},{6,4},{7,5},{8,10},{9,11},{10,... | collective-permute-start | bytes 1179656 | tf_op jit(solution)/shard_map/ppermute | solution.py:27
  213.4 10.3 %collective-permute-start.42 = (bf16[64,768]{1,0:T(8,128)(2,1)S(1)}, bf16[64,768]{1,0:T(8,128)(2,1)S(1)}, u32[]{:S(2)}, u32[]{:S(2)}) collective-permute-start(bf16[64,768]{1,0:T(8,128)(2,1)S(1)} %get-tuple-element.109), channel_id=1, source_target_pairs={{0,8},{4,12},{8,0},{12,4},{16,24},{20,28},{24,16},{28,20},{1,9},{5... | collective-permute-start | bytes 294920 | tf_op jit(solution)/shard_map/ppermute | solution.py:22
  219.9 14.5 %collective-permute-start.45 = (bf16[64,768]{1,0:T(8,128)(2,1)S(1)}, bf16[64,768]{1,0:T(8,128)(2,1)S(1)}, u32[]{:S(2)}, u32[]{:S(2)}) collective-permute-start(bf16[64,768]{1,0:T(8,128)(2,1)S(1)} %get-tuple-element.112), channel_id=1, source_target_pairs={{0,20},{4,16},{8,28},{12,24},{16,4},{20,0},{24,12},{28,8},{1,21},{... | collective-permute-start | bytes 294920 | tf_op jit(solution)/shard_map/ppermute | solution.py:22
  220.6 13.8 %collective-permute-start.46 = (bf16[64,768]{1,0:T(8,128)(2,1)S(1)}, bf16[64,768]{1,0:T(8,128)(2,1)S(1)}, u32[]{:S(2)}, u32[]{:S(2)}) collective-permute-start(bf16[64,768]{1,0:T(8,128)(2,1)S(1)} %get-tuple-element.113), channel_id=1, source_target_pairs={{0,24},{4,28},{8,16},{12,20},{16,8},{20,12},{24,0},{28,4},{1,25},{... | collective-permute-start | bytes 294920 | tf_op jit(solution)/shard_map/ppermute | solution.py:22
  223.7 10.7 %collective-permute-start.47 = (bf16[64,768]{1,0:T(8,128)(2,1)S(1)}, bf16[64,768]{1,0:T(8,128)(2,1)S(1)}, u32[]{:S(2)}, u32[]{:S(2)}) collective-permute-start(bf16[64,768]{1,0:T(8,128)(2,1)S(1)} %get-tuple-element.114), channel_id=1, source_target_pairs={{0,28},{4,24},{8,20},{12,16},{16,12},{20,8},{24,4},{28,0},{1,29},{... | collective-permute-start | bytes 294920 | tf_op jit(solution)/shard_map/ppermute | solution.py:22
  (36 other events, 515.2 us)

commit v5 on v4

--- a/solution.py
+++ b/solution.py
@@ -50,24 +50,41 @@
     return rows, held, extra
 
 
-def state_kernel(me_ref, doc_ref, decay_ref, k_ref, v_ref, *refs):
-    outs, sum_ref, state_ref = refs[:-2], refs[-2], refs[-1]
-    tokens, heads = decay_ref.shape
+def state_kernel(me_ref, doc_ref, decay_ref, k_hbm, v_hbm, *refs):
+    outs, (sum_ref, sum_rows_ref, doc_out_ref) = refs[:-7], refs[-7:-4]
+    state_ref, k_ref, v_ref, sems = refs[-4:]
+    fetches = [
+        pltpu.make_async_copy(k_hbm, k_ref, sems.at[0]),
+        pltpu.make_async_copy(v_hbm, v_ref, sems.at[1]),
+    ]
+    for fetch in fetches:
+        fetch.start()
+    heads, tokens = decay_ref.shape
     n_seq, hw = len(outs), outs[0].shape[1]
     rows, held, extra = chunk_plan(heads, hw, n_seq)
     doc = doc_ref[...].astype(F32)
     row = lax.broadcasted_iota(jnp.int32, (tokens, tokens), 0)
     col = lax.broadcasted_iota(jnp.int32, (tokens, tokens), 1)
-    sums = jnp.dot(
-        (col <= row).astype(F32), decay_ref[...], precision=HIGHEST, preferred_element_type=F32
+    doc_out_ref[...] = doc
+    sums = lax.dot_general(
+        (col <= row).astype(F32),
+        decay_ref[...],
+        (((1,), (1,)), ((), ())),
+        precision=HIGHEST,
+        preferred_element_type=F32,
     )
     sum_ref[...] = sums
+    sum_rows_ref[...] = jnp.dot(
+        decay_ref[...], (row <= col).astype(F32), precision=HIGHEST, preferred_element_type=F32
+    )
     final = sums[tokens - 1 :, :]
     last = doc[:, tokens - 1 :]
     tail = jnp.exp(final - sums) * (doc_column(doc)[:, :1] == last).astype(F32)
     gain = jnp.exp(final) * (doc[:, :1] == last).astype(F32)
     lane = lax.broadcasted_iota(jnp.int32, (1, heads), 1)
     line = lax.broadcasted_iota(jnp.int32, (extra, hw), 0)
+    for fetch in fetches:
+        fetch.wait()
     for d in reversed(range(n_seq)):
         chunk = me_ref[0] ^ d
         note = jnp.where(line == 2 * held, doc[:, :1], 0.0)
@@ -117,13 +134,22 @@
         outs[d][...] = entered_ref[me_ref[0] ^ d]
 
 
-def inside_kernel(doc_ref, sum_ref, sum_rows_ref, q_ref, k_ref, v_ref, out_ref):
+def inside_kernel(doc_ref, sum_ref, sum_rows_ref, q_hbm, k_hbm, v_hbm, out_ref, *scratch):
+    q_ref, k_ref, v_ref, sems = scratch
+    fetches = [
+        pltpu.make_async_copy(source, target, sems.at[i])
+        for i, (source, target) in enumerate(zip((q_hbm, k_hbm, v_hbm), scratch))
+    ]
+    for fetch in fetches:
+        fetch.start()
     tokens, heads = sum_ref.shape
-    hw = q_ref.shape[1] // heads
-    doc = doc_ref[...].astype(F32)
+    hw = q_hbm.shape[1] // heads
+    doc = doc_ref[...]
     row = lax.broadcasted_iota(jnp.int32, (tokens, tokens), 0)
     col = lax.broadcasted_iota(jnp.int32, (tokens, tokens), 1)
     kept = (col <= row) & (doc_column(doc) == doc)
+    for fetch in fetches:
+        fetch.wait()
     for i in range(heads):
         lanes = slice(i * hw, (i + 1) * hw)
         gap = sum_ref[:, i : i + 1] - sum_rows_ref[i : i + 1, :]
@@ -144,7 +170,7 @@
     for d in range(len(ins)):
         start = pl.multiple_of((me_ref[0] ^ d) * rows, rows)
         carried_ref[pl.ds(start, rows), :] = ins[d][...]
-    doc = doc_ref[...].astype(F32)
+    doc = doc_ref[...]
     reach = jnp.exp(sum_ref[...]) * (doc_column(doc)[:, :1] == doc[:, :1]).astype(F32)
     for i in range(heads):
         lanes = slice(i * hw, (i + 1) * hw)
@@ -152,6 +178,13 @@
         raw = inside_ref[:, lanes] + outside * reach[:, i : i + 1]
         scale = lax.rsqrt(jnp.mean(raw * raw, axis=1, keepdims=True) + EPSILON)
         out_ref[:, lanes] = (raw * scale * gain_ref[:, lanes]).astype(BF16)
+
+
+def pack_kernel(*refs):
+    ins, out_ref = refs[:-1], refs[-1]
+    count = ins[0].shape[0]
+    for k in range(len(ins)):
+        out_ref[k * count : (k + 1) * count, :] = ins[k][...]
 
 
 def route_kernel(me_ref, *refs):
@@ -283,7 +316,7 @@
         out_shape=[struct((nx, count, part), BF16), struct((n_head - nx, count, part), BF16)],
         in_specs=[pl.BlockSpec(memory_space=pltpu.SMEM)]
         + [pl.BlockSpec(memory_space=pltpu.VMEM)] * (n_head + 1)
-        + [pl.BlockSpec(memory_space=pl.ANY)] * 3,
+        + [pl.BlockSpec(memory_space=pltpu.HBM)] * 3,
         scratch_shapes=[
             pltpu.VMEM((count, depth), BF16),
             pltpu.VMEM((count, units), BF16),
@@ -302,14 +335,17 @@
     )(owners, *pieces, norm_gain.reshape(1, depth), gate_weight, up_weight, down_weight)
 
 
-def local_call(kernel, name, out_shape, flops, *operands, scratch=(), scalars=0, vmem=SMALL_VMEM):
+def local_call(
+    kernel, name, out_shape, flops, *operands, scratch=(), scalars=0, far=0, vmem=SMALL_VMEM
+):
     shapes = out_shape if isinstance(out_shape, list) else [out_shape]
     sizes = [math.prod(o.shape) * o.dtype.itemsize for o in [*operands, *shapes]]
     return pl.pallas_call(
         kernel,
         out_shape=out_shape,
         in_specs=[pl.BlockSpec(memory_space=pltpu.SMEM)] * scalars
-        + [pl.BlockSpec(memory_space=pltpu.VMEM)] * (len(operands) - scalars),
+        + [pl.BlockSpec(memory_space=pltpu.VMEM)] * (len(operands) - scalars - far)
+        + [pl.BlockSpec(memory_space=pltpu.HBM)] * far,
         scratch_shapes=list(scratch),
         compiler_params=pltpu.CompilerParams(vmem_limit_bytes=vmem),
         cost_estimate=pl.CostEstimate(flops=flops, bytes_accessed=sum(sizes), transcendentals=0),
@@ -365,7 +401,77 @@
 
     experts = n_seq
     capacity = 4 * tokens // experts
-    residual_there, routing_there = crossed(residual), crossed(routing)
+    me = s.astype(jnp.int32).reshape(1)
+    doc_row = doc_ids.reshape(1, tokens)
+    rows, held, extra = chunk_plan(heads, hw, n_seq)
+    work = 2 * tokens * hw * hw * heads
+    whole = pltpu.VMEM((tokens, heads * hw), BF16)
+    *payload, decay_sum, decay_rows, doc_float = local_call(
+        state_kernel,
+        "block_state",
+        [struct((rows + extra, hw), BF16)] * n_seq
+        + [struct((tokens, heads), F32), struct((heads, tokens), F32), struct((1, tokens), F32)],
+        work,
+        me,
+        doc_row,
+        log_decay.T,
+        key_vectors,
+        value_vectors,
+        scratch=[pltpu.VMEM((hw, hw), F32), whole, whole, pltpu.SemaphoreType.DMA((2,))],
+        scalars=1,
+        far=2,
+    )
+    entered = local_call(
+        scan_kernel,
+        "carry",
+        [struct((rows, hw), BF16)] * n_seq,
+        work,
+        me,
+        *swap_seq(payload),
+        scratch=[
+            pltpu.VMEM((n_seq, rows + extra, hw), BF16),
+            pltpu.VMEM((n_seq, rows, hw), BF16),
+        ],
+        scalars=1,
+    )
+    carried = swap_seq(entered)
+    inside = local_call(
+        inside_kernel,
+        "inside",
+        struct((tokens, heads * hw), F32),
+        2 * work,
+        doc_float,
+        decay_sum,
+        decay_rows,
+        queries,
+        key_vectors,
+        value_vectors,
+        scratch=[whole, whole, whole, pltpu.SemaphoreType.DMA((3,))],
+        far=3,
+    )
+    attended = local_call(
+        outside_kernel,
+        "outside",
+        struct((tokens, heads * hw), BF16),
+        work,
+        me,
+        doc_float,
+        decay_sum,
+        queries,
+        inside,
+        head_gain.reshape(1, heads * hw),
+        *carried,
+        scratch=[pltpu.VMEM((heads * hw, hw), BF16)],
+        scalars=1,
+    )
+
+    lanes = max(128, routing.shape[1])
+    ids = jnp.pad(routing.astype(BF16), ((0, 0), (0, lanes - routing.shape[1])))
+    there = jnp.concatenate([residual, ids], axis=1)
+    attended, output_weight, there = lax.optimization_barrier((attended, output_weight, there))
+    there = crossed(there)
+    residual_there = there[:, :part]
+    routing_there = there[:, part : part + routing.shape[1]].astype(jnp.int32)
     slot = jnp.arange(experts * capacity, dtype=jnp.int32)
     slot = (slot // capacity ^ s) * capacity + slot % capacity
     place = slot_places(routing_there, experts, capacity)
@@ -373,69 +479,6 @@
     place = slot_places(routing, experts, capacity)
     here = place[:, None, :] == slot[None, :, None]
     mix = jnp.sum(jnp.where(here, route_weights[:, None, :], 0.0), axis=2)
-
-    me = s.astype(jnp.int32).reshape(1)
-    doc_row = doc_ids.reshape(1, tokens)
-    rows, held, extra = chunk_plan(heads, hw, n_seq)
-    work = 2 * tokens * hw * hw * heads
-    *payload, decay_sum = local_call(
-        state_kernel,
-        "block_state",
-        [struct((rows + extra, hw), BF16)] * n_seq + [struct((tokens, heads), F32)],
-        work,
-        me,
-        doc_row,
-        log_decay,
-        key_vectors,
-        value_vectors,
-        scratch=[pltpu.VMEM((hw, hw), F32)],
-        scalars=1,
-    )
-    inside = local_call(
-        inside_kernel,
-        "inside",
-        struct((tokens, heads * hw), F32),
-        2 * work,
-        doc_row,
-        decay_sum,
-        decay_sum.T,
-        queries,
-        key_vectors,
-        value_vectors,
-    )
-    arrived, inside, residual_there, take = lax.optimization_barrier(
-        (swap_seq(payload), inside, residual_there, take)
-    )
-    entered = local_call(
-        scan_kernel,
-        "carry",
-        [struct((rows, hw), BF16)] * n_seq,
-        work,
-        me,
-        *arrived,
-        scratch=[
-            pltpu.VMEM((n_seq, rows + extra, hw), BF16),
-            pltpu.VMEM((n_seq, rows, hw), BF16),
-        ],
-        scalars=1,
-    )
-    carried = swap_seq(entered)
-    attended = local_call(
-        outside_kernel,
-        "outside",
-        struct((tokens, heads * hw), BF16),
-        work,
-        me,
-        doc_row,
-        decay_sum,
-        queries,
-        inside,
-        head_gain.reshape(1, heads * hw),
-        *carried,
-        scratch=[pltpu.VMEM((heads * hw, hw), BF16)],
-        scalars=1,
-    )
-    attended, output_weight = lax.optimization_barrier((attended, output_weight))
 
     cols = output_weight.shape[1]
     w_z = jnp.zeros((output_weight.shape[0], ny * cols), BF16)
@@ -452,6 +495,7 @@
                 attended, lambda q, k=k: (q // ny - k) % nz * ny + q % ny
             )
         products.append(jnp.dot(rows_k, w_z, preferred_element_type=F32).astype(BF16))
+    products, take, mix = lax.optimization_barrier((products, take, mix))
     block = struct((tokens, part), BF16)
     place_me = jnp.stack([z, h]).astype(jnp.int32)
     own, *sent = local_call(
@@ -477,8 +521,6 @@
         *sums,
     )
 
-    arrived = swap_seq(outgoing)
-    middle = crossed(middle_there)
     in_owner = [h] + [(h + m * CORES) % n_head for m in range(1, nx)]
     in_owner += [
         o // CORES * CORES + (o % CORES + m) % CORES for o in in_owner for m in range(1, CORES)
@@ -489,27 +531,41 @@
     owners = jnp.stack(in_owner + out_owner + [z]).astype(jnp.int32)
     count = n_head * capacity
     returning = [None] * experts
+    arrived, sent, crossing = None, None, None
     for group in range(ny):
-        got = jnp.concatenate([arrived[k * ny + group] for k in range(nz)])
-        pieces = [got]
-        for m in range(1, nx):
-            pieces.append(permute_head(got, lambda q, m=m: (q - m * CORES) % n_head))
-        for piece in list(pieces):
+        sends = [outgoing[k * ny + group] for k in range(nz)]
+        if group:
+            sends = lax.optimization_barrier((sends, arrived))[0]
+        arrived = [
+            permute_seq(sends[k], lambda q, d=k * ny + group: q ^ d) if k + group else sends[k]
+            for k in range(nz)
+        ]
+        got = local_call(
+            pack_kernel, "pack", struct((nz * capacity, part), BF16), count * part, *arrived
+        )
+        far = [permute_head(got, lambda q, m=m: (q - m * CORES) % n_head) for m in range(1, nx)]
+        if group:
+            far = lax.optimization_barrier((far, sent))[0]
+        pieces = [got, *far]
+        for piece in [got, *far]:
             for m in range(1, CORES):
                 pieces.append(
                     permute_head(
                         piece, lambda q, m=m: q // CORES * CORES + (q % CORES - m) % CORES
                     )
                 )
+        if group:
+            pieces = lax.optimization_barrier((pieces, crossing))[0]
         sent, kept = expert_call(owners, pieces, norm_gain, gate_weight, up_weight, down_weight)
+        if group == 0:
+            middle = crossed(lax.optimization_barrier((middle_there, sent))[0])
 
         near = permute_head(sent, lambda q: q // CORES * CORES + (q % CORES + 1) % CORES)
         near_sum = kept.astype(F32) + near.astype(F32)
+        crossing = [near_sum[m].astype(BF16) for m in range(1, nx)]
         parts = [near_sum[0]]
         for m in range(1, nx):
-            parts.append(
-                permute_head(near_sum[m].astype(BF16), lambda q, m=m: (q + m * CORES) % n_head)
-            )
+            parts.append(permute_head(crossing[m - 1], lambda q, m=m: (q + m * CORES) % n_head))
         blocks = local_call(
             functools.partial(sum_kernel, nz),
             "total",
@@ -520,6 +576,8 @@
             scratch=[pltpu.VMEM((count, part), BF16)],
             scalars=1,
         )
+        if group == ny - 1:
+            blocks, middle = lax.optimization_barrier((blocks, middle))
         for k in range(nz):
             returning[k * ny + group] = blocks[k]
     return local_call(

time: 237 us -> 253 us (1.068)
  matrix products: 2.8 us -> 10.8 us
  starting transfers between devices: 86.3 us -> 92.2 us
    ppermute x13, starting transfers between devices: 19.4 us -> 37.5 us  [permute_head(): lax.ppermute(value, 'head', [(source, move(source)) for source in range(c...]
    ppermute x32, starting transfers between devices: 64.2 us -> 52.5 us  [permute_seq(): lax.ppermute(value, 'seq', [(source, move(source)) for source in range(co...]
    ppermute x13, waiting for transfers between devices: 34.9 us -> 43.8 us  [permute_head(): lax.ppermute(value, 'head', [(source, move(source)) for source in range(c...]
    dot_general x4, matrix products: 2.4 us -> 10.4 us  [shards(): jnp.dot(rows_k, w_z, preferred_element_type=F32).astype(BF16)]
    ppermute x32, waiting for transfers between devices: 58.7 us -> 51.9 us  [permute_seq(): lax.ppermute(value, 'seq', [(source, move(source)) for source in range(co...]
    unnamed x48 -> x57, local copies, waits for them, and re-layouts: 13.4 us -> 11.1 us
    pallas_call x9 -> x11, Pallas kernels: 7.95 us -> 8.29 us  [local_call(): pl.pallas_call(kernel, out_shape=out_shape, in_specs=[pl.BlockSpec(memory...]
  transfers between devices with their start and end apart: 48 -> 47, of which waited for: 11 -> 20; matrix products, arithmetic and copies ran while one was open for 4% -> 7% of each run, Pallas kernels for 12% -> 1%
where the time goes in v5:
time: 253 us; the launch traced here: 252 us
  waiting for transfers between devices  95.7 us (38%)
  starting transfers between devices  92.2 us (36%)
  Pallas kernels  32.4 us (13%)
  local copies, waits for them, and re-layouts  18.5 us (7%)
  matrix products  10.8 us (4%)
    ppermute x32, starting transfers between devices, permute_seq(): lax.ppermute(value, 'seq', [(source, move(source)) for source in range(co...  52.5 us
    ppermute x32, waiting for transfers between devices, permute_seq(): lax.ppermute(value, 'seq', [(source, move(source)) for source in range(co...  51.9 us
    ppermute x13, waiting for transfers between devices, permute_head(): lax.ppermute(value, 'head', [(source, move(source)) for source in range(c...  43.8 us
    ppermute x13, starting transfers between devices, permute_head(): lax.ppermute(value, 'head', [(source, move(source)) for source in range(c...  37.5 us
    pallas_call x2, Pallas kernels, expert_call(): pl.pallas_call(functools.partial(expert_kernel, n_head, aligned), out_sha...  24.1 us
    unnamed x57, local copies, waits for them, and re-layouts  11.1 us
    dot_general x4, matrix products, shards(): jnp.dot(rows_k, w_z, preferred_element_type=F32).astype(BF16)  10.4 us
    pallas_call x11, Pallas kernels, local_call(): pl.pallas_call(kernel, out_shape=out_shape, in_specs=[pl.BlockSpec(memory...  8.29 us
  transfers between devices with their start and end apart: 47, of which 20 were waited for; matrix products, arithmetic and copies ran while one was open for 7% of the time, Pallas kernels for 1%

profile of v5, /device:TPU:0, one launch (start us, length us, event | category | flops | bytes accessed | tf_op | source)
XLA Modules:
  0.0 252.3 jit_solution(167580414946673029)
XLA Ops:
  4.5 3.0 %collective-permute-start = (bf16[272,128]{1,0:T(8,128)(2,1)S(1)}, bf16[272,128]{1,0:T(8,128)(2,1)S(1)}, u32[]{:S(2)}, u32[]{:S(2)}) collective-permute-start(bf16[272,128]{1,0:T(8,128)(2,1)S(1)} %get-tuple-element.77), channel_id=1, source_target_pairs={{0,4},{4,0},{8,12},{12,8},{16,20},{20,16},{24,28},{28,24},{1,5},{5... | collective-permute-start | bytes 208904 | tf_op jit(solution)/shard_map/ppermute | solution.py:22
  9.1 3.0 %collective-permute-start.3 = (bf16[272,128]{1,0:T(8,128)(2,1)S(1)}, bf16[272,128]{1,0:T(8,128)(2,1)S(1)}, u32[]{:S(2)}, u32[]{:S(2)}) collective-permute-start(bf16[272,128]{1,0:T(8,128)(2,1)S(1)} %get-tuple-element.80), channel_id=1, source_target_pairs={{0,16},{4,20},{8,24},{12,28},{16,0},{20,4},{24,8},{28,12},{1,17},{... | collective-permute-start | bytes 208904 | tf_op jit(solution)/shard_map/ppermute | solution.py:22
  13.4 3.6 %collective-permute-start.5 = (bf16[272,128]{1,0:T(8,128)(2,1)S(1)}, bf16[272,128]{1,0:T(8,128)(2,1)S(1)}, u32[]{:S(2)}, u32[]{:S(2)}) collective-permute-start(bf16[272,128]{1,0:T(8,128)(2,1)S(1)} %get-tuple-element.82), channel_id=1, source_target_pairs={{0,24},{4,28},{8,16},{12,20},{16,8},{20,12},{24,0},{28,4},{1,25},{... | collective-permute-start | bytes 208904 | tf_op jit(solution)/shard_map/ppermute | solution.py:22
  17.0 5.8 %collective-permute-done.4.refs_5_ = bf16[272,128]{1,0:T(8,128)(2,1)S(1)} collective-permute-done((bf16[272,128]{1,0:T(8,128)(2,1)S(1)}, bf16[272,128]{1,0:T(8,128)(2,1)S(1)}, u32[]{:S(2)}, u32[]{:S(2)}) %collective-permute-start.4) | collective-permute-done | bytes 69664 | tf_op jit(solution)/shard_map/ppermute | solution.py:22
  24.3 3.5 %collective-permute-start.10 = (bf16[256,128]{1,0:T(8,128)(2,1)S(1)}, bf16[256,128]{1,0:T(8,128)(2,1)S(1)}, u32[]{:S(2)}, u32[]{:S(2)}) collective-permute-start(bf16[256,128]{1,0:T(8,128)(2,1)S(1)} %get-tuple-element.88), channel_id=1, source_target_pairs={{0,16},{4,20},{8,24},{12,28},{16,0},{20,4},{24,8},{28,12},{1,17},{... | collective-permute-start | bytes 196616 | tf_op jit(solution)/shard_map/ppermute | solution.py:22
  32.8 2.8 %inside.1.inside_ref = f32[128,2048]{1,0:T(8,128)S(1)} custom-call(f32[1,128]{1,0:T(1,128)S(1)} %get-tuple-element.73.doc_ref, f32[128,16]{1,0:T(8,128)S(1)} %get-tuple-element.74.sum_ref, f32[16,128]{1,0:T(8,128)S(1)} %get-tuple-element.75.sum_rows_ref, bf16[128,2048]{1,0:T(8,128)(2,1)S(1)} %copy-done.5, bf16[128,2048]{1,0:T(8,128)(2,1)S(1)} %copy-done.2, ...), custom_call_target="tpu_custom_call" | custom-call | flops 134217728 | bytes 2638336 | tf_op jit(solution)/shard_map/inside/pallas_call | solution.py:343
  37.2 3.2 %collective-permute-start.13 = (bf16[256,128]{1,0:T(8,128)(2,1)S(1)}, bf16[256,128]{1,0:T(8,128)(2,1)S(1)}, u32[]{:S(2)}, u32[]{:S(2)}) collective-permute-start(bf16[256,128]{1,0:T(8,128)(2,1)S(1)} %get-tuple-element.91), channel_id=1, source_target_pairs={{0,28},{4,24},{8,20},{12,16},{16,12},{20,8},{24,4},{28,0},{1,29},{... | collective-permute-start | bytes 196616 | tf_op jit(solution)/shard_map/ppermute | solution.py:22
  41.2 2.8 %collective-permute-start.9 = (bf16[256,128]{1,0:T(8,128)(2,1)S(1)}, bf16[256,128]{1,0:T(8,128)(2,1)S(1)}, u32[]{:S(2)}, u32[]{:S(2)}) collective-permute-start(bf16[256,128]{1,0:T(8,128)(2,1)S(1)} %get-tuple-element.87), channel_id=1, source_target_pairs={{0,12},{4,8},{8,4},{12,0},{16,28},{20,24},{24,20},{28,16},{1,13},{... | collective-permute-start | bytes 196616 | tf_op jit(solution)/shard_map/ppermute | solution.py:22
  60.9 22.4 %collective-permute-done.15 = bf16[2048,384]{1,0:T(8,128)(2,1)} collective-permute-done((bf16[2048,384]{1,0:T(8,128)(2,1)S(1)}, bf16[2048,384]{1,0:T(8,128)(2,1)}, u32[]{:S(2)}, u32[]{:S(2)}) %collective-permute-start.15) | collective-permute-done | bytes 1572896 | tf_op jit(solution)/shard_map/ppermute | solution.py:22
  83.2 2.8 %constant_dynamic-update-slice_fusion = bf16[2048,768]{1,0:T(8,128)(2,1)} fusion(bf16[2048,768]{1,0:T(8,128)(2,1)} %constant_dynamic-update-slice_fusion.1, bf16[2048,384]{1,0:T(8,128)(2,1)} %collective-permute-done.15, s32[]{:T(128)S(6)} %select_n.109), kind=kLoop, calls=%fused_computation.45 | loop fusion | bytes 3145732 | tf_op jit(solution)/shard_map/dynamic_update_slice | solution.py:488
  86.0 2.5 convolution_convert_fusion.3.refs_0_
  88.5 2.6 %convolution_convert_fusion.refs_3_ = bf16[128,768]{1,0:T(8,128)(2,1)S(1)} fusion(bf16[128,2048]{1,0:T(8,128)(2,1)} %collective-permute-done.18, bf16[2048,768]{1,0:T(8,128)(2,1)} %constant_dynamic-update-slice_fusion), kind=kOutput, calls=%fused_computation.2 | convolution fusion | flops 402751488 | bytes 3866624 | tf_op jit(solution)/shard_map/dot_general | solution.py:497
  91.2 2.5 convolution_convert_fusion.1.refs_2_
  93.7 2.8 %convolution_convert_fusion.2.refs_1_ = bf16[128,768]{1,0:T(8,128)(2,1)S(1)} fusion(bf16[128,2048]{1,0:T(8,128)(2,1)} %collective-permute-done.16, bf16[2048,768]{1,0:T(8,128)(2,1)} %constant_dynamic-update-slice_fusion), kind=kOutput, calls=%fused_computation.4 | convolution fusion | flops 402751488 | bytes 3866624 | tf_op jit(solution)/shard_map/dot_general | solution.py:497
  97.1 6.4 %collective-permute-start.19 = (bf16[128,768]{1,0:T(8,128)(2,1)S(1)}, bf16[128,768]{1,0:T(8,128)(2,1)S(1)}, u32[]{:S(2)}, u32[]{:S(2)}) collective-permute-start(bf16[128,768]{1,0:T(8,128)(2,1)S(1)} %get-tuple-element.101), channel_id=1, source_target_pairs={{0,1},{1,2},{2,3},{3,0},{4,5},{5,6},{6,7},{7,4},{8,9},{9,10},{10,1... | collective-permute-start | bytes 589832 | tf_op jit(solution)/shard_map/ppermute | solution.py:27
  103.6 20.6 %collective-permute-start.20 = (bf16[128,768]{1,0:T(8,128)(2,1)S(1)}, bf16[128,768]{1,0:T(8,128)(2,1)S(1)}, u32[]{:S(2)}, u32[]{:S(2)}) collective-permute-start(bf16[128,768]{1,0:T(8,128)(2,1)S(1)} %get-tuple-element.102), channel_id=1, source_target_pairs={{0,2},{1,3},{2,0},{3,1},{4,6},{5,7},{6,4},{7,5},{8,10},{9,11},{10,... | collective-permute-start | bytes 589832 | tf_op jit(solution)/shard_map/ppermute | solution.py:27
  125.6 3.8 %collective-permute-done.20.refs_2_ = bf16[128,768]{1,0:T(8,128)(2,1)S(1)} collective-permute-done((bf16[128,768]{1,0:T(8,128)(2,1)S(1)}, bf16[128,768]{1,0:T(8,128)(2,1)S(1)}, u32[]{:S(2)}, u32[]{:S(2)}) %collective-permute-start.20) | collective-permute-done | bytes 196640 | tf_op jit(solution)/shard_map/ppermute | solution.py:27
  129.5 3.6 %collective-permute-done.21.refs_3_ = bf16[128,768]{1,0:T(8,128)(2,1)S(1)} collective-permute-done((bf16[128,768]{1,0:T(8,128)(2,1)S(1)}, bf16[128,768]{1,0:T(8,128)(2,1)S(1)}, u32[]{:S(2)}, u32[]{:S(2)}) %collective-permute-start.21) | collective-permute-done | bytes 196640 | tf_op jit(solution)/shard_map/ppermute | solution.py:27
  134.7 3.9 %collective-permute-start.24 = (bf16[64,768]{1,0:T(8,128)(2,1)S(1)}, bf16[64,768]{1,0:T(8,128)(2,1)S(1)}, u32[]{:S(2)}, u32[]{:S(2)}) collective-permute-start(bf16[64,768]{1,0:T(8,128)(2,1)S(1)} %get-tuple-element.111), channel_id=1, source_target_pairs={{0,24},{4,28},{8,16},{12,20},{16,8},{20,12},{24,0},{28,4},{1,25},{... | collective-permute-start | bytes 294920 | tf_op jit(solution)/shard_map/ppermute | solution.py:22
  139.5 5.3 %collective-permute-done.23.refs_2_ = bf16[64,768]{1,0:T(8,128)(2,1)S(1)} collective-permute-done((bf16[64,768]{1,0:T(8,128)(2,1)S(1)}, bf16[64,768]{1,0:T(8,128)(2,1)S(1)}, u32[]{:S(2)}, u32[]{:S(2)}) %collective-permute-start.23) | collective-permute-done | bytes 98336 | tf_op jit(solution)/shard_map/ppermute | solution.py:22
  145.1 9.7 %collective-permute-done.30.refs_1_ = bf16[256,768]{1,0:T(8,128)(2,1)} collective-permute-done((bf16[256,768]{1,0:T(8,128)(2,1)S(1)}, bf16[256,768]{1,0:T(8,128)(2,1)}, u32[]{:S(2)}, u32[]{:S(2)}) %collective-permute-start.30) | collective-permute-done | bytes 393248 | tf_op jit(solution)/shard_map/ppermute | solution.py:27
  156.9 3.0 %copy-done = bf16[1,3072,1152]{2,1,0:T(8,128)(2,1)S(1)} copy-done((bf16[1,3072,1152]{2,1,0:T(8,128)(2,1)S(1)}, bf16[1,3072,1152]{2,1,0:T(8,128)(2,1)}, u32[]{:S(2)}) %copy-start) | copy-done | bytes 7077912
  159.9 12.5 %expert.2 = (bf16[2,256,768]{2,1,0:T(8,128)(2,1)S(1)}, bf16[2,256,768]{2,1,0:T(8,128)(2,1)S(1)}) custom-call(s32[9]{0:T(128)S(1)} %stack.41.owner_ref, bf16[256,768]{1,0:T(8,128)(2,1)S(1)} %pack.3.refs_0_, bf16[256,768]{1,0:T(8,128)(2,1)} %collective-permute-done.30.refs_1_, bf16[256,768]{1,0:T(8,128)(2,1)} %collective-permute-done.31.refs_2_, ...), custom_call_target="tpu_custom_call" | custom-call | flops 5435817984 | bytes 24379392 | tf_op jit(solution)/shard_map/expert/pallas_call | solution.py:314
  173.5 2.3 collective-permute-start.26
  179.8 7.3 %collective-permute-done.27.refs_2_ = bf16[64,768]{1,0:T(8,128)(2,1)S(1)} collective-permute-done((bf16[64,768]{1,0:T(8,128)(2,1)S(1)}, bf16[64,768]{1,0:T(8,128)(2,1)S(1)}, u32[]{:S(2)}, u32[]{:S(2)}) %collective-permute-start.27) | collective-permute-done | bytes 98336 | tf_op jit(solution)/shard_map/ppermute | solution.py:22
  188.6 8.3 %collective-permute-done.29.refs_1_ = bf16[256,768]{1,0:T(8,128)(2,1)S(1)} collective-permute-done((bf16[256,768]{1,0:T(8,128)(2,1)S(1)}, bf16[256,768]{1,0:T(8,128)(2,1)S(1)}, u32[]{:S(2)}, u32[]{:S(2)}) %collective-permute-start.29) | collective-permute-done | bytes 393248 | tf_op jit(solution)/shard_map/ppermute | solution.py:27
  198.6 11.5 %expert.3 = (bf16[2,256,768]{2,1,0:T(8,128)(2,1)S(1)}, bf16[2,256,768]{2,1,0:T(8,128)(2,1)S(1)}) custom-call(s32[9]{0:T(128)S(1)} %stack.41.owner_ref, bf16[256,768]{1,0:T(8,128)(2,1)S(1)} %pack.2.refs_0_, bf16[256,768]{1,0:T(8,128)(2,1)S(1)} %collective-permute-done.29.refs_1_, bf16[256,768]{1,0:T(8,128)(2,1)S(1)} %collective-permute-done.33.refs_2_, ...), custom_call_target="tpu_custom_call" | custom-call | flops 5435817984 | bytes 24379392 | tf_op jit(solution)/shard_map/expert/pallas_call | solution.py:314
  211.0 6.9 %collective-permute-start.39 = (bf16[256,768]{1,0:T(8,128)(2,1)S(1)}, bf16[256,768]{1,0:T(8,128)(2,1)S(1)}, u32[]{:S(2)}, u32[]{:S(2)}) collective-permute-start(bf16[256,768]{1,0:T(8,128)(2,1)S(1)} %fusion.3), channel_id=1, source_target_pairs={{0,2},{1,3},{2,0},{3,1},{4,6},{5,7},{6,4},{7,5},{8,10},{9,11},{10,... | collective-permute-start | bytes 1179656 | tf_op jit(solution)/shard_map/ppermute | solution.py:27
  218.2 11.8 %collective-permute-done.39.refs_1_ = bf16[256,768]{1,0:T(8,128)(2,1)S(1)} collective-permute-done((bf16[256,768]{1,0:T(8,128)(2,1)S(1)}, bf16[256,768]{1,0:T(8,128)(2,1)S(1)}, u32[]{:S(2)}, u32[]{:S(2)}) %collective-permute-start.39) | collective-permute-done | bytes 393248 | tf_op jit(solution)/shard_map/ppermute | solution.py:27
  234.7 3.2 %collective-permute-done.37.refs_1_ = bf16[256,768]{1,0:T(8,128)(2,1)S(1)} collective-permute-done((bf16[256,768]{1,0:T(8,128)(2,1)S(1)}, bf16[256,768]{1,0:T(8,128)(2,1)S(1)}, u32[]{:S(2)}, u32[]{:S(2)}) %collective-permute-start.37) | collective-permute-done | bytes 393248 | tf_op jit(solution)/shard_map/ppermute | solution.py:27
  240.2 3.2 %collective-permute-start.44 = (bf16[64,768]{1,0:T(8,128)(2,1)S(1)}, bf16[64,768]{1,0:T(8,128)(2,1)S(1)}, u32[]{:S(2)}, u32[]{:S(2)}) collective-permute-start(bf16[64,768]{1,0:T(8,128)(2,1)S(1)} %get-tuple-element.138), channel_id=1, source_target_pairs={{0,20},{4,16},{8,28},{12,24},{16,4},{20,0},{24,12},{28,8},{1,21},{... | collective-permute-start | bytes 294920 | tf_op jit(solution)/shard_map/ppermute | solution.py:22
  246.3 4.9 %collective-permute-done.44.refs_5_ = bf16[64,768]{1,0:T(8,128)(2,1)S(1)} collective-permute-done((bf16[64,768]{1,0:T(8,128)(2,1)S(1)}, bf16[64,768]{1,0:T(8,128)(2,1)S(1)}, u32[]{:S(2)}, u32[]{:S(2)}) %collective-permute-start.44) | collective-permute-done | bytes 98336 | tf_op jit(solution)/shard_map/ppermute | solution.py:22
  (171 shorter events, 60.1 us)
Async XLA Ops:
  4.5 8.9 %collective-permute-start = (bf16[272,128]{1,0:T(8,128)(2,1)S(1)}, bf16[272,128]{1,0:T(8,128)(2,1)S(1)}, u32[]{:S(2)}, u32[]{:S(2)}) collective-permute-start(bf16[272,128]{1,0:T(8,128)(2,1)S(1)} %get-tuple-element.77), channel_id=1, source_target_pairs={{0,4},{4,0},{8,12},{12,8},{16,20},{20,16},{24,28},{28,24},{1,5},{5... | collective-permute-start | bytes 208904 | tf_op jit(solution)/shard_map/ppermute | solution.py:22
  7.5 9.5 %collective-permute-start.1 = (bf16[272,128]{1,0:T(8,128)(2,1)S(1)}, bf16[272,128]{1,0:T(8,128)(2,1)S(1)}, u32[]{:S(2)}, u32[]{:S(2)}) collective-permute-start(bf16[272,128]{1,0:T(8,128)(2,1)S(1)} %get-tuple-element.78), channel_id=1, source_target_pairs={{0,8},{4,12},{8,0},{12,4},{16,24},{20,28},{24,16},{28,20},{1,9},{5... | collective-permute-start | bytes 208904 | tf_op jit(solution)/shard_map/ppermute | solution.py:22
  9.1 7.9 %collective-permute-start.2 = (bf16[272,128]{1,0:T(8,128)(2,1)S(1)}, bf16[272,128]{1,0:T(8,128)(2,1)S(1)}, u32[]{:S(2)}, u32[]{:S(2)}) collective-permute-start(bf16[272,128]{1,0:T(8,128)(2,1)S(1)} %get-tuple-element.79), channel_id=1, source_target_pairs={{0,12},{4,8},{8,4},{12,0},{16,28},{20,24},{24,20},{28,16},{1,13},{... | collective-permute-start | bytes 208904 | tf_op jit(solution)/shard_map/ppermute | solution.py:22
  12.1 10.7 %collective-permute-start.4 = (bf16[272,128]{1,0:T(8,128)(2,1)S(1)}, bf16[272,128]{1,0:T(8,128)(2,1)S(1)}, u32[]{:S(2)}, u32[]{:S(2)}) collective-permute-start(bf16[272,128]{1,0:T(8,128)(2,1)S(1)} %get-tuple-element.81), channel_id=1, source_target_pairs={{0,20},{4,16},{8,28},{12,24},{16,4},{20,0},{24,12},{28,8},{1,21},{... | collective-permute-start | bytes 208904 | tf_op jit(solution)/shard_map/ppermute | solution.py:22
  13.4 9.4 %collective-permute-start.5 = (bf16[272,128]{1,0:T(8,128)(2,1)S(1)}, bf16[272,128]{1,0:T(8,128)(2,1)S(1)}, u32[]{:S(2)}, u32[]{:S(2)}) collective-permute-start(bf16[272,128]{1,0:T(8,128)(2,1)S(1)} %get-tuple-element.82), channel_id=1, source_target_pairs={{0,24},{4,28},{8,16},{12,20},{16,8},{20,12},{24,0},{28,4},{1,25},{... | collective-permute-start | bytes 208904 | tf_op jit(solution)/shard_map/ppermute | solution.py:22
  24.3 16.7 %collective-permute-start.10 = (bf16[256,128]{1,0:T(8,128)(2,1)S(1)}, bf16[256,128]{1,0:T(8,128)(2,1)S(1)}, u32[]{:S(2)}, u32[]{:S(2)}) collective-permute-start(bf16[256,128]{1,0:T(8,128)(2,1)S(1)} %get-tuple-element.88), channel_id=1, source_target_pairs={{0,16},{4,20},{8,24},{12,28},{16,0},{20,4},{24,8},{28,12},{1,17},{... | collective-permute-start | bytes 196616 | tf_op jit(solution)/shard_map/ppermute | solution.py:22
  27.8 13.4 %collective-permute-start.11 = (bf16[256,128]{1,0:T(8,128)(2,1)S(1)}, bf16[256,128]{1,0:T(8,128)(2,1)S(1)}, u32[]{:S(2)}, u32[]{:S(2)}) collective-permute-start(bf16[256,128]{1,0:T(8,128)(2,1)S(1)} %get-tuple-element.89), channel_id=1, source_target_pairs={{0,20},{4,16},{8,28},{12,24},{16,4},{20,0},{24,12},{28,8},{1,21},{... | collective-permute-start | bytes 196616 | tf_op jit(solution)/shard_map/ppermute | solution.py:22
  35.6 9.0 %collective-permute-start.12 = (bf16[256,128]{1,0:T(8,128)(2,1)S(1)}, bf16[256,128]{1,0:T(8,128)(2,1)S(1)}, u32[]{:S(2)}, u32[]{:S(2)}) collective-permute-start(bf16[256,128]{1,0:T(8,128)(2,1)S(1)} %get-tuple-element.90), channel_id=1, source_target_pairs={{0,24},{4,28},{8,16},{12,20},{16,8},{20,12},{24,0},{28,4},{1,25},{... | collective-permute-start | bytes 196616 | tf_op jit(solution)/shard_map/ppermute | solution.py:22
  48.6 34.6 %collective-permute-start.15 = (bf16[2048,384]{1,0:T(8,128)(2,1)S(1)}, bf16[2048,384]{1,0:T(8,128)(2,1)}, u32[]{:S(2)}, u32[]{:S(2)}) collective-permute-start(bf16[2048,384]{1,0:T(8,128)(2,1)S(1)} %copy-done.21), channel_id=1, source_target_pairs={{0,4},{4,0},{8,12},{12,8},{16,20},{20,16},{24,28},{28,24},{1,5},{5... | collective-permute-start | bytes 4718600 | tf_op jit(solution)/shard_map/ppermute | solution.py:22
  50.3 38.1 %collective-permute-start.18 = (bf16[128,2048]{1,0:T(8,128)(2,1)S(1)}, bf16[128,2048]{1,0:T(8,128)(2,1)}, u32[]{:S(2)}, u32[]{:S(2)}) collective-permute-start(bf16[128,2048]{1,0:T(8,128)(2,1)S(1)} %outside.1), channel_id=1, source_target_pairs={{0,8},{4,12},{8,16},{12,20},{16,24},{20,28},{24,0},{28,4},{1,9},{5... | collective-permute-start | bytes 1572872 | tf_op jit(solution)/shard_map/ppermute | solution.py:22
  52.4 38.8 %collective-permute-start.17 = (bf16[128,2048]{1,0:T(8,128)(2,1)S(1)}, bf16[128,2048]{1,0:T(8,128)(2,1)S(1)}, u32[]{:S(2)}, u32[]{:S(2)}) collective-permute-start(bf16[128,2048]{1,0:T(8,128)(2,1)S(1)} %outside.1), channel_id=1, source_target_pairs={{0,16},{4,20},{8,24},{12,28},{16,0},{20,4},{24,8},{28,12},{1,17},{... | collective-permute-start | bytes 1572872 | tf_op jit(solution)/shard_map/ppermute | solution.py:22
  53.4 40.3 %collective-permute-start.16 = (bf16[128,2048]{1,0:T(8,128)(2,1)S(1)}, bf16[128,2048]{1,0:T(8,128)(2,1)}, u32[]{:S(2)}, u32[]{:S(2)}) collective-permute-start(bf16[128,2048]{1,0:T(8,128)(2,1)S(1)} %outside.1), channel_id=1, source_target_pairs={{0,24},{4,28},{8,0},{12,4},{16,8},{20,12},{24,16},{28,20},{1,25},{... | collective-permute-start | bytes 1572872 | tf_op jit(solution)/shard_map/ppermute | solution.py:22
  97.1 28.5 %collective-permute-start.19 = (bf16[128,768]{1,0:T(8,128)(2,1)S(1)}, bf16[128,768]{1,0:T(8,128)(2,1)S(1)}, u32[]{:S(2)}, u32[]{:S(2)}) collective-permute-start(bf16[128,768]{1,0:T(8,128)(2,1)S(1)} %get-tuple-element.101), channel_id=1, source_target_pairs={{0,1},{1,2},{2,3},{3,0},{4,5},{5,6},{6,7},{7,4},{8,9},{9,10},{10,1... | collective-permute-start | bytes 589832 | tf_op jit(solution)/shard_map/ppermute | solution.py:27
  103.6 25.9 %collective-permute-start.20 = (bf16[128,768]{1,0:T(8,128)(2,1)S(1)}, bf16[128,768]{1,0:T(8,128)(2,1)S(1)}, u32[]{:S(2)}, u32[]{:S(2)}) collective-permute-start(bf16[128,768]{1,0:T(8,128)(2,1)S(1)} %get-tuple-element.102), channel_id=1, source_target_pairs={{0,2},{1,3},{2,0},{3,1},{4,6},{5,7},{6,4},{7,5},{8,10},{9,11},{10,... | collective-permute-start | bytes 589832 | tf_op jit(solution)/shard_map/ppermute | solution.py:27
  124.2 8.9 %collective-permute-start.21 = (bf16[128,768]{1,0:T(8,128)(2,1)S(1)}, bf16[128,768]{1,0:T(8,128)(2,1)S(1)}, u32[]{:S(2)}, u32[]{:S(2)}) collective-permute-start(bf16[128,768]{1,0:T(8,128)(2,1)S(1)} %get-tuple-element.103), channel_id=1, source_target_pairs={{0,3},{1,0},{2,1},{3,2},{4,7},{5,4},{6,5},{7,6},{8,11},{9,8},{10,9... | collective-permute-start | bytes 589832 | tf_op jit(solution)/shard_map/ppermute | solution.py:27
  134.7 10.1 %collective-permute-start.23 = (bf16[64,768]{1,0:T(8,128)(2,1)S(1)}, bf16[64,768]{1,0:T(8,128)(2,1)S(1)}, u32[]{:S(2)}, u32[]{:S(2)}) collective-permute-start(bf16[64,768]{1,0:T(8,128)(2,1)S(1)} %get-tuple-element.110), channel_id=1, source_target_pairs={{0,16},{4,20},{8,24},{12,28},{16,0},{20,4},{24,8},{28,12},{1,17},{... | collective-permute-start | bytes 294920 | tf_op jit(solution)/shard_map/ppermute | solution.py:22
  134.7 10.1 %collective-permute-start.24 = (bf16[64,768]{1,0:T(8,128)(2,1)S(1)}, bf16[64,768]{1,0:T(8,128)(2,1)S(1)}, u32[]{:S(2)}, u32[]{:S(2)}) collective-permute-start(bf16[64,768]{1,0:T(8,128)(2,1)S(1)} %get-tuple-element.111), channel_id=1, source_target_pairs={{0,24},{4,28},{8,16},{12,20},{16,8},{20,12},{24,0},{28,4},{1,25},{... | collective-permute-start | bytes 294920 | tf_op jit(solution)/shard_map/ppermute | solution.py:22
  144.8 9.9 %collective-permute-start.30 = (bf16[256,768]{1,0:T(8,128)(2,1)S(1)}, bf16[256,768]{1,0:T(8,128)(2,1)}, u32[]{:S(2)}, u32[]{:S(2)}) collective-permute-start(bf16[256,768]{1,0:T(8,128)(2,1)S(1)} %pack.3.refs_0_), channel_id=1, source_target_pairs={{0,2},{1,3},{2,0},{3,1},{4,6},{5,7},{6,4},{7,5},{8,10},{9,11},{10,... | collective-permute-start | bytes 1179656 | tf_op jit(solution)/shard_map/ppermute | solution.py:27
  144.9 10.1 %collective-permute-start.31 = (bf16[256,768]{1,0:T(8,128)(2,1)S(1)}, bf16[256,768]{1,0:T(8,128)(2,1)}, u32[]{:S(2)}, u32[]{:S(2)}) collective-permute-start(bf16[256,768]{1,0:T(8,128)(2,1)S(1)} %pack.3.refs_0_), channel_id=1, source_target_pairs={{0,1},{1,0},{2,3},{3,2},{4,5},{5,4},{6,7},{7,6},{8,9},{9,8},{10,11... | collective-permute-start | bytes 1179656 | tf_op jit(solution)/shard_map/ppermute | solution.py:27
  172.5 24.4 %collective-permute-start.35 = (bf16[2,256,768]{2,1,0:T(8,128)(2,1)S(1)}, bf16[2,256,768]{2,1,0:T(8,128)(2,1)S(1)}, u32[]{:S(2)}, u32[]{:S(2)}) collective-permute-start(bf16[2,256,768]{2,1,0:T(8,128)(2,1)S(1)} %get-tuple-element.116), channel_id=1, source_target_pairs={{0,1},{1,0},{2,3},{3,2},{4,5},{5,4},{6,7},{7,6},{8,9},{9,8},{10,11... | collective-permute-start | bytes 2359304 | tf_op jit(solution)/shard_map/ppermute | solution.py:27
  175.8 11.4 %collective-permute-start.27 = (bf16[64,768]{1,0:T(8,128)(2,1)S(1)}, bf16[64,768]{1,0:T(8,128)(2,1)S(1)}, u32[]{:S(2)}, u32[]{:S(2)}) collective-permute-start(bf16[64,768]{1,0:T(8,128)(2,1)S(1)} %copy-done.16), channel_id=1, source_target_pairs={{0,20},{4,16},{8,28},{12,24},{16,4},{20,0},{24,12},{28,8},{1,21},{... | collective-permute-start | bytes 294920 | tf_op jit(solution)/shard_map/ppermute | solution.py:22
  177.5 9.7 %collective-permute-start.28 = (bf16[64,768]{1,0:T(8,128)(2,1)S(1)}, bf16[64,768]{1,0:T(8,128)(2,1)S(1)}, u32[]{:S(2)}, u32[]{:S(2)}) collective-permute-start(bf16[64,768]{1,0:T(8,128)(2,1)S(1)} %copy-done.14), channel_id=1, source_target_pairs={{0,28},{4,24},{8,20},{12,16},{16,12},{20,8},{24,4},{28,0},{1,29},{... | collective-permute-start | bytes 294920 | tf_op jit(solution)/shard_map/ppermute | solution.py:22
  187.2 9.6 %collective-permute-start.29 = (bf16[256,768]{1,0:T(8,128)(2,1)S(1)}, bf16[256,768]{1,0:T(8,128)(2,1)S(1)}, u32[]{:S(2)}, u32[]{:S(2)}) collective-permute-start(bf16[256,768]{1,0:T(8,128)(2,1)S(1)} %pack.2.refs_0_), channel_id=1, source_target_pairs={{0,2},{1,3},{2,0},{3,1},{4,6},{5,7},{6,4},{7,5},{8,10},{9,11},{10,... | collective-permute-start | bytes 1179656 | tf_op jit(solution)/shard_map/ppermute | solution.py:27
  188.6 8.5 %collective-permute-start.33 = (bf16[256,768]{1,0:T(8,128)(2,1)S(1)}, bf16[256,768]{1,0:T(8,128)(2,1)S(1)}, u32[]{:S(2)}, u32[]{:S(2)}) collective-permute-start(bf16[256,768]{1,0:T(8,128)(2,1)S(1)} %pack.2.refs_0_), channel_id=1, source_target_pairs={{0,1},{1,0},{2,3},{3,2},{4,5},{5,4},{6,7},{7,6},{8,9},{9,8},{10,11... | collective-permute-start | bytes 1179656 | tf_op jit(solution)/shard_map/ppermute | solution.py:27
  210.3 27.8 %collective-permute-start.38 = (bf16[128,768]{1,0:T(8,128)(2,1)S(1)}, bf16[128,768]{1,0:T(8,128)(2,1)S(1)}, u32[]{:S(2)}, u32[]{:S(2)}) collective-permute-start(bf16[128,768]{1,0:T(8,128)(2,1)S(1)} %copy-done.12), channel_id=1, source_target_pairs={{0,0},{1,8},{2,16},{3,24},{4,4},{5,12},{6,20},{7,28},{8,1},{9,9},{... | collective-permute-start | bytes 589832 | tf_op jit(solution)/shard_map/ppermute | solution.py:400
  211.0 19.0 %collective-permute-start.39 = (bf16[256,768]{1,0:T(8,128)(2,1)S(1)}, bf16[256,768]{1,0:T(8,128)(2,1)S(1)}, u32[]{:S(2)}, u32[]{:S(2)}) collective-permute-start(bf16[256,768]{1,0:T(8,128)(2,1)S(1)} %fusion.3), channel_id=1, source_target_pairs={{0,2},{1,3},{2,0},{3,1},{4,6},{5,7},{6,4},{7,5},{8,10},{9,11},{10,... | collective-permute-start | bytes 1179656 | tf_op jit(solution)/shard_map/ppermute | solution.py:27
  218.1 19.9 %collective-permute-start.37 = (bf16[256,768]{1,0:T(8,128)(2,1)S(1)}, bf16[256,768]{1,0:T(8,128)(2,1)S(1)}, u32[]{:S(2)}, u32[]{:S(2)}) collective-permute-start(bf16[256,768]{1,0:T(8,128)(2,1)S(1)} %fusion.4), channel_id=1, source_target_pairs={{0,2},{1,3},{2,0},{3,1},{4,6},{5,7},{6,4},{7,5},{8,10},{9,11},{10,... | collective-permute-start | bytes 1179656 | tf_op jit(solution)/shard_map/ppermute | solution.py:27
  230.2 10.0 %collective-permute-start.41 = (bf16[64,768]{1,0:T(8,128)(2,1)S(1)}, bf16[64,768]{1,0:T(8,128)(2,1)S(1)}, u32[]{:S(2)}, u32[]{:S(2)}) collective-permute-start(bf16[64,768]{1,0:T(8,128)(2,1)S(1)} %get-tuple-element.135), channel_id=1, source_target_pairs={{0,8},{4,12},{8,0},{12,4},{16,24},{20,28},{24,16},{28,20},{1,9},{5... | collective-permute-start | bytes 294920 | tf_op jit(solution)/shard_map/ppermute | solution.py:22
  231.9 11.4 %collective-permute-start.43 = (bf16[64,768]{1,0:T(8,128)(2,1)S(1)}, bf16[64,768]{1,0:T(8,128)(2,1)S(1)}, u32[]{:S(2)}, u32[]{:S(2)}) collective-permute-start(bf16[64,768]{1,0:T(8,128)(2,1)S(1)} %get-tuple-element.137), channel_id=1, source_target_pairs={{0,16},{4,20},{8,24},{12,28},{16,0},{20,4},{24,8},{28,12},{1,17},{... | collective-permute-start | bytes 294920 | tf_op jit(solution)/shard_map/ppermute | solution.py:22
  233.4 11.6 %collective-permute-start.45 = (bf16[64,768]{1,0:T(8,128)(2,1)S(1)}, bf16[64,768]{1,0:T(8,128)(2,1)S(1)}, u32[]{:S(2)}, u32[]{:S(2)}) collective-permute-start(bf16[64,768]{1,0:T(8,128)(2,1)S(1)} %get-tuple-element.139), channel_id=1, source_target_pairs={{0,24},{4,28},{8,16},{12,20},{16,8},{20,12},{24,0},{28,4},{1,25},{... | collective-permute-start | bytes 294920 | tf_op jit(solution)/shard_map/ppermute | solution.py:22
  238.1 8.2 %collective-permute-start.40 = (bf16[64,768]{1,0:T(8,128)(2,1)S(1)}, bf16[64,768]{1,0:T(8,128)(2,1)S(1)}, u32[]{:S(2)}, u32[]{:S(2)}) collective-permute-start(bf16[64,768]{1,0:T(8,128)(2,1)S(1)} %get-tuple-element.134), channel_id=1, source_target_pairs={{0,4},{4,0},{8,12},{12,8},{16,20},{20,16},{24,28},{28,24},{1,5},{5... | collective-permute-start | bytes 294920 | tf_op jit(solution)/shard_map/ppermute | solution.py:22
  240.2 11.0 %collective-permute-start.44 = (bf16[64,768]{1,0:T(8,128)(2,1)S(1)}, bf16[64,768]{1,0:T(8,128)(2,1)S(1)}, u32[]{:S(2)}, u32[]{:S(2)}) collective-permute-start(bf16[64,768]{1,0:T(8,128)(2,1)S(1)} %get-tuple-element.138), channel_id=1, source_target_pairs={{0,20},{4,16},{8,28},{12,24},{16,4},{20,0},{24,12},{28,8},{1,21},{... | collective-permute-start | bytes 294920 | tf_op jit(solution)/shard_map/ppermute | solution.py:22
  (43 other events, 681.0 us)

commit v6 on v5

--- a/solution.py
+++ b/solution.py
@@ -187,11 +187,24 @@
         out_ref[k * count : (k + 1) * count, :] = ins[k][...]
 
 
-def route_kernel(me_ref, *refs):
-    ins, outs, stage_ref = refs[: (len(refs) - 1) // 2], refs[(len(refs) - 1) // 2 : -1], refs[-1]
-    count = len(ins)
-    for k in range(count):
-        stage_ref[(me_ref[0] + k) % count] = ins[k][...]
+def route_kernel(shifts, me_ref, *refs):
+    ins, outs, stage_ref = refs[: len(shifts)], refs[len(shifts) : -1], refs[-1]
+    count, me = len(outs), me_ref[0]
+    for (up, down), ref in zip(shifts, ins):
+        if not up and not down:
+            stage_ref[me] = ref[...]
+        if up:
+
+            @pl.when(me >= up)
+            def _(up=up, ref=ref):
+                stage_ref[me - up] = ref[...]
+
+        if down:
+
+            @pl.when(me < count - down)
+            def _(down=down, ref=ref):
+                stage_ref[me + down] = ref[...]
+
     for m in range(count):
         outs[m][...] = stage_ref[(me_ref[1] + m) % count]
 
@@ -236,38 +249,36 @@
     out_ref[...] = (middle_ref[...].astype(F32) + total).astype(BF16)
 
 
-def expert_kernel(n_head, aligned, owner_ref, *refs):
-    pieces = refs[:n_head]
-    gain_ref, gate_ref, up_ref, down_ref, sent_ref, kept_ref = refs[n_head : n_head + 6]
-    rows_ref, hidden_ref, wide_ref, low_ref, wide_sem, low_sem = refs[n_head + 6 :]
-    _, depth, units = gate_ref.shape
-    part = kept_ref.shape[2]
-    nz, nx = depth // part, sent_ref.shape[0]
+def wide_copies(gate_ref, up_ref, wide_ref, sems, steps, aligned):
+    width = gate_ref.shape[2] // steps
+    copies = []
+    for j in range(steps):
+        for k, weight in enumerate((gate_ref, up_ref)):
+            source, target = weight.at[0], wide_ref.at[k]
+            if aligned:
+                source = weight.at[0, :, pl.ds(j * width, width)]
+                target = wide_ref.at[j, :, pl.ds(k * width, width)]
+            copies.append(pltpu.make_async_copy(source, target, sems.at[j, k]))
+    return copies
+
+
+def low_copies(n_head, owner_ref, down_ref, low_ref, sems):
+    part = low_ref.shape[2]
+    copies = []
+    for j in range(n_head):
+        start = pl.multiple_of(owner_ref[n_head + j] * part, 128)
+        source = down_ref.at[0, :, pl.ds(start, part)]
+        copies.append(pltpu.make_async_copy(source, low_ref.at[j], sems.at[j]))
+    return copies
+
+
+def fill_hidden(n_head, aligned, owner_ref, pieces, gain_ref, rows_ref, wide_ref, hidden_ref, copies):
+    depth, units = gain_ref.shape[1], hidden_ref.shape[1]
+    part = pieces[0].shape[1]
+    nz = depth // part
     count = pieces[0].shape[0] // nz
-    steps = wide_ref.shape[0] // (1 if aligned else 2)
+    steps = len(copies) // 2
     width = units // steps
-
-    def wide_copy(j, k):
-        weight = (gate_ref, up_ref)[k]
-        if aligned:
-            source = weight.at[0, :, pl.ds(j * width, width)]
-            target = wide_ref.at[j, :, pl.ds(k * width, width)]
-        else:
-            source, target = weight.at[0], wide_ref.at[k]
-        return pltpu.make_async_copy(source, target, wide_sem.at[j, k])
-
-    def low_copy(j):
-        start = pl.multiple_of(owner_ref[n_head + j] * part, 128)
-        return pltpu.make_async_copy(
-            down_ref.at[0, :, pl.ds(start, part)], low_ref.at[j], low_sem.at[j]
-        )
-
-    for j in range(steps):
-        for k in range(2):
-            wide_copy(j, k).start()
-    for j in range(n_head):
-        low_copy(j).start()
-
     for i, piece in enumerate(pieces):
         squares = 0.0
         for k in range(nz):
@@ -279,10 +290,9 @@
             lanes = pl.ds(pl.multiple_of((owner_ref[2 * n_head] ^ k) * part, 128), part)
             value = piece[k * count : (k + 1) * count, :].astype(F32) * scale * gain_ref[:, lanes]
             rows_ref[lines, lanes] = value.astype(BF16)
-
     for j in range(steps):
-        for k in range(2):
-            wide_copy(j, k).wait()
+        copies[2 * j].wait()
+        copies[2 * j + 1].wait()
         if aligned:
             both = jnp.dot(rows_ref[...], wide_ref[j], preferred_element_type=F32)
             gate, up = both[:, :width], both[:, width:]
@@ -292,8 +302,11 @@
         hidden = (gate / (1.0 + jnp.exp(-gate)) * up).astype(BF16)
         hidden_ref[:, j * width : (j + 1) * width] = hidden
 
-    for j in range(n_head):
-        low_copy(j).wait()
+
+def write_out(hidden_ref, low_ref, sent_ref, kept_ref, copies):
+    nx = sent_ref.shape[0]
+    for j, copy in enumerate(copies):
+        copy.wait()
         out = jnp.dot(hidden_ref[...], low_ref[j], preferred_element_type=F32).astype(BF16)
         if j < nx:
             sent_ref[j] = out
@@ -301,7 +314,35 @@
             kept_ref[j - nx] = out
 
 
-def expert_call(owners, pieces, norm_gain, gate_weight, up_weight, down_weight):
+def expert_kernel(n_head, steps, aligned, owner_ref, *refs):
+    pieces, gain_ref = refs[:n_head], refs[n_head]
+    gate_ref, up_ref, down_ref, sent_ref, kept_ref = refs[n_head + 1 : n_head + 6]
+    rows_ref, hidden_ref, wide_ref, low_ref, wide_sem, low_sem = refs[n_head + 6 :]
+    wide = wide_copies(gate_ref, up_ref, wide_ref, wide_sem, steps, aligned)
+    low = low_copies(n_head, owner_ref, down_ref, low_ref, low_sem)
+    for copy in wide + low:
+        copy.start()
+    fill_hidden(n_head, aligned, owner_ref, pieces, gain_ref, rows_ref, wide_ref, hidden_ref, wide)
+    write_out(hidden_ref, low_ref, sent_ref, kept_ref, low)
+
+
+def hidden_kernel(n_head, steps, aligned, owner_ref, *refs):
+    pieces, gain_ref = refs[:n_head], refs[n_head]
+    gate_ref, up_ref, hidden_ref, rows_ref, wide_ref, wide_sem = refs[n_head + 1 :]
+    wide = wide_copies(gate_ref, up_ref, wide_ref, wide_sem, steps, aligned)
+    for copy in wide:
+        copy.start()
+    fill_hidden(n_head, aligned, owner_ref, pieces, gain_ref, rows_ref, wide_ref, hidden_ref, wide)
+
+
+def down_kernel(n_head, owner_ref, hidden_ref, down_ref, sent_ref, kept_ref, low_ref, low_sem):
+    low = low_copies(n_head, owner_ref, down_ref, low_ref, low_sem)
+    for copy in low:
+        copy.start()
+    write_out(hidden_ref, low_ref, sent_ref, kept_ref, low)
+
+
+def expert_call(owners, pieces, norm_gain, gate_weight, up_weight, down_weight, before_down=None):
     n_head = len(pieces)
     lines, part = pieces[0].shape
     _, depth, units = gate_weight.shape
@@ -309,30 +350,61 @@
     width = next((w for w in (384, 256, 128) if units % w == 0), units)
     aligned = width % 128 == 0
     steps, nx = units // width, n_head // CORES
-    wide = (steps, depth, 2 * width) if aligned else (2, depth, width)
     struct = jax.ShapeDtypeStruct
-    return pl.pallas_call(
-        functools.partial(expert_kernel, n_head, aligned),
-        out_shape=[struct((nx, count, part), BF16), struct((n_head - nx, count, part), BF16)],
-        in_specs=[pl.BlockSpec(memory_space=pltpu.SMEM)]
-        + [pl.BlockSpec(memory_space=pltpu.VMEM)] * (n_head + 1)
-        + [pl.BlockSpec(memory_space=pltpu.HBM)] * 3,
-        scratch_shapes=[
-            pltpu.VMEM((count, depth), BF16),
-            pltpu.VMEM((count, units), BF16),
-            pltpu.VMEM(wide, BF16),
-            pltpu.VMEM((n_head, units, part), BF16),
-            pltpu.SemaphoreType.DMA((steps, 2)),
-            pltpu.SemaphoreType.DMA((n_head,)),
-        ],
-        compiler_params=pltpu.CompilerParams(vmem_limit_bytes=EXPERT_VMEM),
-        cost_estimate=pl.CostEstimate(
-            flops=6 * count * depth * units,
-            bytes_accessed=6 * depth * units + 4 * count * depth,
-            transcendentals=count * units,
-        ),
-        name="expert",
-    )(owners, *pieces, norm_gain.reshape(1, depth), gate_weight, up_weight, down_weight)
+    rows = pltpu.VMEM((count, depth), BF16)
+    wide = pltpu.VMEM((steps, depth, 2 * width) if aligned else (2, depth, width), BF16)
+    low = pltpu.VMEM((n_head, units, part), BF16)
+    wide_sem, low_sem = pltpu.SemaphoreType.DMA((steps, 2)), pltpu.SemaphoreType.DMA((n_head,))
+    outs = [struct((nx, count, part), BF16), struct((n_head - nx, count, part), BF16)]
+    hidden = struct((count, units), BF16)
+    work = 2 * count * depth * units
+    gain = norm_gain.reshape(1, depth)
+    if before_down is None:
+        return local_call(
+            functools.partial(expert_kernel, n_head, steps, aligned),
+            "expert",
+            outs,
+            3 * work,
+            owners,
+            *pieces,
+            gain,
+            gate_weight,
+            up_weight,
+            down_weight,
+            scratch=[rows, pltpu.VMEM(hidden.shape, BF16), wide, low, wide_sem, low_sem],
+            scalars=1,
+            far=3,
+            vmem=EXPERT_VMEM,
+        )
+    hidden = local_call(
+        functools.partial(hidden_kernel, n_head, steps, aligned),
+        "hidden",
+        hidden,
+        2 * work,
+        owners,
+        *pieces,
+        gain,
+        gate_weight,
+        up_weight,
+        scratch=[rows, wide, wide_sem],
+        scalars=1,
+        far=2,
+        vmem=EXPERT_VMEM,
+    )
+    hidden = lax.optimization_barrier((hidden, before_down))[0]
+    return local_call(
+        functools.partial(down_kernel, n_head),
+        "down",
+        outs,
+        work,
+        owners,
+        hidden,
+        down_weight,
+        scratch=[low, low_sem],
+        scalars=1,
+        far=1,
+        vmem=EXPERT_VMEM,
+    )
 
 
 def local_call(
@@ -421,13 +493,17 @@
         scalars=1,
         far=2,
     )
+    lanes = max(128, routing.shape[1])
+    ids = jnp.pad(routing.astype(BF16), ((0, 0), (0, lanes - routing.shape[1])))
+    there = crossed(jnp.concatenate([residual, ids], axis=1))
+    arrived, there = lax.optimization_barrier((swap_seq(payload), there))
     entered = local_call(
         scan_kernel,
         "carry",
         [struct((rows, hw), BF16)] * n_seq,
         work,
         me,
-        *swap_seq(payload),
+        *arrived,
         scratch=[
             pltpu.VMEM((n_seq, rows + extra, hw), BF16),
             pltpu.VMEM((n_seq, rows, hw), BF16),
@@ -465,11 +541,7 @@
         scalars=1,
     )
 
-    lanes = max(128, routing.shape[1])
-    ids = jnp.pad(routing.astype(BF16), ((0, 0), (0, lanes - routing.shape[1])))
-    there = jnp.concatenate([residual, ids], axis=1)
-    attended, output_weight, there = lax.optimization_barrier((attended, output_weight, there))
-    there = crossed(there)
+    attended, output_weight = lax.optimization_barrier((attended, output_weight))
     residual_there = there[:, :part]
     routing_there = there[:, part : part + routing.shape[1]].astype(jnp.int32)
     slot = jnp.arange(experts * capacity, dtype=jnp.int32)
@@ -487,19 +559,31 @@
         got = permute_seq(output_weight, lambda q, k=k: q // ny * ny + (q % ny - k) % ny)
         w_z = lax.dynamic_update_slice(w_z, got, (0, (y + k) % ny * cols))
 
-    products = []
-    for k in range(nz):
-        rows_k = attended
-        if k:
-            rows_k = permute_seq(
-                attended, lambda q, k=k: (q // ny - k) % nz * ny + q % ny
-            )
-        products.append(jnp.dot(rows_k, w_z, preferred_element_type=F32).astype(BF16))
+    def along(value, pairs):
+        perm = [(a * ny + yy, b * ny + yy) for a, b in pairs for yy in range(ny)]
+        return lax.ppermute(value, "seq", perm)
+
+    ups = lambda j: [(q, q + j) for q in range(nz - j)]
+    downs = lambda j: [(q + j, q) for q in range(nz - j)]
+    below, above = along(attended, ups(1)), along(attended, downs(1))
+    direct = lax.optimization_barrier((attended, below, above))[0]
+    shifts, rows_of = [(0, 0), (1, 0), (0, 1)], [attended, below, above]
+    if nz > 2:
+        shifts += [(2, 0), (0, 2)]
+        rows_of += [along(below, ups(1)), along(above, downs(1))]
+    for j in range(3, nz):
+        if 2 * j >= nz:
+            shifts.append((j, j))
+            rows_of.append(along(direct, ups(j) + downs(j)))
+        else:
+            shifts += [(j, 0), (0, j)]
+            rows_of += [along(direct, ups(j)), along(direct, downs(j))]
+    products = [jnp.dot(r, w_z, preferred_element_type=F32).astype(BF16) for r in rows_of]
     products, take, mix = lax.optimization_barrier((products, take, mix))
     block = struct((tokens, part), BF16)
     place_me = jnp.stack([z, h]).astype(jnp.int32)
     own, *sent = local_call(
-        route_kernel,
+        functools.partial(route_kernel, shifts),
         "route",
         [block] * n_head,
         tokens * part,
@@ -531,7 +615,8 @@
     owners = jnp.stack(in_owner + out_owner + [z]).astype(jnp.int32)
     count = n_head * capacity
     returning = [None] * experts
-    arrived, sent, crossing = None, None, None
+    arrived = None
+    gots, fars = [], []
     for group in range(ny):
         sends = [outgoing[k * ny + group] for k in range(nz)]
         if group:
@@ -543,9 +628,16 @@
         got = local_call(
             pack_kernel, "pack", struct((nz * capacity, part), BF16), count * part, *arrived
         )
-        far = [permute_head(got, lambda q, m=m: (q - m * CORES) % n_head) for m in range(1, nx)]
+        gots.append(got)
+        fars.append(
+            [permute_head(got, lambda q, m=m: (q - m * CORES) % n_head) for m in range(1, nx)]
+        )
+    for group in range(ny):
+        got, far = gots[group], fars[group]
         if group:
             far = lax.optimization_barrier((far, sent))[0]
+        if group + 1 < ny:
+            far = lax.optimization_barrier((far, gots[group + 1]))[0]
         pieces = [got, *far]
         for piece in [got, *far]:
             for m in range(1, CORES):
@@ -556,7 +648,12 @@
                 )
         if group:
             pieces = lax.optimization_barrier((pieces, crossing))[0]
-        sent, kept = expert_call(owners, pieces, norm_gain, gate_weight, up_weight, down_weight)
+        first = [blocks, middle] if group else None
+        if group + 1 < ny:
+            first = (first, fars[group + 1])
+        sent, kept = expert_call(
+            owners, pieces, norm_gain, gate_weight, up_weight, down_weight, first
+        )
         if group == 0:
             middle = crossed(lax.optimization_barrier((middle_there, sent))[0])
 
@@ -576,8 +673,6 @@
             scratch=[pltpu.VMEM((count, part), BF16)],
             scalars=1,
         )
-        if group == ny - 1:
-            blocks, middle = lax.optimization_barrier((blocks, middle))
         for k in range(nz):
             returning[k * ny + group] = blocks[k]
     return local_call(

time: 253 us -> 213 us (0.84)
  waiting for transfers between devices: 95.7 us -> 68.7 us
  starting transfers between devices: 92.2 us -> 79.8 us
  matrix products: 10.8 us -> 4.03 us
  Pallas kernels: 32.4 us -> 35.9 us
    pallas_call x11 -> x15, Pallas kernels: 8.29 us -> 35.9 us  [local_call(): pl.pallas_call(kernel, out_shape=out_shape, in_specs=[pl.BlockSpec(memory...]
    ppermute x13, waiting for transfers between devices: 43.8 us -> 19.2 us  [permute_head(): lax.ppermute(value, 'head', [(source, move(source)) for source in range(c...]
    pallas_call x2 -> x0, Pallas kernels: 24.1 us -> none  [expert_call(): pl.pallas_call(functools.partial(expert_kernel, n_head, aligned), out_sha...]
    ppermute x13, starting transfers between devices: 37.5 us -> 13.5 us  [permute_head(): lax.ppermute(value, 'head', [(source, move(source)) for source in range(c...]
    ppermute x32 -> x29, waiting for transfers between devices: 51.9 us -> 30.7 us  [permute_seq(): lax.ppermute(value, 'seq', [(source, move(source)) for source in range(co...]
    ppermute x0 -> x5, waiting for transfers between devices: none -> 18.8 us  [along(): return lax.ppermute(value, 'seq', perm)]
    ppermute x0 -> x5, starting transfers between devices: none -> 13 us  [along(): return lax.ppermute(value, 'seq', perm)]
    dot_general x4 -> x6, matrix products: 10.4 us -> 3.64 us  [shards(): jnp.dot(r, w_z, preferred_element_type=F32).astype(BF16)]
  transfers between devices with their start and end apart: 47 -> 49, of which waited for: 20 -> 20; matrix products, arithmetic and copies ran while one was open for 7% -> 6% of each run, Pallas kernels for 1% -> 10%
where the time goes in v6:
time: 213 us
  starting transfers between devices  79.8 us (37%)
  waiting for transfers between devices  68.7 us (32%)
  Pallas kernels  35.9 us (17%)
  local copies, waits for them, and re-layouts  18.8 us (9%)
  other arithmetic  4.68 us (2%)
  matrix products  4.03 us (2%)
    ppermute x29, starting transfers between devices, permute_seq(): lax.ppermute(value, 'seq', [(source, move(source)) for source in range(co...  50.3 us
    pallas_call x15, Pallas kernels, local_call(): pl.pallas_call(kernel, out_shape=out_shape, in_specs=[pl.BlockSpec(memory...  35.9 us
    ppermute x29, waiting for transfers between devices, permute_seq(): lax.ppermute(value, 'seq', [(source, move(source)) for source in range(co...  30.7 us
    ppermute x13, waiting for transfers between devices, permute_head(): lax.ppermute(value, 'head', [(source, move(source)) for source in range(c...  19.2 us
    ppermute x5, waiting for transfers between devices, along(): return lax.ppermute(value, 'seq', perm)  18.8 us
    ppermute x13, starting transfers between devices, permute_head(): lax.ppermute(value, 'head', [(source, move(source)) for source in range(c...  13.5 us
    unnamed x37, local copies, waits for them, and re-layouts  13.4 us
    ppermute x5, starting transfers between devices, along(): return lax.ppermute(value, 'seq', perm)  13 us
  transfers between devices with their start and end apart: 49, of which 20 were waited for; matrix products, arithmetic and copies ran while one was open for 6% of the time, Pallas kernels for 10%

profile of v6, /device:TPU:0, one launch (start us, length us, event | category | flops | bytes accessed | tf_op | source)
XLA Modules:
  0.0 212.5 jit_solution(6301664132456889281)
XLA Ops:
  7.7 3.0 %collective-permute-start = (bf16[272,128]{1,0:T(8,128)(2,1)S(1)}, bf16[272,128]{1,0:T(8,128)(2,1)S(1)}, u32[]{:S(2)}, u32[]{:S(2)}) collective-permute-start(bf16[272,128]{1,0:T(8,128)(2,1)S(1)} %get-tuple-element.83), channel_id=1, source_target_pairs={{0,4},{4,0},{8,12},{12,8},{16,20},{20,16},{24,28},{28,24},{1,5},{5... | collective-permute-start | bytes 208904 | tf_op jit(solution)/shard_map/ppermute | solution.py:22
  12.9 4.2 %collective-permute-start.3 = (bf16[272,128]{1,0:T(8,128)(2,1)S(1)}, bf16[272,128]{1,0:T(8,128)(2,1)S(1)}, u32[]{:S(2)}, u32[]{:S(2)}) collective-permute-start(bf16[272,128]{1,0:T(8,128)(2,1)S(1)} %get-tuple-element.86), channel_id=1, source_target_pairs={{0,16},{4,20},{8,24},{12,28},{16,0},{20,4},{24,8},{28,12},{1,17},{... | collective-permute-start | bytes 208904 | tf_op jit(solution)/shard_map/ppermute | solution.py:22
  22.6 5.1 %collective-permute-done.3.refs_4_ = bf16[272,128]{1,0:T(8,128)(2,1)S(1)} collective-permute-done((bf16[272,128]{1,0:T(8,128)(2,1)S(1)}, bf16[272,128]{1,0:T(8,128)(2,1)S(1)}, u32[]{:S(2)}, u32[]{:S(2)}) %collective-permute-start.3) | collective-permute-done | bytes 69664 | tf_op jit(solution)/shard_map/ppermute | solution.py:22
  30.5 3.2 %collective-permute-start.10 = (bf16[256,128]{1,0:T(8,128)(2,1)S(1)}, bf16[256,128]{1,0:T(8,128)(2,1)S(1)}, u32[]{:S(2)}, u32[]{:S(2)}) collective-permute-start(bf16[256,128]{1,0:T(8,128)(2,1)S(1)} %get-tuple-element.105), channel_id=1, source_target_pairs={{0,12},{4,8},{8,4},{12,0},{16,28},{20,24},{24,20},{28,16},{1,13},{... | collective-permute-start | bytes 196616 | tf_op jit(solution)/shard_map/ppermute | solution.py:22
  33.7 3.9 %collective-permute-start.12 = (bf16[256,128]{1,0:T(8,128)(2,1)S(1)}, bf16[256,128]{1,0:T(8,128)(2,1)S(1)}, u32[]{:S(2)}, u32[]{:S(2)}) collective-permute-start(bf16[256,128]{1,0:T(8,128)(2,1)S(1)} %get-tuple-element.107), channel_id=1, source_target_pairs={{0,20},{4,16},{8,28},{12,24},{16,4},{20,0},{24,12},{28,8},{1,21},{... | collective-permute-start | bytes 196616 | tf_op jit(solution)/shard_map/ppermute | solution.py:22
  37.9 3.4 %collective-permute-start.14 = (bf16[256,128]{1,0:T(8,128)(2,1)S(1)}, bf16[256,128]{1,0:T(8,128)(2,1)S(1)}, u32[]{:S(2)}, u32[]{:S(2)}) collective-permute-start(bf16[256,128]{1,0:T(8,128)(2,1)S(1)} %get-tuple-element.109), channel_id=1, source_target_pairs={{0,28},{4,24},{8,20},{12,16},{16,12},{20,8},{24,4},{28,0},{1,29},{... | collective-permute-start | bytes 196616 | tf_op jit(solution)/shard_map/ppermute | solution.py:22
  46.9 2.8 %inside.1.inside_ref = f32[128,2048]{1,0:T(8,128)S(1)} custom-call(f32[1,128]{1,0:T(1,128)S(1)} %get-tuple-element.91.doc_ref, f32[128,16]{1,0:T(8,128)S(1)} %get-tuple-element.92.sum_ref, f32[16,128]{1,0:T(8,128)S(1)} %get-tuple-element.93.sum_rows_ref, bf16[128,2048]{1,0:T(8,128)(2,1)S(1)} %copy-done.6, bf16[128,2048]{1,0:T(8,128)(2,1)S(1)} %copy-done.3, ...), custom_call_target="tpu_custom_call" | custom-call | flops 134217728 | bytes 2638336 | tf_op jit(solution)/shard_map/inside/pallas_call | solution.py:415
  55.1 4.0 %collective-permute-start.16 = (bf16[128,2048]{1,0:T(8,128)(2,1)S(1)}, bf16[128,2048]{1,0:T(8,128)(2,1)S(1)}, u32[]{:S(2)}, u32[]{:S(2)}) collective-permute-start(bf16[128,2048]{1,0:T(8,128)(2,1)S(1)} %outside.1), channel_id=1, source_target_pairs={{0,8},{4,12},{8,16},{12,20},{16,24},{20,28},{1,9},{5,13},{9,17},{1... | collective-permute-start | bytes 1572872 | tf_op jit(solution)/shard_map/ppermute | solution.py:564
  62.7 6.0 %collective-permute-done.16 = bf16[128,2048]{1,0:T(8,128)(2,1)S(1)} collective-permute-done((bf16[128,2048]{1,0:T(8,128)(2,1)S(1)}, bf16[128,2048]{1,0:T(8,128)(2,1)S(1)}, u32[]{:S(2)}, u32[]{:S(2)}) %collective-permute-start.16) | collective-permute-done | bytes 524320 | tf_op jit(solution)/shard_map/ppermute | solution.py:564
  68.7 4.1 %collective-permute-done.17 = bf16[128,2048]{1,0:T(8,128)(2,1)S(1)} collective-permute-done((bf16[128,2048]{1,0:T(8,128)(2,1)S(1)}, bf16[128,2048]{1,0:T(8,128)(2,1)S(1)}, u32[]{:S(2)}, u32[]{:S(2)}) %collective-permute-start.17) | collective-permute-done | bytes 524320 | tf_op jit(solution)/shard_map/ppermute | solution.py:564
  76.1 4.6 %collective-permute-start.18 = (bf16[128,2048]{1,0:T(8,128)(2,1)S(1)}, bf16[128,2048]{1,0:T(8,128)(2,1)S(1)}, u32[]{:S(2)}, u32[]{:S(2)}) collective-permute-start(bf16[128,2048]{1,0:T(8,128)(2,1)S(1)} %collective-permute-done.16), channel_id=1, source_target_pairs={{0,8},{4,12},{8,16},{12,20},{16,24},{20,28},{1,9},{5,13},{9,17},{1... | collective-permute-start | bytes 1572872 | tf_op jit(solution)/shard_map/ppermute | solution.py:564
  80.7 5.4 %collective-permute-done.15 = bf16[2048,384]{1,0:T(8,128)(2,1)} collective-permute-done((bf16[2048,384]{1,0:T(8,128)(2,1)S(1)}, bf16[2048,384]{1,0:T(8,128)(2,1)}, u32[]{:S(2)}, u32[]{:S(2)}) %collective-permute-start.15) | collective-permute-done | bytes 1572896 | tf_op jit(solution)/shard_map/ppermute | solution.py:22
  92.0 6.9 %collective-permute-done.19 = bf16[128,2048]{1,0:T(8,128)(2,1)S(1)} collective-permute-done((bf16[128,2048]{1,0:T(8,128)(2,1)S(1)}, bf16[128,2048]{1,0:T(8,128)(2,1)S(1)}, u32[]{:S(2)}, u32[]{:S(2)}) %collective-permute-start.19) | collective-permute-done | bytes 524320 | tf_op jit(solution)/shard_map/ppermute | solution.py:564
  103.6 3.9 %collective-permute-done.21.refs_1_ = bf16[128,768]{1,0:T(8,128)(2,1)S(1)} collective-permute-done((bf16[128,768]{1,0:T(8,128)(2,1)S(1)}, bf16[128,768]{1,0:T(8,128)(2,1)S(1)}, u32[]{:S(2)}, u32[]{:S(2)}) %collective-permute-start.21) | collective-permute-done | bytes 196640 | tf_op jit(solution)/shard_map/ppermute | solution.py:27
  110.8 4.4 %collective-permute-start.26 = (bf16[64,768]{1,0:T(8,128)(2,1)S(1)}, bf16[64,768]{1,0:T(8,128)(2,1)S(1)}, u32[]{:S(2)}, u32[]{:S(2)}) collective-permute-start(bf16[64,768]{1,0:T(8,128)(2,1)S(1)} %get-tuple-element.128), channel_id=1, source_target_pairs={{0,24},{4,28},{8,16},{12,20},{16,8},{20,12},{24,0},{28,4},{1,25},{... | collective-permute-start | bytes 294920 | tf_op jit(solution)/shard_map/ppermute | solution.py:22
  116.4 3.5 %collective-permute-done.26.refs_3_ = bf16[64,768]{1,0:T(8,128)(2,1)S(1)} collective-permute-done((bf16[64,768]{1,0:T(8,128)(2,1)S(1)}, bf16[64,768]{1,0:T(8,128)(2,1)S(1)}, u32[]{:S(2)}, u32[]{:S(2)}) %collective-permute-start.26) | collective-permute-done | bytes 98336 | tf_op jit(solution)/shard_map/ppermute | solution.py:22
  120.8 3.7 %collective-permute-start.27 = (bf16[256,768]{1,0:T(8,128)(2,1)}, bf16[256,768]{1,0:T(8,128)(2,1)}, u32[]{:S(2)}, u32[]{:S(2)}) collective-permute-start(bf16[256,768]{1,0:T(8,128)(2,1)} %pack.2.refs_0_), channel_id=1, source_target_pairs={{0,2},{1,3},{2,0},{3,1},{4,6},{5,7},{6,4},{7,5},{8,10},{9,11},{10,... | collective-permute-start | bytes 1179656 | tf_op jit(solution)/shard_map/ppermute | solution.py:27
  124.5 3.4 %collective-permute-start.29 = (bf16[64,768]{1,0:T(8,128)(2,1)S(1)}, bf16[64,768]{1,0:T(8,128)(2,1)S(1)}, u32[]{:S(2)}, u32[]{:S(2)}) collective-permute-start(bf16[64,768]{1,0:T(8,128)(2,1)S(1)} %get-tuple-element.134), channel_id=1, source_target_pairs={{0,12},{4,8},{8,4},{12,0},{16,28},{20,24},{24,20},{28,16},{1,13},{... | collective-permute-start | bytes 294920 | tf_op jit(solution)/shard_map/ppermute | solution.py:22
  127.9 3.3 %collective-permute-start.31 = (bf16[64,768]{1,0:T(8,128)(2,1)S(1)}, bf16[64,768]{1,0:T(8,128)(2,1)S(1)}, u32[]{:S(2)}, u32[]{:S(2)}) collective-permute-start(bf16[64,768]{1,0:T(8,128)(2,1)S(1)} %get-tuple-element.136), channel_id=1, source_target_pairs={{0,28},{4,24},{8,20},{12,16},{16,12},{20,8},{24,4},{28,0},{1,29},{... | collective-permute-start | bytes 294920 | tf_op jit(solution)/shard_map/ppermute | solution.py:22
  131.2 6.8 %collective-permute-done.30.refs_2_ = bf16[64,768]{1,0:T(8,128)(2,1)S(1)} collective-permute-done((bf16[64,768]{1,0:T(8,128)(2,1)S(1)}, bf16[64,768]{1,0:T(8,128)(2,1)S(1)}, u32[]{:S(2)}, u32[]{:S(2)}) %collective-permute-start.30) | collective-permute-done | bytes 98336 | tf_op jit(solution)/shard_map/ppermute | solution.py:22
  140.2 3.0 %copy-done = bf16[1,3072,1152]{2,1,0:T(8,128)(2,1)S(1)} copy-done((bf16[1,3072,1152]{2,1,0:T(8,128)(2,1)S(1)}, bf16[1,3072,1152]{2,1,0:T(8,128)(2,1)}, u32[]{:S(2)}) %copy-start) | copy-done | bytes 7077912
  143.2 8.4 %hidden.2.hidden_ref = bf16[256,1152]{1,0:T(8,128)(2,1)S(1)} custom-call(s32[9]{0:T(128)S(1)} %stack.45.owner_ref, bf16[256,768]{1,0:T(8,128)(2,1)} %pack.2.refs_0_, bf16[256,768]{1,0:T(8,128)(2,1)} %collective-permute-done.27.refs_1_, bf16[256,768]{1,0:T(8,128)(2,1)} %collective-permute-done.32.refs_2_, bf16[256,768]{1,0:T(8,128)(2,1)} %collective-permute-done.33.refs_3_, ...), custom_call_target="tpu_custom_call" | custom-call | flops 3623878656 | bytes 16330788 | tf_op jit(solution)/shard_map/hidden/pallas_call | solution.py:415
  151.7 3.0 %copy-done.1 = bf16[1,1152,3072]{2,1,0:T(8,128)(2,1)S(1)} copy-done((bf16[1,1152,3072]{2,1,0:T(8,128)(2,1)S(1)}, bf16[1,1152,3072]{2,1,0:T(8,128)(2,1)}, u32[]{:S(2)}) %copy-start.1) | copy-done | bytes 7077912
  154.7 4.9 %down.2 = (bf16[2,256,768]{2,1,0:T(8,128)(2,1)S(1)}, bf16[2,256,768]{2,1,0:T(8,128)(2,1)S(1)}) custom-call(s32[9]{0:T(128)S(1)} %stack.45.owner_ref, bf16[256,1152]{1,0:T(8,128)(2,1)S(1)} %hidden.2.hidden_ref, bf16[1,1152,3072]{2,1,0:T(8,128)(2,1)S(1)} %copy-done.1), custom_call_target="tpu_custom_call" | custom-call | flops 1811939328 | bytes 9240612 | tf_op jit(solution)/shard_map/down/pallas_call | solution.py:415
  162.2 3.8 %collective-permute-start.37 = (bf16[256,768]{1,0:T(8,128)(2,1)S(1)}, bf16[256,768]{1,0:T(8,128)(2,1)S(1)}, u32[]{:S(2)}, u32[]{:S(2)}) collective-permute-start(bf16[256,768]{1,0:T(8,128)(2,1)S(1)} %fusion.3), channel_id=1, source_target_pairs={{0,2},{1,3},{2,0},{3,1},{4,6},{5,7},{6,4},{7,5},{8,10},{9,11},{10,... | collective-permute-start | bytes 1179656 | tf_op jit(solution)/shard_map/ppermute | solution.py:27
  166.1 7.9 %hidden.3.hidden_ref = bf16[256,1152]{1,0:T(8,128)(2,1)S(1)} custom-call(s32[9]{0:T(128)S(1)} %stack.45.owner_ref, bf16[256,768]{1,0:T(8,128)(2,1)S(1)} %pack.3.refs_0_, bf16[256,768]{1,0:T(8,128)(2,1)} %collective-permute-done.34.refs_1_, bf16[256,768]{1,0:T(8,128)(2,1)S(1)} %collective-permute-done.38.refs_2_, ...), custom_call_target="tpu_custom_call" | custom-call | flops 3623878656 | bytes 16330788 | tf_op jit(solution)/shard_map/hidden/pallas_call | solution.py:415
  174.1 4.7 %collective-permute-done.37.refs_1_ = bf16[256,768]{1,0:T(8,128)(2,1)S(1)} collective-permute-done((bf16[256,768]{1,0:T(8,128)(2,1)S(1)}, bf16[256,768]{1,0:T(8,128)(2,1)S(1)}, u32[]{:S(2)}, u32[]{:S(2)}) %collective-permute-start.37) | collective-permute-done | bytes 393248 | tf_op jit(solution)/shard_map/ppermute | solution.py:27
  178.9 4.9 %down.3 = (bf16[2,256,768]{2,1,0:T(8,128)(2,1)S(1)}, bf16[2,256,768]{2,1,0:T(8,128)(2,1)S(1)}) custom-call(s32[9]{0:T(128)S(1)} %stack.45.owner_ref, bf16[256,1152]{1,0:T(8,128)(2,1)S(1)} %hidden.3.hidden_ref, bf16[1,1152,3072]{2,1,0:T(8,128)(2,1)S(1)} %bitcast.39), custom_call_target="tpu_custom_call" | custom-call | flops 1811939328 | bytes 9240612 | tf_op jit(solution)/shard_map/down/pallas_call | solution.py:415
  190.1 3.3 %collective-permute-start.47 = (bf16[64,768]{1,0:T(8,128)(2,1)S(1)}, bf16[64,768]{1,0:T(8,128)(2,1)S(1)}, u32[]{:S(2)}, u32[]{:S(2)}) collective-permute-start(bf16[64,768]{1,0:T(8,128)(2,1)S(1)} %get-tuple-element.151), channel_id=1, source_target_pairs={{0,24},{4,28},{8,16},{12,20},{16,8},{20,12},{24,0},{28,4},{1,25},{... | collective-permute-start | bytes 294920 | tf_op jit(solution)/shard_map/ppermute | solution.py:22
  193.4 5.0 %collective-permute-done.41.refs_1_ = bf16[256,768]{1,0:T(8,128)(2,1)S(1)} collective-permute-done((bf16[256,768]{1,0:T(8,128)(2,1)S(1)}, bf16[256,768]{1,0:T(8,128)(2,1)S(1)}, u32[]{:S(2)}, u32[]{:S(2)}) %collective-permute-start.41) | collective-permute-done | bytes 393248 | tf_op jit(solution)/shard_map/ppermute | solution.py:27
  200.6 2.7 %collective-permute-start.46 = (bf16[64,768]{1,0:T(8,128)(2,1)S(1)}, bf16[64,768]{1,0:T(8,128)(2,1)S(1)}, u32[]{:S(2)}, u32[]{:S(2)}) collective-permute-start(bf16[64,768]{1,0:T(8,128)(2,1)S(1)} %get-tuple-element.157), channel_id=1, source_target_pairs={{0,20},{4,16},{8,28},{12,24},{16,4},{20,0},{24,12},{28,8},{1,21},{... | collective-permute-start | bytes 294920 | tf_op jit(solution)/shard_map/ppermute | solution.py:22
  206.6 4.8 %collective-permute-done.46.refs_5_ = bf16[64,768]{1,0:T(8,128)(2,1)S(1)} collective-permute-done((bf16[64,768]{1,0:T(8,128)(2,1)S(1)}, bf16[64,768]{1,0:T(8,128)(2,1)S(1)}, u32[]{:S(2)}, u32[]{:S(2)}) %collective-permute-start.46) | collective-permute-done | bytes 98336 | tf_op jit(solution)/shard_map/ppermute | solution.py:22
  (160 shorter events, 69.7 us)
Async XLA Ops:
  1.8 28.4 %collective-permute-start.7 = (bf16[128,896]{1,0:T(8,128)(2,1)S(1)}, bf16[128,896]{1,0:T(8,128)(2,1)}, u32[]{:S(2)}, u32[]{:S(2)}) collective-permute-start(bf16[128,896]{1,0:T(8,128)(2,1)S(1)} %fusion.5), channel_id=1, source_target_pairs={{0,0},{1,8},{2,16},{3,24},{4,4},{5,12},{6,20},{7,28},{8,1},{9,9},{... | collective-permute-start | bytes 688136 | tf_op jit(solution)/shard_map/ppermute | solution.py:472
  7.7 9.4 %collective-permute-start = (bf16[272,128]{1,0:T(8,128)(2,1)S(1)}, bf16[272,128]{1,0:T(8,128)(2,1)S(1)}, u32[]{:S(2)}, u32[]{:S(2)}) collective-permute-start(bf16[272,128]{1,0:T(8,128)(2,1)S(1)} %get-tuple-element.83), channel_id=1, source_target_pairs={{0,4},{4,0},{8,12},{12,8},{16,20},{20,16},{24,28},{28,24},{1,5},{5... | collective-permute-start | bytes 208904 | tf_op jit(solution)/shard_map/ppermute | solution.py:22
  12.9 8.5 %collective-permute-start.2 = (bf16[272,128]{1,0:T(8,128)(2,1)S(1)}, bf16[272,128]{1,0:T(8,128)(2,1)S(1)}, u32[]{:S(2)}, u32[]{:S(2)}) collective-permute-start(bf16[272,128]{1,0:T(8,128)(2,1)S(1)} %get-tuple-element.85), channel_id=1, source_target_pairs={{0,12},{4,8},{8,4},{12,0},{16,28},{20,24},{24,20},{28,16},{1,13},{... | collective-permute-start | bytes 208904 | tf_op jit(solution)/shard_map/ppermute | solution.py:22
  12.9 14.9 %collective-permute-start.3 = (bf16[272,128]{1,0:T(8,128)(2,1)S(1)}, bf16[272,128]{1,0:T(8,128)(2,1)S(1)}, u32[]{:S(2)}, u32[]{:S(2)}) collective-permute-start(bf16[272,128]{1,0:T(8,128)(2,1)S(1)} %get-tuple-element.86), channel_id=1, source_target_pairs={{0,16},{4,20},{8,24},{12,28},{16,0},{20,4},{24,8},{28,12},{1,17},{... | collective-permute-start | bytes 208904 | tf_op jit(solution)/shard_map/ppermute | solution.py:22
  17.1 13.1 %collective-permute-start.4 = (bf16[272,128]{1,0:T(8,128)(2,1)S(1)}, bf16[272,128]{1,0:T(8,128)(2,1)S(1)}, u32[]{:S(2)}, u32[]{:S(2)}) collective-permute-start(bf16[272,128]{1,0:T(8,128)(2,1)S(1)} %get-tuple-element.87), channel_id=1, source_target_pairs={{0,20},{4,16},{8,28},{12,24},{16,4},{20,0},{24,12},{28,8},{1,21},{... | collective-permute-start | bytes 208904 | tf_op jit(solution)/shard_map/ppermute | solution.py:22
  18.9 11.3 %collective-permute-start.5 = (bf16[272,128]{1,0:T(8,128)(2,1)S(1)}, bf16[272,128]{1,0:T(8,128)(2,1)S(1)}, u32[]{:S(2)}, u32[]{:S(2)}) collective-permute-start(bf16[272,128]{1,0:T(8,128)(2,1)S(1)} %get-tuple-element.88), channel_id=1, source_target_pairs={{0,24},{4,28},{8,16},{12,20},{16,8},{20,12},{24,0},{28,4},{1,25},{... | collective-permute-start | bytes 208904 | tf_op jit(solution)/shard_map/ppermute | solution.py:22
  21.3 8.9 %collective-permute-start.6 = (bf16[272,128]{1,0:T(8,128)(2,1)S(1)}, bf16[272,128]{1,0:T(8,128)(2,1)S(1)}, u32[]{:S(2)}, u32[]{:S(2)}) collective-permute-start(bf16[272,128]{1,0:T(8,128)(2,1)S(1)} %get-tuple-element.89), channel_id=1, source_target_pairs={{0,28},{4,24},{8,20},{12,16},{16,12},{20,8},{24,4},{28,0},{1,29},{... | collective-permute-start | bytes 208904 | tf_op jit(solution)/shard_map/ppermute | solution.py:22
  30.5 10.8 %collective-permute-start.10 = (bf16[256,128]{1,0:T(8,128)(2,1)S(1)}, bf16[256,128]{1,0:T(8,128)(2,1)S(1)}, u32[]{:S(2)}, u32[]{:S(2)}) collective-permute-start(bf16[256,128]{1,0:T(8,128)(2,1)S(1)} %get-tuple-element.105), channel_id=1, source_target_pairs={{0,12},{4,8},{8,4},{12,0},{16,28},{20,24},{24,20},{28,16},{1,13},{... | collective-permute-start | bytes 196616 | tf_op jit(solution)/shard_map/ppermute | solution.py:22
  33.7 9.2 %collective-permute-start.11 = (bf16[256,128]{1,0:T(8,128)(2,1)S(1)}, bf16[256,128]{1,0:T(8,128)(2,1)S(1)}, u32[]{:S(2)}, u32[]{:S(2)}) collective-permute-start(bf16[256,128]{1,0:T(8,128)(2,1)S(1)} %get-tuple-element.106), channel_id=1, source_target_pairs={{0,16},{4,20},{8,24},{12,28},{16,0},{20,4},{24,8},{28,12},{1,17},{... | collective-permute-start | bytes 196616 | tf_op jit(solution)/shard_map/ppermute | solution.py:22
  33.7 16.1 %collective-permute-start.12 = (bf16[256,128]{1,0:T(8,128)(2,1)S(1)}, bf16[256,128]{1,0:T(8,128)(2,1)S(1)}, u32[]{:S(2)}, u32[]{:S(2)}) collective-permute-start(bf16[256,128]{1,0:T(8,128)(2,1)S(1)} %get-tuple-element.107), channel_id=1, source_target_pairs={{0,20},{4,16},{8,28},{12,24},{16,4},{20,0},{24,12},{28,8},{1,21},{... | collective-permute-start | bytes 196616 | tf_op jit(solution)/shard_map/ppermute | solution.py:22
  37.5 12.2 %collective-permute-start.13 = (bf16[256,128]{1,0:T(8,128)(2,1)S(1)}, bf16[256,128]{1,0:T(8,128)(2,1)S(1)}, u32[]{:S(2)}, u32[]{:S(2)}) collective-permute-start(bf16[256,128]{1,0:T(8,128)(2,1)S(1)} %get-tuple-element.108), channel_id=1, source_target_pairs={{0,24},{4,28},{8,16},{12,20},{16,8},{20,12},{24,0},{28,4},{1,25},{... | collective-permute-start | bytes 196616 | tf_op jit(solution)/shard_map/ppermute | solution.py:22
  37.9 11.9 %collective-permute-start.14 = (bf16[256,128]{1,0:T(8,128)(2,1)S(1)}, bf16[256,128]{1,0:T(8,128)(2,1)S(1)}, u32[]{:S(2)}, u32[]{:S(2)}) collective-permute-start(bf16[256,128]{1,0:T(8,128)(2,1)S(1)} %get-tuple-element.109), channel_id=1, source_target_pairs={{0,28},{4,24},{8,20},{12,16},{16,12},{20,8},{24,4},{28,0},{1,29},{... | collective-permute-start | bytes 196616 | tf_op jit(solution)/shard_map/ppermute | solution.py:22
  41.3 8.5 %collective-permute-start.8 = (bf16[256,128]{1,0:T(8,128)(2,1)S(1)}, bf16[256,128]{1,0:T(8,128)(2,1)S(1)}, u32[]{:S(2)}, u32[]{:S(2)}) collective-permute-start(bf16[256,128]{1,0:T(8,128)(2,1)S(1)} %get-tuple-element.103), channel_id=1, source_target_pairs={{0,4},{4,0},{8,12},{12,8},{16,20},{20,16},{24,28},{28,24},{1,5},{5... | collective-permute-start | bytes 196616 | tf_op jit(solution)/shard_map/ppermute | solution.py:22
  51.6 34.5 %collective-permute-start.15 = (bf16[2048,384]{1,0:T(8,128)(2,1)S(1)}, bf16[2048,384]{1,0:T(8,128)(2,1)}, u32[]{:S(2)}, u32[]{:S(2)}) collective-permute-start(bf16[2048,384]{1,0:T(8,128)(2,1)S(1)} %copy-done.12), channel_id=1, source_target_pairs={{0,4},{4,0},{8,12},{12,8},{16,20},{20,16},{24,28},{28,24},{1,5},{5... | collective-permute-start | bytes 4718600 | tf_op jit(solution)/shard_map/ppermute | solution.py:22
  55.1 13.6 %collective-permute-start.16 = (bf16[128,2048]{1,0:T(8,128)(2,1)S(1)}, bf16[128,2048]{1,0:T(8,128)(2,1)S(1)}, u32[]{:S(2)}, u32[]{:S(2)}) collective-permute-start(bf16[128,2048]{1,0:T(8,128)(2,1)S(1)} %outside.1), channel_id=1, source_target_pairs={{0,8},{4,12},{8,16},{12,20},{16,24},{20,28},{1,9},{5,13},{9,17},{1... | collective-permute-start | bytes 1572872 | tf_op jit(solution)/shard_map/ppermute | solution.py:564
  59.1 13.8 %collective-permute-start.17 = (bf16[128,2048]{1,0:T(8,128)(2,1)S(1)}, bf16[128,2048]{1,0:T(8,128)(2,1)S(1)}, u32[]{:S(2)}, u32[]{:S(2)}) collective-permute-start(bf16[128,2048]{1,0:T(8,128)(2,1)S(1)} %outside.1), channel_id=1, source_target_pairs={{8,0},{12,4},{16,8},{20,12},{24,16},{28,20},{9,1},{13,5},{17,9},{2... | collective-permute-start | bytes 1572872 | tf_op jit(solution)/shard_map/ppermute | solution.py:564
  72.9 18.5 %collective-permute-start.20 = (bf16[128,2048]{1,0:T(8,128)(2,1)S(1)}, bf16[128,2048]{1,0:T(8,128)(2,1)S(1)}, u32[]{:S(2)}, u32[]{:S(2)}) collective-permute-start(bf16[128,2048]{1,0:T(8,128)(2,1)S(1)} %outside.1), channel_id=1, source_target_pairs={{0,24},{4,28},{24,0},{28,4},{1,25},{5,29},{25,1},{29,5},{2,26},{6,... | collective-permute-start | bytes 1572872 | tf_op jit(solution)/shard_map/ppermute | solution.py:564
  74.8 24.1 %collective-permute-start.19 = (bf16[128,2048]{1,0:T(8,128)(2,1)S(1)}, bf16[128,2048]{1,0:T(8,128)(2,1)S(1)}, u32[]{:S(2)}, u32[]{:S(2)}) collective-permute-start(bf16[128,2048]{1,0:T(8,128)(2,1)S(1)} %collective-permute-done.17), channel_id=1, source_target_pairs={{8,0},{12,4},{16,8},{20,12},{24,16},{28,20},{9,1},{13,5},{17,9},{2... | collective-permute-start | bytes 1572872 | tf_op jit(solution)/shard_map/ppermute | solution.py:564
  76.1 23.5 %collective-permute-start.18 = (bf16[128,2048]{1,0:T(8,128)(2,1)S(1)}, bf16[128,2048]{1,0:T(8,128)(2,1)S(1)}, u32[]{:S(2)}, u32[]{:S(2)}) collective-permute-start(bf16[128,2048]{1,0:T(8,128)(2,1)S(1)} %collective-permute-done.16), channel_id=1, source_target_pairs={{0,8},{4,12},{8,16},{12,20},{16,24},{20,28},{1,9},{5,13},{9,17},{1... | collective-permute-start | bytes 1572872 | tf_op jit(solution)/shard_map/ppermute | solution.py:564
  101.0 8.7 %collective-permute-start.23 = (bf16[128,768]{1,0:T(8,128)(2,1)S(1)}, bf16[128,768]{1,0:T(8,128)(2,1)S(1)}, u32[]{:S(2)}, u32[]{:S(2)}) collective-permute-start(bf16[128,768]{1,0:T(8,128)(2,1)S(1)} %get-tuple-element.123), channel_id=1, source_target_pairs={{0,3},{1,0},{2,1},{3,2},{4,7},{5,4},{6,5},{7,6},{8,11},{9,8},{10,9... | collective-permute-start | bytes 589832 | tf_op jit(solution)/shard_map/ppermute | solution.py:27
  110.8 9.2 %collective-permute-start.26 = (bf16[64,768]{1,0:T(8,128)(2,1)S(1)}, bf16[64,768]{1,0:T(8,128)(2,1)S(1)}, u32[]{:S(2)}, u32[]{:S(2)}) collective-permute-start(bf16[64,768]{1,0:T(8,128)(2,1)S(1)} %get-tuple-element.128), channel_id=1, source_target_pairs={{0,24},{4,28},{8,16},{12,20},{16,8},{20,12},{24,0},{28,4},{1,25},{... | collective-permute-start | bytes 294920 | tf_op jit(solution)/shard_map/ppermute | solution.py:22
  120.8 17.3 %collective-permute-start.27 = (bf16[256,768]{1,0:T(8,128)(2,1)}, bf16[256,768]{1,0:T(8,128)(2,1)}, u32[]{:S(2)}, u32[]{:S(2)}) collective-permute-start(bf16[256,768]{1,0:T(8,128)(2,1)} %pack.2.refs_0_), channel_id=1, source_target_pairs={{0,2},{1,3},{2,0},{3,1},{4,6},{5,7},{6,4},{7,5},{8,10},{9,11},{10,... | collective-permute-start | bytes 1179656 | tf_op jit(solution)/shard_map/ppermute | solution.py:27
  127.8 10.2 %collective-permute-start.30 = (bf16[64,768]{1,0:T(8,128)(2,1)S(1)}, bf16[64,768]{1,0:T(8,128)(2,1)S(1)}, u32[]{:S(2)}, u32[]{:S(2)}) collective-permute-start(bf16[64,768]{1,0:T(8,128)(2,1)S(1)} %get-tuple-element.135), channel_id=1, source_target_pairs={{0,20},{4,16},{8,28},{12,24},{16,4},{20,0},{24,12},{28,8},{1,21},{... | collective-permute-start | bytes 294920 | tf_op jit(solution)/shard_map/ppermute | solution.py:22
  127.9 10.1 %collective-permute-start.31 = (bf16[64,768]{1,0:T(8,128)(2,1)S(1)}, bf16[64,768]{1,0:T(8,128)(2,1)S(1)}, u32[]{:S(2)}, u32[]{:S(2)}) collective-permute-start(bf16[64,768]{1,0:T(8,128)(2,1)S(1)} %get-tuple-element.136), channel_id=1, source_target_pairs={{0,28},{4,24},{8,20},{12,16},{16,12},{20,8},{24,4},{28,0},{1,29},{... | collective-permute-start | bytes 294920 | tf_op jit(solution)/shard_map/ppermute | solution.py:22
  138.2 13.5 %collective-permute-start.34 = (bf16[256,768]{1,0:T(8,128)(2,1)S(1)}, bf16[256,768]{1,0:T(8,128)(2,1)}, u32[]{:S(2)}, u32[]{:S(2)}) collective-permute-start(bf16[256,768]{1,0:T(8,128)(2,1)S(1)} %pack.3.refs_0_), channel_id=1, source_target_pairs={{0,2},{1,3},{2,0},{3,1},{4,6},{5,7},{6,4},{7,5},{8,10},{9,11},{10,... | collective-permute-start | bytes 1179656 | tf_op jit(solution)/shard_map/ppermute | solution.py:27
  160.3 18.6 %collective-permute-start.35 = (bf16[128,768]{1,0:T(8,128)(2,1)}, bf16[128,768]{1,0:T(8,128)(2,1)S(1)}, u32[]{:S(2)}, u32[]{:S(2)}) collective-permute-start(bf16[128,768]{1,0:T(8,128)(2,1)} %get-tuple-element.140), channel_id=1, source_target_pairs={{0,0},{1,8},{2,16},{3,24},{4,4},{5,12},{6,20},{7,28},{8,1},{9,9},{... | collective-permute-start | bytes 589832 | tf_op jit(solution)/shard_map/ppermute | solution.py:472
  162.2 16.5 %collective-permute-start.37 = (bf16[256,768]{1,0:T(8,128)(2,1)S(1)}, bf16[256,768]{1,0:T(8,128)(2,1)S(1)}, u32[]{:S(2)}, u32[]{:S(2)}) collective-permute-start(bf16[256,768]{1,0:T(8,128)(2,1)S(1)} %fusion.3), channel_id=1, source_target_pairs={{0,2},{1,3},{2,0},{3,1},{4,6},{5,7},{6,4},{7,5},{8,10},{9,11},{10,... | collective-permute-start | bytes 1179656 | tf_op jit(solution)/shard_map/ppermute | solution.py:27
  186.4 12.0 %collective-permute-start.41 = (bf16[256,768]{1,0:T(8,128)(2,1)S(1)}, bf16[256,768]{1,0:T(8,128)(2,1)S(1)}, u32[]{:S(2)}, u32[]{:S(2)}) collective-permute-start(bf16[256,768]{1,0:T(8,128)(2,1)S(1)} %fusion.4), channel_id=1, source_target_pairs={{0,2},{1,3},{2,0},{3,1},{4,6},{5,7},{6,4},{7,5},{8,10},{9,11},{10,... | collective-permute-start | bytes 1179656 | tf_op jit(solution)/shard_map/ppermute | solution.py:27
  189.0 11.6 %collective-permute-start.43 = (bf16[64,768]{1,0:T(8,128)(2,1)S(1)}, bf16[64,768]{1,0:T(8,128)(2,1)S(1)}, u32[]{:S(2)}, u32[]{:S(2)}) collective-permute-start(bf16[64,768]{1,0:T(8,128)(2,1)S(1)} %get-tuple-element.149), channel_id=1, source_target_pairs={{0,8},{4,12},{8,0},{12,4},{16,24},{20,28},{24,16},{28,20},{1,9},{5... | collective-permute-start | bytes 294920 | tf_op jit(solution)/shard_map/ppermute | solution.py:22
  189.5 13.8 %collective-permute-start.45 = (bf16[64,768]{1,0:T(8,128)(2,1)S(1)}, bf16[64,768]{1,0:T(8,128)(2,1)S(1)}, u32[]{:S(2)}, u32[]{:S(2)}) collective-permute-start(bf16[64,768]{1,0:T(8,128)(2,1)S(1)} %get-tuple-element.150), channel_id=1, source_target_pairs={{0,16},{4,20},{8,24},{12,28},{16,0},{20,4},{24,8},{28,12},{1,17},{... | collective-permute-start | bytes 294920 | tf_op jit(solution)/shard_map/ppermute | solution.py:22
  190.1 15.3 %collective-permute-start.47 = (bf16[64,768]{1,0:T(8,128)(2,1)S(1)}, bf16[64,768]{1,0:T(8,128)(2,1)S(1)}, u32[]{:S(2)}, u32[]{:S(2)}) collective-permute-start(bf16[64,768]{1,0:T(8,128)(2,1)S(1)} %get-tuple-element.151), channel_id=1, source_target_pairs={{0,24},{4,28},{8,16},{12,20},{16,8},{20,12},{24,0},{28,4},{1,25},{... | collective-permute-start | bytes 294920 | tf_op jit(solution)/shard_map/ppermute | solution.py:22
  200.6 10.9 %collective-permute-start.46 = (bf16[64,768]{1,0:T(8,128)(2,1)S(1)}, bf16[64,768]{1,0:T(8,128)(2,1)S(1)}, u32[]{:S(2)}, u32[]{:S(2)}) collective-permute-start(bf16[64,768]{1,0:T(8,128)(2,1)S(1)} %get-tuple-element.157), channel_id=1, source_target_pairs={{0,20},{4,16},{8,28},{12,24},{16,4},{20,0},{24,12},{28,8},{1,21},{... | collective-permute-start | bytes 294920 | tf_op jit(solution)/shard_map/ppermute | solution.py:22
  (35 other events, 399.9 us)

commit v7 on v6

--- a/solution.py
+++ b/solution.py
@@ -14,7 +14,7 @@
 BF16 = jnp.bfloat16
 HIGHEST = lax.Precision.HIGHEST
 SMALL_VMEM = 12 * 1024 * 1024
-EXPERT_VMEM = 40 * 1024 * 1024
+EXPERT_VMEM = 48 * 1024 * 1024
 
 
 def permute_seq(value, move):
@@ -50,15 +50,8 @@
     return rows, held, extra
 
 
-def state_kernel(me_ref, doc_ref, decay_ref, k_hbm, v_hbm, *refs):
-    outs, (sum_ref, sum_rows_ref, doc_out_ref) = refs[:-7], refs[-7:-4]
-    state_ref, k_ref, v_ref, sems = refs[-4:]
-    fetches = [
-        pltpu.make_async_copy(k_hbm, k_ref, sems.at[0]),
-        pltpu.make_async_copy(v_hbm, v_ref, sems.at[1]),
-    ]
-    for fetch in fetches:
-        fetch.start()
+def state_kernel(me_ref, doc_ref, decay_ref, k_ref, v_ref, *refs):
+    outs, (sum_ref, sum_rows_ref, doc_out_ref, state_ref) = refs[:-4], refs[-4:]
     heads, tokens = decay_ref.shape
     n_seq, hw = len(outs), outs[0].shape[1]
     rows, held, extra = chunk_plan(heads, hw, n_seq)
@@ -83,8 +76,6 @@
     gain = jnp.exp(final) * (doc[:, :1] == last).astype(F32)
     lane = lax.broadcasted_iota(jnp.int32, (1, heads), 1)
     line = lax.broadcasted_iota(jnp.int32, (extra, hw), 0)
-    for fetch in fetches:
-        fetch.wait()
     for d in reversed(range(n_seq)):
         chunk = me_ref[0] ^ d
         note = jnp.where(line == 2 * held, doc[:, :1], 0.0)
@@ -134,35 +125,9 @@
         outs[d][...] = entered_ref[me_ref[0] ^ d]
 
 
-def inside_kernel(doc_ref, sum_ref, sum_rows_ref, q_hbm, k_hbm, v_hbm, out_ref, *scratch):
-    q_ref, k_ref, v_ref, sems = scratch
-    fetches = [
-        pltpu.make_async_copy(source, target, sems.at[i])
-        for i, (source, target) in enumerate(zip((q_hbm, k_hbm, v_hbm), scratch))
-    ]
-    for fetch in fetches:
-        fetch.start()
-    tokens, heads = sum_ref.shape
-    hw = q_hbm.shape[1] // heads
-    doc = doc_ref[...]
-    row = lax.broadcasted_iota(jnp.int32, (tokens, tokens), 0)
-    col = lax.broadcasted_iota(jnp.int32, (tokens, tokens), 1)
-    kept = (col <= row) & (doc_column(doc) == doc)
-    for fetch in fetches:
-        fetch.wait()
-    for i in range(heads):
-        lanes = slice(i * hw, (i + 1) * hw)
-        gap = sum_ref[:, i : i + 1] - sum_rows_ref[i : i + 1, :]
-        fade = jnp.where(kept, jnp.exp(jnp.minimum(gap, 0.0)), 0.0)
-        scores = lax.dot_general(
-            q_ref[:, lanes], k_ref[:, lanes], (((1,), (1,)), ((), ())), preferred_element_type=F32
-        )
-        out_ref[:, lanes] = jnp.dot(
-            (scores * fade).astype(BF16), v_ref[:, lanes], preferred_element_type=F32
-        )
-
-
-def outside_kernel(me_ref, doc_ref, sum_ref, q_ref, inside_ref, gain_ref, *refs):
+def attend_kernel(
+    me_ref, doc_ref, sum_ref, sum_rows_ref, q_ref, k_ref, v_ref, gain_ref, *refs
+):
     ins, out_ref, carried_ref = refs[:-2], refs[-2], refs[-1]
     tokens, heads = sum_ref.shape
     hw = q_ref.shape[1] // heads
@@ -171,20 +136,36 @@
         start = pl.multiple_of((me_ref[0] ^ d) * rows, rows)
         carried_ref[pl.ds(start, rows), :] = ins[d][...]
     doc = doc_ref[...]
-    reach = jnp.exp(sum_ref[...]) * (doc_column(doc)[:, :1] == doc[:, :1]).astype(F32)
+    column = doc_column(doc)
+    row = lax.broadcasted_iota(jnp.int32, (tokens, tokens), 0)
+    col = lax.broadcasted_iota(jnp.int32, (tokens, tokens), 1)
+    kept = (col <= row) & (column == doc)
+    reach = jnp.exp(sum_ref[...]) * (column[:, :1] == doc[:, :1]).astype(F32)
     for i in range(heads):
         lanes = slice(i * hw, (i + 1) * hw)
+        gap = sum_ref[:, i : i + 1] - sum_rows_ref[i : i + 1, :]
+        fade = jnp.where(kept, jnp.exp(jnp.minimum(gap, 0.0)), 0.0)
+        scores = lax.dot_general(
+            q_ref[:, lanes], k_ref[:, lanes], (((1,), (1,)), ((), ())), preferred_element_type=F32
+        )
+        raw = jnp.dot((scores * fade).astype(BF16), v_ref[:, lanes], preferred_element_type=F32)
         outside = jnp.dot(q_ref[:, lanes], carried_ref[lanes, :], preferred_element_type=F32)
-        raw = inside_ref[:, lanes] + outside * reach[:, i : i + 1]
+        raw = raw + outside * reach[:, i : i + 1]
         scale = lax.rsqrt(jnp.mean(raw * raw, axis=1, keepdims=True) + EPSILON)
         out_ref[:, lanes] = (raw * scale * gain_ref[:, lanes]).astype(BF16)
 
 
-def pack_kernel(*refs):
+def pack_kernel(me_ref, gain_ref, *refs):
     ins, out_ref = refs[:-1], refs[-1]
-    count = ins[0].shape[0]
-    for k in range(len(ins)):
-        out_ref[k * count : (k + 1) * count, :] = ins[k][...]
+    part, depth = ins[0].shape[1], out_ref.shape[1]
+    squares = 0.0
+    for ref in ins:
+        value = ref[...].astype(F32)
+        squares = squares + jnp.sum(value * value, axis=1, keepdims=True)
+    scale = lax.rsqrt(squares / depth + EPSILON)
+    for k, ref in enumerate(ins):
+        lanes = pl.ds(pl.multiple_of((me_ref[0] ^ k) * part, 128), part)
+        out_ref[:, lanes] = (ref[...].astype(F32) * scale * gain_ref[:, lanes]).astype(BF16)
 
 
 def route_kernel(shifts, me_ref, *refs):
@@ -272,24 +253,13 @@
     return copies
 
 
-def fill_hidden(n_head, aligned, owner_ref, pieces, gain_ref, rows_ref, wide_ref, hidden_ref, copies):
-    depth, units = gain_ref.shape[1], hidden_ref.shape[1]
-    part = pieces[0].shape[1]
-    nz = depth // part
-    count = pieces[0].shape[0] // nz
+def fill_hidden(aligned, owner_ref, pieces, rows_ref, wide_ref, hidden_ref, copies):
     steps = len(copies) // 2
-    width = units // steps
+    width = hidden_ref.shape[1] // steps
+    count = pieces[0].shape[0]
     for i, piece in enumerate(pieces):
-        squares = 0.0
-        for k in range(nz):
-            value = piece[k * count : (k + 1) * count, :].astype(F32)
-            squares = squares + jnp.sum(value * value, axis=1, keepdims=True)
-        scale = lax.rsqrt(squares / depth + EPSILON)
         lines = pl.ds(pl.multiple_of(owner_ref[i] * count, count), count)
-        for k in range(nz):
-            lanes = pl.ds(pl.multiple_of((owner_ref[2 * n_head] ^ k) * part, 128), part)
-            value = piece[k * count : (k + 1) * count, :].astype(F32) * scale * gain_ref[:, lanes]
-            rows_ref[lines, lanes] = value.astype(BF16)
+        rows_ref[lines, :] = piece[...]
     for j in range(steps):
         copies[2 * j].wait()
         copies[2 * j + 1].wait()
@@ -314,25 +284,13 @@
             kept_ref[j - nx] = out
 
 
-def expert_kernel(n_head, steps, aligned, owner_ref, *refs):
-    pieces, gain_ref = refs[:n_head], refs[n_head]
-    gate_ref, up_ref, down_ref, sent_ref, kept_ref = refs[n_head + 1 : n_head + 6]
-    rows_ref, hidden_ref, wide_ref, low_ref, wide_sem, low_sem = refs[n_head + 6 :]
-    wide = wide_copies(gate_ref, up_ref, wide_ref, wide_sem, steps, aligned)
-    low = low_copies(n_head, owner_ref, down_ref, low_ref, low_sem)
-    for copy in wide + low:
-        copy.start()
-    fill_hidden(n_head, aligned, owner_ref, pieces, gain_ref, rows_ref, wide_ref, hidden_ref, wide)
-    write_out(hidden_ref, low_ref, sent_ref, kept_ref, low)
-
-
 def hidden_kernel(n_head, steps, aligned, owner_ref, *refs):
-    pieces, gain_ref = refs[:n_head], refs[n_head]
-    gate_ref, up_ref, hidden_ref, rows_ref, wide_ref, wide_sem = refs[n_head + 1 :]
+    pieces = refs[:n_head]
+    gate_ref, up_ref, hidden_ref, rows_ref, wide_ref, wide_sem = refs[n_head:]
     wide = wide_copies(gate_ref, up_ref, wide_ref, wide_sem, steps, aligned)
     for copy in wide:
         copy.start()
-    fill_hidden(n_head, aligned, owner_ref, pieces, gain_ref, rows_ref, wide_ref, hidden_ref, wide)
+    fill_hidden(aligned, owner_ref, pieces, rows_ref, wide_ref, hidden_ref, wide)
 
 
 def down_kernel(n_head, owner_ref, hidden_ref, down_ref, sent_ref, kept_ref, low_ref, low_sem):
@@ -342,11 +300,10 @@
     write_out(hidden_ref, low_ref, sent_ref, kept_ref, low)
 
 
-def expert_call(owners, pieces, norm_gain, gate_weight, up_weight, down_weight, before_down=None):
+def expert_call(owners, pieces, gate_weight, up_weight, down_weight, before_down):
     n_head = len(pieces)
-    lines, part = pieces[0].shape
     _, depth, units = gate_weight.shape
-    count = lines * part * n_head // depth
+    count, part = pieces[0].shape[0] * n_head, depth // n_head
     width = next((w for w in (384, 256, 128) if units % w == 0), units)
     aligned = width % 128 == 0
     steps, nx = units // width, n_head // CORES
@@ -358,24 +315,6 @@
     outs = [struct((nx, count, part), BF16), struct((n_head - nx, count, part), BF16)]
     hidden = struct((count, units), BF16)
     work = 2 * count * depth * units
-    gain = norm_gain.reshape(1, depth)
-    if before_down is None:
-        return local_call(
-            functools.partial(expert_kernel, n_head, steps, aligned),
-            "expert",
-            outs,
-            3 * work,
-            owners,
-            *pieces,
-            gain,
-            gate_weight,
-            up_weight,
-            down_weight,
-            scratch=[rows, pltpu.VMEM(hidden.shape, BF16), wide, low, wide_sem, low_sem],
-            scalars=1,
-            far=3,
-            vmem=EXPERT_VMEM,
-        )
     hidden = local_call(
         functools.partial(hidden_kernel, n_head, steps, aligned),
         "hidden",
@@ -383,7 +322,6 @@
         2 * work,
         owners,
         *pieces,
-        gain,
         gate_weight,
         up_weight,
         scratch=[rows, wide, wide_sem],
@@ -477,7 +415,6 @@
     doc_row = doc_ids.reshape(1, tokens)
     rows, held, extra = chunk_plan(heads, hw, n_seq)
     work = 2 * tokens * hw * hw * heads
-    whole = pltpu.VMEM((tokens, heads * hw), BF16)
     *payload, decay_sum, decay_rows, doc_float = local_call(
         state_kernel,
         "block_state",
@@ -489,13 +426,14 @@
         log_decay.T,
         key_vectors,
         value_vectors,
-        scratch=[pltpu.VMEM((hw, hw), F32), whole, whole, pltpu.SemaphoreType.DMA((2,))],
+        scratch=[pltpu.VMEM((hw, hw), F32)],
         scalars=1,
-        far=2,
     )
     lanes = max(128, routing.shape[1])
     ids = jnp.pad(routing.astype(BF16), ((0, 0), (0, lanes - routing.shape[1])))
-    there = crossed(jnp.concatenate([residual, ids], axis=1))
+    there = jnp.concatenate([residual, ids], axis=1)
+    payload, there = lax.optimization_barrier((payload, there))
+    there = crossed(there)
     arrived, there = lax.optimization_barrier((swap_seq(payload), there))
     entered = local_call(
         scan_kernel,
@@ -511,30 +449,18 @@
         scalars=1,
     )
     carried = swap_seq(entered)
-    inside = local_call(
-        inside_kernel,
-        "inside",
-        struct((tokens, heads * hw), F32),
-        2 * work,
+    attended = local_call(
+        attend_kernel,
+        "attend",
+        struct((tokens, heads * hw), BF16),
+        3 * work,
+        me,
         doc_float,
         decay_sum,
         decay_rows,
         queries,
         key_vectors,
         value_vectors,
-        scratch=[whole, whole, whole, pltpu.SemaphoreType.DMA((3,))],
-        far=3,
-    )
-    attended = local_call(
-        outside_kernel,
-        "outside",
-        struct((tokens, heads * hw), BF16),
-        work,
-        me,
-        doc_float,
-        decay_sum,
-        queries,
-        inside,
         head_gain.reshape(1, heads * hw),
         *carried,
         scratch=[pltpu.VMEM((heads * hw, hw), BF16)],
@@ -542,31 +468,32 @@
     )
 
     attended, output_weight = lax.optimization_barrier((attended, output_weight))
+    cols = output_weight.shape[1]
+    w_z = jnp.zeros((output_weight.shape[0], ny * cols), BF16)
+    w_z = lax.dynamic_update_slice(w_z, output_weight, (0, y * cols))
+    for k in range(1, ny):
+        got = permute_seq(output_weight, lambda q, k=k: q // ny * ny + (q % ny - k) % ny)
+        w_z = lax.dynamic_update_slice(w_z, got, (0, (y + k) % ny * cols))
+
+    def along(value, pairs):
+        perm = [(a * ny + yy, b * ny + yy) for a, b in pairs for yy in range(ny)]
+        return lax.ppermute(value, "seq", perm)
+
+    ups = lambda j: [(q, q + j) for q in range(nz - j)]
+    downs = lambda j: [(q + j, q) for q in range(nz - j)]
+    below, above = along(attended, ups(1)), along(attended, downs(1))
+    direct, there, own_routing = lax.optimization_barrier(
+        (attended, there, routing, below, above)
+    )[:3]
     residual_there = there[:, :part]
     routing_there = there[:, part : part + routing.shape[1]].astype(jnp.int32)
     slot = jnp.arange(experts * capacity, dtype=jnp.int32)
     slot = (slot // capacity ^ s) * capacity + slot % capacity
     place = slot_places(routing_there, experts, capacity)
     take = jnp.any(place[:, None, :] == slot[None, :, None], axis=2).astype(BF16).T
-    place = slot_places(routing, experts, capacity)
+    place = slot_places(own_routing, experts, capacity)
     here = place[:, None, :] == slot[None, :, None]
     mix = jnp.sum(jnp.where(here, route_weights[:, None, :], 0.0), axis=2)
-
-    cols = output_weight.shape[1]
-    w_z = jnp.zeros((output_weight.shape[0], ny * cols), BF16)
-    w_z = lax.dynamic_update_slice(w_z, output_weight, (0, y * cols))
-    for k in range(1, ny):
-        got = permute_seq(output_weight, lambda q, k=k: q // ny * ny + (q % ny - k) % ny)
-        w_z = lax.dynamic_update_slice(w_z, got, (0, (y + k) % ny * cols))
-
-    def along(value, pairs):
-        perm = [(a * ny + yy, b * ny + yy) for a, b in pairs for yy in range(ny)]
-        return lax.ppermute(value, "seq", perm)
-
-    ups = lambda j: [(q, q + j) for q in range(nz - j)]
-    downs = lambda j: [(q + j, q) for q in range(nz - j)]
-    below, above = along(attended, ups(1)), along(attended, downs(1))
-    direct = lax.optimization_barrier((attended, below, above))[0]
     shifts, rows_of = [(0, 0), (1, 0), (0, 1)], [attended, below, above]
     if nz > 2:
         shifts += [(2, 0), (0, 2)]
@@ -626,7 +553,14 @@
             for k in range(nz)
         ]
         got = local_call(
-            pack_kernel, "pack", struct((nz * capacity, part), BF16), count * part, *arrived
+            pack_kernel,
+            "pack",
+            struct((capacity, model_width), BF16),
+            count * part,
+            z.astype(jnp.int32).reshape(1),
+            norm_gain.reshape(1, model_width),
+            *arrived,
+            scalars=1,
         )
         gots.append(got)
         fars.append(
@@ -634,8 +568,6 @@
         )
     for group in range(ny):
         got, far = gots[group], fars[group]
-        if group:
-            far = lax.optimization_barrier((far, sent))[0]
         if group + 1 < ny:
             far = lax.optimization_barrier((far, gots[group + 1]))[0]
         pieces = [got, *far]
@@ -646,14 +578,10 @@
                         piece, lambda q, m=m: q // CORES * CORES + (q % CORES - m) % CORES
                     )
                 )
-        if group:
-            pieces = lax.optimization_barrier((pieces, crossing))[0]
-        first = [blocks, middle] if group else None
+        first = [crossing, middle] if group else None
         if group + 1 < ny:
             first = (first, fars[group + 1])
-        sent, kept = expert_call(
-            owners, pieces, norm_gain, gate_weight, up_weight, down_weight, first
-        )
+        sent, kept = expert_call(owners, pieces, gate_weight, up_weight, down_weight, first)
         if group == 0:
             middle = crossed(lax.optimization_barrier((middle_there, sent))[0])
 

time: 213 us -> 221 us (1.038)
  waiting for transfers between devices: 68.7 us -> 83.1 us
  local copies, waits for them, and re-layouts: 18.8 us -> 13.2 us
  matrix products: 4.03 us -> 6.98 us
    ppermute x29, waiting for transfers between devices: 30.7 us -> 48.3 us  [permute_seq(): lax.ppermute(value, 'seq', [(source, move(source)) for source in range(co...]
    ppermute x5, waiting for transfers between devices: 18.8 us -> 12.3 us  [along(): return lax.ppermute(value, 'seq', perm)]
    unnamed x37 -> x28, local copies, waits for them, and re-layouts: 13.4 us -> 7.48 us
    ppermute x13, waiting for transfers between devices: 19.2 us -> 22.5 us  [permute_head(): lax.ppermute(value, 'head', [(source, move(source)) for source in range(c...]
    dot_general x6, matrix products: 3.64 us -> 6.58 us  [shards(): jnp.dot(r, w_z, preferred_element_type=F32).astype(BF16)]
    pallas_call x15 -> x14, Pallas kernels: 35.9 us -> 33.8 us  [local_call(): pl.pallas_call(kernel, out_shape=out_shape, in_specs=[pl.BlockSpec(memory...]
  transfers between devices with their start and end apart: 49 -> 49, of which waited for: 20 -> 24; matrix products, arithmetic and copies ran while one was open for 6% -> 6% of each run, Pallas kernels for 10% -> 7%
where the time goes in v7:
time: 221 us
  waiting for transfers between devices  83.1 us (38%)
  starting transfers between devices  78.9 us (36%)
  Pallas kernels  33.8 us (15%)
  local copies, waits for them, and re-layouts  13.2 us (6%)
  matrix products  6.98 us (3%)
  other arithmetic  3.92 us (2%)
    ppermute x29, starting transfers between devices, permute_seq(): lax.ppermute(value, 'seq', [(source, move(source)) for source in range(co...  51.9 us
    ppermute x29, waiting for transfers between devices, permute_seq(): lax.ppermute(value, 'seq', [(source, move(source)) for source in range(co...  48.3 us
    pallas_call x14, Pallas kernels, local_call(): pl.pallas_call(kernel, out_shape=out_shape, in_specs=[pl.BlockSpec(memory...  33.8 us
    ppermute x13, waiting for transfers between devices, permute_head(): lax.ppermute(value, 'head', [(source, move(source)) for source in range(c...  22.5 us
    ppermute x5, starting transfers between devices, along(): return lax.ppermute(value, 'seq', perm)  12.6 us
    ppermute x5, waiting for transfers between devices, along(): return lax.ppermute(value, 'seq', perm)  12.3 us
    ppermute x13, starting transfers between devices, permute_head(): lax.ppermute(value, 'head', [(source, move(source)) for source in range(c...  12.2 us
    unnamed x28, local copies, waits for them, and re-layouts  7.48 us
  transfers between devices with their start and end apart: 49, of which 24 were waited for; matrix products, arithmetic and copies ran while one was open for 6% of the time, Pallas kernels for 7%

profile of v7, /device:TPU:0, one launch (start us, length us, event | category | flops | bytes accessed | tf_op | source)
XLA Modules:
  0.0 220.6 jit_solution(14947435677820215747)
XLA Ops:
  7.5 3.0 %collective-permute-start = (bf16[272,128]{1,0:T(8,128)(2,1)S(1)}, bf16[272,128]{1,0:T(8,128)(2,1)S(1)}, u32[]{:S(2)}, u32[]{:S(2)}) collective-permute-start(bf16[272,128]{1,0:T(8,128)(2,1)S(1)} %get-tuple-element.100), channel_id=1, source_target_pairs={{0,4},{4,0},{8,12},{12,8},{16,20},{20,16},{24,28},{28,24},{1,5},{5... | collective-permute-start | bytes 208904 | tf_op jit(solution)/shard_map/ppermute | solution.py:22
  12.7 4.2 %collective-permute-start.3 = (bf16[272,128]{1,0:T(8,128)(2,1)S(1)}, bf16[272,128]{1,0:T(8,128)(2,1)S(1)}, u32[]{:S(2)}, u32[]{:S(2)}) collective-permute-start(bf16[272,128]{1,0:T(8,128)(2,1)S(1)} %get-tuple-element.103), channel_id=1, source_target_pairs={{0,16},{4,20},{8,24},{12,28},{16,0},{20,4},{24,8},{28,12},{1,17},{... | collective-permute-start | bytes 208904 | tf_op jit(solution)/shard_map/ppermute | solution.py:22
  18.7 2.4 %collective-permute-start.5 = (bf16[272,128]{1,0:T(8,128)(2,1)S(1)}, bf16[272,128]{1,0:T(8,128)(2,1)S(1)}, u32[]{:S(2)}, u32[]{:S(2)}) collective-permute-start(bf16[272,128]{1,0:T(8,128)(2,1)S(1)} %get-tuple-element.105), channel_id=1, source_target_pairs={{0,24},{4,28},{8,16},{12,20},{16,8},{20,12},{24,0},{28,4},{1,25},{... | collective-permute-start | bytes 208904 | tf_op jit(solution)/shard_map/ppermute | solution.py:22
  24.2 7.9 %collective-permute-done.3.refs_4_ = bf16[272,128]{1,0:T(8,128)(2,1)S(1)} collective-permute-done((bf16[272,128]{1,0:T(8,128)(2,1)S(1)}, bf16[272,128]{1,0:T(8,128)(2,1)S(1)}, u32[]{:S(2)}, u32[]{:S(2)}) %collective-permute-start.3) | collective-permute-done | bytes 69664 | tf_op jit(solution)/shard_map/ppermute | solution.py:22
  32.1 2.4 %collective-permute-done.4.refs_5_ = bf16[272,128]{1,0:T(8,128)(2,1)S(1)} collective-permute-done((bf16[272,128]{1,0:T(8,128)(2,1)S(1)}, bf16[272,128]{1,0:T(8,128)(2,1)S(1)}, u32[]{:S(2)}, u32[]{:S(2)}) %collective-permute-start.4) | collective-permute-done | bytes 69664 | tf_op jit(solution)/shard_map/ppermute | solution.py:22
  34.8 3.2 %collective-permute-start.10 = (bf16[256,128]{1,0:T(8,128)(2,1)S(1)}, bf16[256,128]{1,0:T(8,128)(2,1)S(1)}, u32[]{:S(2)}, u32[]{:S(2)}) collective-permute-start(bf16[256,128]{1,0:T(8,128)(2,1)S(1)} %get-tuple-element.119), channel_id=1, source_target_pairs={{0,12},{4,8},{8,4},{12,0},{16,28},{20,24},{24,20},{28,16},{1,13},{... | collective-permute-start | bytes 196616 | tf_op jit(solution)/shard_map/ppermute | solution.py:22
  38.0 3.9 %collective-permute-start.12 = (bf16[256,128]{1,0:T(8,128)(2,1)S(1)}, bf16[256,128]{1,0:T(8,128)(2,1)S(1)}, u32[]{:S(2)}, u32[]{:S(2)}) collective-permute-start(bf16[256,128]{1,0:T(8,128)(2,1)S(1)} %get-tuple-element.121), channel_id=1, source_target_pairs={{0,20},{4,16},{8,28},{12,24},{16,4},{20,0},{24,12},{28,8},{1,21},{... | collective-permute-start | bytes 196616 | tf_op jit(solution)/shard_map/ppermute | solution.py:22
  41.9 3.8 %collective-permute-start.14 = (bf16[256,128]{1,0:T(8,128)(2,1)S(1)}, bf16[256,128]{1,0:T(8,128)(2,1)S(1)}, u32[]{:S(2)}, u32[]{:S(2)}) collective-permute-start(bf16[256,128]{1,0:T(8,128)(2,1)S(1)} %get-tuple-element.123), channel_id=1, source_target_pairs={{0,28},{4,24},{8,20},{12,16},{16,12},{20,8},{24,4},{28,0},{1,29},{... | collective-permute-start | bytes 196616 | tf_op jit(solution)/shard_map/ppermute | solution.py:22
  47.1 2.6 %collective-permute-done.12.refs_5_ = bf16[256,128]{1,0:T(8,128)(2,1)S(1)} collective-permute-done((bf16[256,128]{1,0:T(8,128)(2,1)S(1)}, bf16[256,128]{1,0:T(8,128)(2,1)S(1)}, u32[]{:S(2)}, u32[]{:S(2)}) %collective-permute-start.12) | collective-permute-done | bytes 65568 | tf_op jit(solution)/shard_map/ppermute | solution.py:22
  55.2 2.9 %attend.1 = bf16[128,2048]{1,0:T(8,128)(2,1)S(1)} custom-call(s32[1]{0:T(128)} %bitcast.me_ref, f32[1,128]{1,0:T(1,128)S(1)} %get-tuple-element.88.doc_ref, f32[128,16]{1,0:T(8,128)S(1)} %get-tuple-element.89.sum_ref, f32[16,128]{1,0:T(8,128)S(1)} %get-tuple-element.90.sum_rows_ref, bf16[128,2048]{1,0:T(8,128)(2,1)S(1)} %copy-done.4, ...), custom_call_target="tpu_custom_call" | custom-call | flops 201326592 | bytes 2646532 | tf_op jit(solution)/shard_map/attend/pallas_call | solution.py:353
  58.1 3.5 %collective-permute-start.15 = (bf16[128,2048]{1,0:T(8,128)(2,1)S(1)}, bf16[128,2048]{1,0:T(8,128)(2,1)S(1)}, u32[]{:S(2)}, u32[]{:S(2)}) collective-permute-start(bf16[128,2048]{1,0:T(8,128)(2,1)S(1)} %attend.1), channel_id=1, source_target_pairs={{0,8},{4,12},{8,16},{12,20},{16,24},{20,28},{1,9},{5,13},{9,17},{1... | collective-permute-start | bytes 1572872 | tf_op jit(solution)/shard_map/ppermute | solution.py:480
  64.8 8.1 %collective-permute-done.15 = bf16[128,2048]{1,0:T(8,128)(2,1)S(1)} collective-permute-done((bf16[128,2048]{1,0:T(8,128)(2,1)S(1)}, bf16[128,2048]{1,0:T(8,128)(2,1)S(1)}, u32[]{:S(2)}, u32[]{:S(2)}) %collective-permute-start.15) | collective-permute-done | bytes 524320 | tf_op jit(solution)/shard_map/ppermute | solution.py:480
  72.9 4.1 %collective-permute-done.16 = bf16[128,2048]{1,0:T(8,128)(2,1)S(1)} collective-permute-done((bf16[128,2048]{1,0:T(8,128)(2,1)S(1)}, bf16[128,2048]{1,0:T(8,128)(2,1)S(1)}, u32[]{:S(2)}, u32[]{:S(2)}) %collective-permute-start.16) | collective-permute-done | bytes 524320 | tf_op jit(solution)/shard_map/ppermute | solution.py:480
  83.5 4.6 %collective-permute-start.18 = (bf16[128,2048]{1,0:T(8,128)(2,1)S(1)}, bf16[128,2048]{1,0:T(8,128)(2,1)S(1)}, u32[]{:S(2)}, u32[]{:S(2)}) collective-permute-start(bf16[128,2048]{1,0:T(8,128)(2,1)S(1)} %collective-permute-done.15), channel_id=1, source_target_pairs={{0,8},{4,12},{8,16},{12,20},{16,24},{20,28},{1,9},{5,13},{9,17},{1... | collective-permute-start | bytes 1572872 | tf_op jit(solution)/shard_map/ppermute | solution.py:480
  88.3 10.9 %collective-permute-done.17 = bf16[2048,384]{1,0:T(8,128)(2,1)} collective-permute-done((bf16[2048,384]{1,0:T(8,128)(2,1)S(1)}, bf16[2048,384]{1,0:T(8,128)(2,1)}, u32[]{:S(2)}, u32[]{:S(2)}) %collective-permute-start.17) | collective-permute-done | bytes 1572896 | tf_op jit(solution)/shard_map/ppermute | solution.py:22
  99.3 2.8 %constant_dynamic-update-slice_fusion = bf16[2048,768]{1,0:T(8,128)(2,1)} fusion(bf16[2048,768]{1,0:T(8,128)(2,1)} %copy-done.9, bf16[2048,384]{1,0:T(8,128)(2,1)} %collective-permute-done.17, s32[]{:T(128)S(6)} %select_n.98), kind=kLoop, calls=%fused_computation.47 | loop fusion | bytes 3145732 | tf_op jit(solution)/shard_map/dynamic_update_slice | solution.py:476
  102.1 2.6 %convolution_convert_fusion.5.refs_0_ = bf16[128,768]{1,0:T(8,128)(2,1)S(1)} fusion(bf16[128,2048]{1,0:T(8,128)(2,1)S(1)} %attend.1, bf16[2048,768]{1,0:T(8,128)(2,1)} %constant_dynamic-update-slice_fusion), kind=kOutput, calls=%fused_computation.7 | convolution fusion | flops 402751488 | bytes 3866624 | tf_op jit(solution)/shard_map/dot_general | solution.py:508
  112.4 3.8 %collective-permute-done.21.refs_1_ = bf16[128,768]{1,0:T(8,128)(2,1)S(1)} collective-permute-done((bf16[128,768]{1,0:T(8,128)(2,1)S(1)}, bf16[128,768]{1,0:T(8,128)(2,1)S(1)}, u32[]{:S(2)}, u32[]{:S(2)}) %collective-permute-start.21) | collective-permute-done | bytes 196640 | tf_op jit(solution)/shard_map/ppermute | solution.py:27
  124.4 3.5 %collective-permute-done.25.refs_2_ = bf16[64,768]{1,0:T(8,128)(2,1)S(1)} collective-permute-done((bf16[64,768]{1,0:T(8,128)(2,1)S(1)}, bf16[64,768]{1,0:T(8,128)(2,1)S(1)}, u32[]{:S(2)}, u32[]{:S(2)}) %collective-permute-start.25) | collective-permute-done | bytes 98336 | tf_op jit(solution)/shard_map/ppermute | solution.py:22
  127.9 4.0 %collective-permute-done.26.refs_3_ = bf16[64,768]{1,0:T(8,128)(2,1)S(1)} collective-permute-done((bf16[64,768]{1,0:T(8,128)(2,1)S(1)}, bf16[64,768]{1,0:T(8,128)(2,1)S(1)}, u32[]{:S(2)}, u32[]{:S(2)}) %collective-permute-start.26) | collective-permute-done | bytes 98336 | tf_op jit(solution)/shard_map/ppermute | solution.py:22
  135.5 2.6 %collective-permute-start.29 = (bf16[64,768]{1,0:T(8,128)(2,1)S(1)}, bf16[64,768]{1,0:T(8,128)(2,1)S(1)}, u32[]{:S(2)}, u32[]{:S(2)}) collective-permute-start(bf16[64,768]{1,0:T(8,128)(2,1)S(1)} %get-tuple-element.151), channel_id=1, source_target_pairs={{0,12},{4,8},{8,4},{12,0},{16,28},{20,24},{24,20},{28,16},{1,13},{... | collective-permute-start | bytes 294920 | tf_op jit(solution)/shard_map/ppermute | solution.py:22
  138.1 3.0 %collective-permute-start.31 = (bf16[64,768]{1,0:T(8,128)(2,1)S(1)}, bf16[64,768]{1,0:T(8,128)(2,1)S(1)}, u32[]{:S(2)}, u32[]{:S(2)}) collective-permute-start(bf16[64,768]{1,0:T(8,128)(2,1)S(1)} %get-tuple-element.153), channel_id=1, source_target_pairs={{0,28},{4,24},{8,20},{12,16},{16,12},{20,8},{24,4},{28,0},{1,29},{... | collective-permute-start | bytes 294920 | tf_op jit(solution)/shard_map/ppermute | solution.py:22
  141.1 7.6 %collective-permute-done.30.refs_2_ = bf16[64,768]{1,0:T(8,128)(2,1)S(1)} collective-permute-done((bf16[64,768]{1,0:T(8,128)(2,1)S(1)}, bf16[64,768]{1,0:T(8,128)(2,1)S(1)}, u32[]{:S(2)}, u32[]{:S(2)}) %collective-permute-start.30) | collective-permute-done | bytes 98336 | tf_op jit(solution)/shard_map/ppermute | solution.py:22
  150.8 8.0 %hidden.2.hidden_ref = bf16[256,1152]{1,0:T(8,128)(2,1)S(1)} custom-call(s32[9]{0:T(128)S(1)} %stack.45.owner_ref, bf16[64,3072]{1,0:T(8,128)(2,1)S(1)} %pack.2.refs_0_, bf16[64,3072]{1,0:T(8,128)(2,1)S(1)} %collective-permute-done.27.refs_1_, bf16[64,3072]{1,0:T(8,128)(2,1)S(1)} %collective-permute-done.32.refs_2_, ...), custom_call_target="tpu_custom_call" | custom-call | flops 3623878656 | bytes 16318500 | tf_op jit(solution)/shard_map/hidden/pallas_call | solution.py:353
  160.6 5.4 %down.2 = (bf16[2,256,768]{2,1,0:T(8,128)(2,1)S(1)}, bf16[2,256,768]{2,1,0:T(8,128)(2,1)S(1)}) custom-call(s32[9]{0:T(128)S(1)} %stack.45.owner_ref, bf16[256,1152]{1,0:T(8,128)(2,1)S(1)} %hidden.2.hidden_ref, bf16[1,1152,3072]{2,1,0:T(8,128)(2,1)} %down_ref.3), custom_call_target="tpu_custom_call" | custom-call | flops 1811939328 | bytes 9240612 | tf_op jit(solution)/shard_map/down/pallas_call | solution.py:353
  169.5 8.0 %hidden.3.hidden_ref = bf16[256,1152]{1,0:T(8,128)(2,1)S(1)} custom-call(s32[9]{0:T(128)S(1)} %stack.45.owner_ref, bf16[64,3072]{1,0:T(8,128)(2,1)S(1)} %pack.3.refs_0_, bf16[64,3072]{1,0:T(8,128)(2,1)S(1)} %collective-permute-done.34.refs_1_, bf16[64,3072]{1,0:T(8,128)(2,1)S(1)} %collective-permute-done.38.refs_2_, ...), custom_call_target="tpu_custom_call" | custom-call | flops 3623878656 | bytes 16318500 | tf_op jit(solution)/shard_map/hidden/pallas_call | solution.py:353
  177.8 5.4 %down.3 = (bf16[2,256,768]{2,1,0:T(8,128)(2,1)S(1)}, bf16[2,256,768]{2,1,0:T(8,128)(2,1)S(1)}) custom-call(s32[9]{0:T(128)S(1)} %stack.45.owner_ref, bf16[256,1152]{1,0:T(8,128)(2,1)S(1)} %hidden.3.hidden_ref, bf16[1,1152,3072]{2,1,0:T(8,128)(2,1)} %down_ref.3), custom_call_target="tpu_custom_call" | custom-call | flops 1811939328 | bytes 9240612 | tf_op jit(solution)/shard_map/down/pallas_call | solution.py:353
  184.3 3.8 %collective-permute-start.37 = (bf16[256,768]{1,0:T(8,128)(2,1)S(1)}, bf16[256,768]{1,0:T(8,128)(2,1)S(1)}, u32[]{:S(2)}, u32[]{:S(2)}) collective-permute-start(bf16[256,768]{1,0:T(8,128)(2,1)S(1)} %fusion.3), channel_id=1, source_target_pairs={{0,2},{1,3},{2,0},{3,1},{4,6},{5,7},{6,4},{7,5},{8,10},{9,11},{10,... | collective-permute-start | bytes 1179656 | tf_op jit(solution)/shard_map/ppermute | solution.py:27
  190.7 7.4 %collective-permute-done.37.refs_1_ = bf16[256,768]{1,0:T(8,128)(2,1)S(1)} collective-permute-done((bf16[256,768]{1,0:T(8,128)(2,1)S(1)}, bf16[256,768]{1,0:T(8,128)(2,1)S(1)}, u32[]{:S(2)}, u32[]{:S(2)}) %collective-permute-start.37) | collective-permute-done | bytes 393248 | tf_op jit(solution)/shard_map/ppermute | solution.py:27
  202.8 3.5 %collective-permute-done.41.refs_1_ = bf16[256,768]{1,0:T(8,128)(2,1)S(1)} collective-permute-done((bf16[256,768]{1,0:T(8,128)(2,1)S(1)}, bf16[256,768]{1,0:T(8,128)(2,1)S(1)}, u32[]{:S(2)}, u32[]{:S(2)}) %collective-permute-start.41) | collective-permute-done | bytes 393248 | tf_op jit(solution)/shard_map/ppermute | solution.py:27
  209.8 3.5 %collective-permute-start.48 = (bf16[64,768]{1,0:T(8,128)(2,1)S(1)}, bf16[64,768]{1,0:T(8,128)(2,1)S(1)}, u32[]{:S(2)}, u32[]{:S(2)}) collective-permute-start(bf16[64,768]{1,0:T(8,128)(2,1)S(1)} %get-tuple-element.170), channel_id=1, source_target_pairs={{0,28},{4,24},{8,20},{12,16},{16,12},{20,8},{24,4},{28,0},{1,29},{... | collective-permute-start | bytes 294920 | tf_op jit(solution)/shard_map/ppermute | solution.py:22
  214.3 5.3 %collective-permute-done.46.refs_5_ = bf16[64,768]{1,0:T(8,128)(2,1)S(1)} collective-permute-done((bf16[64,768]{1,0:T(8,128)(2,1)S(1)}, bf16[64,768]{1,0:T(8,128)(2,1)S(1)}, u32[]{:S(2)}, u32[]{:S(2)}) %collective-permute-start.46) | collective-permute-done | bytes 98336 | tf_op jit(solution)/shard_map/ppermute | solution.py:22
  (150 shorter events, 72.0 us)
Async XLA Ops:
  6.2 28.4 %collective-permute-start.7 = (bf16[128,896]{1,0:T(8,128)(2,1)S(1)}, bf16[128,896]{1,0:T(8,128)(2,1)}, u32[]{:S(2)}, u32[]{:S(2)}) collective-permute-start(bf16[128,896]{1,0:T(8,128)(2,1)S(1)} %fusion.5), channel_id=1, source_target_pairs={{0,0},{1,8},{2,16},{3,24},{4,4},{5,12},{6,20},{7,28},{8,1},{9,9},{... | collective-permute-start | bytes 688136 | tf_op jit(solution)/shard_map/ppermute | solution.py:410
  7.5 9.4 %collective-permute-start = (bf16[272,128]{1,0:T(8,128)(2,1)S(1)}, bf16[272,128]{1,0:T(8,128)(2,1)S(1)}, u32[]{:S(2)}, u32[]{:S(2)}) collective-permute-start(bf16[272,128]{1,0:T(8,128)(2,1)S(1)} %get-tuple-element.100), channel_id=1, source_target_pairs={{0,4},{4,0},{8,12},{12,8},{16,20},{20,16},{24,28},{28,24},{1,5},{5... | collective-permute-start | bytes 208904 | tf_op jit(solution)/shard_map/ppermute | solution.py:22
  12.7 9.6 %collective-permute-start.2 = (bf16[272,128]{1,0:T(8,128)(2,1)S(1)}, bf16[272,128]{1,0:T(8,128)(2,1)S(1)}, u32[]{:S(2)}, u32[]{:S(2)}) collective-permute-start(bf16[272,128]{1,0:T(8,128)(2,1)S(1)} %get-tuple-element.102), channel_id=1, source_target_pairs={{0,12},{4,8},{8,4},{12,0},{16,28},{20,24},{24,20},{28,16},{1,13},{... | collective-permute-start | bytes 208904 | tf_op jit(solution)/shard_map/ppermute | solution.py:22
  12.7 19.4 %collective-permute-start.3 = (bf16[272,128]{1,0:T(8,128)(2,1)S(1)}, bf16[272,128]{1,0:T(8,128)(2,1)S(1)}, u32[]{:S(2)}, u32[]{:S(2)}) collective-permute-start(bf16[272,128]{1,0:T(8,128)(2,1)S(1)} %get-tuple-element.103), channel_id=1, source_target_pairs={{0,16},{4,20},{8,24},{12,28},{16,0},{20,4},{24,8},{28,12},{1,17},{... | collective-permute-start | bytes 208904 | tf_op jit(solution)/shard_map/ppermute | solution.py:22
  16.9 17.6 %collective-permute-start.4 = (bf16[272,128]{1,0:T(8,128)(2,1)S(1)}, bf16[272,128]{1,0:T(8,128)(2,1)S(1)}, u32[]{:S(2)}, u32[]{:S(2)}) collective-permute-start(bf16[272,128]{1,0:T(8,128)(2,1)S(1)} %get-tuple-element.104), channel_id=1, source_target_pairs={{0,20},{4,16},{8,28},{12,24},{16,4},{20,0},{24,12},{28,8},{1,21},{... | collective-permute-start | bytes 208904 | tf_op jit(solution)/shard_map/ppermute | solution.py:22
  18.7 15.8 %collective-permute-start.5 = (bf16[272,128]{1,0:T(8,128)(2,1)S(1)}, bf16[272,128]{1,0:T(8,128)(2,1)S(1)}, u32[]{:S(2)}, u32[]{:S(2)}) collective-permute-start(bf16[272,128]{1,0:T(8,128)(2,1)S(1)} %get-tuple-element.105), channel_id=1, source_target_pairs={{0,24},{4,28},{8,16},{12,20},{16,8},{20,12},{24,0},{28,4},{1,25},{... | collective-permute-start | bytes 208904 | tf_op jit(solution)/shard_map/ppermute | solution.py:22
  22.3 12.2 %collective-permute-start.6 = (bf16[272,128]{1,0:T(8,128)(2,1)S(1)}, bf16[272,128]{1,0:T(8,128)(2,1)S(1)}, u32[]{:S(2)}, u32[]{:S(2)}) collective-permute-start(bf16[272,128]{1,0:T(8,128)(2,1)S(1)} %get-tuple-element.106), channel_id=1, source_target_pairs={{0,28},{4,24},{8,20},{12,16},{16,12},{20,8},{24,4},{28,0},{1,29},{... | collective-permute-start | bytes 208904 | tf_op jit(solution)/shard_map/ppermute | solution.py:22
  34.8 10.8 %collective-permute-start.10 = (bf16[256,128]{1,0:T(8,128)(2,1)S(1)}, bf16[256,128]{1,0:T(8,128)(2,1)S(1)}, u32[]{:S(2)}, u32[]{:S(2)}) collective-permute-start(bf16[256,128]{1,0:T(8,128)(2,1)S(1)} %get-tuple-element.119), channel_id=1, source_target_pairs={{0,12},{4,8},{8,4},{12,0},{16,28},{20,24},{24,20},{28,16},{1,13},{... | collective-permute-start | bytes 196616 | tf_op jit(solution)/shard_map/ppermute | solution.py:22
  38.0 9.2 %collective-permute-start.11 = (bf16[256,128]{1,0:T(8,128)(2,1)S(1)}, bf16[256,128]{1,0:T(8,128)(2,1)S(1)}, u32[]{:S(2)}, u32[]{:S(2)}) collective-permute-start(bf16[256,128]{1,0:T(8,128)(2,1)S(1)} %get-tuple-element.120), channel_id=1, source_target_pairs={{0,16},{4,20},{8,24},{12,28},{16,0},{20,4},{24,8},{28,12},{1,17},{... | collective-permute-start | bytes 196616 | tf_op jit(solution)/shard_map/ppermute | solution.py:22
  38.0 11.8 %collective-permute-start.12 = (bf16[256,128]{1,0:T(8,128)(2,1)S(1)}, bf16[256,128]{1,0:T(8,128)(2,1)S(1)}, u32[]{:S(2)}, u32[]{:S(2)}) collective-permute-start(bf16[256,128]{1,0:T(8,128)(2,1)S(1)} %get-tuple-element.121), channel_id=1, source_target_pairs={{0,20},{4,16},{8,28},{12,24},{16,4},{20,0},{24,12},{28,8},{1,21},{... | collective-permute-start | bytes 196616 | tf_op jit(solution)/shard_map/ppermute | solution.py:22
  58.1 14.8 %collective-permute-start.15 = (bf16[128,2048]{1,0:T(8,128)(2,1)S(1)}, bf16[128,2048]{1,0:T(8,128)(2,1)S(1)}, u32[]{:S(2)}, u32[]{:S(2)}) collective-permute-start(bf16[128,2048]{1,0:T(8,128)(2,1)S(1)} %attend.1), channel_id=1, source_target_pairs={{0,8},{4,12},{8,16},{12,20},{16,24},{20,28},{1,9},{5,13},{9,17},{1... | collective-permute-start | bytes 1572872 | tf_op jit(solution)/shard_map/ppermute | solution.py:480
  61.7 15.4 %collective-permute-start.16 = (bf16[128,2048]{1,0:T(8,128)(2,1)S(1)}, bf16[128,2048]{1,0:T(8,128)(2,1)S(1)}, u32[]{:S(2)}, u32[]{:S(2)}) collective-permute-start(bf16[128,2048]{1,0:T(8,128)(2,1)S(1)} %attend.1), channel_id=1, source_target_pairs={{8,0},{12,4},{16,8},{20,12},{24,16},{28,20},{9,1},{13,5},{17,9},{2... | collective-permute-start | bytes 1572872 | tf_op jit(solution)/shard_map/ppermute | solution.py:480
  63.1 36.1 %collective-permute-start.17 = (bf16[2048,384]{1,0:T(8,128)(2,1)S(1)}, bf16[2048,384]{1,0:T(8,128)(2,1)}, u32[]{:S(2)}, u32[]{:S(2)}) collective-permute-start(bf16[2048,384]{1,0:T(8,128)(2,1)S(1)} %copy-done.11), channel_id=1, source_target_pairs={{0,4},{4,0},{8,12},{12,8},{16,20},{20,16},{24,28},{28,24},{1,5},{5... | collective-permute-start | bytes 4718600 | tf_op jit(solution)/shard_map/ppermute | solution.py:22
  77.1 29.0 %collective-permute-start.20 = (bf16[128,2048]{1,0:T(8,128)(2,1)S(1)}, bf16[128,2048]{1,0:T(8,128)(2,1)}, u32[]{:S(2)}, u32[]{:S(2)}) collective-permute-start(bf16[128,2048]{1,0:T(8,128)(2,1)S(1)} %attend.1), channel_id=1, source_target_pairs={{0,24},{4,28},{24,0},{28,4},{1,25},{5,29},{25,1},{29,5},{2,26},{6,... | collective-permute-start | bytes 1572872 | tf_op jit(solution)/shard_map/ppermute | solution.py:480
  82.2 25.5 %collective-permute-start.19 = (bf16[128,2048]{1,0:T(8,128)(2,1)S(1)}, bf16[128,2048]{1,0:T(8,128)(2,1)S(1)}, u32[]{:S(2)}, u32[]{:S(2)}) collective-permute-start(bf16[128,2048]{1,0:T(8,128)(2,1)S(1)} %collective-permute-done.16), channel_id=1, source_target_pairs={{8,0},{12,4},{16,8},{20,12},{24,16},{28,20},{9,1},{13,5},{17,9},{2... | collective-permute-start | bytes 1572872 | tf_op jit(solution)/shard_map/ppermute | solution.py:480
  83.5 24.8 %collective-permute-start.18 = (bf16[128,2048]{1,0:T(8,128)(2,1)S(1)}, bf16[128,2048]{1,0:T(8,128)(2,1)S(1)}, u32[]{:S(2)}, u32[]{:S(2)}) collective-permute-start(bf16[128,2048]{1,0:T(8,128)(2,1)S(1)} %collective-permute-done.15), channel_id=1, source_target_pairs={{0,8},{4,12},{8,16},{12,20},{16,24},{20,28},{1,9},{5,13},{9,17},{1... | collective-permute-start | bytes 1572872 | tf_op jit(solution)/shard_map/ppermute | solution.py:480
  110.1 8.9 %collective-permute-start.23 = (bf16[128,768]{1,0:T(8,128)(2,1)S(1)}, bf16[128,768]{1,0:T(8,128)(2,1)S(1)}, u32[]{:S(2)}, u32[]{:S(2)}) collective-permute-start(bf16[128,768]{1,0:T(8,128)(2,1)S(1)} %get-tuple-element.140), channel_id=1, source_target_pairs={{0,3},{1,0},{2,1},{3,2},{4,7},{5,4},{6,5},{7,6},{8,11},{9,8},{10,9... | collective-permute-start | bytes 589832 | tf_op jit(solution)/shard_map/ppermute | solution.py:27
  123.1 8.9 %collective-permute-start.26 = (bf16[64,768]{1,0:T(8,128)(2,1)S(1)}, bf16[64,768]{1,0:T(8,128)(2,1)S(1)}, u32[]{:S(2)}, u32[]{:S(2)}) collective-permute-start(bf16[64,768]{1,0:T(8,128)(2,1)S(1)} %get-tuple-element.145), channel_id=1, source_target_pairs={{0,24},{4,28},{8,16},{12,20},{16,8},{20,12},{24,0},{28,4},{1,25},{... | collective-permute-start | bytes 294920 | tf_op jit(solution)/shard_map/ppermute | solution.py:22
  132.2 16.8 %collective-permute-start.27 = (bf16[64,3072]{1,0:T(8,128)(2,1)S(1)}, bf16[64,3072]{1,0:T(8,128)(2,1)S(1)}, u32[]{:S(2)}, u32[]{:S(2)}) collective-permute-start(bf16[64,3072]{1,0:T(8,128)(2,1)S(1)} %pack.2.refs_0_), channel_id=1, source_target_pairs={{0,2},{1,3},{2,0},{3,1},{4,6},{5,7},{6,4},{7,5},{8,10},{9,11},{10,... | collective-permute-start | bytes 1179656 | tf_op jit(solution)/shard_map/ppermute | solution.py:27
  138.1 10.7 %collective-permute-start.30 = (bf16[64,768]{1,0:T(8,128)(2,1)S(1)}, bf16[64,768]{1,0:T(8,128)(2,1)S(1)}, u32[]{:S(2)}, u32[]{:S(2)}) collective-permute-start(bf16[64,768]{1,0:T(8,128)(2,1)S(1)} %get-tuple-element.152), channel_id=1, source_target_pairs={{0,20},{4,16},{8,28},{12,24},{16,4},{20,0},{24,12},{28,8},{1,21},{... | collective-permute-start | bytes 294920 | tf_op jit(solution)/shard_map/ppermute | solution.py:22
  138.1 10.6 %collective-permute-start.31 = (bf16[64,768]{1,0:T(8,128)(2,1)S(1)}, bf16[64,768]{1,0:T(8,128)(2,1)S(1)}, u32[]{:S(2)}, u32[]{:S(2)}) collective-permute-start(bf16[64,768]{1,0:T(8,128)(2,1)S(1)} %get-tuple-element.153), channel_id=1, source_target_pairs={{0,28},{4,24},{8,20},{12,16},{16,12},{20,8},{24,4},{28,0},{1,29},{... | collective-permute-start | bytes 294920 | tf_op jit(solution)/shard_map/ppermute | solution.py:22
  141.1 8.4 %collective-permute-start.32 = (bf16[64,3072]{1,0:T(8,128)(2,1)S(1)}, bf16[64,3072]{1,0:T(8,128)(2,1)S(1)}, u32[]{:S(2)}, u32[]{:S(2)}) collective-permute-start(bf16[64,3072]{1,0:T(8,128)(2,1)S(1)} %pack.2.refs_0_), channel_id=1, source_target_pairs={{0,1},{1,0},{2,3},{3,2},{4,5},{5,4},{6,7},{7,6},{8,9},{9,8},{10,11... | collective-permute-start | bytes 1179656 | tf_op jit(solution)/shard_map/ppermute | solution.py:27
  149.1 11.5 %collective-permute-start.34 = (bf16[64,3072]{1,0:T(8,128)(2,1)S(1)}, bf16[64,3072]{1,0:T(8,128)(2,1)S(1)}, u32[]{:S(2)}, u32[]{:S(2)}) collective-permute-start(bf16[64,3072]{1,0:T(8,128)(2,1)S(1)} %pack.3.refs_0_), channel_id=1, source_target_pairs={{0,2},{1,3},{2,0},{3,1},{4,6},{5,7},{6,4},{7,5},{8,10},{9,11},{10,... | collective-permute-start | bytes 1179656 | tf_op jit(solution)/shard_map/ppermute | solution.py:27
  166.1 11.5 %collective-permute-start.36 = (bf16[2,256,768]{2,1,0:T(8,128)(2,1)S(1)}, bf16[2,256,768]{2,1,0:T(8,128)(2,1)S(1)}, u32[]{:S(2)}, u32[]{:S(2)}) collective-permute-start(bf16[2,256,768]{2,1,0:T(8,128)(2,1)S(1)} %get-tuple-element.156), channel_id=1, source_target_pairs={{0,1},{1,0},{2,3},{3,2},{4,5},{5,4},{6,7},{7,6},{8,9},{9,8},{10,11... | collective-permute-start | bytes 2359304 | tf_op jit(solution)/shard_map/ppermute | solution.py:27
  166.7 11.0 %collective-permute-start.35 = (bf16[128,768]{1,0:T(8,128)(2,1)S(1)}, bf16[128,768]{1,0:T(8,128)(2,1)S(1)}, u32[]{:S(2)}, u32[]{:S(2)}) collective-permute-start(bf16[128,768]{1,0:T(8,128)(2,1)S(1)} %get-tuple-element.157), channel_id=1, source_target_pairs={{0,0},{1,8},{2,16},{3,24},{4,4},{5,12},{6,20},{7,28},{8,1},{9,9},{... | collective-permute-start | bytes 589832 | tf_op jit(solution)/shard_map/ppermute | solution.py:410
  184.3 13.8 %collective-permute-start.37 = (bf16[256,768]{1,0:T(8,128)(2,1)S(1)}, bf16[256,768]{1,0:T(8,128)(2,1)S(1)}, u32[]{:S(2)}, u32[]{:S(2)}) collective-permute-start(bf16[256,768]{1,0:T(8,128)(2,1)S(1)} %fusion.3), channel_id=1, source_target_pairs={{0,2},{1,3},{2,0},{3,1},{4,6},{5,7},{6,4},{7,5},{8,10},{9,11},{10,... | collective-permute-start | bytes 1179656 | tf_op jit(solution)/shard_map/ppermute | solution.py:27
  188.3 17.9 %collective-permute-start.41 = (bf16[256,768]{1,0:T(8,128)(2,1)S(1)}, bf16[256,768]{1,0:T(8,128)(2,1)S(1)}, u32[]{:S(2)}, u32[]{:S(2)}) collective-permute-start(bf16[256,768]{1,0:T(8,128)(2,1)S(1)} %fusion.4), channel_id=1, source_target_pairs={{0,2},{1,3},{2,0},{3,1},{4,6},{5,7},{6,4},{7,5},{8,10},{9,11},{10,... | collective-permute-start | bytes 1179656 | tf_op jit(solution)/shard_map/ppermute | solution.py:27
  198.2 10.1 %collective-permute-start.43 = (bf16[64,768]{1,0:T(8,128)(2,1)S(1)}, bf16[64,768]{1,0:T(8,128)(2,1)S(1)}, u32[]{:S(2)}, u32[]{:S(2)}) collective-permute-start(bf16[64,768]{1,0:T(8,128)(2,1)S(1)} %get-tuple-element.165), channel_id=1, source_target_pairs={{0,8},{4,12},{8,0},{12,4},{16,24},{20,28},{24,16},{28,20},{1,9},{5... | collective-permute-start | bytes 294920 | tf_op jit(solution)/shard_map/ppermute | solution.py:22
  198.7 11.0 %collective-permute-start.45 = (bf16[64,768]{1,0:T(8,128)(2,1)S(1)}, bf16[64,768]{1,0:T(8,128)(2,1)S(1)}, u32[]{:S(2)}, u32[]{:S(2)}) collective-permute-start(bf16[64,768]{1,0:T(8,128)(2,1)S(1)} %get-tuple-element.167), channel_id=1, source_target_pairs={{0,16},{4,20},{8,24},{12,28},{16,0},{20,4},{24,8},{28,12},{1,17},{... | collective-permute-start | bytes 294920 | tf_op jit(solution)/shard_map/ppermute | solution.py:22
  200.4 12.8 %collective-permute-start.47 = (bf16[64,768]{1,0:T(8,128)(2,1)S(1)}, bf16[64,768]{1,0:T(8,128)(2,1)S(1)}, u32[]{:S(2)}, u32[]{:S(2)}) collective-permute-start(bf16[64,768]{1,0:T(8,128)(2,1)S(1)} %get-tuple-element.169), channel_id=1, source_target_pairs={{0,24},{4,28},{8,16},{12,20},{16,8},{20,12},{24,0},{28,4},{1,25},{... | collective-permute-start | bytes 294920 | tf_op jit(solution)/shard_map/ppermute | solution.py:22
  208.4 11.2 %collective-permute-start.46 = (bf16[64,768]{1,0:T(8,128)(2,1)S(1)}, bf16[64,768]{1,0:T(8,128)(2,1)S(1)}, u32[]{:S(2)}, u32[]{:S(2)}) collective-permute-start(bf16[64,768]{1,0:T(8,128)(2,1)S(1)} %get-tuple-element.168), channel_id=1, source_target_pairs={{0,20},{4,16},{8,28},{12,24},{16,4},{20,0},{24,12},{28,8},{1,21},{... | collective-permute-start | bytes 294920 | tf_op jit(solution)/shard_map/ppermute | solution.py:22
  209.8 9.8 %collective-permute-start.48 = (bf16[64,768]{1,0:T(8,128)(2,1)S(1)}, bf16[64,768]{1,0:T(8,128)(2,1)S(1)}, u32[]{:S(2)}, u32[]{:S(2)}) collective-permute-start(bf16[64,768]{1,0:T(8,128)(2,1)S(1)} %get-tuple-element.170), channel_id=1, source_target_pairs={{0,28},{4,24},{8,20},{12,16},{16,12},{20,8},{24,4},{28,0},{1,29},{... | collective-permute-start | bytes 294920 | tf_op jit(solution)/shard_map/ppermute | solution.py:22
  (31 other events, 242.7 us)

commit v8 on v7

--- a/solution.py
+++ b/solution.py
@@ -51,7 +51,10 @@
 
 
 def state_kernel(me_ref, doc_ref, decay_ref, k_ref, v_ref, *refs):
-    outs, (sum_ref, sum_rows_ref, doc_out_ref, state_ref) = refs[:-4], refs[-4:]
+    outs, refs = refs[:-6], refs[-6:]
+    sum_ref, sum_rows_ref, doc_out_ref, k_out_ref, v_out_ref, state_ref = refs
+    k_out_ref[...] = k_ref[...]
+    v_out_ref[...] = v_ref[...]
     heads, tokens = decay_ref.shape
     n_seq, hw = len(outs), outs[0].shape[1]
     rows, held, extra = chunk_plan(heads, hw, n_seq)
@@ -199,7 +202,9 @@
     middle = (total + sums).astype(BF16)
     middle_ref[...] = middle
     count = outs[0].shape[0]
-    rows = jnp.dot(take_ref[...], middle, preferred_element_type=F32).astype(BF16)
+    rows = lax.dot_general(
+        take_ref[...], middle, (((0,), (0,)), ((), ())), preferred_element_type=F32
+    ).astype(BF16)
     for d in range(len(outs)):
         outs[d][...] = rows[d * count : (d + 1) * count]
 
@@ -363,15 +368,27 @@
     )(*operands)
 
 
-def slot_places(routing, experts, capacity):
-    tokens = routing.shape[0]
-    flat_ids = routing.reshape(-1)
-    hits = (flat_ids[:, None] == jnp.arange(experts, dtype=jnp.int32)[None, :]).astype(F32)
-    pair_row = lax.broadcasted_iota(jnp.int32, (2 * tokens, 2 * tokens), 0)
-    pair_col = lax.broadcasted_iota(jnp.int32, (2 * tokens, 2 * tokens), 1)
-    earlier = jnp.dot((pair_col < pair_row).astype(F32), hits)
-    rank = jnp.sum(earlier * hits, axis=1).astype(jnp.int32)
-    return (flat_ids * capacity + rank).reshape(tokens, 2)
+def plan_kernel(capacity, me_ref, ids_ref, routing_ref, weights_ref, take_ref, mix_ref):
+    tokens, slots = take_ref.shape
+    experts = slots // capacity
+    row = lax.broadcasted_iota(jnp.int32, (tokens, tokens), 0)
+    col = lax.broadcasted_iota(jnp.int32, (tokens, tokens), 1)
+    before = (col < row).astype(BF16)
+    expert = lax.broadcasted_iota(jnp.int32, (tokens, experts), 1)
+    slot = lax.broadcasted_iota(jnp.int32, (tokens, slots), 1)
+
+    def found(ids):
+        hits = [(expert == one).astype(F32) for one in ids]
+        earlier = jnp.dot(before, (hits[0] + hits[1]).astype(BF16), preferred_element_type=F32)
+        ranks = [jnp.sum(earlier * hit, axis=1, keepdims=True).astype(jnp.int32) for hit in hits]
+        return [slot == (one ^ me_ref[0]) * capacity + rank for one, rank in zip(ids, ranks)]
+
+    there = ids_ref[...].astype(F32).astype(jnp.int32)
+    first, second = found([there[:, :1], there[:, 1:2]])
+    take_ref[...] = (first | second).astype(F32).astype(BF16)
+    first, second = found([routing_ref[:, :1], routing_ref[:, 1:2]])
+    weights = weights_ref[...]
+    mix_ref[...] = jnp.where(first, weights[:, :1], 0.0) + jnp.where(second, weights[:, 1:2], 0.0)
 
 
 def shards(
@@ -415,11 +432,12 @@
     doc_row = doc_ids.reshape(1, tokens)
     rows, held, extra = chunk_plan(heads, hw, n_seq)
     work = 2 * tokens * hw * hw * heads
-    *payload, decay_sum, decay_rows, doc_float = local_call(
+    *payload, decay_sum, decay_rows, doc_float, keys_near, values_near = local_call(
         state_kernel,
         "block_state",
         [struct((rows + extra, hw), BF16)] * n_seq
-        + [struct((tokens, heads), F32), struct((heads, tokens), F32), struct((1, tokens), F32)],
+        + [struct((tokens, heads), F32), struct((heads, tokens), F32), struct((1, tokens), F32)]
+        + [struct((tokens, heads * hw), BF16)] * 2,
         work,
         me,
         doc_row,
@@ -429,12 +447,8 @@
         scratch=[pltpu.VMEM((hw, hw), F32)],
         scalars=1,
     )
-    lanes = max(128, routing.shape[1])
-    ids = jnp.pad(routing.astype(BF16), ((0, 0), (0, lanes - routing.shape[1])))
-    there = jnp.concatenate([residual, ids], axis=1)
-    payload, there = lax.optimization_barrier((payload, there))
-    there = crossed(there)
-    arrived, there = lax.optimization_barrier((swap_seq(payload), there))
+    residual_there = crossed(residual)
+    arrived, residual_there = lax.optimization_barrier((swap_seq(payload), residual_there))
     entered = local_call(
         scan_kernel,
         "carry",
@@ -448,7 +462,7 @@
         ],
         scalars=1,
     )
-    carried = swap_seq(entered)
+    carried, output_weight = lax.optimization_barrier((swap_seq(entered), output_weight))
     attended = local_call(
         attend_kernel,
         "attend",
@@ -459,15 +473,16 @@
         decay_sum,
         decay_rows,
         queries,
-        key_vectors,
-        value_vectors,
+        keys_near,
+        values_near,
         head_gain.reshape(1, heads * hw),
         *carried,
         scratch=[pltpu.VMEM((heads * hw, hw), BF16)],
         scalars=1,
     )
 
-    attended, output_weight = lax.optimization_barrier((attended, output_weight))
+    ids = jnp.pad(routing.astype(BF16), ((0, 0), (0, 128 - routing.shape[1])))
+    ids = crossed(lax.optimization_barrier((ids, attended))[0])
     cols = output_weight.shape[1]
     w_z = jnp.zeros((output_weight.shape[0], ny * cols), BF16)
     w_z = lax.dynamic_update_slice(w_z, output_weight, (0, y * cols))
@@ -482,18 +497,18 @@
     ups = lambda j: [(q, q + j) for q in range(nz - j)]
     downs = lambda j: [(q + j, q) for q in range(nz - j)]
     below, above = along(attended, ups(1)), along(attended, downs(1))
-    direct, there, own_routing = lax.optimization_barrier(
-        (attended, there, routing, below, above)
-    )[:3]
-    residual_there = there[:, :part]
-    routing_there = there[:, part : part + routing.shape[1]].astype(jnp.int32)
-    slot = jnp.arange(experts * capacity, dtype=jnp.int32)
-    slot = (slot // capacity ^ s) * capacity + slot % capacity
-    place = slot_places(routing_there, experts, capacity)
-    take = jnp.any(place[:, None, :] == slot[None, :, None], axis=2).astype(BF16).T
-    place = slot_places(own_routing, experts, capacity)
-    here = place[:, None, :] == slot[None, :, None]
-    mix = jnp.sum(jnp.where(here, route_weights[:, None, :], 0.0), axis=2)
+    direct = lax.optimization_barrier((attended, below, above))[0]
+    take, mix = local_call(
+        functools.partial(plan_kernel, capacity),
+        "plan",
+        [struct((tokens, experts * capacity), BF16), struct((tokens, experts * capacity), F32)],
+        4 * tokens * tokens * experts,
+        me,
+        ids,
+        routing,
+        route_weights,
+        scalars=1,
+    )
     shifts, rows_of = [(0, 0), (1, 0), (0, 1)], [attended, below, above]
     if nz > 2:
         shifts += [(2, 0), (0, 2)]

time: 221 us -> 213 us (0.964)
  local copies, waits for them, and re-layouts: 13.2 us -> 8.08 us
  other arithmetic: 3.92 us -> 0.4 us
  matrix products: 6.98 us -> 4.68 us
    ppermute x5, waiting for transfers between devices: 12.3 us -> 25.8 us  [along(): return lax.ppermute(value, 'seq', perm)]
    ppermute x29, waiting for transfers between devices: 48.3 us -> 35.8 us  [permute_seq(): lax.ppermute(value, 'seq', [(source, move(source)) for source in range(co...]
    unnamed x28 -> x22, local copies, waits for them, and re-layouts: 7.48 us -> 5.41 us
    pallas_call x14 -> x15, Pallas kernels: 33.8 us -> 34.5 us  [local_call(): pl.pallas_call(kernel, out_shape=out_shape, in_specs=[pl.BlockSpec(memory...]
  transfers between devices with their start and end apart: 49 -> 50, of which waited for: 24 -> 24; matrix products, arithmetic and copies ran while one was open for 6% -> 3% of each run, Pallas kernels for 7% -> 10%
where the time goes in v8:
time: 213 us; the launch traced here: 212 us
  waiting for transfers between devices  84.4 us (40%)
  starting transfers between devices  79.4 us (37%)
  Pallas kernels  34.5 us (16%)
  local copies, waits for them, and re-layouts  8.08 us (4%)
  matrix products  4.68 us (2%)
    ppermute x29, starting transfers between devices, permute_seq(): lax.ppermute(value, 'seq', [(source, move(source)) for source in range(co...  51.4 us
    ppermute x29, waiting for transfers between devices, permute_seq(): lax.ppermute(value, 'seq', [(source, move(source)) for source in range(co...  35.8 us
    pallas_call x15, Pallas kernels, local_call(): pl.pallas_call(kernel, out_shape=out_shape, in_specs=[pl.BlockSpec(memory...  34.5 us
    ppermute x5, waiting for transfers between devices, along(): return lax.ppermute(value, 'seq', perm)  25.8 us
    ppermute x13, waiting for transfers between devices, permute_head(): lax.ppermute(value, 'head', [(source, move(source)) for source in range(c...  22.7 us
    ppermute x13, starting transfers between devices, permute_head(): lax.ppermute(value, 'head', [(source, move(source)) for source in range(c...  12.7 us
    ppermute x5, starting transfers between devices, along(): return lax.ppermute(value, 'seq', perm)  12.1 us
    unnamed x22, local copies, waits for them, and re-layouts  5.41 us
  transfers between devices with their start and end apart: 50, of which 24 were waited for; matrix products, arithmetic and copies ran while one was open for 3% of the time, Pallas kernels for 10%

profile of v8, /device:TPU:0, one launch (start us, length us, event | category | flops | bytes accessed | tf_op | source)
XLA Modules:
  0.0 211.9 jit_solution(17816412261974038827)
XLA Ops:
  6.1 3.0 %collective-permute-start = (bf16[272,128]{1,0:T(8,128)(2,1)S(1)}, bf16[272,128]{1,0:T(8,128)(2,1)S(1)}, u32[]{:S(2)}, u32[]{:S(2)}) collective-permute-start(bf16[272,128]{1,0:T(8,128)(2,1)S(1)} %get-tuple-element.90), channel_id=1, source_target_pairs={{0,4},{4,0},{8,12},{12,8},{16,20},{20,16},{24,28},{28,24},{1,5},{5... | collective-permute-start | bytes 208904 | tf_op jit(solution)/shard_map/ppermute | solution.py:22
  11.1 4.2 %collective-permute-start.3 = (bf16[272,128]{1,0:T(8,128)(2,1)S(1)}, bf16[272,128]{1,0:T(8,128)(2,1)S(1)}, u32[]{:S(2)}, u32[]{:S(2)}) collective-permute-start(bf16[272,128]{1,0:T(8,128)(2,1)S(1)} %get-tuple-element.93), channel_id=1, source_target_pairs={{0,16},{4,20},{8,24},{12,28},{16,0},{20,4},{24,8},{28,12},{1,17},{... | collective-permute-start | bytes 208904 | tf_op jit(solution)/shard_map/ppermute | solution.py:22
  17.1 2.4 %collective-permute-start.5 = (bf16[272,128]{1,0:T(8,128)(2,1)S(1)}, bf16[272,128]{1,0:T(8,128)(2,1)S(1)}, u32[]{:S(2)}, u32[]{:S(2)}) collective-permute-start(bf16[272,128]{1,0:T(8,128)(2,1)S(1)} %get-tuple-element.95), channel_id=1, source_target_pairs={{0,24},{4,28},{8,16},{12,20},{16,8},{20,12},{24,0},{28,4},{1,25},{... | collective-permute-start | bytes 208904 | tf_op jit(solution)/shard_map/ppermute | solution.py:22
  20.9 2.5 %collective-permute-done.3.refs_4_ = bf16[272,128]{1,0:T(8,128)(2,1)S(1)} collective-permute-done((bf16[272,128]{1,0:T(8,128)(2,1)S(1)}, bf16[272,128]{1,0:T(8,128)(2,1)S(1)}, u32[]{:S(2)}, u32[]{:S(2)}) %collective-permute-start.3) | collective-permute-done | bytes 69664 | tf_op jit(solution)/shard_map/ppermute | solution.py:22
  23.4 3.9 %collective-permute-done.4.refs_5_ = bf16[272,128]{1,0:T(8,128)(2,1)S(1)} collective-permute-done((bf16[272,128]{1,0:T(8,128)(2,1)S(1)}, bf16[272,128]{1,0:T(8,128)(2,1)S(1)}, u32[]{:S(2)}, u32[]{:S(2)}) %collective-permute-start.4) | collective-permute-done | bytes 69664 | tf_op jit(solution)/shard_map/ppermute | solution.py:22
  28.4 2.9 %collective-permute-start.9 = (bf16[256,128]{1,0:T(8,128)(2,1)S(1)}, bf16[256,128]{1,0:T(8,128)(2,1)S(1)}, u32[]{:S(2)}, u32[]{:S(2)}) collective-permute-start(bf16[256,128]{1,0:T(8,128)(2,1)S(1)} %get-tuple-element.113), channel_id=1, source_target_pairs={{0,8},{4,12},{8,0},{12,4},{16,24},{20,28},{24,16},{28,20},{1,9},{5... | collective-permute-start | bytes 196616 | tf_op jit(solution)/shard_map/ppermute | solution.py:22
  36.7 3.2 %collective-permute-start.14 = (bf16[256,128]{1,0:T(8,128)(2,1)S(1)}, bf16[256,128]{1,0:T(8,128)(2,1)S(1)}, u32[]{:S(2)}, u32[]{:S(2)}) collective-permute-start(bf16[256,128]{1,0:T(8,128)(2,1)S(1)} %get-tuple-element.118), channel_id=1, source_target_pairs={{0,28},{4,24},{8,20},{12,16},{16,12},{20,8},{24,4},{28,0},{1,29},{... | collective-permute-start | bytes 196616 | tf_op jit(solution)/shard_map/ppermute | solution.py:22
  39.9 2.6 %collective-permute-done.11.refs_4_ = bf16[256,128]{1,0:T(8,128)(2,1)S(1)} collective-permute-done((bf16[256,128]{1,0:T(8,128)(2,1)S(1)}, bf16[256,128]{1,0:T(8,128)(2,1)S(1)}, u32[]{:S(2)}, u32[]{:S(2)}) %collective-permute-start.11) | collective-permute-done | bytes 65568 | tf_op jit(solution)/shard_map/ppermute | solution.py:22
  47.8 2.9 %attend.1 = bf16[128,2048]{1,0:T(8,128)(2,1)S(1)} custom-call(s32[1]{0:T(128)} %bitcast.me_ref, f32[1,128]{1,0:T(1,128)S(1)} %get-tuple-element.98.doc_ref, f32[128,16]{1,0:T(8,128)S(1)} %get-tuple-element.99.sum_ref, f32[16,128]{1,0:T(8,128)S(1)} %get-tuple-element.100.sum_rows_ref, bf16[128,2048]{1,0:T(8,128)(2,1)S(1)} %copy-done, ...), custom_call_target="tpu_custom_call" | custom-call | flops 201326592 | bytes 2646532 | tf_op jit(solution)/shard_map/attend/pallas_call | solution.py:358
  50.7 5.3 %collective-permute-start.16 = (bf16[128,2048]{1,0:T(8,128)(2,1)S(1)}, bf16[128,2048]{1,0:T(8,128)(2,1)}, u32[]{:S(2)}, u32[]{:S(2)}) collective-permute-start(bf16[128,2048]{1,0:T(8,128)(2,1)S(1)} %attend.1), channel_id=1, source_target_pairs={{0,8},{4,12},{8,16},{12,20},{16,24},{20,28},{1,9},{5,13},{9,17},{1... | collective-permute-start | bytes 1572872 | tf_op jit(solution)/shard_map/ppermute | solution.py:495
  59.7 6.1 %collective-permute-done.16 = bf16[128,2048]{1,0:T(8,128)(2,1)} collective-permute-done((bf16[128,2048]{1,0:T(8,128)(2,1)S(1)}, bf16[128,2048]{1,0:T(8,128)(2,1)}, u32[]{:S(2)}, u32[]{:S(2)}) %collective-permute-start.16) | collective-permute-done | bytes 524320 | tf_op jit(solution)/shard_map/ppermute | solution.py:495
  65.7 4.6 %collective-permute-done.17 = bf16[128,2048]{1,0:T(8,128)(2,1)S(1)} collective-permute-done((bf16[128,2048]{1,0:T(8,128)(2,1)S(1)}, bf16[128,2048]{1,0:T(8,128)(2,1)S(1)}, u32[]{:S(2)}, u32[]{:S(2)}) %collective-permute-start.17) | collective-permute-done | bytes 524320 | tf_op jit(solution)/shard_map/ppermute | solution.py:495
  75.8 3.8 %collective-permute-done.15 = bf16[2048,384]{1,0:T(8,128)(2,1)} collective-permute-done((bf16[2048,384]{1,0:T(8,128)(2,1)}, bf16[2048,384]{1,0:T(8,128)(2,1)}, u32[]{:S(2)}, u32[]{:S(2)}) %collective-permute-start.15) | collective-permute-done | bytes 1572896 | tf_op jit(solution)/shard_map/ppermute | solution.py:22
  84.2 11.9 %collective-permute-done.18 = bf16[128,2048]{1,0:T(8,128)(2,1)S(1)} collective-permute-done((bf16[128,2048]{1,0:T(8,128)(2,1)}, bf16[128,2048]{1,0:T(8,128)(2,1)S(1)}, u32[]{:S(2)}, u32[]{:S(2)}) %collective-permute-start.18) | collective-permute-done | bytes 524320 | tf_op jit(solution)/shard_map/ppermute | solution.py:495
  96.7 3.3 %collective-permute-done.19 = bf16[128,2048]{1,0:T(8,128)(2,1)S(1)} collective-permute-done((bf16[128,2048]{1,0:T(8,128)(2,1)S(1)}, bf16[128,2048]{1,0:T(8,128)(2,1)S(1)}, u32[]{:S(2)}, u32[]{:S(2)}) %collective-permute-start.19) | collective-permute-done | bytes 524320 | tf_op jit(solution)/shard_map/ppermute | solution.py:495
  104.8 3.7 %collective-permute-done.22.refs_1_ = bf16[128,768]{1,0:T(8,128)(2,1)S(1)} collective-permute-done((bf16[128,768]{1,0:T(8,128)(2,1)S(1)}, bf16[128,768]{1,0:T(8,128)(2,1)S(1)}, u32[]{:S(2)}, u32[]{:S(2)}) %collective-permute-start.22) | collective-permute-done | bytes 196640 | tf_op jit(solution)/shard_map/ppermute | solution.py:27
  109.8 2.5 %collective-permute-done.24.refs_3_ = bf16[128,768]{1,0:T(8,128)(2,1)S(1)} collective-permute-done((bf16[128,768]{1,0:T(8,128)(2,1)S(1)}, bf16[128,768]{1,0:T(8,128)(2,1)S(1)}, u32[]{:S(2)}, u32[]{:S(2)}) %collective-permute-start.24) | collective-permute-done | bytes 196640 | tf_op jit(solution)/shard_map/ppermute | solution.py:27
  114.4 2.8 %collective-permute-start.27 = (bf16[64,768]{1,0:T(8,128)(2,1)S(1)}, bf16[64,768]{1,0:T(8,128)(2,1)S(1)}, u32[]{:S(2)}, u32[]{:S(2)}) collective-permute-start(bf16[64,768]{1,0:T(8,128)(2,1)S(1)} %get-tuple-element.147), channel_id=1, source_target_pairs={{0,24},{4,28},{8,16},{12,20},{16,8},{20,12},{24,0},{28,4},{1,25},{... | collective-permute-start | bytes 294920 | tf_op jit(solution)/shard_map/ppermute | solution.py:22
  119.4 4.8 %collective-permute-done.26.refs_2_ = bf16[64,768]{1,0:T(8,128)(2,1)S(1)} collective-permute-done((bf16[64,768]{1,0:T(8,128)(2,1)S(1)}, bf16[64,768]{1,0:T(8,128)(2,1)S(1)}, u32[]{:S(2)}, u32[]{:S(2)}) %collective-permute-start.26) | collective-permute-done | bytes 98336 | tf_op jit(solution)/shard_map/ppermute | solution.py:22
  126.0 2.9 %collective-permute-start.30 = (bf16[64,768]{1,0:T(8,128)(2,1)S(1)}, bf16[64,768]{1,0:T(8,128)(2,1)S(1)}, u32[]{:S(2)}, u32[]{:S(2)}) collective-permute-start(bf16[64,768]{1,0:T(8,128)(2,1)S(1)} %get-tuple-element.153), channel_id=1, source_target_pairs={{0,12},{4,8},{8,4},{12,0},{16,28},{20,24},{24,20},{28,16},{1,13},{... | collective-permute-start | bytes 294920 | tf_op jit(solution)/shard_map/ppermute | solution.py:22
  128.9 3.1 %collective-permute-start.32 = (bf16[64,768]{1,0:T(8,128)(2,1)S(1)}, bf16[64,768]{1,0:T(8,128)(2,1)S(1)}, u32[]{:S(2)}, u32[]{:S(2)}) collective-permute-start(bf16[64,768]{1,0:T(8,128)(2,1)S(1)} %get-tuple-element.155), channel_id=1, source_target_pairs={{0,28},{4,24},{8,20},{12,16},{16,12},{20,8},{24,4},{28,0},{1,29},{... | collective-permute-start | bytes 294920 | tf_op jit(solution)/shard_map/ppermute | solution.py:22
  132.1 7.4 %collective-permute-done.31.refs_2_ = bf16[64,768]{1,0:T(8,128)(2,1)S(1)} collective-permute-done((bf16[64,768]{1,0:T(8,128)(2,1)S(1)}, bf16[64,768]{1,0:T(8,128)(2,1)S(1)}, u32[]{:S(2)}, u32[]{:S(2)}) %collective-permute-start.31) | collective-permute-done | bytes 98336 | tf_op jit(solution)/shard_map/ppermute | solution.py:22
  141.6 8.0 %hidden.2.hidden_ref = bf16[256,1152]{1,0:T(8,128)(2,1)S(1)} custom-call(s32[9]{0:T(128)S(1)} %stack.45.owner_ref, bf16[64,3072]{1,0:T(8,128)(2,1)S(1)} %pack.2.refs_0_, bf16[64,3072]{1,0:T(8,128)(2,1)S(1)} %collective-permute-done.28.refs_1_, bf16[64,3072]{1,0:T(8,128)(2,1)S(1)} %collective-permute-done.33.refs_2_, ...), custom_call_target="tpu_custom_call" | custom-call | flops 3623878656 | bytes 16318500 | tf_op jit(solution)/shard_map/hidden/pallas_call | solution.py:358
  151.4 5.5 %down.2 = (bf16[2,256,768]{2,1,0:T(8,128)(2,1)S(1)}, bf16[2,256,768]{2,1,0:T(8,128)(2,1)S(1)}) custom-call(s32[9]{0:T(128)S(1)} %stack.45.owner_ref, bf16[256,1152]{1,0:T(8,128)(2,1)S(1)} %hidden.2.hidden_ref, bf16[1,1152,3072]{2,1,0:T(8,128)(2,1)} %down_ref.3), custom_call_target="tpu_custom_call" | custom-call | flops 1811939328 | bytes 9240612 | tf_op jit(solution)/shard_map/down/pallas_call | solution.py:358
  160.4 8.0 %hidden.3.hidden_ref = bf16[256,1152]{1,0:T(8,128)(2,1)S(1)} custom-call(s32[9]{0:T(128)S(1)} %stack.45.owner_ref, bf16[64,3072]{1,0:T(8,128)(2,1)S(1)} %pack.3.refs_0_, bf16[64,3072]{1,0:T(8,128)(2,1)S(1)} %collective-permute-done.35.refs_1_, bf16[64,3072]{1,0:T(8,128)(2,1)S(1)} %collective-permute-done.39.refs_2_, ...), custom_call_target="tpu_custom_call" | custom-call | flops 3623878656 | bytes 16318500 | tf_op jit(solution)/shard_map/hidden/pallas_call | solution.py:358
  168.6 5.5 %down.3 = (bf16[2,256,768]{2,1,0:T(8,128)(2,1)S(1)}, bf16[2,256,768]{2,1,0:T(8,128)(2,1)S(1)}) custom-call(s32[9]{0:T(128)S(1)} %stack.45.owner_ref, bf16[256,1152]{1,0:T(8,128)(2,1)S(1)} %hidden.3.hidden_ref, bf16[1,1152,3072]{2,1,0:T(8,128)(2,1)} %down_ref.3), custom_call_target="tpu_custom_call" | custom-call | flops 1811939328 | bytes 9240612 | tf_op jit(solution)/shard_map/down/pallas_call | solution.py:358
  175.4 4.1 %collective-permute-start.38 = (bf16[256,768]{1,0:T(8,128)(2,1)S(1)}, bf16[256,768]{1,0:T(8,128)(2,1)S(1)}, u32[]{:S(2)}, u32[]{:S(2)}) collective-permute-start(bf16[256,768]{1,0:T(8,128)(2,1)S(1)} %fusion), channel_id=1, source_target_pairs={{0,2},{1,3},{2,0},{3,1},{4,6},{5,7},{6,4},{7,5},{8,10},{9,11},{10,... | collective-permute-start | bytes 1179656 | tf_op jit(solution)/shard_map/ppermute | solution.py:27
  182.0 7.4 %collective-permute-done.38.refs_1_ = bf16[256,768]{1,0:T(8,128)(2,1)S(1)} collective-permute-done((bf16[256,768]{1,0:T(8,128)(2,1)S(1)}, bf16[256,768]{1,0:T(8,128)(2,1)S(1)}, u32[]{:S(2)}, u32[]{:S(2)}) %collective-permute-start.38) | collective-permute-done | bytes 393248 | tf_op jit(solution)/shard_map/ppermute | solution.py:27
  191.2 2.9 %collective-permute-start.48 = (bf16[64,768]{1,0:T(8,128)(2,1)S(1)}, bf16[64,768]{1,0:T(8,128)(2,1)S(1)}, u32[]{:S(2)}, u32[]{:S(2)}) collective-permute-start(bf16[64,768]{1,0:T(8,128)(2,1)S(1)} %get-tuple-element.171), channel_id=1, source_target_pairs={{0,24},{4,28},{8,16},{12,20},{16,8},{20,12},{24,0},{28,4},{1,25},{... | collective-permute-start | bytes 294920 | tf_op jit(solution)/shard_map/ppermute | solution.py:22
  194.1 3.5 %collective-permute-done.42.refs_1_ = bf16[256,768]{1,0:T(8,128)(2,1)S(1)} collective-permute-done((bf16[256,768]{1,0:T(8,128)(2,1)S(1)}, bf16[256,768]{1,0:T(8,128)(2,1)S(1)}, u32[]{:S(2)}, u32[]{:S(2)}) %collective-permute-start.42) | collective-permute-done | bytes 393248 | tf_op jit(solution)/shard_map/ppermute | solution.py:27
  201.0 3.6 %collective-permute-start.49 = (bf16[64,768]{1,0:T(8,128)(2,1)S(1)}, bf16[64,768]{1,0:T(8,128)(2,1)S(1)}, u32[]{:S(2)}, u32[]{:S(2)}) collective-permute-start(bf16[64,768]{1,0:T(8,128)(2,1)S(1)} %get-tuple-element.172), channel_id=1, source_target_pairs={{0,28},{4,24},{8,20},{12,16},{16,12},{20,8},{24,4},{28,0},{1,29},{... | collective-permute-start | bytes 294920 | tf_op jit(solution)/shard_map/ppermute | solution.py:22
  205.6 5.2 %collective-permute-done.47.refs_5_ = bf16[64,768]{1,0:T(8,128)(2,1)S(1)} collective-permute-done((bf16[64,768]{1,0:T(8,128)(2,1)S(1)}, bf16[64,768]{1,0:T(8,128)(2,1)S(1)}, u32[]{:S(2)}, u32[]{:S(2)}) %collective-permute-start.47) | collective-permute-done | bytes 98336 | tf_op jit(solution)/shard_map/ppermute | solution.py:22
  (125 shorter events, 67.9 us)
Async XLA Ops:
  0.0 27.3 %collective-permute-start.7 = (bf16[128,768]{1,0:T(8,128)(2,1)}, bf16[128,768]{1,0:T(8,128)(2,1)S(1)}, u32[]{:S(2)}, u32[]{:S(2)}) collective-permute-start(bf16[128,768]{1,0:T(8,128)(2,1)} %param.21), channel_id=1, source_target_pairs={{0,0},{1,8},{2,16},{3,24},{4,4},{5,12},{6,20},{7,28},{8,1},{9,9},{... | collective-permute-start | bytes 589832 | tf_op jit(solution)/shard_map/ppermute | solution.py:427
  6.1 9.2 %collective-permute-start = (bf16[272,128]{1,0:T(8,128)(2,1)S(1)}, bf16[272,128]{1,0:T(8,128)(2,1)S(1)}, u32[]{:S(2)}, u32[]{:S(2)}) collective-permute-start(bf16[272,128]{1,0:T(8,128)(2,1)S(1)} %get-tuple-element.90), channel_id=1, source_target_pairs={{0,4},{4,0},{8,12},{12,8},{16,20},{20,16},{24,28},{28,24},{1,5},{5... | collective-permute-start | bytes 208904 | tf_op jit(solution)/shard_map/ppermute | solution.py:22
  11.1 12.3 %collective-permute-start.3 = (bf16[272,128]{1,0:T(8,128)(2,1)S(1)}, bf16[272,128]{1,0:T(8,128)(2,1)S(1)}, u32[]{:S(2)}, u32[]{:S(2)}) collective-permute-start(bf16[272,128]{1,0:T(8,128)(2,1)S(1)} %get-tuple-element.93), channel_id=1, source_target_pairs={{0,16},{4,20},{8,24},{12,28},{16,0},{20,4},{24,8},{28,12},{1,17},{... | collective-permute-start | bytes 208904 | tf_op jit(solution)/shard_map/ppermute | solution.py:22
  15.3 12.0 %collective-permute-start.4 = (bf16[272,128]{1,0:T(8,128)(2,1)S(1)}, bf16[272,128]{1,0:T(8,128)(2,1)S(1)}, u32[]{:S(2)}, u32[]{:S(2)}) collective-permute-start(bf16[272,128]{1,0:T(8,128)(2,1)S(1)} %get-tuple-element.94), channel_id=1, source_target_pairs={{0,20},{4,16},{8,28},{12,24},{16,4},{20,0},{24,12},{28,8},{1,21},{... | collective-permute-start | bytes 208904 | tf_op jit(solution)/shard_map/ppermute | solution.py:22
  17.1 10.2 %collective-permute-start.5 = (bf16[272,128]{1,0:T(8,128)(2,1)S(1)}, bf16[272,128]{1,0:T(8,128)(2,1)S(1)}, u32[]{:S(2)}, u32[]{:S(2)}) collective-permute-start(bf16[272,128]{1,0:T(8,128)(2,1)S(1)} %get-tuple-element.95), channel_id=1, source_target_pairs={{0,24},{4,28},{8,16},{12,20},{16,8},{20,12},{24,0},{28,4},{1,25},{... | collective-permute-start | bytes 208904 | tf_op jit(solution)/shard_map/ppermute | solution.py:22
  31.3 8.6 %collective-permute-start.10 = (bf16[256,128]{1,0:T(8,128)(2,1)S(1)}, bf16[256,128]{1,0:T(8,128)(2,1)S(1)}, u32[]{:S(2)}, u32[]{:S(2)}) collective-permute-start(bf16[256,128]{1,0:T(8,128)(2,1)S(1)} %get-tuple-element.114), channel_id=1, source_target_pairs={{0,12},{4,8},{8,4},{12,0},{16,28},{20,24},{24,20},{28,16},{1,13},{... | collective-permute-start | bytes 196616 | tf_op jit(solution)/shard_map/ppermute | solution.py:22
  32.3 10.2 %collective-permute-start.11 = (bf16[256,128]{1,0:T(8,128)(2,1)S(1)}, bf16[256,128]{1,0:T(8,128)(2,1)S(1)}, u32[]{:S(2)}, u32[]{:S(2)}) collective-permute-start(bf16[256,128]{1,0:T(8,128)(2,1)S(1)} %get-tuple-element.115), channel_id=1, source_target_pairs={{0,16},{4,20},{8,24},{12,28},{16,0},{20,4},{24,8},{28,12},{1,17},{... | collective-permute-start | bytes 196616 | tf_op jit(solution)/shard_map/ppermute | solution.py:22
  34.3 10.3 %collective-permute-start.12 = (bf16[256,128]{1,0:T(8,128)(2,1)S(1)}, bf16[256,128]{1,0:T(8,128)(2,1)S(1)}, u32[]{:S(2)}, u32[]{:S(2)}) collective-permute-start(bf16[256,128]{1,0:T(8,128)(2,1)S(1)} %get-tuple-element.116), channel_id=1, source_target_pairs={{0,20},{4,16},{8,28},{12,24},{16,4},{20,0},{24,12},{28,8},{1,21},{... | collective-permute-start | bytes 196616 | tf_op jit(solution)/shard_map/ppermute | solution.py:22
  35.2 9.5 %collective-permute-start.13 = (bf16[256,128]{1,0:T(8,128)(2,1)S(1)}, bf16[256,128]{1,0:T(8,128)(2,1)S(1)}, u32[]{:S(2)}, u32[]{:S(2)}) collective-permute-start(bf16[256,128]{1,0:T(8,128)(2,1)S(1)} %get-tuple-element.117), channel_id=1, source_target_pairs={{0,24},{4,28},{8,16},{12,20},{16,8},{20,12},{24,0},{28,4},{1,25},{... | collective-permute-start | bytes 196616 | tf_op jit(solution)/shard_map/ppermute | solution.py:22
  44.7 34.9 %collective-permute-start.15 = (bf16[2048,384]{1,0:T(8,128)(2,1)}, bf16[2048,384]{1,0:T(8,128)(2,1)}, u32[]{:S(2)}, u32[]{:S(2)}) collective-permute-start(bf16[2048,384]{1,0:T(8,128)(2,1)} %param.20), channel_id=1, source_target_pairs={{0,4},{4,0},{8,12},{12,8},{16,20},{20,16},{24,28},{28,24},{1,5},{5... | collective-permute-start | bytes 4718600 | tf_op jit(solution)/shard_map/ppermute | solution.py:22
  50.7 15.0 %collective-permute-start.16 = (bf16[128,2048]{1,0:T(8,128)(2,1)S(1)}, bf16[128,2048]{1,0:T(8,128)(2,1)}, u32[]{:S(2)}, u32[]{:S(2)}) collective-permute-start(bf16[128,2048]{1,0:T(8,128)(2,1)S(1)} %attend.1), channel_id=1, source_target_pairs={{0,8},{4,12},{8,16},{12,20},{16,24},{20,28},{1,9},{5,13},{9,17},{1... | collective-permute-start | bytes 1572872 | tf_op jit(solution)/shard_map/ppermute | solution.py:495
  56.1 14.2 %collective-permute-start.17 = (bf16[128,2048]{1,0:T(8,128)(2,1)S(1)}, bf16[128,2048]{1,0:T(8,128)(2,1)S(1)}, u32[]{:S(2)}, u32[]{:S(2)}) collective-permute-start(bf16[128,2048]{1,0:T(8,128)(2,1)S(1)} %attend.1), channel_id=1, source_target_pairs={{8,0},{12,4},{16,8},{20,12},{24,16},{28,20},{9,1},{13,5},{17,9},{2... | collective-permute-start | bytes 1572872 | tf_op jit(solution)/shard_map/ppermute | solution.py:495
  70.3 30.3 %collective-permute-start.20 = (bf16[128,2048]{1,0:T(8,128)(2,1)S(1)}, bf16[128,2048]{1,0:T(8,128)(2,1)S(1)}, u32[]{:S(2)}, u32[]{:S(2)}) collective-permute-start(bf16[128,2048]{1,0:T(8,128)(2,1)S(1)} %attend.1), channel_id=1, source_target_pairs={{0,24},{4,28},{24,0},{28,4},{1,25},{5,29},{25,1},{29,5},{2,26},{6,... | collective-permute-start | bytes 1572872 | tf_op jit(solution)/shard_map/ppermute | solution.py:495
  72.7 23.4 %collective-permute-start.18 = (bf16[128,2048]{1,0:T(8,128)(2,1)}, bf16[128,2048]{1,0:T(8,128)(2,1)S(1)}, u32[]{:S(2)}, u32[]{:S(2)}) collective-permute-start(bf16[128,2048]{1,0:T(8,128)(2,1)} %collective-permute-done.16), channel_id=1, source_target_pairs={{0,8},{4,12},{8,16},{12,20},{16,24},{20,28},{1,9},{5,13},{9,17},{1... | collective-permute-start | bytes 1572872 | tf_op jit(solution)/shard_map/ppermute | solution.py:495
  74.5 25.5 %collective-permute-start.19 = (bf16[128,2048]{1,0:T(8,128)(2,1)S(1)}, bf16[128,2048]{1,0:T(8,128)(2,1)S(1)}, u32[]{:S(2)}, u32[]{:S(2)}) collective-permute-start(bf16[128,2048]{1,0:T(8,128)(2,1)S(1)} %collective-permute-done.17), channel_id=1, source_target_pairs={{8,0},{12,4},{16,8},{20,12},{24,16},{28,20},{9,1},{13,5},{17,9},{2... | collective-permute-start | bytes 1572872 | tf_op jit(solution)/shard_map/ppermute | solution.py:495
  103.4 8.9 %collective-permute-start.24 = (bf16[128,768]{1,0:T(8,128)(2,1)S(1)}, bf16[128,768]{1,0:T(8,128)(2,1)S(1)}, u32[]{:S(2)}, u32[]{:S(2)}) collective-permute-start(bf16[128,768]{1,0:T(8,128)(2,1)S(1)} %get-tuple-element.142), channel_id=1, source_target_pairs={{0,3},{1,0},{2,1},{3,2},{4,7},{5,4},{6,5},{7,6},{8,11},{9,8},{10,9... | collective-permute-start | bytes 589832 | tf_op jit(solution)/shard_map/ppermute | solution.py:27
  113.4 10.8 %collective-permute-start.26 = (bf16[64,768]{1,0:T(8,128)(2,1)S(1)}, bf16[64,768]{1,0:T(8,128)(2,1)S(1)}, u32[]{:S(2)}, u32[]{:S(2)}) collective-permute-start(bf16[64,768]{1,0:T(8,128)(2,1)S(1)} %get-tuple-element.146), channel_id=1, source_target_pairs={{0,16},{4,20},{8,24},{12,28},{16,0},{20,4},{24,8},{28,12},{1,17},{... | collective-permute-start | bytes 294920 | tf_op jit(solution)/shard_map/ppermute | solution.py:22
  114.4 9.8 %collective-permute-start.27 = (bf16[64,768]{1,0:T(8,128)(2,1)S(1)}, bf16[64,768]{1,0:T(8,128)(2,1)S(1)}, u32[]{:S(2)}, u32[]{:S(2)}) collective-permute-start(bf16[64,768]{1,0:T(8,128)(2,1)S(1)} %get-tuple-element.147), channel_id=1, source_target_pairs={{0,24},{4,28},{8,16},{12,20},{16,8},{20,12},{24,0},{28,4},{1,25},{... | collective-permute-start | bytes 294920 | tf_op jit(solution)/shard_map/ppermute | solution.py:22
  124.4 15.4 %collective-permute-start.28 = (bf16[64,3072]{1,0:T(8,128)(2,1)S(1)}, bf16[64,3072]{1,0:T(8,128)(2,1)S(1)}, u32[]{:S(2)}, u32[]{:S(2)}) collective-permute-start(bf16[64,3072]{1,0:T(8,128)(2,1)S(1)} %pack.2.refs_0_), channel_id=1, source_target_pairs={{0,2},{1,3},{2,0},{3,1},{4,6},{5,7},{6,4},{7,5},{8,10},{9,11},{10,... | collective-permute-start | bytes 1179656 | tf_op jit(solution)/shard_map/ppermute | solution.py:27
  128.9 10.7 %collective-permute-start.31 = (bf16[64,768]{1,0:T(8,128)(2,1)S(1)}, bf16[64,768]{1,0:T(8,128)(2,1)S(1)}, u32[]{:S(2)}, u32[]{:S(2)}) collective-permute-start(bf16[64,768]{1,0:T(8,128)(2,1)S(1)} %get-tuple-element.154), channel_id=1, source_target_pairs={{0,20},{4,16},{8,28},{12,24},{16,4},{20,0},{24,12},{28,8},{1,21},{... | collective-permute-start | bytes 294920 | tf_op jit(solution)/shard_map/ppermute | solution.py:22
  128.9 10.7 %collective-permute-start.32 = (bf16[64,768]{1,0:T(8,128)(2,1)S(1)}, bf16[64,768]{1,0:T(8,128)(2,1)S(1)}, u32[]{:S(2)}, u32[]{:S(2)}) collective-permute-start(bf16[64,768]{1,0:T(8,128)(2,1)S(1)} %get-tuple-element.155), channel_id=1, source_target_pairs={{0,28},{4,24},{8,20},{12,16},{16,12},{20,8},{24,4},{28,0},{1,29},{... | collective-permute-start | bytes 294920 | tf_op jit(solution)/shard_map/ppermute | solution.py:22
  132.0 9.1 %collective-permute-start.33 = (bf16[64,3072]{1,0:T(8,128)(2,1)S(1)}, bf16[64,3072]{1,0:T(8,128)(2,1)S(1)}, u32[]{:S(2)}, u32[]{:S(2)}) collective-permute-start(bf16[64,3072]{1,0:T(8,128)(2,1)S(1)} %pack.2.refs_0_), channel_id=1, source_target_pairs={{0,1},{1,0},{2,3},{3,2},{4,5},{5,4},{6,7},{7,6},{8,9},{9,8},{10,11... | collective-permute-start | bytes 1179656 | tf_op jit(solution)/shard_map/ppermute | solution.py:27
  139.9 11.5 %collective-permute-start.35 = (bf16[64,3072]{1,0:T(8,128)(2,1)S(1)}, bf16[64,3072]{1,0:T(8,128)(2,1)S(1)}, u32[]{:S(2)}, u32[]{:S(2)}) collective-permute-start(bf16[64,3072]{1,0:T(8,128)(2,1)S(1)} %pack.3.refs_0_), channel_id=1, source_target_pairs={{0,2},{1,3},{2,0},{3,1},{4,6},{5,7},{6,4},{7,5},{8,10},{9,11},{10,... | collective-permute-start | bytes 1179656 | tf_op jit(solution)/shard_map/ppermute | solution.py:27
  156.9 11.5 %collective-permute-start.37 = (bf16[2,256,768]{2,1,0:T(8,128)(2,1)S(1)}, bf16[2,256,768]{2,1,0:T(8,128)(2,1)S(1)}, u32[]{:S(2)}, u32[]{:S(2)}) collective-permute-start(bf16[2,256,768]{2,1,0:T(8,128)(2,1)S(1)} %get-tuple-element.158), channel_id=1, source_target_pairs={{0,1},{1,0},{2,3},{3,2},{4,5},{5,4},{6,7},{7,6},{8,9},{9,8},{10,11... | collective-permute-start | bytes 2359304 | tf_op jit(solution)/shard_map/ppermute | solution.py:27
  157.6 11.0 %collective-permute-start.36 = (bf16[128,768]{1,0:T(8,128)(2,1)S(1)}, bf16[128,768]{1,0:T(8,128)(2,1)S(1)}, u32[]{:S(2)}, u32[]{:S(2)}) collective-permute-start(bf16[128,768]{1,0:T(8,128)(2,1)S(1)} %get-tuple-element.159), channel_id=1, source_target_pairs={{0,0},{1,8},{2,16},{3,24},{4,4},{5,12},{6,20},{7,28},{8,1},{9,9},{... | collective-permute-start | bytes 589832 | tf_op jit(solution)/shard_map/ppermute | solution.py:427
  175.4 14.0 %collective-permute-start.38 = (bf16[256,768]{1,0:T(8,128)(2,1)S(1)}, bf16[256,768]{1,0:T(8,128)(2,1)S(1)}, u32[]{:S(2)}, u32[]{:S(2)}) collective-permute-start(bf16[256,768]{1,0:T(8,128)(2,1)S(1)} %fusion), channel_id=1, source_target_pairs={{0,2},{1,3},{2,0},{3,1},{4,6},{5,7},{6,4},{7,5},{8,10},{9,11},{10,... | collective-permute-start | bytes 1179656 | tf_op jit(solution)/shard_map/ppermute | solution.py:27
  179.7 17.9 %collective-permute-start.42 = (bf16[256,768]{1,0:T(8,128)(2,1)S(1)}, bf16[256,768]{1,0:T(8,128)(2,1)S(1)}, u32[]{:S(2)}, u32[]{:S(2)}) collective-permute-start(bf16[256,768]{1,0:T(8,128)(2,1)S(1)} %fusion.1), channel_id=1, source_target_pairs={{0,2},{1,3},{2,0},{3,1},{4,6},{5,7},{6,4},{7,5},{8,10},{9,11},{10,... | collective-permute-start | bytes 1179656 | tf_op jit(solution)/shard_map/ppermute | solution.py:27
  189.6 9.9 %collective-permute-start.44 = (bf16[64,768]{1,0:T(8,128)(2,1)S(1)}, bf16[64,768]{1,0:T(8,128)(2,1)S(1)}, u32[]{:S(2)}, u32[]{:S(2)}) collective-permute-start(bf16[64,768]{1,0:T(8,128)(2,1)S(1)} %get-tuple-element.167), channel_id=1, source_target_pairs={{0,8},{4,12},{8,0},{12,4},{16,24},{20,28},{24,16},{28,20},{1,9},{5... | collective-permute-start | bytes 294920 | tf_op jit(solution)/shard_map/ppermute | solution.py:22
  189.9 11.1 %collective-permute-start.46 = (bf16[64,768]{1,0:T(8,128)(2,1)S(1)}, bf16[64,768]{1,0:T(8,128)(2,1)S(1)}, u32[]{:S(2)}, u32[]{:S(2)}) collective-permute-start(bf16[64,768]{1,0:T(8,128)(2,1)S(1)} %get-tuple-element.169), channel_id=1, source_target_pairs={{0,16},{4,20},{8,24},{12,28},{16,0},{20,4},{24,8},{28,12},{1,17},{... | collective-permute-start | bytes 294920 | tf_op jit(solution)/shard_map/ppermute | solution.py:22
  191.2 13.4 %collective-permute-start.48 = (bf16[64,768]{1,0:T(8,128)(2,1)S(1)}, bf16[64,768]{1,0:T(8,128)(2,1)S(1)}, u32[]{:S(2)}, u32[]{:S(2)}) collective-permute-start(bf16[64,768]{1,0:T(8,128)(2,1)S(1)} %get-tuple-element.171), channel_id=1, source_target_pairs={{0,24},{4,28},{8,16},{12,20},{16,8},{20,12},{24,0},{28,4},{1,25},{... | collective-permute-start | bytes 294920 | tf_op jit(solution)/shard_map/ppermute | solution.py:22
  199.6 11.3 %collective-permute-start.47 = (bf16[64,768]{1,0:T(8,128)(2,1)S(1)}, bf16[64,768]{1,0:T(8,128)(2,1)S(1)}, u32[]{:S(2)}, u32[]{:S(2)}) collective-permute-start(bf16[64,768]{1,0:T(8,128)(2,1)S(1)} %get-tuple-element.170), channel_id=1, source_target_pairs={{0,20},{4,16},{8,28},{12,24},{16,4},{20,0},{24,12},{28,8},{1,21},{... | collective-permute-start | bytes 294920 | tf_op jit(solution)/shard_map/ppermute | solution.py:22
  201.0 9.9 %collective-permute-start.49 = (bf16[64,768]{1,0:T(8,128)(2,1)S(1)}, bf16[64,768]{1,0:T(8,128)(2,1)S(1)}, u32[]{:S(2)}, u32[]{:S(2)}) collective-permute-start(bf16[64,768]{1,0:T(8,128)(2,1)S(1)} %get-tuple-element.172), channel_id=1, source_target_pairs={{0,28},{4,24},{8,20},{12,16},{16,12},{20,8},{24,4},{28,0},{1,29},{... | collective-permute-start | bytes 294920 | tf_op jit(solution)/shard_map/ppermute | solution.py:22
  (28 other events, 308.5 us)

commit v9 on v8

--- a/solution.py
+++ b/solution.py
@@ -14,7 +14,7 @@
 BF16 = jnp.bfloat16
 HIGHEST = lax.Precision.HIGHEST
 SMALL_VMEM = 12 * 1024 * 1024
-EXPERT_VMEM = 48 * 1024 * 1024
+EXPERT_VMEM = 42 * 1024 * 1024
 
 
 def permute_seq(value, move):
@@ -278,31 +278,27 @@
         hidden_ref[:, j * width : (j + 1) * width] = hidden
 
 
-def write_out(hidden_ref, low_ref, sent_ref, kept_ref, copies):
+def hidden_kernel(n_head, steps, aligned, owner_ref, *refs):
+    pieces = refs[:n_head]
+    gate_ref, up_ref, down_ref, hidden_ref, low_ref = refs[n_head : n_head + 5]
+    rows_ref, wide_ref, wide_sem, low_sem = refs[n_head + 5 :]
+    wide = wide_copies(gate_ref, up_ref, wide_ref, wide_sem, steps, aligned)
+    low = low_copies(n_head, owner_ref, down_ref, low_ref, low_sem)
+    for copy in wide + low:
+        copy.start()
+    fill_hidden(aligned, owner_ref, pieces, rows_ref, wide_ref, hidden_ref, wide)
+    for copy in low:
+        copy.wait()
+
+
+def down_kernel(hidden_ref, low_ref, sent_ref, kept_ref):
     nx = sent_ref.shape[0]
-    for j, copy in enumerate(copies):
-        copy.wait()
+    for j in range(low_ref.shape[0]):
         out = jnp.dot(hidden_ref[...], low_ref[j], preferred_element_type=F32).astype(BF16)
         if j < nx:
             sent_ref[j] = out
         else:
             kept_ref[j - nx] = out
-
-
-def hidden_kernel(n_head, steps, aligned, owner_ref, *refs):
-    pieces = refs[:n_head]
-    gate_ref, up_ref, hidden_ref, rows_ref, wide_ref, wide_sem = refs[n_head:]
-    wide = wide_copies(gate_ref, up_ref, wide_ref, wide_sem, steps, aligned)
-    for copy in wide:
-        copy.start()
-    fill_hidden(aligned, owner_ref, pieces, rows_ref, wide_ref, hidden_ref, wide)
-
-
-def down_kernel(n_head, owner_ref, hidden_ref, down_ref, sent_ref, kept_ref, low_ref, low_sem):
-    low = low_copies(n_head, owner_ref, down_ref, low_ref, low_sem)
-    for copy in low:
-        copy.start()
-    write_out(hidden_ref, low_ref, sent_ref, kept_ref, low)
 
 
 def expert_call(owners, pieces, gate_weight, up_weight, down_weight, before_down):
@@ -315,37 +311,33 @@
     struct = jax.ShapeDtypeStruct
     rows = pltpu.VMEM((count, depth), BF16)
     wide = pltpu.VMEM((steps, depth, 2 * width) if aligned else (2, depth, width), BF16)
-    low = pltpu.VMEM((n_head, units, part), BF16)
     wide_sem, low_sem = pltpu.SemaphoreType.DMA((steps, 2)), pltpu.SemaphoreType.DMA((n_head,))
     outs = [struct((nx, count, part), BF16), struct((n_head - nx, count, part), BF16)]
     hidden = struct((count, units), BF16)
     work = 2 * count * depth * units
-    hidden = local_call(
+    hidden, low = local_call(
         functools.partial(hidden_kernel, n_head, steps, aligned),
         "hidden",
-        hidden,
+        [hidden, struct((n_head, units, part), BF16)],
         2 * work,
         owners,
         *pieces,
         gate_weight,
         up_weight,
-        scratch=[rows, wide, wide_sem],
+        down_weight,
+        scratch=[rows, wide, wide_sem, low_sem],
         scalars=1,
-        far=2,
+        far=3,
         vmem=EXPERT_VMEM,
     )
     hidden = lax.optimization_barrier((hidden, before_down))[0]
     return local_call(
-        functools.partial(down_kernel, n_head),
+        down_kernel,
         "down",
         outs,
         work,
-        owners,
         hidden,
-        down_weight,
-        scratch=[low, low_sem],
-        scalars=1,
-        far=1,
+        low,
         vmem=EXPERT_VMEM,
     )
 
@@ -497,7 +489,6 @@
     ups = lambda j: [(q, q + j) for q in range(nz - j)]
     downs = lambda j: [(q + j, q) for q in range(nz - j)]
     below, above = along(attended, ups(1)), along(attended, downs(1))
-    direct = lax.optimization_barrier((attended, below, above))[0]
     take, mix = local_call(
         functools.partial(plan_kernel, capacity),
         "plan",
@@ -516,10 +507,10 @@
     for j in range(3, nz):
         if 2 * j >= nz:
             shifts.append((j, j))
-            rows_of.append(along(direct, ups(j) + downs(j)))
+            rows_of.append(along(attended, ups(j) + downs(j)))
         else:
             shifts += [(j, 0), (0, j)]
-            rows_of += [along(direct, ups(j)), along(direct, downs(j))]
+            rows_of += [along(attended, ups(j)), along(attended, downs(j))]
     products = [jnp.dot(r, w_z, preferred_element_type=F32).astype(BF16) for r in rows_of]
     products, take, mix = lax.optimization_barrier((products, take, mix))
     block = struct((tokens, part), BF16)
@@ -593,9 +584,11 @@
                         piece, lambda q, m=m: q // CORES * CORES + (q % CORES - m) % CORES
                     )
                 )
-        first = [crossing, middle] if group else None
+        first = [blocks, middle] if group else None
         if group + 1 < ny:
             first = (first, fars[group + 1])
+        if group:
+            pieces = lax.optimization_barrier((pieces, crossing))[0]
         sent, kept = expert_call(owners, pieces, gate_weight, up_weight, down_weight, first)
         if group == 0:
             middle = crossed(lax.optimization_barrier((middle_there, sent))[0])

time: 213 us -> 204 us (0.958)
  waiting for transfers between devices: 84.4 us -> 64.9 us
  starting transfers between devices: 79.4 us -> 94.9 us
  Pallas kernels: 34.5 us -> 30.3 us
    ppermute x5, starting transfers between devices: 12.1 us -> 28 us  [along(): return lax.ppermute(value, 'seq', perm)]
    ppermute x5, waiting for transfers between devices: 25.8 us -> 13.4 us  [along(): return lax.ppermute(value, 'seq', perm)]
    ppermute x29, waiting for transfers between devices: 35.8 us -> 31.2 us  [permute_seq(): lax.ppermute(value, 'seq', [(source, move(source)) for source in range(co...]
    pallas_call x15, Pallas kernels: 34.5 us -> 30.3 us  [local_call(): pl.pallas_call(kernel, out_shape=out_shape, in_specs=[pl.BlockSpec(memory...]
    ppermute x13, waiting for transfers between devices: 22.7 us -> 20.3 us  [permute_head(): lax.ppermute(value, 'head', [(source, move(source)) for source in range(c...]
  transfers between devices with their start and end apart: 50 -> 50, of which waited for: 24 -> 21; matrix products, arithmetic and copies ran while one was open for 3% -> 4% of each run, Pallas kernels for 10% -> 11%
where the time goes in v9:
time: 204 us
  starting transfers between devices  94.9 us (47%)
  waiting for transfers between devices  64.9 us (32%)
  Pallas kernels  30.3 us (15%)
  local copies, waits for them, and re-layouts  8.09 us (4%)
  matrix products  4.67 us (2%)
    ppermute x29, starting transfers between devices, permute_seq(): lax.ppermute(value, 'seq', [(source, move(source)) for source in range(co...  51 us
    ppermute x29, waiting for transfers between devices, permute_seq(): lax.ppermute(value, 'seq', [(source, move(source)) for source in range(co...  31.2 us
    pallas_call x15, Pallas kernels, local_call(): pl.pallas_call(kernel, out_shape=out_shape, in_specs=[pl.BlockSpec(memory...  30.3 us
    ppermute x5, starting transfers between devices, along(): return lax.ppermute(value, 'seq', perm)  28 us
    ppermute x13, waiting for transfers between devices, permute_head(): lax.ppermute(value, 'head', [(source, move(source)) for source in range(c...  20.3 us
    ppermute x5, waiting for transfers between devices, along(): return lax.ppermute(value, 'seq', perm)  13.4 us
    ppermute x13, starting transfers between devices, permute_head(): lax.ppermute(value, 'head', [(source, move(source)) for source in range(c...  12.7 us
    unnamed x22, local copies, waits for them, and re-layouts  5.41 us
  transfers between devices with their start and end apart: 50, of which 21 were waited for; matrix products, arithmetic and copies ran while one was open for 4% of the time, Pallas kernels for 11%

profile of v9, /device:TPU:0, one launch (start us, length us, event | category | flops | bytes accessed | tf_op | source)
XLA Modules:
  0.0 203.7 jit_solution(169624196188435922)
XLA Ops:
  6.1 3.0 %collective-permute-start = (bf16[272,128]{1,0:T(8,128)(2,1)S(1)}, bf16[272,128]{1,0:T(8,128)(2,1)S(1)}, u32[]{:S(2)}, u32[]{:S(2)}) collective-permute-start(bf16[272,128]{1,0:T(8,128)(2,1)S(1)} %get-tuple-element.97), channel_id=1, source_target_pairs={{0,4},{4,0},{8,12},{12,8},{16,20},{20,16},{24,28},{28,24},{1,5},{5... | collective-permute-start | bytes 208904 | tf_op jit(solution)/shard_map/ppermute | solution.py:22
  11.1 4.2 %collective-permute-start.3 = (bf16[272,128]{1,0:T(8,128)(2,1)S(1)}, bf16[272,128]{1,0:T(8,128)(2,1)S(1)}, u32[]{:S(2)}, u32[]{:S(2)}) collective-permute-start(bf16[272,128]{1,0:T(8,128)(2,1)S(1)} %get-tuple-element.100), channel_id=1, source_target_pairs={{0,16},{4,20},{8,24},{12,28},{16,0},{20,4},{24,8},{28,12},{1,17},{... | collective-permute-start | bytes 208904 | tf_op jit(solution)/shard_map/ppermute | solution.py:22
  17.1 2.4 %collective-permute-start.5 = (bf16[272,128]{1,0:T(8,128)(2,1)S(1)}, bf16[272,128]{1,0:T(8,128)(2,1)S(1)}, u32[]{:S(2)}, u32[]{:S(2)}) collective-permute-start(bf16[272,128]{1,0:T(8,128)(2,1)S(1)} %get-tuple-element.102), channel_id=1, source_target_pairs={{0,24},{4,28},{8,16},{12,20},{16,8},{20,12},{24,0},{28,4},{1,25},{... | collective-permute-start | bytes 208904 | tf_op jit(solution)/shard_map/ppermute | solution.py:22
  20.9 2.5 %collective-permute-done.3.refs_4_ = bf16[272,128]{1,0:T(8,128)(2,1)S(1)} collective-permute-done((bf16[272,128]{1,0:T(8,128)(2,1)S(1)}, bf16[272,128]{1,0:T(8,128)(2,1)S(1)}, u32[]{:S(2)}, u32[]{:S(2)}) %collective-permute-start.3) | collective-permute-done | bytes 69664 | tf_op jit(solution)/shard_map/ppermute | solution.py:22
  23.4 3.9 %collective-permute-done.4.refs_5_ = bf16[272,128]{1,0:T(8,128)(2,1)S(1)} collective-permute-done((bf16[272,128]{1,0:T(8,128)(2,1)S(1)}, bf16[272,128]{1,0:T(8,128)(2,1)S(1)}, u32[]{:S(2)}, u32[]{:S(2)}) %collective-permute-start.4) | collective-permute-done | bytes 69664 | tf_op jit(solution)/shard_map/ppermute | solution.py:22
  28.4 2.9 %collective-permute-start.9 = (bf16[256,128]{1,0:T(8,128)(2,1)S(1)}, bf16[256,128]{1,0:T(8,128)(2,1)S(1)}, u32[]{:S(2)}, u32[]{:S(2)}) collective-permute-start(bf16[256,128]{1,0:T(8,128)(2,1)S(1)} %get-tuple-element.120), channel_id=1, source_target_pairs={{0,8},{4,12},{8,0},{12,4},{16,24},{20,28},{24,16},{28,20},{1,9},{5... | collective-permute-start | bytes 196616 | tf_op jit(solution)/shard_map/ppermute | solution.py:22
  36.7 3.2 %collective-permute-start.14 = (bf16[256,128]{1,0:T(8,128)(2,1)S(1)}, bf16[256,128]{1,0:T(8,128)(2,1)S(1)}, u32[]{:S(2)}, u32[]{:S(2)}) collective-permute-start(bf16[256,128]{1,0:T(8,128)(2,1)S(1)} %get-tuple-element.125), channel_id=1, source_target_pairs={{0,28},{4,24},{8,20},{12,16},{16,12},{20,8},{24,4},{28,0},{1,29},{... | collective-permute-start | bytes 196616 | tf_op jit(solution)/shard_map/ppermute | solution.py:22
  39.9 2.6 %collective-permute-done.11.refs_4_ = bf16[256,128]{1,0:T(8,128)(2,1)S(1)} collective-permute-done((bf16[256,128]{1,0:T(8,128)(2,1)S(1)}, bf16[256,128]{1,0:T(8,128)(2,1)S(1)}, u32[]{:S(2)}, u32[]{:S(2)}) %collective-permute-start.11) | collective-permute-done | bytes 65568 | tf_op jit(solution)/shard_map/ppermute | solution.py:22
  47.8 2.9 %attend.1 = bf16[128,2048]{1,0:T(8,128)(2,1)S(1)} custom-call(s32[1]{0:T(128)} %bitcast.me_ref, f32[1,128]{1,0:T(1,128)S(1)} %get-tuple-element.105.doc_ref, f32[128,16]{1,0:T(8,128)S(1)} %get-tuple-element.106.sum_ref, f32[16,128]{1,0:T(8,128)S(1)} %get-tuple-element.107.sum_rows_ref, bf16[128,2048]{1,0:T(8,128)(2,1)S(1)} %copy-done, ...), custom_call_target="tpu_custom_call" | custom-call | flops 201326592 | bytes 2646532 | tf_op jit(solution)/shard_map/attend/pallas_call | solution.py:350
  50.7 5.4 %collective-permute-start.16 = (bf16[128,2048]{1,0:T(8,128)(2,1)S(1)}, bf16[128,2048]{1,0:T(8,128)(2,1)}, u32[]{:S(2)}, u32[]{:S(2)}) collective-permute-start(bf16[128,2048]{1,0:T(8,128)(2,1)S(1)} %attend.1), channel_id=1, source_target_pairs={{0,8},{4,12},{8,16},{12,20},{16,24},{20,28},{1,9},{5,13},{9,17},{1... | collective-permute-start | bytes 1572872 | tf_op jit(solution)/shard_map/ppermute | solution.py:487
  57.9 3.4 %collective-permute-start.20 = (bf16[128,2048]{1,0:T(8,128)(2,1)S(1)}, bf16[128,2048]{1,0:T(8,128)(2,1)S(1)}, u32[]{:S(2)}, u32[]{:S(2)}) collective-permute-start(bf16[128,2048]{1,0:T(8,128)(2,1)S(1)} %attend.1), channel_id=1, source_target_pairs={{0,24},{4,28},{24,0},{28,4},{1,25},{5,29},{25,1},{29,5},{2,26},{6,... | collective-permute-start | bytes 1572872 | tf_op jit(solution)/shard_map/ppermute | solution.py:487
  63.1 4.6 %collective-permute-done.16 = bf16[128,2048]{1,0:T(8,128)(2,1)} collective-permute-done((bf16[128,2048]{1,0:T(8,128)(2,1)S(1)}, bf16[128,2048]{1,0:T(8,128)(2,1)}, u32[]{:S(2)}, u32[]{:S(2)}) %collective-permute-start.16) | collective-permute-done | bytes 524320 | tf_op jit(solution)/shard_map/ppermute | solution.py:487
  67.6 16.7 %collective-permute-start.18 = (bf16[128,2048]{1,0:T(8,128)(2,1)}, bf16[128,2048]{1,0:T(8,128)(2,1)S(1)}, u32[]{:S(2)}, u32[]{:S(2)}) collective-permute-start(bf16[128,2048]{1,0:T(8,128)(2,1)} %collective-permute-done.16), channel_id=1, source_target_pairs={{0,8},{4,12},{8,16},{12,20},{16,24},{20,28},{1,9},{5,13},{9,17},{1... | collective-permute-start | bytes 1572872 | tf_op jit(solution)/shard_map/ppermute | solution.py:487
  90.3 5.6 %collective-permute-done.18 = bf16[128,2048]{1,0:T(8,128)(2,1)S(1)} collective-permute-done((bf16[128,2048]{1,0:T(8,128)(2,1)}, bf16[128,2048]{1,0:T(8,128)(2,1)S(1)}, u32[]{:S(2)}, u32[]{:S(2)}) %collective-permute-start.18) | collective-permute-done | bytes 524320 | tf_op jit(solution)/shard_map/ppermute | solution.py:487
  96.4 3.2 %collective-permute-done.19 = bf16[128,2048]{1,0:T(8,128)(2,1)S(1)} collective-permute-done((bf16[128,2048]{1,0:T(8,128)(2,1)S(1)}, bf16[128,2048]{1,0:T(8,128)(2,1)S(1)}, u32[]{:S(2)}, u32[]{:S(2)}) %collective-permute-start.19) | collective-permute-done | bytes 524320 | tf_op jit(solution)/shard_map/ppermute | solution.py:487
  104.8 3.4 %collective-permute-done.22.refs_1_ = bf16[128,768]{1,0:T(8,128)(2,1)S(1)} collective-permute-done((bf16[128,768]{1,0:T(8,128)(2,1)S(1)}, bf16[128,768]{1,0:T(8,128)(2,1)S(1)}, u32[]{:S(2)}, u32[]{:S(2)}) %collective-permute-start.22) | collective-permute-done | bytes 196640 | tf_op jit(solution)/shard_map/ppermute | solution.py:27
  109.5 2.8 %collective-permute-done.24.refs_3_ = bf16[128,768]{1,0:T(8,128)(2,1)S(1)} collective-permute-done((bf16[128,768]{1,0:T(8,128)(2,1)S(1)}, bf16[128,768]{1,0:T(8,128)(2,1)S(1)}, u32[]{:S(2)}, u32[]{:S(2)}) %collective-permute-start.24) | collective-permute-done | bytes 196640 | tf_op jit(solution)/shard_map/ppermute | solution.py:27
  114.3 2.8 %collective-permute-start.27 = (bf16[64,768]{1,0:T(8,128)(2,1)S(1)}, bf16[64,768]{1,0:T(8,128)(2,1)S(1)}, u32[]{:S(2)}, u32[]{:S(2)}) collective-permute-start(bf16[64,768]{1,0:T(8,128)(2,1)S(1)} %get-tuple-element.153), channel_id=1, source_target_pairs={{0,24},{4,28},{8,16},{12,20},{16,8},{20,12},{24,0},{28,4},{1,25},{... | collective-permute-start | bytes 294920 | tf_op jit(solution)/shard_map/ppermute | solution.py:22
  119.3 4.2 %collective-permute-done.26.refs_2_ = bf16[64,768]{1,0:T(8,128)(2,1)S(1)} collective-permute-done((bf16[64,768]{1,0:T(8,128)(2,1)S(1)}, bf16[64,768]{1,0:T(8,128)(2,1)S(1)}, u32[]{:S(2)}, u32[]{:S(2)}) %collective-permute-start.26) | collective-permute-done | bytes 98336 | tf_op jit(solution)/shard_map/ppermute | solution.py:22
  127.0 2.5 %collective-permute-start.30 = (bf16[64,768]{1,0:T(8,128)(2,1)S(1)}, bf16[64,768]{1,0:T(8,128)(2,1)S(1)}, u32[]{:S(2)}, u32[]{:S(2)}) collective-permute-start(bf16[64,768]{1,0:T(8,128)(2,1)S(1)} %get-tuple-element.159), channel_id=1, source_target_pairs={{0,12},{4,8},{8,4},{12,0},{16,28},{20,24},{24,20},{28,16},{1,13},{... | collective-permute-start | bytes 294920 | tf_op jit(solution)/shard_map/ppermute | solution.py:22
  129.4 3.1 %collective-permute-start.32 = (bf16[64,768]{1,0:T(8,128)(2,1)S(1)}, bf16[64,768]{1,0:T(8,128)(2,1)S(1)}, u32[]{:S(2)}, u32[]{:S(2)}) collective-permute-start(bf16[64,768]{1,0:T(8,128)(2,1)S(1)} %get-tuple-element.161), channel_id=1, source_target_pairs={{0,28},{4,24},{8,20},{12,16},{16,12},{20,8},{24,4},{28,0},{1,29},{... | collective-permute-start | bytes 294920 | tf_op jit(solution)/shard_map/ppermute | solution.py:22
  132.5 7.5 %collective-permute-done.31.refs_2_ = bf16[64,768]{1,0:T(8,128)(2,1)S(1)} collective-permute-done((bf16[64,768]{1,0:T(8,128)(2,1)S(1)}, bf16[64,768]{1,0:T(8,128)(2,1)S(1)}, u32[]{:S(2)}, u32[]{:S(2)}) %collective-permute-start.31) | collective-permute-done | bytes 98336 | tf_op jit(solution)/shard_map/ppermute | solution.py:22
  142.1 9.2 %hidden.2 = (bf16[256,1152]{1,0:T(8,128)(2,1)S(1)}, bf16[4,1152,768]{2,1,0:T(8,128)(2,1)S(1)}) custom-call(s32[9]{0:T(128)S(1)} %stack.45.owner_ref, bf16[64,3072]{1,0:T(8,128)(2,1)S(1)} %pack.2.refs_0_, bf16[64,3072]{1,0:T(8,128)(2,1)S(1)} %collective-permute-done.28.refs_1_, bf16[64,3072]{1,0:T(8,128)(2,1)S(1)} %collective-permute-done.33.refs_2_, ...), custom_call_target="tpu_custom_call" | custom-call | flops 3623878656 | bytes 30474276 | tf_op jit(solution)/shard_map/hidden/pallas_call | solution.py:350
  156.7 3.9 %collective-permute-start.38 = (bf16[256,768]{1,0:T(8,128)(2,1)S(1)}, bf16[256,768]{1,0:T(8,128)(2,1)S(1)}, u32[]{:S(2)}, u32[]{:S(2)}) collective-permute-start(bf16[256,768]{1,0:T(8,128)(2,1)S(1)} %fusion), channel_id=1, source_target_pairs={{0,2},{1,3},{2,0},{3,1},{4,6},{5,7},{6,4},{7,5},{8,10},{9,11},{10,... | collective-permute-start | bytes 1179656 | tf_op jit(solution)/shard_map/ppermute | solution.py:27
  160.6 9.2 %hidden.3 = (bf16[256,1152]{1,0:T(8,128)(2,1)S(1)}, bf16[4,1152,768]{2,1,0:T(8,128)(2,1)S(1)}) custom-call(s32[9]{0:T(128)S(1)} %stack.45.owner_ref, bf16[64,3072]{1,0:T(8,128)(2,1)S(1)} %pack.3.refs_0_, bf16[64,3072]{1,0:T(8,128)(2,1)S(1)} %collective-permute-done.35.refs_1_, bf16[64,3072]{1,0:T(8,128)(2,1)S(1)} %collective-permute-done.39.refs_2_, ...), custom_call_target="tpu_custom_call" | custom-call | flops 3623878656 | bytes 30474276 | tf_op jit(solution)/shard_map/hidden/pallas_call | solution.py:350
  169.8 2.8 %collective-permute-done.38.refs_1_ = bf16[256,768]{1,0:T(8,128)(2,1)S(1)} collective-permute-done((bf16[256,768]{1,0:T(8,128)(2,1)S(1)}, bf16[256,768]{1,0:T(8,128)(2,1)S(1)}, u32[]{:S(2)}, u32[]{:S(2)}) %collective-permute-start.38) | collective-permute-done | bytes 393248 | tf_op jit(solution)/shard_map/ppermute | solution.py:27
  175.1 2.3 %collective-permute-done.41 = bf16[2,256,768]{2,1,0:T(8,128)(2,1)S(1)} collective-permute-done((bf16[2,256,768]{2,1,0:T(8,128)(2,1)S(1)}, bf16[2,256,768]{2,1,0:T(8,128)(2,1)S(1)}, u32[]{:S(2)}, u32[]{:S(2)}) %collective-permute-start.41) | collective-permute-done | bytes 786464 | tf_op jit(solution)/shard_map/ppermute | solution.py:27
  177.6 2.5 %collective-permute-start.42 = (bf16[256,768]{1,0:T(8,128)(2,1)S(1)}, bf16[256,768]{1,0:T(8,128)(2,1)S(1)}, u32[]{:S(2)}, u32[]{:S(2)}) collective-permute-start(bf16[256,768]{1,0:T(8,128)(2,1)S(1)} %fusion.1), channel_id=1, source_target_pairs={{0,2},{1,3},{2,0},{3,1},{4,6},{5,7},{6,4},{7,5},{8,10},{9,11},{10,... | collective-permute-start | bytes 1179656 | tf_op jit(solution)/shard_map/ppermute | solution.py:27
  181.2 3.3 %collective-permute-start.48 = (bf16[64,768]{1,0:T(8,128)(2,1)S(1)}, bf16[64,768]{1,0:T(8,128)(2,1)S(1)}, u32[]{:S(2)}, u32[]{:S(2)}) collective-permute-start(bf16[64,768]{1,0:T(8,128)(2,1)S(1)} %get-tuple-element.178), channel_id=1, source_target_pairs={{0,24},{4,28},{8,16},{12,20},{16,8},{20,12},{24,0},{28,4},{1,25},{... | collective-permute-start | bytes 294920 | tf_op jit(solution)/shard_map/ppermute | solution.py:22
  184.6 5.0 %collective-permute-done.42.refs_1_ = bf16[256,768]{1,0:T(8,128)(2,1)S(1)} collective-permute-done((bf16[256,768]{1,0:T(8,128)(2,1)S(1)}, bf16[256,768]{1,0:T(8,128)(2,1)S(1)}, u32[]{:S(2)}, u32[]{:S(2)}) %collective-permute-start.42) | collective-permute-done | bytes 393248 | tf_op jit(solution)/shard_map/ppermute | solution.py:27
  191.9 2.7 %collective-permute-start.47 = (bf16[64,768]{1,0:T(8,128)(2,1)S(1)}, bf16[64,768]{1,0:T(8,128)(2,1)S(1)}, u32[]{:S(2)}, u32[]{:S(2)}) collective-permute-start(bf16[64,768]{1,0:T(8,128)(2,1)S(1)} %get-tuple-element.185), channel_id=1, source_target_pairs={{0,20},{4,16},{8,28},{12,24},{16,4},{20,0},{24,12},{28,8},{1,21},{... | collective-permute-start | bytes 294920 | tf_op jit(solution)/shard_map/ppermute | solution.py:22
  197.7 5.0 %collective-permute-done.47.refs_5_ = bf16[64,768]{1,0:T(8,128)(2,1)S(1)} collective-permute-done((bf16[64,768]{1,0:T(8,128)(2,1)S(1)}, bf16[64,768]{1,0:T(8,128)(2,1)S(1)}, u32[]{:S(2)}, u32[]{:S(2)}) %collective-permute-start.47) | collective-permute-done | bytes 98336 | tf_op jit(solution)/shard_map/ppermute | solution.py:22
  (125 shorter events, 64.7 us)
Async XLA Ops:
  0.0 27.3 %collective-permute-start.7 = (bf16[128,768]{1,0:T(8,128)(2,1)}, bf16[128,768]{1,0:T(8,128)(2,1)S(1)}, u32[]{:S(2)}, u32[]{:S(2)}) collective-permute-start(bf16[128,768]{1,0:T(8,128)(2,1)} %param.21), channel_id=1, source_target_pairs={{0,0},{1,8},{2,16},{3,24},{4,4},{5,12},{6,20},{7,28},{8,1},{9,9},{... | collective-permute-start | bytes 589832 | tf_op jit(solution)/shard_map/ppermute | solution.py:419
  6.1 9.2 %collective-permute-start = (bf16[272,128]{1,0:T(8,128)(2,1)S(1)}, bf16[272,128]{1,0:T(8,128)(2,1)S(1)}, u32[]{:S(2)}, u32[]{:S(2)}) collective-permute-start(bf16[272,128]{1,0:T(8,128)(2,1)S(1)} %get-tuple-element.97), channel_id=1, source_target_pairs={{0,4},{4,0},{8,12},{12,8},{16,20},{20,16},{24,28},{28,24},{1,5},{5... | collective-permute-start | bytes 208904 | tf_op jit(solution)/shard_map/ppermute | solution.py:22
  11.1 8.5 %collective-permute-start.2 = (bf16[272,128]{1,0:T(8,128)(2,1)S(1)}, bf16[272,128]{1,0:T(8,128)(2,1)S(1)}, u32[]{:S(2)}, u32[]{:S(2)}) collective-permute-start(bf16[272,128]{1,0:T(8,128)(2,1)S(1)} %get-tuple-element.99), channel_id=1, source_target_pairs={{0,12},{4,8},{8,4},{12,0},{16,28},{20,24},{24,20},{28,16},{1,13},{... | collective-permute-start | bytes 208904 | tf_op jit(solution)/shard_map/ppermute | solution.py:22
  11.1 12.3 %collective-permute-start.3 = (bf16[272,128]{1,0:T(8,128)(2,1)S(1)}, bf16[272,128]{1,0:T(8,128)(2,1)S(1)}, u32[]{:S(2)}, u32[]{:S(2)}) collective-permute-start(bf16[272,128]{1,0:T(8,128)(2,1)S(1)} %get-tuple-element.100), channel_id=1, source_target_pairs={{0,16},{4,20},{8,24},{12,28},{16,0},{20,4},{24,8},{28,12},{1,17},{... | collective-permute-start | bytes 208904 | tf_op jit(solution)/shard_map/ppermute | solution.py:22
  15.3 12.0 %collective-permute-start.4 = (bf16[272,128]{1,0:T(8,128)(2,1)S(1)}, bf16[272,128]{1,0:T(8,128)(2,1)S(1)}, u32[]{:S(2)}, u32[]{:S(2)}) collective-permute-start(bf16[272,128]{1,0:T(8,128)(2,1)S(1)} %get-tuple-element.101), channel_id=1, source_target_pairs={{0,20},{4,16},{8,28},{12,24},{16,4},{20,0},{24,12},{28,8},{1,21},{... | collective-permute-start | bytes 208904 | tf_op jit(solution)/shard_map/ppermute | solution.py:22
  17.1 10.2 %collective-permute-start.5 = (bf16[272,128]{1,0:T(8,128)(2,1)S(1)}, bf16[272,128]{1,0:T(8,128)(2,1)S(1)}, u32[]{:S(2)}, u32[]{:S(2)}) collective-permute-start(bf16[272,128]{1,0:T(8,128)(2,1)S(1)} %get-tuple-element.102), channel_id=1, source_target_pairs={{0,24},{4,28},{8,16},{12,20},{16,8},{20,12},{24,0},{28,4},{1,25},{... | collective-permute-start | bytes 208904 | tf_op jit(solution)/shard_map/ppermute | solution.py:22
  28.4 8.3 %collective-permute-start.9 = (bf16[256,128]{1,0:T(8,128)(2,1)S(1)}, bf16[256,128]{1,0:T(8,128)(2,1)S(1)}, u32[]{:S(2)}, u32[]{:S(2)}) collective-permute-start(bf16[256,128]{1,0:T(8,128)(2,1)S(1)} %get-tuple-element.120), channel_id=1, source_target_pairs={{0,8},{4,12},{8,0},{12,4},{16,24},{20,28},{24,16},{28,20},{1,9},{5... | collective-permute-start | bytes 196616 | tf_op jit(solution)/shard_map/ppermute | solution.py:22
  31.3 8.6 %collective-permute-start.10 = (bf16[256,128]{1,0:T(8,128)(2,1)S(1)}, bf16[256,128]{1,0:T(8,128)(2,1)S(1)}, u32[]{:S(2)}, u32[]{:S(2)}) collective-permute-start(bf16[256,128]{1,0:T(8,128)(2,1)S(1)} %get-tuple-element.121), channel_id=1, source_target_pairs={{0,12},{4,8},{8,4},{12,0},{16,28},{20,24},{24,20},{28,16},{1,13},{... | collective-permute-start | bytes 196616 | tf_op jit(solution)/shard_map/ppermute | solution.py:22
  32.3 10.2 %collective-permute-start.11 = (bf16[256,128]{1,0:T(8,128)(2,1)S(1)}, bf16[256,128]{1,0:T(8,128)(2,1)S(1)}, u32[]{:S(2)}, u32[]{:S(2)}) collective-permute-start(bf16[256,128]{1,0:T(8,128)(2,1)S(1)} %get-tuple-element.122), channel_id=1, source_target_pairs={{0,16},{4,20},{8,24},{12,28},{16,0},{20,4},{24,8},{28,12},{1,17},{... | collective-permute-start | bytes 196616 | tf_op jit(solution)/shard_map/ppermute | solution.py:22
  34.3 10.3 %collective-permute-start.12 = (bf16[256,128]{1,0:T(8,128)(2,1)S(1)}, bf16[256,128]{1,0:T(8,128)(2,1)S(1)}, u32[]{:S(2)}, u32[]{:S(2)}) collective-permute-start(bf16[256,128]{1,0:T(8,128)(2,1)S(1)} %get-tuple-element.123), channel_id=1, source_target_pairs={{0,20},{4,16},{8,28},{12,24},{16,4},{20,0},{24,12},{28,8},{1,21},{... | collective-permute-start | bytes 196616 | tf_op jit(solution)/shard_map/ppermute | solution.py:22
  35.2 9.5 %collective-permute-start.13 = (bf16[256,128]{1,0:T(8,128)(2,1)S(1)}, bf16[256,128]{1,0:T(8,128)(2,1)S(1)}, u32[]{:S(2)}, u32[]{:S(2)}) collective-permute-start(bf16[256,128]{1,0:T(8,128)(2,1)S(1)} %get-tuple-element.124), channel_id=1, source_target_pairs={{0,24},{4,28},{8,16},{12,20},{16,8},{20,12},{24,0},{28,4},{1,25},{... | collective-permute-start | bytes 196616 | tf_op jit(solution)/shard_map/ppermute | solution.py:22
  44.7 41.0 %collective-permute-start.15 = (bf16[2048,384]{1,0:T(8,128)(2,1)}, bf16[2048,384]{1,0:T(8,128)(2,1)}, u32[]{:S(2)}, u32[]{:S(2)}) collective-permute-start(bf16[2048,384]{1,0:T(8,128)(2,1)} %param.20), channel_id=1, source_target_pairs={{0,4},{4,0},{8,12},{12,8},{16,20},{20,16},{24,28},{28,24},{1,5},{5... | collective-permute-start | bytes 4718600 | tf_op jit(solution)/shard_map/ppermute | solution.py:22
  50.7 16.9 %collective-permute-start.16 = (bf16[128,2048]{1,0:T(8,128)(2,1)S(1)}, bf16[128,2048]{1,0:T(8,128)(2,1)}, u32[]{:S(2)}, u32[]{:S(2)}) collective-permute-start(bf16[128,2048]{1,0:T(8,128)(2,1)S(1)} %attend.1), channel_id=1, source_target_pairs={{0,8},{4,12},{8,16},{12,20},{16,24},{20,28},{1,9},{5,13},{9,17},{1... | collective-permute-start | bytes 1572872 | tf_op jit(solution)/shard_map/ppermute | solution.py:487
  56.1 28.3 %collective-permute-start.17 = (bf16[128,2048]{1,0:T(8,128)(2,1)S(1)}, bf16[128,2048]{1,0:T(8,128)(2,1)S(1)}, u32[]{:S(2)}, u32[]{:S(2)}) collective-permute-start(bf16[128,2048]{1,0:T(8,128)(2,1)S(1)} %attend.1), channel_id=1, source_target_pairs={{8,0},{12,4},{16,8},{20,12},{24,16},{28,20},{9,1},{13,5},{17,9},{2... | collective-permute-start | bytes 1572872 | tf_op jit(solution)/shard_map/ppermute | solution.py:487
  57.9 42.4 %collective-permute-start.20 = (bf16[128,2048]{1,0:T(8,128)(2,1)S(1)}, bf16[128,2048]{1,0:T(8,128)(2,1)S(1)}, u32[]{:S(2)}, u32[]{:S(2)}) collective-permute-start(bf16[128,2048]{1,0:T(8,128)(2,1)S(1)} %attend.1), channel_id=1, source_target_pairs={{0,24},{4,28},{24,0},{28,4},{1,25},{5,29},{25,1},{29,5},{2,26},{6,... | collective-permute-start | bytes 1572872 | tf_op jit(solution)/shard_map/ppermute | solution.py:487
  67.6 28.2 %collective-permute-start.18 = (bf16[128,2048]{1,0:T(8,128)(2,1)}, bf16[128,2048]{1,0:T(8,128)(2,1)S(1)}, u32[]{:S(2)}, u32[]{:S(2)}) collective-permute-start(bf16[128,2048]{1,0:T(8,128)(2,1)} %collective-permute-done.16), channel_id=1, source_target_pairs={{0,8},{4,12},{8,16},{12,20},{16,24},{20,28},{1,9},{5,13},{9,17},{1... | collective-permute-start | bytes 1572872 | tf_op jit(solution)/shard_map/ppermute | solution.py:487
  84.3 15.4 %collective-permute-start.19 = (bf16[128,2048]{1,0:T(8,128)(2,1)S(1)}, bf16[128,2048]{1,0:T(8,128)(2,1)S(1)}, u32[]{:S(2)}, u32[]{:S(2)}) collective-permute-start(bf16[128,2048]{1,0:T(8,128)(2,1)S(1)} %collective-permute-done.17), channel_id=1, source_target_pairs={{8,0},{12,4},{16,8},{20,12},{24,16},{28,20},{9,1},{13,5},{17,9},{2... | collective-permute-start | bytes 1572872 | tf_op jit(solution)/shard_map/ppermute | solution.py:487
  103.5 8.8 %collective-permute-start.24 = (bf16[128,768]{1,0:T(8,128)(2,1)S(1)}, bf16[128,768]{1,0:T(8,128)(2,1)S(1)}, u32[]{:S(2)}, u32[]{:S(2)}) collective-permute-start(bf16[128,768]{1,0:T(8,128)(2,1)S(1)} %get-tuple-element.148), channel_id=1, source_target_pairs={{0,3},{1,0},{2,1},{3,2},{4,7},{5,4},{6,5},{7,6},{8,11},{9,8},{10,9... | collective-permute-start | bytes 589832 | tf_op jit(solution)/shard_map/ppermute | solution.py:27
  113.1 10.3 %collective-permute-start.26 = (bf16[64,768]{1,0:T(8,128)(2,1)S(1)}, bf16[64,768]{1,0:T(8,128)(2,1)S(1)}, u32[]{:S(2)}, u32[]{:S(2)}) collective-permute-start(bf16[64,768]{1,0:T(8,128)(2,1)S(1)} %get-tuple-element.152), channel_id=1, source_target_pairs={{0,16},{4,20},{8,24},{12,28},{16,0},{20,4},{24,8},{28,12},{1,17},{... | collective-permute-start | bytes 294920 | tf_op jit(solution)/shard_map/ppermute | solution.py:22
  114.3 9.1 %collective-permute-start.27 = (bf16[64,768]{1,0:T(8,128)(2,1)S(1)}, bf16[64,768]{1,0:T(8,128)(2,1)S(1)}, u32[]{:S(2)}, u32[]{:S(2)}) collective-permute-start(bf16[64,768]{1,0:T(8,128)(2,1)S(1)} %get-tuple-element.153), channel_id=1, source_target_pairs={{0,24},{4,28},{8,16},{12,20},{16,8},{20,12},{24,0},{28,4},{1,25},{... | collective-permute-start | bytes 294920 | tf_op jit(solution)/shard_map/ppermute | solution.py:22
  123.7 16.6 %collective-permute-start.28 = (bf16[64,3072]{1,0:T(8,128)(2,1)S(1)}, bf16[64,3072]{1,0:T(8,128)(2,1)S(1)}, u32[]{:S(2)}, u32[]{:S(2)}) collective-permute-start(bf16[64,3072]{1,0:T(8,128)(2,1)S(1)} %pack.2.refs_0_), channel_id=1, source_target_pairs={{0,2},{1,3},{2,0},{3,1},{4,6},{5,7},{6,4},{7,5},{8,10},{9,11},{10,... | collective-permute-start | bytes 1179656 | tf_op jit(solution)/shard_map/ppermute | solution.py:27
  129.4 10.7 %collective-permute-start.31 = (bf16[64,768]{1,0:T(8,128)(2,1)S(1)}, bf16[64,768]{1,0:T(8,128)(2,1)S(1)}, u32[]{:S(2)}, u32[]{:S(2)}) collective-permute-start(bf16[64,768]{1,0:T(8,128)(2,1)S(1)} %get-tuple-element.160), channel_id=1, source_target_pairs={{0,20},{4,16},{8,28},{12,24},{16,4},{20,0},{24,12},{28,8},{1,21},{... | collective-permute-start | bytes 294920 | tf_op jit(solution)/shard_map/ppermute | solution.py:22
  129.4 10.6 %collective-permute-start.32 = (bf16[64,768]{1,0:T(8,128)(2,1)S(1)}, bf16[64,768]{1,0:T(8,128)(2,1)S(1)}, u32[]{:S(2)}, u32[]{:S(2)}) collective-permute-start(bf16[64,768]{1,0:T(8,128)(2,1)S(1)} %get-tuple-element.161), channel_id=1, source_target_pairs={{0,28},{4,24},{8,20},{12,16},{16,12},{20,8},{24,4},{28,0},{1,29},{... | collective-permute-start | bytes 294920 | tf_op jit(solution)/shard_map/ppermute | solution.py:22
  132.5 8.3 %collective-permute-start.33 = (bf16[64,3072]{1,0:T(8,128)(2,1)S(1)}, bf16[64,3072]{1,0:T(8,128)(2,1)S(1)}, u32[]{:S(2)}, u32[]{:S(2)}) collective-permute-start(bf16[64,3072]{1,0:T(8,128)(2,1)S(1)} %pack.2.refs_0_), channel_id=1, source_target_pairs={{0,1},{1,0},{2,3},{3,2},{4,5},{5,4},{6,7},{7,6},{8,9},{9,8},{10,11... | collective-permute-start | bytes 1179656 | tf_op jit(solution)/shard_map/ppermute | solution.py:27
  140.4 11.5 %collective-permute-start.35 = (bf16[64,3072]{1,0:T(8,128)(2,1)S(1)}, bf16[64,3072]{1,0:T(8,128)(2,1)S(1)}, u32[]{:S(2)}, u32[]{:S(2)}) collective-permute-start(bf16[64,3072]{1,0:T(8,128)(2,1)S(1)} %pack.3.refs_0_), channel_id=1, source_target_pairs={{0,2},{1,3},{2,0},{3,1},{4,6},{5,7},{6,4},{7,5},{8,10},{9,11},{10,... | collective-permute-start | bytes 1179656 | tf_op jit(solution)/shard_map/ppermute | solution.py:27
  154.8 18.0 %collective-permute-start.36 = (bf16[128,768]{1,0:T(8,128)(2,1)S(1)}, bf16[128,768]{1,0:T(8,128)(2,1)S(1)}, u32[]{:S(2)}, u32[]{:S(2)}) collective-permute-start(bf16[128,768]{1,0:T(8,128)(2,1)S(1)} %get-tuple-element.167), channel_id=1, source_target_pairs={{0,0},{1,8},{2,16},{3,24},{4,4},{5,12},{6,20},{7,28},{8,1},{9,9},{... | collective-permute-start | bytes 589832 | tf_op jit(solution)/shard_map/ppermute | solution.py:419
  156.7 15.9 %collective-permute-start.38 = (bf16[256,768]{1,0:T(8,128)(2,1)S(1)}, bf16[256,768]{1,0:T(8,128)(2,1)S(1)}, u32[]{:S(2)}, u32[]{:S(2)}) collective-permute-start(bf16[256,768]{1,0:T(8,128)(2,1)S(1)} %fusion), channel_id=1, source_target_pairs={{0,2},{1,3},{2,0},{3,1},{4,6},{5,7},{6,4},{7,5},{8,10},{9,11},{10,... | collective-permute-start | bytes 1179656 | tf_op jit(solution)/shard_map/ppermute | solution.py:27
  177.6 12.0 %collective-permute-start.42 = (bf16[256,768]{1,0:T(8,128)(2,1)S(1)}, bf16[256,768]{1,0:T(8,128)(2,1)S(1)}, u32[]{:S(2)}, u32[]{:S(2)}) collective-permute-start(bf16[256,768]{1,0:T(8,128)(2,1)S(1)} %fusion.1), channel_id=1, source_target_pairs={{0,2},{1,3},{2,0},{3,1},{4,6},{5,7},{6,4},{7,5},{8,10},{9,11},{10,... | collective-permute-start | bytes 1179656 | tf_op jit(solution)/shard_map/ppermute | solution.py:27
  180.1 11.8 %collective-permute-start.44 = (bf16[64,768]{1,0:T(8,128)(2,1)S(1)}, bf16[64,768]{1,0:T(8,128)(2,1)S(1)}, u32[]{:S(2)}, u32[]{:S(2)}) collective-permute-start(bf16[64,768]{1,0:T(8,128)(2,1)S(1)} %get-tuple-element.176), channel_id=1, source_target_pairs={{0,8},{4,12},{8,0},{12,4},{16,24},{20,28},{24,16},{28,20},{1,9},{5... | collective-permute-start | bytes 294920 | tf_op jit(solution)/shard_map/ppermute | solution.py:22
  180.8 13.8 %collective-permute-start.46 = (bf16[64,768]{1,0:T(8,128)(2,1)S(1)}, bf16[64,768]{1,0:T(8,128)(2,1)S(1)}, u32[]{:S(2)}, u32[]{:S(2)}) collective-permute-start(bf16[64,768]{1,0:T(8,128)(2,1)S(1)} %get-tuple-element.177), channel_id=1, source_target_pairs={{0,16},{4,20},{8,24},{12,28},{16,0},{20,4},{24,8},{28,12},{1,17},{... | collective-permute-start | bytes 294920 | tf_op jit(solution)/shard_map/ppermute | solution.py:22
  181.2 15.3 %collective-permute-start.48 = (bf16[64,768]{1,0:T(8,128)(2,1)S(1)}, bf16[64,768]{1,0:T(8,128)(2,1)S(1)}, u32[]{:S(2)}, u32[]{:S(2)}) collective-permute-start(bf16[64,768]{1,0:T(8,128)(2,1)S(1)} %get-tuple-element.178), channel_id=1, source_target_pairs={{0,24},{4,28},{8,16},{12,20},{16,8},{20,12},{24,0},{28,4},{1,25},{... | collective-permute-start | bytes 294920 | tf_op jit(solution)/shard_map/ppermute | solution.py:22
  191.9 10.8 %collective-permute-start.47 = (bf16[64,768]{1,0:T(8,128)(2,1)S(1)}, bf16[64,768]{1,0:T(8,128)(2,1)S(1)}, u32[]{:S(2)}, u32[]{:S(2)}) collective-permute-start(bf16[64,768]{1,0:T(8,128)(2,1)S(1)} %get-tuple-element.185), channel_id=1, source_target_pairs={{0,20},{4,16},{8,28},{12,24},{16,4},{20,0},{24,12},{28,8},{1,21},{... | collective-permute-start | bytes 294920 | tf_op jit(solution)/shard_map/ppermute | solution.py:22
  (28 other events, 307.8 us)

commit v10 on v9

--- a/solution.py
+++ b/solution.py
@@ -28,10 +28,12 @@
 
 
 def swap_seq(blocks):
-    swapped = [blocks[0]]
-    for d in range(1, len(blocks)):
-        swapped.append(permute_seq(blocks[d], lambda q, d=d: q ^ d))
-    return swapped
+    half = len(blocks) // 2
+    order = [*range(2, min(3, half)), *reversed(range(half, len(blocks))), *range(3, half)]
+    order += [d for d in range(1, len(blocks)) if d not in order]
+    swapped = [permute_seq(blocks[d], lambda q, d=d: q ^ d) for d in order]
+    swapped = dict(zip(order, lax.optimization_barrier(swapped)))
+    return [blocks[0]] + [swapped[d] for d in range(1, len(blocks))]
 
 
 def pick(stack, index, axis=0):
@@ -556,8 +558,9 @@
             sends = lax.optimization_barrier((sends, arrived))[0]
         arrived = [
             permute_seq(sends[k], lambda q, d=k * ny + group: q ^ d) if k + group else sends[k]
-            for k in range(nz)
+            for k in reversed(range(nz))
         ]
+        arrived = lax.optimization_barrier(arrived)[::-1]
         got = local_call(
             pack_kernel,
             "pack",

time: 204 us -> 203 us (level)
  starting transfers between devices: 94.9 us -> 86.9 us
  waiting for transfers between devices: 64.9 us -> 71.1 us
    ppermute x5, starting transfers between devices: 28 us -> 19 us  [along(): return lax.ppermute(value, 'seq', perm)]
    ppermute x29, waiting for transfers between devices: 31.2 us -> 37 us  [permute_seq(): lax.ppermute(value, 'seq', [(source, move(source)) for source in range(co...]
    ppermute x29, starting transfers between devices: 51 us -> 54.5 us  [permute_seq(): lax.ppermute(value, 'seq', [(source, move(source)) for source in range(co...]
    ppermute x13, starting transfers between devices: 12.7 us -> 10.2 us  [permute_head(): lax.ppermute(value, 'head', [(source, move(source)) for source in range(c...]
  transfers between devices with their start and end apart: 50 -> 50, of which waited for: 21 -> 28; matrix products, arithmetic and copies ran while one was open for 4% -> 4% of each run, Pallas kernels for 11% -> 12%
where the time goes in v10:
time: 203 us; the launch traced here: 202 us
  starting transfers between devices  86.9 us (43%)
  waiting for transfers between devices  71.1 us (35%)
  Pallas kernels  30.3 us (15%)
  local copies, waits for them, and re-layouts  8.08 us (4%)
  matrix products  4.67 us (2%)
    ppermute x29, starting transfers between devices, permute_seq(): lax.ppermute(value, 'seq', [(source, move(source)) for source in range(co...  54.5 us
    ppermute x29, waiting for transfers between devices, permute_seq(): lax.ppermute(value, 'seq', [(source, move(source)) for source in range(co...  37 us
    pallas_call x15, Pallas kernels, local_call(): pl.pallas_call(kernel, out_shape=out_shape, in_specs=[pl.BlockSpec(memory...  30.3 us
    ppermute x13, waiting for transfers between devices, permute_head(): lax.ppermute(value, 'head', [(source, move(source)) for source in range(c...  20.4 us
    ppermute x5, starting transfers between devices, along(): return lax.ppermute(value, 'seq', perm)  19 us
    ppermute x5, waiting for transfers between devices, along(): return lax.ppermute(value, 'seq', perm)  13.6 us
    ppermute x13, starting transfers between devices, permute_head(): lax.ppermute(value, 'head', [(source, move(source)) for source in range(c...  10.2 us
    unnamed x22, local copies, waits for them, and re-layouts  5.41 us
  transfers between devices with their start and end apart: 50, of which 28 were waited for; matrix products, arithmetic and copies ran while one was open for 4% of the time, Pallas kernels for 12%

profile of v10, /device:TPU:0, one launch (start us, length us, event | category | flops | bytes accessed | tf_op | source)
XLA Modules:
  0.0 201.9 jit_solution(10679252602856201900)
XLA Ops:
  6.1 3.4 %collective-permute-start = (bf16[272,128]{1,0:T(8,128)(2,1)S(1)}, bf16[272,128]{1,0:T(8,128)(2,1)S(1)}, u32[]{:S(2)}, u32[]{:S(2)}) collective-permute-start(bf16[272,128]{1,0:T(8,128)(2,1)S(1)} %get-tuple-element.126), channel_id=1, source_target_pairs={{0,8},{4,12},{8,0},{12,4},{16,24},{20,28},{24,16},{28,20},{1,9},{5... | collective-permute-start | bytes 208904 | tf_op jit(solution)/shard_map/ppermute | solution.py:22
  9.6 4.7 %collective-permute-start.1 = (bf16[272,128]{1,0:T(8,128)(2,1)S(1)}, bf16[272,128]{1,0:T(8,128)(2,1)S(1)}, u32[]{:S(2)}, u32[]{:S(2)}) collective-permute-start(bf16[272,128]{1,0:T(8,128)(2,1)S(1)} %get-tuple-element.127), channel_id=1, source_target_pairs={{0,28},{4,24},{8,20},{12,16},{16,12},{20,8},{24,4},{28,0},{1,29},{... | collective-permute-start | bytes 208904 | tf_op jit(solution)/shard_map/ppermute | solution.py:22
  18.1 8.2 %collective-permute-start.5 = (bf16[272,128]{1,0:T(8,128)(2,1)S(1)}, bf16[272,128]{1,0:T(8,128)(2,1)S(1)}, u32[]{:S(2)}, u32[]{:S(2)}) collective-permute-start(bf16[272,128]{1,0:T(8,128)(2,1)S(1)} %get-tuple-element.131), channel_id=1, source_target_pairs={{0,12},{4,8},{8,4},{12,0},{16,28},{20,24},{24,20},{28,16},{1,13},{... | collective-permute-start | bytes 208904 | tf_op jit(solution)/shard_map/ppermute | solution.py:22
  29.1 2.1 %collective-permute-done.5.refs_3_ = bf16[272,128]{1,0:T(8,128)(2,1)S(1)} collective-permute-done((bf16[272,128]{1,0:T(8,128)(2,1)S(1)}, bf16[272,128]{1,0:T(8,128)(2,1)S(1)}, u32[]{:S(2)}, u32[]{:S(2)}) %collective-permute-start.5) | collective-permute-done | bytes 69664 | tf_op jit(solution)/shard_map/ppermute | solution.py:22
  33.3 3.1 %collective-permute-start.10 = (bf16[256,128]{1,0:T(8,128)(2,1)S(1)}, bf16[256,128]{1,0:T(8,128)(2,1)S(1)}, u32[]{:S(2)}, u32[]{:S(2)}) collective-permute-start(bf16[256,128]{1,0:T(8,128)(2,1)S(1)} %get-tuple-element.157), channel_id=1, source_target_pairs={{0,24},{4,28},{8,16},{12,20},{16,8},{20,12},{24,0},{28,4},{1,25},{... | collective-permute-start | bytes 196616 | tf_op jit(solution)/shard_map/ppermute | solution.py:22
  36.4 3.5 %collective-permute-start.12 = (bf16[256,128]{1,0:T(8,128)(2,1)S(1)}, bf16[256,128]{1,0:T(8,128)(2,1)S(1)}, u32[]{:S(2)}, u32[]{:S(2)}) collective-permute-start(bf16[256,128]{1,0:T(8,128)(2,1)S(1)} %get-tuple-element.159), channel_id=1, source_target_pairs={{0,16},{4,20},{8,24},{12,28},{16,0},{20,4},{24,8},{28,12},{1,17},{... | collective-permute-start | bytes 196616 | tf_op jit(solution)/shard_map/ppermute | solution.py:22
  41.3 5.0 %collective-permute-done.11.refs_5_ = bf16[256,128]{1,0:T(8,128)(2,1)S(1)} collective-permute-done((bf16[256,128]{1,0:T(8,128)(2,1)S(1)}, bf16[256,128]{1,0:T(8,128)(2,1)S(1)}, u32[]{:S(2)}, u32[]{:S(2)}) %collective-permute-start.11) | collective-permute-done | bytes 65568 | tf_op jit(solution)/shard_map/ppermute | solution.py:22
  50.1 2.9 %attend.1 = bf16[128,2048]{1,0:T(8,128)(2,1)S(1)} custom-call(s32[1]{0:T(128)} %bitcast.me_ref, f32[1,128]{1,0:T(1,128)S(1)} %get-tuple-element.141.doc_ref, f32[128,16]{1,0:T(8,128)S(1)} %get-tuple-element.142.sum_ref, f32[16,128]{1,0:T(8,128)S(1)} %get-tuple-element.143.sum_rows_ref, bf16[128,2048]{1,0:T(8,128)(2,1)S(1)} %copy-done, ...), custom_call_target="tpu_custom_call" | custom-call | flops 201326592 | bytes 2646532 | tf_op jit(solution)/shard_map/attend/pallas_call | solution.py:352
  53.1 4.6 %collective-permute-start.16 = (bf16[128,2048]{1,0:T(8,128)(2,1)S(1)}, bf16[128,2048]{1,0:T(8,128)(2,1)}, u32[]{:S(2)}, u32[]{:S(2)}) collective-permute-start(bf16[128,2048]{1,0:T(8,128)(2,1)S(1)} %attend.1), channel_id=1, source_target_pairs={{0,8},{4,12},{8,16},{12,20},{16,24},{20,28},{1,9},{5,13},{9,17},{1... | collective-permute-start | bytes 1572872 | tf_op jit(solution)/shard_map/ppermute | solution.py:489
  59.5 2.2 %collective-permute-start.20 = (bf16[128,2048]{1,0:T(8,128)(2,1)S(1)}, bf16[128,2048]{1,0:T(8,128)(2,1)S(1)}, u32[]{:S(2)}, u32[]{:S(2)}) collective-permute-start(bf16[128,2048]{1,0:T(8,128)(2,1)S(1)} %attend.1), channel_id=1, source_target_pairs={{0,24},{4,28},{24,0},{28,4},{1,25},{5,29},{25,1},{29,5},{2,26},{6,... | collective-permute-start | bytes 1572872 | tf_op jit(solution)/shard_map/ppermute | solution.py:489
  63.4 4.2 %collective-permute-done.16 = bf16[128,2048]{1,0:T(8,128)(2,1)} collective-permute-done((bf16[128,2048]{1,0:T(8,128)(2,1)S(1)}, bf16[128,2048]{1,0:T(8,128)(2,1)}, u32[]{:S(2)}, u32[]{:S(2)}) %collective-permute-start.16) | collective-permute-done | bytes 524320 | tf_op jit(solution)/shard_map/ppermute | solution.py:489
  67.6 9.6 %collective-permute-start.18 = (bf16[128,2048]{1,0:T(8,128)(2,1)}, bf16[128,2048]{1,0:T(8,128)(2,1)S(1)}, u32[]{:S(2)}, u32[]{:S(2)}) collective-permute-start(bf16[128,2048]{1,0:T(8,128)(2,1)} %collective-permute-done.16), channel_id=1, source_target_pairs={{0,8},{4,12},{8,16},{12,20},{16,24},{20,28},{1,9},{5,13},{9,17},{1... | collective-permute-start | bytes 1572872 | tf_op jit(solution)/shard_map/ppermute | solution.py:489
  78.5 4.1 %collective-permute-done.15 = bf16[2048,384]{1,0:T(8,128)(2,1)} collective-permute-done((bf16[2048,384]{1,0:T(8,128)(2,1)}, bf16[2048,384]{1,0:T(8,128)(2,1)}, u32[]{:S(2)}, u32[]{:S(2)}) %collective-permute-start.15) | collective-permute-done | bytes 1572896 | tf_op jit(solution)/shard_map/ppermute | solution.py:22
  87.9 9.5 %collective-permute-done.19 = bf16[128,2048]{1,0:T(8,128)(2,1)S(1)} collective-permute-done((bf16[128,2048]{1,0:T(8,128)(2,1)S(1)}, bf16[128,2048]{1,0:T(8,128)(2,1)S(1)}, u32[]{:S(2)}, u32[]{:S(2)}) %collective-permute-start.19) | collective-permute-done | bytes 524320 | tf_op jit(solution)/shard_map/ppermute | solution.py:489
  101.1 4.8 %collective-permute-done.22.refs_1_ = bf16[128,768]{1,0:T(8,128)(2,1)S(1)} collective-permute-done((bf16[128,768]{1,0:T(8,128)(2,1)S(1)}, bf16[128,768]{1,0:T(8,128)(2,1)S(1)}, u32[]{:S(2)}, u32[]{:S(2)}) %collective-permute-start.22) | collective-permute-done | bytes 196640 | tf_op jit(solution)/shard_map/ppermute | solution.py:27
  108.3 4.5 %collective-permute-start.25 = (bf16[64,768]{1,0:T(8,128)(2,1)S(1)}, bf16[64,768]{1,0:T(8,128)(2,1)S(1)}, u32[]{:S(2)}, u32[]{:S(2)}) collective-permute-start(bf16[64,768]{1,0:T(8,128)(2,1)S(1)} %get-tuple-element.193), channel_id=1, source_target_pairs={{0,24},{4,28},{8,16},{12,20},{16,8},{20,12},{24,0},{28,4},{1,25},{... | collective-permute-start | bytes 294920 | tf_op jit(solution)/shard_map/ppermute | solution.py:22
  116.0 6.8 %collective-permute-done.26.refs_2_ = bf16[64,768]{1,0:T(8,128)(2,1)S(1)} collective-permute-done((bf16[64,768]{1,0:T(8,128)(2,1)S(1)}, bf16[64,768]{1,0:T(8,128)(2,1)S(1)}, u32[]{:S(2)}, u32[]{:S(2)}) %collective-permute-start.26) | collective-permute-done | bytes 98336 | tf_op jit(solution)/shard_map/ppermute | solution.py:22
  123.6 2.7 %collective-permute-start.29 = (bf16[64,768]{1,0:T(8,128)(2,1)S(1)}, bf16[64,768]{1,0:T(8,128)(2,1)S(1)}, u32[]{:S(2)}, u32[]{:S(2)}) collective-permute-start(bf16[64,768]{1,0:T(8,128)(2,1)S(1)} %get-tuple-element.205), channel_id=1, source_target_pairs={{0,28},{4,24},{8,20},{12,16},{16,12},{20,8},{24,4},{28,0},{1,29},{... | collective-permute-start | bytes 294920 | tf_op jit(solution)/shard_map/ppermute | solution.py:22
  126.3 3.5 %collective-permute-start.31 = (bf16[64,768]{1,0:T(8,128)(2,1)S(1)}, bf16[64,768]{1,0:T(8,128)(2,1)S(1)}, u32[]{:S(2)}, u32[]{:S(2)}) collective-permute-start(bf16[64,768]{1,0:T(8,128)(2,1)S(1)} %get-tuple-element.207), channel_id=1, source_target_pairs={{0,12},{4,8},{8,4},{12,0},{16,28},{20,24},{24,20},{28,16},{1,13},{... | collective-permute-start | bytes 294920 | tf_op jit(solution)/shard_map/ppermute | solution.py:22
  132.1 3.3 %collective-permute-done.30.refs_2_ = bf16[64,768]{1,0:T(8,128)(2,1)S(1)} collective-permute-done((bf16[64,768]{1,0:T(8,128)(2,1)S(1)}, bf16[64,768]{1,0:T(8,128)(2,1)S(1)}, u32[]{:S(2)}, u32[]{:S(2)}) %collective-permute-start.30) | collective-permute-done | bytes 98336 | tf_op jit(solution)/shard_map/ppermute | solution.py:22
  139.5 9.2 %hidden.2 = (bf16[256,1152]{1,0:T(8,128)(2,1)S(1)}, bf16[4,1152,768]{2,1,0:T(8,128)(2,1)S(1)}) custom-call(s32[9]{0:T(128)S(1)} %stack.45.owner_ref, bf16[64,3072]{1,0:T(8,128)(2,1)S(1)} %pack.2.refs_0_, bf16[64,3072]{1,0:T(8,128)(2,1)S(1)} %collective-permute-done.28.refs_1_, bf16[64,3072]{1,0:T(8,128)(2,1)S(1)} %collective-permute-done.33.refs_2_, ...), custom_call_target="tpu_custom_call" | custom-call | flops 3623878656 | bytes 30474276 | tf_op jit(solution)/shard_map/hidden/pallas_call | solution.py:352
  149.4 2.2 %down.2 = (bf16[2,256,768]{2,1,0:T(8,128)(2,1)S(1)}, bf16[2,256,768]{2,1,0:T(8,128)(2,1)S(1)}) custom-call(bf16[256,1152]{1,0:T(8,128)(2,1)S(1)} %get-tuple-element.215.hidden_ref, bf16[4,1152,768]{2,1,0:T(8,128)(2,1)S(1)} %get-tuple-element.216.low_ref), custom_call_target="tpu_custom_call" | custom-call | flops 1811939328 | bytes 9240576 | tf_op jit(solution)/shard_map/down/pallas_call | solution.py:352
  154.1 2.7 %collective-permute-start.38 = (bf16[256,768]{1,0:T(8,128)(2,1)S(1)}, bf16[256,768]{1,0:T(8,128)(2,1)S(1)}, u32[]{:S(2)}, u32[]{:S(2)}) collective-permute-start(bf16[256,768]{1,0:T(8,128)(2,1)S(1)} %fusion), channel_id=1, source_target_pairs={{0,2},{1,3},{2,0},{3,1},{4,6},{5,7},{6,4},{7,5},{8,10},{9,11},{10,... | collective-permute-start | bytes 1179656 | tf_op jit(solution)/shard_map/ppermute | solution.py:27
  156.8 9.2 %hidden.3 = (bf16[256,1152]{1,0:T(8,128)(2,1)S(1)}, bf16[4,1152,768]{2,1,0:T(8,128)(2,1)S(1)}) custom-call(s32[9]{0:T(128)S(1)} %stack.45.owner_ref, bf16[64,3072]{1,0:T(8,128)(2,1)S(1)} %pack.3.refs_0_, bf16[64,3072]{1,0:T(8,128)(2,1)S(1)} %collective-permute-done.35.refs_1_, bf16[64,3072]{1,0:T(8,128)(2,1)S(1)} %collective-permute-done.40.refs_2_, ...), custom_call_target="tpu_custom_call" | custom-call | flops 3623878656 | bytes 30474276 | tf_op jit(solution)/shard_map/hidden/pallas_call | solution.py:352
  166.1 3.7 %collective-permute-done.38.refs_1_ = bf16[256,768]{1,0:T(8,128)(2,1)S(1)} collective-permute-done((bf16[256,768]{1,0:T(8,128)(2,1)S(1)}, bf16[256,768]{1,0:T(8,128)(2,1)S(1)}, u32[]{:S(2)}, u32[]{:S(2)}) %collective-permute-start.38) | collective-permute-done | bytes 393248 | tf_op jit(solution)/shard_map/ppermute | solution.py:27
  169.9 2.2 %down.3 = (bf16[2,256,768]{2,1,0:T(8,128)(2,1)S(1)}, bf16[2,256,768]{2,1,0:T(8,128)(2,1)S(1)}) custom-call(bf16[256,1152]{1,0:T(8,128)(2,1)S(1)} %get-tuple-element.230.hidden_ref, bf16[4,1152,768]{2,1,0:T(8,128)(2,1)S(1)} %get-tuple-element.231.low_ref), custom_call_target="tpu_custom_call" | custom-call | flops 1811939328 | bytes 9240576 | tf_op jit(solution)/shard_map/down/pallas_call | solution.py:352
  175.2 2.3 %collective-permute-start.43 = (bf16[256,768]{1,0:T(8,128)(2,1)S(1)}, bf16[256,768]{1,0:T(8,128)(2,1)S(1)}, u32[]{:S(2)}, u32[]{:S(2)}) collective-permute-start(bf16[256,768]{1,0:T(8,128)(2,1)S(1)} %fusion.1), channel_id=1, source_target_pairs={{0,2},{1,3},{2,0},{3,1},{4,6},{5,7},{6,4},{7,5},{8,10},{9,11},{10,... | collective-permute-start | bytes 1179656 | tf_op jit(solution)/shard_map/ppermute | solution.py:27
  178.5 2.5 %collective-permute-start.47 = (bf16[64,768]{1,0:T(8,128)(2,1)S(1)}, bf16[64,768]{1,0:T(8,128)(2,1)S(1)}, u32[]{:S(2)}, u32[]{:S(2)}) collective-permute-start(bf16[64,768]{1,0:T(8,128)(2,1)S(1)} %get-tuple-element.228), channel_id=1, source_target_pairs={{0,16},{4,20},{8,24},{12,28},{16,0},{20,4},{24,8},{28,12},{1,17},{... | collective-permute-start | bytes 294920 | tf_op jit(solution)/shard_map/ppermute | solution.py:22
  181.0 6.1 %collective-permute-done.43.refs_1_ = bf16[256,768]{1,0:T(8,128)(2,1)S(1)} collective-permute-done((bf16[256,768]{1,0:T(8,128)(2,1)S(1)}, bf16[256,768]{1,0:T(8,128)(2,1)S(1)}, u32[]{:S(2)}, u32[]{:S(2)}) %collective-permute-start.43) | collective-permute-done | bytes 393248 | tf_op jit(solution)/shard_map/ppermute | solution.py:27
  187.3 2.2 %collective-permute-start.44 = (bf16[64,768]{1,0:T(8,128)(2,1)S(1)}, bf16[64,768]{1,0:T(8,128)(2,1)S(1)}, u32[]{:S(2)}, u32[]{:S(2)}) collective-permute-start(bf16[64,768]{1,0:T(8,128)(2,1)S(1)} %get-tuple-element.234), channel_id=1, source_target_pairs={{0,28},{4,24},{8,20},{12,16},{16,12},{20,8},{24,4},{28,0},{1,29},{... | collective-permute-start | bytes 294920 | tf_op jit(solution)/shard_map/ppermute | solution.py:22
  189.5 3.5 %collective-permute-start.48 = (bf16[64,768]{1,0:T(8,128)(2,1)S(1)}, bf16[64,768]{1,0:T(8,128)(2,1)S(1)}, u32[]{:S(2)}, u32[]{:S(2)}) collective-permute-start(bf16[64,768]{1,0:T(8,128)(2,1)S(1)} %get-tuple-element.236), channel_id=1, source_target_pairs={{0,12},{4,8},{8,4},{12,0},{16,28},{20,24},{24,20},{28,16},{1,13},{... | collective-permute-start | bytes 294920 | tf_op jit(solution)/shard_map/ppermute | solution.py:22
  195.9 2.9 %collective-permute-done.46.refs_5_ = bf16[64,768]{1,0:T(8,128)(2,1)S(1)} collective-permute-done((bf16[64,768]{1,0:T(8,128)(2,1)S(1)}, bf16[64,768]{1,0:T(8,128)(2,1)S(1)}, u32[]{:S(2)}, u32[]{:S(2)}) %collective-permute-start.46) | collective-permute-done | bytes 98336 | tf_op jit(solution)/shard_map/ppermute | solution.py:22
  (125 shorter events, 60.2 us)
Async XLA Ops:
  0.0 31.6 %collective-permute-start.7 = (bf16[128,768]{1,0:T(8,128)(2,1)}, bf16[128,768]{1,0:T(8,128)(2,1)S(1)}, u32[]{:S(2)}, u32[]{:S(2)}) collective-permute-start(bf16[128,768]{1,0:T(8,128)(2,1)} %param.21), channel_id=1, source_target_pairs={{0,0},{1,8},{2,16},{3,24},{4,4},{5,12},{6,20},{7,28},{8,1},{9,9},{... | collective-permute-start | bytes 589832 | tf_op jit(solution)/shard_map/ppermute | solution.py:421
  6.1 9.5 %collective-permute-start = (bf16[272,128]{1,0:T(8,128)(2,1)S(1)}, bf16[272,128]{1,0:T(8,128)(2,1)S(1)}, u32[]{:S(2)}, u32[]{:S(2)}) collective-permute-start(bf16[272,128]{1,0:T(8,128)(2,1)S(1)} %get-tuple-element.126), channel_id=1, source_target_pairs={{0,8},{4,12},{8,0},{12,4},{16,24},{20,28},{24,16},{28,20},{1,9},{5... | collective-permute-start | bytes 208904 | tf_op jit(solution)/shard_map/ppermute | solution.py:22
  9.6 8.6 %collective-permute-start.1 = (bf16[272,128]{1,0:T(8,128)(2,1)S(1)}, bf16[272,128]{1,0:T(8,128)(2,1)S(1)}, u32[]{:S(2)}, u32[]{:S(2)}) collective-permute-start(bf16[272,128]{1,0:T(8,128)(2,1)S(1)} %get-tuple-element.127), channel_id=1, source_target_pairs={{0,28},{4,24},{8,20},{12,16},{16,12},{20,8},{24,4},{28,0},{1,29},{... | collective-permute-start | bytes 208904 | tf_op jit(solution)/shard_map/ppermute | solution.py:22
  14.2 12.1 %collective-permute-start.2 = (bf16[272,128]{1,0:T(8,128)(2,1)S(1)}, bf16[272,128]{1,0:T(8,128)(2,1)S(1)}, u32[]{:S(2)}, u32[]{:S(2)}) collective-permute-start(bf16[272,128]{1,0:T(8,128)(2,1)S(1)} %get-tuple-element.128), channel_id=1, source_target_pairs={{0,24},{4,28},{8,16},{12,20},{16,8},{20,12},{24,0},{28,4},{1,25},{... | collective-permute-start | bytes 208904 | tf_op jit(solution)/shard_map/ppermute | solution.py:22
  14.3 14.5 %collective-permute-start.3 = (bf16[272,128]{1,0:T(8,128)(2,1)S(1)}, bf16[272,128]{1,0:T(8,128)(2,1)S(1)}, u32[]{:S(2)}, u32[]{:S(2)}) collective-permute-start(bf16[272,128]{1,0:T(8,128)(2,1)S(1)} %get-tuple-element.129), channel_id=1, source_target_pairs={{0,20},{4,16},{8,28},{12,24},{16,4},{20,0},{24,12},{28,8},{1,21},{... | collective-permute-start | bytes 208904 | tf_op jit(solution)/shard_map/ppermute | solution.py:22
  15.7 13.4 %collective-permute-start.4 = (bf16[272,128]{1,0:T(8,128)(2,1)S(1)}, bf16[272,128]{1,0:T(8,128)(2,1)S(1)}, u32[]{:S(2)}, u32[]{:S(2)}) collective-permute-start(bf16[272,128]{1,0:T(8,128)(2,1)S(1)} %get-tuple-element.130), channel_id=1, source_target_pairs={{0,16},{4,20},{8,24},{12,28},{16,0},{20,4},{24,8},{28,12},{1,17},{... | collective-permute-start | bytes 208904 | tf_op jit(solution)/shard_map/ppermute | solution.py:22
  18.1 13.0 %collective-permute-start.5 = (bf16[272,128]{1,0:T(8,128)(2,1)S(1)}, bf16[272,128]{1,0:T(8,128)(2,1)S(1)}, u32[]{:S(2)}, u32[]{:S(2)}) collective-permute-start(bf16[272,128]{1,0:T(8,128)(2,1)S(1)} %get-tuple-element.131), channel_id=1, source_target_pairs={{0,12},{4,8},{8,4},{12,0},{16,28},{20,24},{24,20},{28,16},{1,13},{... | collective-permute-start | bytes 208904 | tf_op jit(solution)/shard_map/ppermute | solution.py:22
  31.9 8.0 %collective-permute-start.8 = (bf16[256,128]{1,0:T(8,128)(2,1)S(1)}, bf16[256,128]{1,0:T(8,128)(2,1)S(1)}, u32[]{:S(2)}, u32[]{:S(2)}) collective-permute-start(bf16[256,128]{1,0:T(8,128)(2,1)S(1)} %get-tuple-element.155), channel_id=1, source_target_pairs={{0,8},{4,12},{8,0},{12,4},{16,24},{20,28},{24,16},{28,20},{1,9},{5... | collective-permute-start | bytes 196616 | tf_op jit(solution)/shard_map/ppermute | solution.py:22
  36.4 9.8 %collective-permute-start.11 = (bf16[256,128]{1,0:T(8,128)(2,1)S(1)}, bf16[256,128]{1,0:T(8,128)(2,1)S(1)}, u32[]{:S(2)}, u32[]{:S(2)}) collective-permute-start(bf16[256,128]{1,0:T(8,128)(2,1)S(1)} %get-tuple-element.158), channel_id=1, source_target_pairs={{0,20},{4,16},{8,28},{12,24},{16,4},{20,0},{24,12},{28,8},{1,21},{... | collective-permute-start | bytes 196616 | tf_op jit(solution)/shard_map/ppermute | solution.py:22
  36.4 10.4 %collective-permute-start.12 = (bf16[256,128]{1,0:T(8,128)(2,1)S(1)}, bf16[256,128]{1,0:T(8,128)(2,1)S(1)}, u32[]{:S(2)}, u32[]{:S(2)}) collective-permute-start(bf16[256,128]{1,0:T(8,128)(2,1)S(1)} %get-tuple-element.159), channel_id=1, source_target_pairs={{0,16},{4,20},{8,24},{12,28},{16,0},{20,4},{24,8},{28,12},{1,17},{... | collective-permute-start | bytes 196616 | tf_op jit(solution)/shard_map/ppermute | solution.py:22
  47.3 35.4 %collective-permute-start.15 = (bf16[2048,384]{1,0:T(8,128)(2,1)}, bf16[2048,384]{1,0:T(8,128)(2,1)}, u32[]{:S(2)}, u32[]{:S(2)}) collective-permute-start(bf16[2048,384]{1,0:T(8,128)(2,1)} %param.20), channel_id=1, source_target_pairs={{0,4},{4,0},{8,12},{12,8},{16,20},{20,16},{24,28},{28,24},{1,5},{5... | collective-permute-start | bytes 4718600 | tf_op jit(solution)/shard_map/ppermute | solution.py:22
  53.1 14.6 %collective-permute-start.16 = (bf16[128,2048]{1,0:T(8,128)(2,1)S(1)}, bf16[128,2048]{1,0:T(8,128)(2,1)}, u32[]{:S(2)}, u32[]{:S(2)}) collective-permute-start(bf16[128,2048]{1,0:T(8,128)(2,1)S(1)} %attend.1), channel_id=1, source_target_pairs={{0,8},{4,12},{8,16},{12,20},{16,24},{20,28},{1,9},{5,13},{9,17},{1... | collective-permute-start | bytes 1572872 | tf_op jit(solution)/shard_map/ppermute | solution.py:489
  57.6 19.6 %collective-permute-start.17 = (bf16[128,2048]{1,0:T(8,128)(2,1)S(1)}, bf16[128,2048]{1,0:T(8,128)(2,1)S(1)}, u32[]{:S(2)}, u32[]{:S(2)}) collective-permute-start(bf16[128,2048]{1,0:T(8,128)(2,1)S(1)} %attend.1), channel_id=1, source_target_pairs={{8,0},{12,4},{16,8},{20,12},{24,16},{28,20},{9,1},{13,5},{17,9},{2... | collective-permute-start | bytes 1572872 | tf_op jit(solution)/shard_map/ppermute | solution.py:489
  59.5 38.5 %collective-permute-start.20 = (bf16[128,2048]{1,0:T(8,128)(2,1)S(1)}, bf16[128,2048]{1,0:T(8,128)(2,1)S(1)}, u32[]{:S(2)}, u32[]{:S(2)}) collective-permute-start(bf16[128,2048]{1,0:T(8,128)(2,1)S(1)} %attend.1), channel_id=1, source_target_pairs={{0,24},{4,28},{24,0},{28,4},{1,25},{5,29},{25,1},{29,5},{2,26},{6,... | collective-permute-start | bytes 1572872 | tf_op jit(solution)/shard_map/ppermute | solution.py:489
  67.6 19.6 %collective-permute-start.18 = (bf16[128,2048]{1,0:T(8,128)(2,1)}, bf16[128,2048]{1,0:T(8,128)(2,1)S(1)}, u32[]{:S(2)}, u32[]{:S(2)}) collective-permute-start(bf16[128,2048]{1,0:T(8,128)(2,1)} %collective-permute-done.16), channel_id=1, source_target_pairs={{0,8},{4,12},{8,16},{12,20},{16,24},{20,28},{1,9},{5,13},{9,17},{1... | collective-permute-start | bytes 1572872 | tf_op jit(solution)/shard_map/ppermute | solution.py:489
  77.2 20.1 %collective-permute-start.19 = (bf16[128,2048]{1,0:T(8,128)(2,1)S(1)}, bf16[128,2048]{1,0:T(8,128)(2,1)S(1)}, u32[]{:S(2)}, u32[]{:S(2)}) collective-permute-start(bf16[128,2048]{1,0:T(8,128)(2,1)S(1)} %collective-permute-done.17), channel_id=1, source_target_pairs={{8,0},{12,4},{16,8},{20,12},{24,16},{28,20},{9,1},{13,5},{17,9},{2... | collective-permute-start | bytes 1572872 | tf_op jit(solution)/shard_map/ppermute | solution.py:489
  112.8 10.0 %collective-permute-start.26 = (bf16[64,768]{1,0:T(8,128)(2,1)S(1)}, bf16[64,768]{1,0:T(8,128)(2,1)S(1)}, u32[]{:S(2)}, u32[]{:S(2)}) collective-permute-start(bf16[64,768]{1,0:T(8,128)(2,1)S(1)} %get-tuple-element.194), channel_id=1, source_target_pairs={{0,16},{4,20},{8,24},{12,28},{16,0},{20,4},{24,8},{28,12},{1,17},{... | collective-permute-start | bytes 294920 | tf_op jit(solution)/shard_map/ppermute | solution.py:22
  113.9 8.9 %collective-permute-start.27 = (bf16[64,768]{1,0:T(8,128)(2,1)S(1)}, bf16[64,768]{1,0:T(8,128)(2,1)S(1)}, u32[]{:S(2)}, u32[]{:S(2)}) collective-permute-start(bf16[64,768]{1,0:T(8,128)(2,1)S(1)} %get-tuple-element.195), channel_id=1, source_target_pairs={{0,8},{4,12},{8,0},{12,4},{16,24},{20,28},{24,16},{28,20},{1,9},{5... | collective-permute-start | bytes 294920 | tf_op jit(solution)/shard_map/ppermute | solution.py:22
  123.0 14.7 %collective-permute-start.28 = (bf16[64,3072]{1,0:T(8,128)(2,1)S(1)}, bf16[64,3072]{1,0:T(8,128)(2,1)S(1)}, u32[]{:S(2)}, u32[]{:S(2)}) collective-permute-start(bf16[64,3072]{1,0:T(8,128)(2,1)S(1)} %pack.2.refs_0_), channel_id=1, source_target_pairs={{0,2},{1,3},{2,0},{3,1},{4,6},{5,7},{6,4},{7,5},{8,10},{9,11},{10,... | collective-permute-start | bytes 1179656 | tf_op jit(solution)/shard_map/ppermute | solution.py:27
  123.6 8.5 %collective-permute-start.29 = (bf16[64,768]{1,0:T(8,128)(2,1)S(1)}, bf16[64,768]{1,0:T(8,128)(2,1)S(1)}, u32[]{:S(2)}, u32[]{:S(2)}) collective-permute-start(bf16[64,768]{1,0:T(8,128)(2,1)S(1)} %get-tuple-element.205), channel_id=1, source_target_pairs={{0,28},{4,24},{8,20},{12,16},{16,12},{20,8},{24,4},{28,0},{1,29},{... | collective-permute-start | bytes 294920 | tf_op jit(solution)/shard_map/ppermute | solution.py:22
  126.3 9.1 %collective-permute-start.30 = (bf16[64,768]{1,0:T(8,128)(2,1)S(1)}, bf16[64,768]{1,0:T(8,128)(2,1)S(1)}, u32[]{:S(2)}, u32[]{:S(2)}) collective-permute-start(bf16[64,768]{1,0:T(8,128)(2,1)S(1)} %get-tuple-element.206), channel_id=1, source_target_pairs={{0,20},{4,16},{8,28},{12,24},{16,4},{20,0},{24,12},{28,8},{1,21},{... | collective-permute-start | bytes 294920 | tf_op jit(solution)/shard_map/ppermute | solution.py:22
  126.3 9.2 %collective-permute-start.31 = (bf16[64,768]{1,0:T(8,128)(2,1)S(1)}, bf16[64,768]{1,0:T(8,128)(2,1)S(1)}, u32[]{:S(2)}, u32[]{:S(2)}) collective-permute-start(bf16[64,768]{1,0:T(8,128)(2,1)S(1)} %get-tuple-element.207), channel_id=1, source_target_pairs={{0,12},{4,8},{8,4},{12,0},{16,28},{20,24},{24,20},{28,16},{1,13},{... | collective-permute-start | bytes 294920 | tf_op jit(solution)/shard_map/ppermute | solution.py:22
  137.8 11.5 %collective-permute-start.35 = (bf16[64,3072]{1,0:T(8,128)(2,1)S(1)}, bf16[64,3072]{1,0:T(8,128)(2,1)S(1)}, u32[]{:S(2)}, u32[]{:S(2)}) collective-permute-start(bf16[64,3072]{1,0:T(8,128)(2,1)S(1)} %pack.3.refs_0_), channel_id=1, source_target_pairs={{0,2},{1,3},{2,0},{3,1},{4,6},{5,7},{6,4},{7,5},{8,10},{9,11},{10,... | collective-permute-start | bytes 1179656 | tf_op jit(solution)/shard_map/ppermute | solution.py:27
  152.2 17.7 %collective-permute-start.36 = (bf16[128,768]{1,0:T(8,128)(2,1)S(1)}, bf16[128,768]{1,0:T(8,128)(2,1)S(1)}, u32[]{:S(2)}, u32[]{:S(2)}) collective-permute-start(bf16[128,768]{1,0:T(8,128)(2,1)S(1)} %get-tuple-element.218), channel_id=1, source_target_pairs={{0,0},{1,8},{2,16},{3,24},{4,4},{5,12},{6,20},{7,28},{8,1},{9,9},{... | collective-permute-start | bytes 589832 | tf_op jit(solution)/shard_map/ppermute | solution.py:421
  154.1 15.6 %collective-permute-start.38 = (bf16[256,768]{1,0:T(8,128)(2,1)S(1)}, bf16[256,768]{1,0:T(8,128)(2,1)S(1)}, u32[]{:S(2)}, u32[]{:S(2)}) collective-permute-start(bf16[256,768]{1,0:T(8,128)(2,1)S(1)} %fusion), channel_id=1, source_target_pairs={{0,2},{1,3},{2,0},{3,1},{4,6},{5,7},{6,4},{7,5},{8,10},{9,11},{10,... | collective-permute-start | bytes 1179656 | tf_op jit(solution)/shard_map/ppermute | solution.py:27
  175.2 11.9 %collective-permute-start.43 = (bf16[256,768]{1,0:T(8,128)(2,1)S(1)}, bf16[256,768]{1,0:T(8,128)(2,1)S(1)}, u32[]{:S(2)}, u32[]{:S(2)}) collective-permute-start(bf16[256,768]{1,0:T(8,128)(2,1)S(1)} %fusion.1), channel_id=1, source_target_pairs={{0,2},{1,3},{2,0},{3,1},{4,6},{5,7},{6,4},{7,5},{8,10},{9,11},{10,... | collective-permute-start | bytes 1179656 | tf_op jit(solution)/shard_map/ppermute | solution.py:27
  177.5 12.0 %collective-permute-start.39 = (bf16[64,768]{1,0:T(8,128)(2,1)S(1)}, bf16[64,768]{1,0:T(8,128)(2,1)S(1)}, u32[]{:S(2)}, u32[]{:S(2)}) collective-permute-start(bf16[64,768]{1,0:T(8,128)(2,1)S(1)} %get-tuple-element.222), channel_id=1, source_target_pairs={{0,8},{4,12},{8,0},{12,4},{16,24},{20,28},{24,16},{28,20},{1,9},{5... | collective-permute-start | bytes 294920 | tf_op jit(solution)/shard_map/ppermute | solution.py:22
  177.5 15.5 %collective-permute-start.45 = (bf16[64,768]{1,0:T(8,128)(2,1)S(1)}, bf16[64,768]{1,0:T(8,128)(2,1)S(1)}, u32[]{:S(2)}, u32[]{:S(2)}) collective-permute-start(bf16[64,768]{1,0:T(8,128)(2,1)S(1)} %get-tuple-element.229), channel_id=1, source_target_pairs={{0,24},{4,28},{8,16},{12,20},{16,8},{20,12},{24,0},{28,4},{1,25},{... | collective-permute-start | bytes 294920 | tf_op jit(solution)/shard_map/ppermute | solution.py:22
  178.5 15.6 %collective-permute-start.47 = (bf16[64,768]{1,0:T(8,128)(2,1)S(1)}, bf16[64,768]{1,0:T(8,128)(2,1)S(1)}, u32[]{:S(2)}, u32[]{:S(2)}) collective-permute-start(bf16[64,768]{1,0:T(8,128)(2,1)S(1)} %get-tuple-element.228), channel_id=1, source_target_pairs={{0,16},{4,20},{8,24},{12,28},{16,0},{20,4},{24,8},{28,12},{1,17},{... | collective-permute-start | bytes 294920 | tf_op jit(solution)/shard_map/ppermute | solution.py:22
  187.3 8.6 %collective-permute-start.44 = (bf16[64,768]{1,0:T(8,128)(2,1)S(1)}, bf16[64,768]{1,0:T(8,128)(2,1)S(1)}, u32[]{:S(2)}, u32[]{:S(2)}) collective-permute-start(bf16[64,768]{1,0:T(8,128)(2,1)S(1)} %get-tuple-element.234), channel_id=1, source_target_pairs={{0,28},{4,24},{8,20},{12,16},{16,12},{20,8},{24,4},{28,0},{1,29},{... | collective-permute-start | bytes 294920 | tf_op jit(solution)/shard_map/ppermute | solution.py:22
  189.5 9.3 %collective-permute-start.46 = (bf16[64,768]{1,0:T(8,128)(2,1)S(1)}, bf16[64,768]{1,0:T(8,128)(2,1)S(1)}, u32[]{:S(2)}, u32[]{:S(2)}) collective-permute-start(bf16[64,768]{1,0:T(8,128)(2,1)S(1)} %get-tuple-element.235), channel_id=1, source_target_pairs={{0,20},{4,16},{8,28},{12,24},{16,4},{20,0},{24,12},{28,8},{1,21},{... | collective-permute-start | bytes 294920 | tf_op jit(solution)/shard_map/ppermute | solution.py:22
  189.5 9.3 %collective-permute-start.48 = (bf16[64,768]{1,0:T(8,128)(2,1)S(1)}, bf16[64,768]{1,0:T(8,128)(2,1)S(1)}, u32[]{:S(2)}, u32[]{:S(2)}) collective-permute-start(bf16[64,768]{1,0:T(8,128)(2,1)S(1)} %get-tuple-element.236), channel_id=1, source_target_pairs={{0,12},{4,8},{8,4},{12,0},{16,28},{20,24},{24,20},{28,16},{1,13},{... | collective-permute-start | bytes 294920 | tf_op jit(solution)/shard_map/ppermute | solution.py:22
  (28 other events, 311.3 us)

commit v11 on v10

--- a/solution.py
+++ b/solution.py
@@ -27,10 +27,11 @@
     return lax.ppermute(value, "head", [(source, move(source)) for source in range(count)])
 
 
-def swap_seq(blocks):
+def swap_seq(blocks, far_first=True):
     half = len(blocks) // 2
     order = [*range(2, min(3, half)), *reversed(range(half, len(blocks))), *range(3, half)]
     order += [d for d in range(1, len(blocks)) if d not in order]
+    order = order if far_first else list(range(1, len(blocks)))
     swapped = [permute_seq(blocks[d], lambda q, d=d: q ^ d) for d in order]
     swapped = dict(zip(order, lax.optimization_barrier(swapped)))
     return [blocks[0]] + [swapped[d] for d in range(1, len(blocks))]
@@ -442,7 +443,7 @@
         scalars=1,
     )
     residual_there = crossed(residual)
-    arrived, residual_there = lax.optimization_barrier((swap_seq(payload), residual_there))
+    arrived, residual_there = lax.optimization_barrier((swap_seq(payload, far_first=False), residual_there))
     entered = local_call(
         scan_kernel,
         "carry",

time: 203 us -> 201 us (level)
  waiting for transfers between devices: 71.1 us -> 66 us
  starting transfers between devices: 86.9 us -> 90.5 us
    ppermute x5, waiting for transfers between devices: 13.6 us -> 8.98 us  [along(): return lax.ppermute(value, 'seq', perm)]
    ppermute x13, starting transfers between devices: 10.2 us -> 14 us  [permute_head(): lax.ppermute(value, 'head', [(source, move(source)) for source in range(c...]
    ppermute x29, starting transfers between devices: 54.5 us -> 51 us  [permute_seq(): lax.ppermute(value, 'seq', [(source, move(source)) for source in range(co...]
    ppermute x5, starting transfers between devices: 19 us -> 22.3 us  [along(): return lax.ppermute(value, 'seq', perm)]
  transfers between devices with their start and end apart: 50 -> 50, of which waited for: 28 -> 25; matrix products, arithmetic and copies ran while one was open for 4% -> 4% of each run, Pallas kernels for 12% -> 12%
where the time goes in v11:
time: 201 us; the launch traced here: 200 us
  starting transfers between devices  90.5 us (45%)
  waiting for transfers between devices  66 us (33%)
  Pallas kernels  30.3 us (15%)
  local copies, waits for them, and re-layouts  8.08 us (4%)
  matrix products  4.66 us (2%)
    ppermute x29, starting transfers between devices, permute_seq(): lax.ppermute(value, 'seq', [(source, move(source)) for source in range(co...  51 us
    ppermute x29, waiting for transfers between devices, permute_seq(): lax.ppermute(value, 'seq', [(source, move(source)) for source in range(co...  36.9 us
    pallas_call x15, Pallas kernels, local_call(): pl.pallas_call(kernel, out_shape=out_shape, in_specs=[pl.BlockSpec(memory...  30.3 us
    ppermute x5, starting transfers between devices, along(): return lax.ppermute(value, 'seq', perm)  22.3 us
    ppermute x13, waiting for transfers between devices, permute_head(): lax.ppermute(value, 'head', [(source, move(source)) for source in range(c...  20.1 us
    ppermute x13, starting transfers between devices, permute_head(): lax.ppermute(value, 'head', [(source, move(source)) for source in range(c...  14 us
    ppermute x5, waiting for transfers between devices, along(): return lax.ppermute(value, 'seq', perm)  8.98 us
    unnamed x22, local copies, waits for them, and re-layouts  5.41 us
  transfers between devices with their start and end apart: 50, of which 25 were waited for; matrix products, arithmetic and copies ran while one was open for 4% of the time, Pallas kernels for 12%

profile of v11, /device:TPU:0, one launch (start us, length us, event | category | flops | bytes accessed | tf_op | source)
XLA Modules:
  0.0 200.4 jit_solution(9741760703411500365)
XLA Ops:
  6.1 3.0 %collective-permute-start = (bf16[272,128]{1,0:T(8,128)(2,1)S(1)}, bf16[272,128]{1,0:T(8,128)(2,1)S(1)}, u32[]{:S(2)}, u32[]{:S(2)}) collective-permute-start(bf16[272,128]{1,0:T(8,128)(2,1)S(1)} %get-tuple-element.126), channel_id=1, source_target_pairs={{0,4},{4,0},{8,12},{12,8},{16,20},{20,16},{24,28},{28,24},{1,5},{5... | collective-permute-start | bytes 208904 | tf_op jit(solution)/shard_map/ppermute | solution.py:22
  11.1 4.2 %collective-permute-start.3 = (bf16[272,128]{1,0:T(8,128)(2,1)S(1)}, bf16[272,128]{1,0:T(8,128)(2,1)S(1)}, u32[]{:S(2)}, u32[]{:S(2)}) collective-permute-start(bf16[272,128]{1,0:T(8,128)(2,1)S(1)} %get-tuple-element.129), channel_id=1, source_target_pairs={{0,16},{4,20},{8,24},{12,28},{16,0},{20,4},{24,8},{28,12},{1,17},{... | collective-permute-start | bytes 208904 | tf_op jit(solution)/shard_map/ppermute | solution.py:22
  17.1 2.4 %collective-permute-start.5 = (bf16[272,128]{1,0:T(8,128)(2,1)S(1)}, bf16[272,128]{1,0:T(8,128)(2,1)S(1)}, u32[]{:S(2)}, u32[]{:S(2)}) collective-permute-start(bf16[272,128]{1,0:T(8,128)(2,1)S(1)} %get-tuple-element.131), channel_id=1, source_target_pairs={{0,24},{4,28},{8,16},{12,20},{16,8},{20,12},{24,0},{28,4},{1,25},{... | collective-permute-start | bytes 208904 | tf_op jit(solution)/shard_map/ppermute | solution.py:22
  20.9 2.5 %collective-permute-done.3.refs_4_ = bf16[272,128]{1,0:T(8,128)(2,1)S(1)} collective-permute-done((bf16[272,128]{1,0:T(8,128)(2,1)S(1)}, bf16[272,128]{1,0:T(8,128)(2,1)S(1)}, u32[]{:S(2)}, u32[]{:S(2)}) %collective-permute-start.3) | collective-permute-done | bytes 69664 | tf_op jit(solution)/shard_map/ppermute | solution.py:22
  23.4 3.9 %collective-permute-done.4.refs_5_ = bf16[272,128]{1,0:T(8,128)(2,1)S(1)} collective-permute-done((bf16[272,128]{1,0:T(8,128)(2,1)S(1)}, bf16[272,128]{1,0:T(8,128)(2,1)S(1)}, u32[]{:S(2)}, u32[]{:S(2)}) %collective-permute-start.4) | collective-permute-done | bytes 69664 | tf_op jit(solution)/shard_map/ppermute | solution.py:22
  27.6 3.2 %collective-permute-start.8 = (bf16[256,128]{1,0:T(8,128)(2,1)S(1)}, bf16[256,128]{1,0:T(8,128)(2,1)S(1)}, u32[]{:S(2)}, u32[]{:S(2)}) collective-permute-start(bf16[256,128]{1,0:T(8,128)(2,1)S(1)} %get-tuple-element.155), channel_id=1, source_target_pairs={{0,8},{4,12},{8,0},{12,4},{16,24},{20,28},{24,16},{28,20},{1,9},{5... | collective-permute-start | bytes 196616 | tf_op jit(solution)/shard_map/ppermute | solution.py:22
  32.3 2.2 %collective-permute-start.10 = (bf16[256,128]{1,0:T(8,128)(2,1)S(1)}, bf16[256,128]{1,0:T(8,128)(2,1)S(1)}, u32[]{:S(2)}, u32[]{:S(2)}) collective-permute-start(bf16[256,128]{1,0:T(8,128)(2,1)S(1)} %get-tuple-element.157), channel_id=1, source_target_pairs={{0,24},{4,28},{8,16},{12,20},{16,8},{20,12},{24,0},{28,4},{1,25},{... | collective-permute-start | bytes 196616 | tf_op jit(solution)/shard_map/ppermute | solution.py:22
  34.6 3.9 %collective-permute-start.12 = (bf16[256,128]{1,0:T(8,128)(2,1)S(1)}, bf16[256,128]{1,0:T(8,128)(2,1)S(1)}, u32[]{:S(2)}, u32[]{:S(2)}) collective-permute-start(bf16[256,128]{1,0:T(8,128)(2,1)S(1)} %get-tuple-element.159), channel_id=1, source_target_pairs={{0,16},{4,20},{8,24},{12,28},{16,0},{20,4},{24,8},{28,12},{1,17},{... | collective-permute-start | bytes 196616 | tf_op jit(solution)/shard_map/ppermute | solution.py:22
  39.1 4.9 %collective-permute-done.11.refs_5_ = bf16[256,128]{1,0:T(8,128)(2,1)S(1)} collective-permute-done((bf16[256,128]{1,0:T(8,128)(2,1)S(1)}, bf16[256,128]{1,0:T(8,128)(2,1)S(1)}, u32[]{:S(2)}, u32[]{:S(2)}) %collective-permute-start.11) | collective-permute-done | bytes 65568 | tf_op jit(solution)/shard_map/ppermute | solution.py:22
  47.4 2.9 %attend.1 = bf16[128,2048]{1,0:T(8,128)(2,1)S(1)} custom-call(s32[1]{0:T(128)} %bitcast.me_ref, f32[1,128]{1,0:T(1,128)S(1)} %get-tuple-element.141.doc_ref, f32[128,16]{1,0:T(8,128)S(1)} %get-tuple-element.142.sum_ref, f32[16,128]{1,0:T(8,128)S(1)} %get-tuple-element.143.sum_rows_ref, bf16[128,2048]{1,0:T(8,128)(2,1)S(1)} %copy-done, ...), custom_call_target="tpu_custom_call" | custom-call | flops 201326592 | bytes 2646532 | tf_op jit(solution)/shard_map/attend/pallas_call | solution.py:353
  50.3 3.3 %collective-permute-start.16 = (bf16[128,2048]{1,0:T(8,128)(2,1)S(1)}, bf16[128,2048]{1,0:T(8,128)(2,1)}, u32[]{:S(2)}, u32[]{:S(2)}) collective-permute-start(bf16[128,2048]{1,0:T(8,128)(2,1)S(1)} %attend.1), channel_id=1, source_target_pairs={{0,8},{4,12},{8,16},{12,20},{16,24},{20,28},{1,9},{5,13},{9,17},{1... | collective-permute-start | bytes 1572872 | tf_op jit(solution)/shard_map/ppermute | solution.py:490
  55.4 5.0 %collective-permute-start.20 = (bf16[128,2048]{1,0:T(8,128)(2,1)S(1)}, bf16[128,2048]{1,0:T(8,128)(2,1)S(1)}, u32[]{:S(2)}, u32[]{:S(2)}) collective-permute-start(bf16[128,2048]{1,0:T(8,128)(2,1)S(1)} %attend.1), channel_id=1, source_target_pairs={{0,24},{4,28},{24,0},{28,4},{1,25},{5,29},{25,1},{29,5},{2,26},{6,... | collective-permute-start | bytes 1572872 | tf_op jit(solution)/shard_map/ppermute | solution.py:490
  62.2 2.8 %collective-permute-done.16 = bf16[128,2048]{1,0:T(8,128)(2,1)} collective-permute-done((bf16[128,2048]{1,0:T(8,128)(2,1)S(1)}, bf16[128,2048]{1,0:T(8,128)(2,1)}, u32[]{:S(2)}, u32[]{:S(2)}) %collective-permute-start.16) | collective-permute-done | bytes 524320 | tf_op jit(solution)/shard_map/ppermute | solution.py:490
  65.0 11.4 %collective-permute-start.18 = (bf16[128,2048]{1,0:T(8,128)(2,1)}, bf16[128,2048]{1,0:T(8,128)(2,1)S(1)}, u32[]{:S(2)}, u32[]{:S(2)}) collective-permute-start(bf16[128,2048]{1,0:T(8,128)(2,1)} %collective-permute-done.16), channel_id=1, source_target_pairs={{0,8},{4,12},{8,16},{12,20},{16,24},{20,28},{1,9},{5,13},{9,17},{1... | collective-permute-start | bytes 1572872 | tf_op jit(solution)/shard_map/ppermute | solution.py:490
  77.7 2.6 %collective-permute-done.15 = bf16[2048,384]{1,0:T(8,128)(2,1)} collective-permute-done((bf16[2048,384]{1,0:T(8,128)(2,1)}, bf16[2048,384]{1,0:T(8,128)(2,1)}, u32[]{:S(2)}, u32[]{:S(2)}) %collective-permute-start.15) | collective-permute-done | bytes 1572896 | tf_op jit(solution)/shard_map/ppermute | solution.py:22
  85.9 5.8 %collective-permute-done.19 = bf16[128,2048]{1,0:T(8,128)(2,1)S(1)} collective-permute-done((bf16[128,2048]{1,0:T(8,128)(2,1)S(1)}, bf16[128,2048]{1,0:T(8,128)(2,1)S(1)}, u32[]{:S(2)}, u32[]{:S(2)}) %collective-permute-start.19) | collective-permute-done | bytes 524320 | tf_op jit(solution)/shard_map/ppermute | solution.py:490
  93.7 4.9 %collective-permute-start.23 = (bf16[128,768]{1,0:T(8,128)(2,1)S(1)}, bf16[128,768]{1,0:T(8,128)(2,1)S(1)}, u32[]{:S(2)}, u32[]{:S(2)}) collective-permute-start(bf16[128,768]{1,0:T(8,128)(2,1)S(1)} %get-tuple-element.190), channel_id=1, source_target_pairs={{0,2},{1,3},{2,0},{3,1},{4,6},{5,7},{6,4},{7,5},{8,10},{9,11},{10,... | collective-permute-start | bytes 589832 | tf_op jit(solution)/shard_map/ppermute | solution.py:27
  98.7 4.4 %collective-permute-done.22.refs_1_ = bf16[128,768]{1,0:T(8,128)(2,1)S(1)} collective-permute-done((bf16[128,768]{1,0:T(8,128)(2,1)S(1)}, bf16[128,768]{1,0:T(8,128)(2,1)S(1)}, u32[]{:S(2)}, u32[]{:S(2)}) %collective-permute-start.22) | collective-permute-done | bytes 196640 | tf_op jit(solution)/shard_map/ppermute | solution.py:27
  105.6 6.0 %collective-permute-start.25 = (bf16[64,768]{1,0:T(8,128)(2,1)S(1)}, bf16[64,768]{1,0:T(8,128)(2,1)S(1)}, u32[]{:S(2)}, u32[]{:S(2)}) collective-permute-start(bf16[64,768]{1,0:T(8,128)(2,1)S(1)} %get-tuple-element.193), channel_id=1, source_target_pairs={{0,24},{4,28},{8,16},{12,20},{16,8},{20,12},{24,0},{28,4},{1,25},{... | collective-permute-start | bytes 294920 | tf_op jit(solution)/shard_map/ppermute | solution.py:22
  114.8 6.2 %collective-permute-done.26.refs_2_ = bf16[64,768]{1,0:T(8,128)(2,1)S(1)} collective-permute-done((bf16[64,768]{1,0:T(8,128)(2,1)S(1)}, bf16[64,768]{1,0:T(8,128)(2,1)S(1)}, u32[]{:S(2)}, u32[]{:S(2)}) %collective-permute-start.26) | collective-permute-done | bytes 98336 | tf_op jit(solution)/shard_map/ppermute | solution.py:22
  121.9 2.5 %collective-permute-start.29 = (bf16[64,768]{1,0:T(8,128)(2,1)S(1)}, bf16[64,768]{1,0:T(8,128)(2,1)S(1)}, u32[]{:S(2)}, u32[]{:S(2)}) collective-permute-start(bf16[64,768]{1,0:T(8,128)(2,1)S(1)} %get-tuple-element.205), channel_id=1, source_target_pairs={{0,28},{4,24},{8,20},{12,16},{16,12},{20,8},{24,4},{28,0},{1,29},{... | collective-permute-start | bytes 294920 | tf_op jit(solution)/shard_map/ppermute | solution.py:22
  124.4 2.8 %collective-permute-start.31 = (bf16[64,768]{1,0:T(8,128)(2,1)S(1)}, bf16[64,768]{1,0:T(8,128)(2,1)S(1)}, u32[]{:S(2)}, u32[]{:S(2)}) collective-permute-start(bf16[64,768]{1,0:T(8,128)(2,1)S(1)} %get-tuple-element.207), channel_id=1, source_target_pairs={{0,12},{4,8},{8,4},{12,0},{16,28},{20,24},{24,20},{28,16},{1,13},{... | collective-permute-start | bytes 294920 | tf_op jit(solution)/shard_map/ppermute | solution.py:22
  130.4 3.1 %collective-permute-done.30.refs_2_ = bf16[64,768]{1,0:T(8,128)(2,1)S(1)} collective-permute-done((bf16[64,768]{1,0:T(8,128)(2,1)S(1)}, bf16[64,768]{1,0:T(8,128)(2,1)S(1)}, u32[]{:S(2)}, u32[]{:S(2)}) %collective-permute-start.30) | collective-permute-done | bytes 98336 | tf_op jit(solution)/shard_map/ppermute | solution.py:22
  137.5 9.2 %hidden.2 = (bf16[256,1152]{1,0:T(8,128)(2,1)S(1)}, bf16[4,1152,768]{2,1,0:T(8,128)(2,1)S(1)}) custom-call(s32[9]{0:T(128)S(1)} %stack.45.owner_ref, bf16[64,3072]{1,0:T(8,128)(2,1)S(1)} %pack.2.refs_0_, bf16[64,3072]{1,0:T(8,128)(2,1)S(1)} %collective-permute-done.28.refs_1_, bf16[64,3072]{1,0:T(8,128)(2,1)S(1)} %collective-permute-done.33.refs_2_, ...), custom_call_target="tpu_custom_call" | custom-call | flops 3623878656 | bytes 30474276 | tf_op jit(solution)/shard_map/hidden/pallas_call | solution.py:353
  152.1 3.2 %collective-permute-start.38 = (bf16[256,768]{1,0:T(8,128)(2,1)S(1)}, bf16[256,768]{1,0:T(8,128)(2,1)S(1)}, u32[]{:S(2)}, u32[]{:S(2)}) collective-permute-start(bf16[256,768]{1,0:T(8,128)(2,1)S(1)} %fusion), channel_id=1, source_target_pairs={{0,2},{1,3},{2,0},{3,1},{4,6},{5,7},{6,4},{7,5},{8,10},{9,11},{10,... | collective-permute-start | bytes 1179656 | tf_op jit(solution)/shard_map/ppermute | solution.py:27
  155.3 9.2 %hidden.3 = (bf16[256,1152]{1,0:T(8,128)(2,1)S(1)}, bf16[4,1152,768]{2,1,0:T(8,128)(2,1)S(1)}) custom-call(s32[9]{0:T(128)S(1)} %stack.45.owner_ref, bf16[64,3072]{1,0:T(8,128)(2,1)S(1)} %pack.3.refs_0_, bf16[64,3072]{1,0:T(8,128)(2,1)S(1)} %collective-permute-done.35.refs_1_, bf16[64,3072]{1,0:T(8,128)(2,1)S(1)} %collective-permute-done.40.refs_2_, ...), custom_call_target="tpu_custom_call" | custom-call | flops 3623878656 | bytes 30474276 | tf_op jit(solution)/shard_map/hidden/pallas_call | solution.py:353
  164.5 4.1 %collective-permute-done.38.refs_1_ = bf16[256,768]{1,0:T(8,128)(2,1)S(1)} collective-permute-done((bf16[256,768]{1,0:T(8,128)(2,1)S(1)}, bf16[256,768]{1,0:T(8,128)(2,1)S(1)}, u32[]{:S(2)}, u32[]{:S(2)}) %collective-permute-start.38) | collective-permute-done | bytes 393248 | tf_op jit(solution)/shard_map/ppermute | solution.py:27
  173.7 2.4 %collective-permute-start.43 = (bf16[256,768]{1,0:T(8,128)(2,1)S(1)}, bf16[256,768]{1,0:T(8,128)(2,1)S(1)}, u32[]{:S(2)}, u32[]{:S(2)}) collective-permute-start(bf16[256,768]{1,0:T(8,128)(2,1)S(1)} %fusion.1), channel_id=1, source_target_pairs={{0,2},{1,3},{2,0},{3,1},{4,6},{5,7},{6,4},{7,5},{8,10},{9,11},{10,... | collective-permute-start | bytes 1179656 | tf_op jit(solution)/shard_map/ppermute | solution.py:27
  177.0 2.6 %collective-permute-start.47 = (bf16[64,768]{1,0:T(8,128)(2,1)S(1)}, bf16[64,768]{1,0:T(8,128)(2,1)S(1)}, u32[]{:S(2)}, u32[]{:S(2)}) collective-permute-start(bf16[64,768]{1,0:T(8,128)(2,1)S(1)} %get-tuple-element.228), channel_id=1, source_target_pairs={{0,16},{4,20},{8,24},{12,28},{16,0},{20,4},{24,8},{28,12},{1,17},{... | collective-permute-start | bytes 294920 | tf_op jit(solution)/shard_map/ppermute | solution.py:22
  179.6 6.0 %collective-permute-done.43.refs_1_ = bf16[256,768]{1,0:T(8,128)(2,1)S(1)} collective-permute-done((bf16[256,768]{1,0:T(8,128)(2,1)S(1)}, bf16[256,768]{1,0:T(8,128)(2,1)S(1)}, u32[]{:S(2)}, u32[]{:S(2)}) %collective-permute-start.43) | collective-permute-done | bytes 393248 | tf_op jit(solution)/shard_map/ppermute | solution.py:27
  187.5 3.6 %collective-permute-start.48 = (bf16[64,768]{1,0:T(8,128)(2,1)S(1)}, bf16[64,768]{1,0:T(8,128)(2,1)S(1)}, u32[]{:S(2)}, u32[]{:S(2)}) collective-permute-start(bf16[64,768]{1,0:T(8,128)(2,1)S(1)} %get-tuple-element.236), channel_id=1, source_target_pairs={{0,12},{4,8},{8,4},{12,0},{16,28},{20,24},{24,20},{28,16},{1,13},{... | collective-permute-start | bytes 294920 | tf_op jit(solution)/shard_map/ppermute | solution.py:22
  194.3 2.9 %collective-permute-done.46.refs_5_ = bf16[64,768]{1,0:T(8,128)(2,1)S(1)} collective-permute-done((bf16[64,768]{1,0:T(8,128)(2,1)S(1)}, bf16[64,768]{1,0:T(8,128)(2,1)S(1)}, u32[]{:S(2)}, u32[]{:S(2)}) %collective-permute-start.46) | collective-permute-done | bytes 98336 | tf_op jit(solution)/shard_map/ppermute | solution.py:22
  (125 shorter events, 62.8 us)
Async XLA Ops:
  0.0 27.3 %collective-permute-start.7 = (bf16[128,768]{1,0:T(8,128)(2,1)}, bf16[128,768]{1,0:T(8,128)(2,1)S(1)}, u32[]{:S(2)}, u32[]{:S(2)}) collective-permute-start(bf16[128,768]{1,0:T(8,128)(2,1)} %param.21), channel_id=1, source_target_pairs={{0,0},{1,8},{2,16},{3,24},{4,4},{5,12},{6,20},{7,28},{8,1},{9,9},{... | collective-permute-start | bytes 589832 | tf_op jit(solution)/shard_map/ppermute | solution.py:422
  6.1 9.2 %collective-permute-start = (bf16[272,128]{1,0:T(8,128)(2,1)S(1)}, bf16[272,128]{1,0:T(8,128)(2,1)S(1)}, u32[]{:S(2)}, u32[]{:S(2)}) collective-permute-start(bf16[272,128]{1,0:T(8,128)(2,1)S(1)} %get-tuple-element.126), channel_id=1, source_target_pairs={{0,4},{4,0},{8,12},{12,8},{16,20},{20,16},{24,28},{28,24},{1,5},{5... | collective-permute-start | bytes 208904 | tf_op jit(solution)/shard_map/ppermute | solution.py:22
  11.1 12.3 %collective-permute-start.3 = (bf16[272,128]{1,0:T(8,128)(2,1)S(1)}, bf16[272,128]{1,0:T(8,128)(2,1)S(1)}, u32[]{:S(2)}, u32[]{:S(2)}) collective-permute-start(bf16[272,128]{1,0:T(8,128)(2,1)S(1)} %get-tuple-element.129), channel_id=1, source_target_pairs={{0,16},{4,20},{8,24},{12,28},{16,0},{20,4},{24,8},{28,12},{1,17},{... | collective-permute-start | bytes 208904 | tf_op jit(solution)/shard_map/ppermute | solution.py:22
  15.3 12.0 %collective-permute-start.4 = (bf16[272,128]{1,0:T(8,128)(2,1)S(1)}, bf16[272,128]{1,0:T(8,128)(2,1)S(1)}, u32[]{:S(2)}, u32[]{:S(2)}) collective-permute-start(bf16[272,128]{1,0:T(8,128)(2,1)S(1)} %get-tuple-element.130), channel_id=1, source_target_pairs={{0,20},{4,16},{8,28},{12,24},{16,4},{20,0},{24,12},{28,8},{1,21},{... | collective-permute-start | bytes 208904 | tf_op jit(solution)/shard_map/ppermute | solution.py:22
  17.1 10.2 %collective-permute-start.5 = (bf16[272,128]{1,0:T(8,128)(2,1)S(1)}, bf16[272,128]{1,0:T(8,128)(2,1)S(1)}, u32[]{:S(2)}, u32[]{:S(2)}) collective-permute-start(bf16[272,128]{1,0:T(8,128)(2,1)S(1)} %get-tuple-element.131), channel_id=1, source_target_pairs={{0,24},{4,28},{8,16},{12,20},{16,8},{20,12},{24,0},{28,4},{1,25},{... | collective-permute-start | bytes 208904 | tf_op jit(solution)/shard_map/ppermute | solution.py:22
  27.6 10.9 %collective-permute-start.8 = (bf16[256,128]{1,0:T(8,128)(2,1)S(1)}, bf16[256,128]{1,0:T(8,128)(2,1)S(1)}, u32[]{:S(2)}, u32[]{:S(2)}) collective-permute-start(bf16[256,128]{1,0:T(8,128)(2,1)S(1)} %get-tuple-element.155), channel_id=1, source_target_pairs={{0,8},{4,12},{8,0},{12,4},{16,24},{20,28},{24,16},{28,20},{1,9},{5... | collective-permute-start | bytes 196616 | tf_op jit(solution)/shard_map/ppermute | solution.py:22
  34.6 9.4 %collective-permute-start.11 = (bf16[256,128]{1,0:T(8,128)(2,1)S(1)}, bf16[256,128]{1,0:T(8,128)(2,1)S(1)}, u32[]{:S(2)}, u32[]{:S(2)}) collective-permute-start(bf16[256,128]{1,0:T(8,128)(2,1)S(1)} %get-tuple-element.158), channel_id=1, source_target_pairs={{0,20},{4,16},{8,28},{12,24},{16,4},{20,0},{24,12},{28,8},{1,21},{... | collective-permute-start | bytes 196616 | tf_op jit(solution)/shard_map/ppermute | solution.py:22
  34.6 9.4 %collective-permute-start.12 = (bf16[256,128]{1,0:T(8,128)(2,1)S(1)}, bf16[256,128]{1,0:T(8,128)(2,1)S(1)}, u32[]{:S(2)}, u32[]{:S(2)}) collective-permute-start(bf16[256,128]{1,0:T(8,128)(2,1)S(1)} %get-tuple-element.159), channel_id=1, source_target_pairs={{0,16},{4,20},{8,24},{12,28},{16,0},{20,4},{24,8},{28,12},{1,17},{... | collective-permute-start | bytes 196616 | tf_op jit(solution)/shard_map/ppermute | solution.py:22
  45.5 34.8 %collective-permute-start.15 = (bf16[2048,384]{1,0:T(8,128)(2,1)}, bf16[2048,384]{1,0:T(8,128)(2,1)}, u32[]{:S(2)}, u32[]{:S(2)}) collective-permute-start(bf16[2048,384]{1,0:T(8,128)(2,1)} %param.20), channel_id=1, source_target_pairs={{0,4},{4,0},{8,12},{12,8},{16,20},{20,16},{24,28},{28,24},{1,5},{5... | collective-permute-start | bytes 4718600 | tf_op jit(solution)/shard_map/ppermute | solution.py:22
  50.3 14.7 %collective-permute-start.16 = (bf16[128,2048]{1,0:T(8,128)(2,1)S(1)}, bf16[128,2048]{1,0:T(8,128)(2,1)}, u32[]{:S(2)}, u32[]{:S(2)}) collective-permute-start(bf16[128,2048]{1,0:T(8,128)(2,1)S(1)} %attend.1), channel_id=1, source_target_pairs={{0,8},{4,12},{8,16},{12,20},{16,24},{20,28},{1,9},{5,13},{9,17},{1... | collective-permute-start | bytes 1572872 | tf_op jit(solution)/shard_map/ppermute | solution.py:490
  53.6 22.8 %collective-permute-start.17 = (bf16[128,2048]{1,0:T(8,128)(2,1)S(1)}, bf16[128,2048]{1,0:T(8,128)(2,1)S(1)}, u32[]{:S(2)}, u32[]{:S(2)}) collective-permute-start(bf16[128,2048]{1,0:T(8,128)(2,1)S(1)} %attend.1), channel_id=1, source_target_pairs={{8,0},{12,4},{16,8},{20,12},{24,16},{28,20},{9,1},{13,5},{17,9},{2... | collective-permute-start | bytes 1572872 | tf_op jit(solution)/shard_map/ppermute | solution.py:490
  55.4 37.0 %collective-permute-start.20 = (bf16[128,2048]{1,0:T(8,128)(2,1)S(1)}, bf16[128,2048]{1,0:T(8,128)(2,1)S(1)}, u32[]{:S(2)}, u32[]{:S(2)}) collective-permute-start(bf16[128,2048]{1,0:T(8,128)(2,1)S(1)} %attend.1), channel_id=1, source_target_pairs={{0,24},{4,28},{24,0},{28,4},{1,25},{5,29},{25,1},{29,5},{2,26},{6,... | collective-permute-start | bytes 1572872 | tf_op jit(solution)/shard_map/ppermute | solution.py:490
  65.0 20.4 %collective-permute-start.18 = (bf16[128,2048]{1,0:T(8,128)(2,1)}, bf16[128,2048]{1,0:T(8,128)(2,1)S(1)}, u32[]{:S(2)}, u32[]{:S(2)}) collective-permute-start(bf16[128,2048]{1,0:T(8,128)(2,1)} %collective-permute-done.16), channel_id=1, source_target_pairs={{0,8},{4,12},{8,16},{12,20},{16,24},{20,28},{1,9},{5,13},{9,17},{1... | collective-permute-start | bytes 1572872 | tf_op jit(solution)/shard_map/ppermute | solution.py:490
  76.4 15.3 %collective-permute-start.19 = (bf16[128,2048]{1,0:T(8,128)(2,1)S(1)}, bf16[128,2048]{1,0:T(8,128)(2,1)S(1)}, u32[]{:S(2)}, u32[]{:S(2)}) collective-permute-start(bf16[128,2048]{1,0:T(8,128)(2,1)S(1)} %collective-permute-done.17), channel_id=1, source_target_pairs={{8,0},{12,4},{16,8},{20,12},{24,16},{28,20},{9,1},{13,5},{17,9},{2... | collective-permute-start | bytes 1572872 | tf_op jit(solution)/shard_map/ppermute | solution.py:490
  93.7 9.4 %collective-permute-start.22 = (bf16[128,768]{1,0:T(8,128)(2,1)S(1)}, bf16[128,768]{1,0:T(8,128)(2,1)S(1)}, u32[]{:S(2)}, u32[]{:S(2)}) collective-permute-start(bf16[128,768]{1,0:T(8,128)(2,1)S(1)} %get-tuple-element.189), channel_id=1, source_target_pairs={{0,1},{1,2},{2,3},{3,0},{4,5},{5,6},{6,7},{7,4},{8,9},{9,10},{10,1... | collective-permute-start | bytes 589832 | tf_op jit(solution)/shard_map/ppermute | solution.py:27
  93.7 10.6 %collective-permute-start.23 = (bf16[128,768]{1,0:T(8,128)(2,1)S(1)}, bf16[128,768]{1,0:T(8,128)(2,1)S(1)}, u32[]{:S(2)}, u32[]{:S(2)}) collective-permute-start(bf16[128,768]{1,0:T(8,128)(2,1)S(1)} %get-tuple-element.190), channel_id=1, source_target_pairs={{0,2},{1,3},{2,0},{3,1},{4,6},{5,7},{6,4},{7,5},{8,10},{9,11},{10,... | collective-permute-start | bytes 589832 | tf_op jit(solution)/shard_map/ppermute | solution.py:27
  105.6 9.3 %collective-permute-start.25 = (bf16[64,768]{1,0:T(8,128)(2,1)S(1)}, bf16[64,768]{1,0:T(8,128)(2,1)S(1)}, u32[]{:S(2)}, u32[]{:S(2)}) collective-permute-start(bf16[64,768]{1,0:T(8,128)(2,1)S(1)} %get-tuple-element.193), channel_id=1, source_target_pairs={{0,24},{4,28},{8,16},{12,20},{16,8},{20,12},{24,0},{28,4},{1,25},{... | collective-permute-start | bytes 294920 | tf_op jit(solution)/shard_map/ppermute | solution.py:22
  111.5 9.5 %collective-permute-start.26 = (bf16[64,768]{1,0:T(8,128)(2,1)S(1)}, bf16[64,768]{1,0:T(8,128)(2,1)S(1)}, u32[]{:S(2)}, u32[]{:S(2)}) collective-permute-start(bf16[64,768]{1,0:T(8,128)(2,1)S(1)} %get-tuple-element.194), channel_id=1, source_target_pairs={{0,16},{4,20},{8,24},{12,28},{16,0},{20,4},{24,8},{28,12},{1,17},{... | collective-permute-start | bytes 294920 | tf_op jit(solution)/shard_map/ppermute | solution.py:22
  121.3 14.4 %collective-permute-start.28 = (bf16[64,3072]{1,0:T(8,128)(2,1)S(1)}, bf16[64,3072]{1,0:T(8,128)(2,1)S(1)}, u32[]{:S(2)}, u32[]{:S(2)}) collective-permute-start(bf16[64,3072]{1,0:T(8,128)(2,1)S(1)} %pack.2.refs_0_), channel_id=1, source_target_pairs={{0,2},{1,3},{2,0},{3,1},{4,6},{5,7},{6,4},{7,5},{8,10},{9,11},{10,... | collective-permute-start | bytes 1179656 | tf_op jit(solution)/shard_map/ppermute | solution.py:27
  121.9 8.5 %collective-permute-start.29 = (bf16[64,768]{1,0:T(8,128)(2,1)S(1)}, bf16[64,768]{1,0:T(8,128)(2,1)S(1)}, u32[]{:S(2)}, u32[]{:S(2)}) collective-permute-start(bf16[64,768]{1,0:T(8,128)(2,1)S(1)} %get-tuple-element.205), channel_id=1, source_target_pairs={{0,28},{4,24},{8,20},{12,16},{16,12},{20,8},{24,4},{28,0},{1,29},{... | collective-permute-start | bytes 294920 | tf_op jit(solution)/shard_map/ppermute | solution.py:22
  124.4 9.1 %collective-permute-start.30 = (bf16[64,768]{1,0:T(8,128)(2,1)S(1)}, bf16[64,768]{1,0:T(8,128)(2,1)S(1)}, u32[]{:S(2)}, u32[]{:S(2)}) collective-permute-start(bf16[64,768]{1,0:T(8,128)(2,1)S(1)} %get-tuple-element.206), channel_id=1, source_target_pairs={{0,20},{4,16},{8,28},{12,24},{16,4},{20,0},{24,12},{28,8},{1,21},{... | collective-permute-start | bytes 294920 | tf_op jit(solution)/shard_map/ppermute | solution.py:22
  124.4 9.1 %collective-permute-start.31 = (bf16[64,768]{1,0:T(8,128)(2,1)S(1)}, bf16[64,768]{1,0:T(8,128)(2,1)S(1)}, u32[]{:S(2)}, u32[]{:S(2)}) collective-permute-start(bf16[64,768]{1,0:T(8,128)(2,1)S(1)} %get-tuple-element.207), channel_id=1, source_target_pairs={{0,12},{4,8},{8,4},{12,0},{16,28},{20,24},{24,20},{28,16},{1,13},{... | collective-permute-start | bytes 294920 | tf_op jit(solution)/shard_map/ppermute | solution.py:22
  135.8 11.5 %collective-permute-start.35 = (bf16[64,3072]{1,0:T(8,128)(2,1)S(1)}, bf16[64,3072]{1,0:T(8,128)(2,1)S(1)}, u32[]{:S(2)}, u32[]{:S(2)}) collective-permute-start(bf16[64,3072]{1,0:T(8,128)(2,1)S(1)} %pack.3.refs_0_), channel_id=1, source_target_pairs={{0,2},{1,3},{2,0},{3,1},{4,6},{5,7},{6,4},{7,5},{8,10},{9,11},{10,... | collective-permute-start | bytes 1179656 | tf_op jit(solution)/shard_map/ppermute | solution.py:27
  150.2 18.6 %collective-permute-start.36 = (bf16[128,768]{1,0:T(8,128)(2,1)S(1)}, bf16[128,768]{1,0:T(8,128)(2,1)S(1)}, u32[]{:S(2)}, u32[]{:S(2)}) collective-permute-start(bf16[128,768]{1,0:T(8,128)(2,1)S(1)} %get-tuple-element.218), channel_id=1, source_target_pairs={{0,0},{1,8},{2,16},{3,24},{4,4},{5,12},{6,20},{7,28},{8,1},{9,9},{... | collective-permute-start | bytes 589832 | tf_op jit(solution)/shard_map/ppermute | solution.py:422
  152.1 16.5 %collective-permute-start.38 = (bf16[256,768]{1,0:T(8,128)(2,1)S(1)}, bf16[256,768]{1,0:T(8,128)(2,1)S(1)}, u32[]{:S(2)}, u32[]{:S(2)}) collective-permute-start(bf16[256,768]{1,0:T(8,128)(2,1)S(1)} %fusion), channel_id=1, source_target_pairs={{0,2},{1,3},{2,0},{3,1},{4,6},{5,7},{6,4},{7,5},{8,10},{9,11},{10,... | collective-permute-start | bytes 1179656 | tf_op jit(solution)/shard_map/ppermute | solution.py:27
  173.7 11.9 %collective-permute-start.43 = (bf16[256,768]{1,0:T(8,128)(2,1)S(1)}, bf16[256,768]{1,0:T(8,128)(2,1)S(1)}, u32[]{:S(2)}, u32[]{:S(2)}) collective-permute-start(bf16[256,768]{1,0:T(8,128)(2,1)S(1)} %fusion.1), channel_id=1, source_target_pairs={{0,2},{1,3},{2,0},{3,1},{4,6},{5,7},{6,4},{7,5},{8,10},{9,11},{10,... | collective-permute-start | bytes 1179656 | tf_op jit(solution)/shard_map/ppermute | solution.py:27
  176.1 11.4 %collective-permute-start.39 = (bf16[64,768]{1,0:T(8,128)(2,1)S(1)}, bf16[64,768]{1,0:T(8,128)(2,1)S(1)}, u32[]{:S(2)}, u32[]{:S(2)}) collective-permute-start(bf16[64,768]{1,0:T(8,128)(2,1)S(1)} %get-tuple-element.222), channel_id=1, source_target_pairs={{0,8},{4,12},{8,0},{12,4},{16,24},{20,28},{24,16},{28,20},{1,9},{5... | collective-permute-start | bytes 294920 | tf_op jit(solution)/shard_map/ppermute | solution.py:22
  176.1 15.0 %collective-permute-start.45 = (bf16[64,768]{1,0:T(8,128)(2,1)S(1)}, bf16[64,768]{1,0:T(8,128)(2,1)S(1)}, u32[]{:S(2)}, u32[]{:S(2)}) collective-permute-start(bf16[64,768]{1,0:T(8,128)(2,1)S(1)} %get-tuple-element.229), channel_id=1, source_target_pairs={{0,24},{4,28},{8,16},{12,20},{16,8},{20,12},{24,0},{28,4},{1,25},{... | collective-permute-start | bytes 294920 | tf_op jit(solution)/shard_map/ppermute | solution.py:22
  177.0 15.6 %collective-permute-start.47 = (bf16[64,768]{1,0:T(8,128)(2,1)S(1)}, bf16[64,768]{1,0:T(8,128)(2,1)S(1)}, u32[]{:S(2)}, u32[]{:S(2)}) collective-permute-start(bf16[64,768]{1,0:T(8,128)(2,1)S(1)} %get-tuple-element.228), channel_id=1, source_target_pairs={{0,16},{4,20},{8,24},{12,28},{16,0},{20,4},{24,8},{28,12},{1,17},{... | collective-permute-start | bytes 294920 | tf_op jit(solution)/shard_map/ppermute | solution.py:22
  185.8 8.6 %collective-permute-start.44 = (bf16[64,768]{1,0:T(8,128)(2,1)S(1)}, bf16[64,768]{1,0:T(8,128)(2,1)S(1)}, u32[]{:S(2)}, u32[]{:S(2)}) collective-permute-start(bf16[64,768]{1,0:T(8,128)(2,1)S(1)} %get-tuple-element.234), channel_id=1, source_target_pairs={{0,28},{4,24},{8,20},{12,16},{16,12},{20,8},{24,4},{28,0},{1,29},{... | collective-permute-start | bytes 294920 | tf_op jit(solution)/shard_map/ppermute | solution.py:22
  187.4 9.8 %collective-permute-start.46 = (bf16[64,768]{1,0:T(8,128)(2,1)S(1)}, bf16[64,768]{1,0:T(8,128)(2,1)S(1)}, u32[]{:S(2)}, u32[]{:S(2)}) collective-permute-start(bf16[64,768]{1,0:T(8,128)(2,1)S(1)} %get-tuple-element.235), channel_id=1, source_target_pairs={{0,20},{4,16},{8,28},{12,24},{16,4},{20,0},{24,12},{28,8},{1,21},{... | collective-permute-start | bytes 294920 | tf_op jit(solution)/shard_map/ppermute | solution.py:22
  187.5 9.8 %collective-permute-start.48 = (bf16[64,768]{1,0:T(8,128)(2,1)S(1)}, bf16[64,768]{1,0:T(8,128)(2,1)S(1)}, u32[]{:S(2)}, u32[]{:S(2)}) collective-permute-start(bf16[64,768]{1,0:T(8,128)(2,1)S(1)} %get-tuple-element.236), channel_id=1, source_target_pairs={{0,12},{4,8},{8,4},{12,0},{16,28},{20,24},{24,20},{28,16},{1,13},{... | collective-permute-start | bytes 294920 | tf_op jit(solution)/shard_map/ppermute | solution.py:22
  (28 other events, 310.0 us)
